TPU v7x, 32 devices: a whole 2x2x4 slice. The times are simulated.
32 devices in a mesh: groups: 2 (over y), blk: 4 (over x, core), ulysses: 4 (over z).
Axes of the slice: x: 2, y: 2, z: 4, core: 2. Of those that a mesh axis runs over, the one named last changes fastest.
Arguments:
- query_proj: bfloat16 [1024, 1024], P(('groups', 'blk', 'ulysses')), parts along dimension 0, may hold values from -200 to 200
- key_proj: bfloat16 [1024, 1024], P(('groups', 'blk', 'ulysses')), parts along dimension 0, may hold values from -200 to 200
- value_proj: bfloat16 [1024, 1024], P(('groups', 'blk', 'ulysses')), parts along dimension 0, may hold values from -6 to 6
- query_gain: float32 [1024], replicated, may hold values from 1.2 to 2.4
- key_gain: float32 [1024], replicated, may hold values from 1.2 to 2.4
- control: bfloat16 [1024, 384], P(('groups', 'blk', 'ulysses')), parts along dimension 0, may hold values from -6 to 6
- hint_weight: bfloat16 [384, 1024], replicated, may hold values from -0.3125 to 0.3125
- hint_gain: float32 [8, 1024], replicated, may hold values from 0.3 to 3
- owner_map: int32 [32, 4], P(('groups', 'blk', 'ulysses')), parts along dimension 0, may hold values from 0 to 3, each once within a row
- layer_index: int32 [32], P(('groups', 'blk', 'ulysses')), parts along dimension 0, may hold values from 0 to 7
Outputs:
- block_out: bfloat16 [1024, 1024], P(('groups', 'blk', 'ulysses')), parts along dimension 0
There are 2 independent parts, one for each index of `groups`. A program takes and returns all parts, laid end to end along the dimension named above; an argument that names none is the same for every part. Nothing has to cross between parts.
Inputs may be any that keep to these rules, and one draw needn't show every extreme that they name: `owner_map`: each row is a permutation of 0 to 3.
All inputs are finite; a program needn't handle non-finite values.
Results may differ from a plain program's by a relative error of at most 0.008.
Values may be sent and summed in bfloat16 or wider, within the bound.
No kernel may reach another device: no remote copies, remote signals or barrier semaphores. Data moves between devices by JAX's collectives and lax.ppermute only.
A program may use at most 64 MiB of HBM per device.

v0:
```python
import jax
import jax.numpy as jnp
from jax import lax
from jax.sharding import PartitionSpec as P

HEAD_DIM = 128


def normalize_rows(rows, gain):
    values = rows.astype(jnp.float32)
    scale = lax.rsqrt(jnp.mean(values * values, axis=-1, keepdims=True) + 1e-06)
    return (values * scale * gain).astype(jnp.bfloat16)


def block_size(count):
    block = min(count, 1024)
    while count % block:
        block = block - 1
    return block


def make_fold(queries):
    rows = queries.shape[0]
    heads = queries.shape[1] // HEAD_DIM
    shaped = queries.reshape(rows, heads, HEAD_DIM)
    factor = HEAD_DIM ** (-0.5)

    def update(state, pair):
        peak, totals, accum = state
        key_block, value_block = pair
        scores = (
            jnp.einsum("qhd,khd->hqk", shaped, key_block, preferred_element_type=jnp.float32)
            * factor
        )
        new_peak = jnp.maximum(peak, jnp.max(scores, axis=-1))
        correction = jnp.exp(peak - new_peak)
        expo = jnp.exp(scores - new_peak[:, :, None])
        totals = totals * correction + jnp.sum(expo, axis=-1)
        mixed = jnp.einsum(
            "hqk,khd->hqd",
            expo.astype(jnp.bfloat16),
            value_block,
            preferred_element_type=jnp.float32,
        )
        accum = accum * correction[:, :, None] + mixed
        return ((new_peak, totals, accum), None)

    def fold(carry, piece, start):
        keys, values = piece
        count = keys.shape[0]
        block = block_size(count)
        key_blocks = keys.reshape(count // block, block, heads, HEAD_DIM)
        value_blocks = values.reshape(count // block, block, heads, HEAD_DIM)
        result, unused = lax.scan(update, carry, (key_blocks, value_blocks))
        return result

    start_state = (
        jnp.full((heads, rows), -1e30, jnp.float32),
        jnp.zeros((heads, rows), jnp.float32),
        jnp.zeros((heads, rows, HEAD_DIM), jnp.float32),
    )
    return (fold, start_state)


def finish(state):
    peak, totals, accum = state
    heads, rows = totals.shape
    output = (accum / totals[:, :, None]).astype(jnp.bfloat16)
    return output.transpose(1, 0, 2).reshape(rows, heads * HEAD_DIM)


def make_hint(patches, hint_weight):
    normed = normalize_rows(patches, jnp.float32(1.0))
    return jnp.dot(normed, hint_weight, preferred_element_type=jnp.float32).astype(jnp.bfloat16)


def shards(
    query_proj,
    key_proj,
    value_proj,
    query_gain,
    key_gain,
    control,
    hint_weight,
    hint_gain,
    owner_map,
    layer_index,
):
    query_normed = normalize_rows(query_proj, query_gain)
    key_normed = normalize_rows(key_proj, key_gain)
    query_heads, key_heads, value_heads = (
        lax.all_to_all(query_normed, "ulysses", split_axis=1, concat_axis=0, tiled=True),
        lax.all_to_all(key_normed, "ulysses", split_axis=1, concat_axis=0, tiled=True),
        lax.all_to_all(value_proj, "ulysses", split_axis=1, concat_axis=0, tiled=True),
    )
    fold, start_state = make_fold(query_heads)
    state = fold(
        start_state,
        (
            lax.all_gather(key_heads, "blk", axis=0, tiled=True),
            lax.all_gather(value_heads, "blk", axis=0, tiled=True),
        ),
        jnp.int32(0),
    )
    attended = lax.all_to_all(finish(state), "ulysses", split_axis=0, concat_axis=1, tiled=True)
    owners = lax.axis_size("ulysses")
    tok_rows = control.shape[0]
    slab_rows = tok_rows // owners
    positions = jnp.arange(owners, dtype=jnp.int32)
    match = (owner_map[0][:, None] == positions[None, :]).astype(jnp.int32)
    inverse = jnp.sum(positions[:, None] * match, axis=0)
    gain_row = lax.dynamic_index_in_dim(hint_gain, layer_index[0], 0, keepdims=False)
    outgoing = jnp.take(control.reshape(owners, slab_rows, control.shape[1]), inverse, axis=0)
    arrived = lax.all_to_all(outgoing, "ulysses", split_axis=0, concat_axis=0, tiled=True).reshape(
        tok_rows, control.shape[1]
    )
    placed = make_hint(arrived, hint_weight)
    return (attended.astype(jnp.float32) + placed.astype(jnp.float32) * gain_row).astype(
        jnp.bfloat16
    )


def solution(mesh):
    return jax.shard_map(
        shards,
        mesh=mesh,
        in_specs=(
            P(("groups", "blk", "ulysses"), None),
            P(("groups", "blk", "ulysses"), None),
            P(("groups", "blk", "ulysses"), None),
            P(),
            P(),
            P(("groups", "blk", "ulysses"), None),
            P(),
            P(),
            P(("groups", "blk", "ulysses"), None),
            P(("groups", "blk", "ulysses")),
        ),
        out_specs=P(("groups", "blk", "ulysses"), None),
        check_vma=False,
    )
```

profile of v0, /device:TPU:0, one launch (start us, length us, event | category | flops | bytes accessed | tf_op | source)
XLA Modules:
  0.0 61.8 jit_solution(5780773453348342455)
XLA Ops:
  0.0 0.0 copy-start
  0.0 0.0 copy-start.6
  0.0 0.7 %copy-done.6 = s32[1,4]{1,0:T(1,128)S(1)} copy-done((s32[1,4]{1,0:T(1,128)S(1)}, s32[1,4]{1,0:T(1,128)}, u32[]{:S(2)}) %copy-start.6) | copy-done | bytes 40
  0.7 0.1 select_reduce_fusion
  0.8 0.0 copy-start.1
  0.9 1.3 %gather_fusion = bf16[4,8,384]{2,1,0:T(8,128)(2,1)S(1)} fusion(bf16[4,8,384]{2,1,0:T(8,128)(2,1)} %bitcast.69, s32[1024]{0:T(1024)S(1)} %pad_clamp_fusion), kind=kCustom, calls=%fused_computation | custom fusion | bytes 49168 | tf_op jit(solution)/shard_map/jit(_take)/gather | solution.py:113
  2.2 0.7 %broadcast_select_fusion = bf16[4,8,384]{2,1,0:T(8,128)(2,1)} fusion(bf16[4,8,384]{2,1,0:T(8,128)(2,1)S(1)} %gather_fusion, pred[4]{0:T(512)(128)(4,1)S(1)} %compare_and_fusion), kind=kLoop, calls=%fused_computation.36 | loop fusion | flops 12288 | bytes 49156 | tf_op jit(solution)/shard_map/jit(_take)/select_n | solution.py:113
  2.9 0.0 copy-start.2
  2.9 6.4 %all-to-all-start.4 = ((bf16[4,8,384]{2,1,0:T(8,128)(2,1)}), bf16[4,8,384]{2,1,0:T(8,128)(2,1)S(1)}, u32[]{:S(2)}, u32[]{:S(2)}) async-start(bf16[4,8,384]{2,1,0:T(8,128)(2,1)} %broadcast_select_fusion), calls=%async_computation.4 | async-start | bytes 49152 | tf_op jit(solution)/shard_map/all_to_all | solution.py:114
  9.3 0.0 copy-done.1
  9.3 0.1 fusion.14
  9.5 0.0 copy-done.2
  9.5 0.0 copy-start.4
  9.5 0.1 fusion.11
  10.3 0.0 copy-done.4
  10.3 0.0 copy-start.5
  10.3 0.1 fusion.16
  10.4 0.6 copy-done.5
  11.0 0.1 fusion.13
  11.1 0.8 %constant_dynamic-slice_fusion = f32[1,1024]{1,0:T(1,128)S(1)} fusion(f32[8,1024]{1,0:T(8,128)} %param.17, s32[]{:T(128)S(6)} %select_n.27), kind=kLoop, calls=%fused_computation.50 | loop fusion | bytes 8196 | tf_op jit(solution)/shard_map/jit(dynamic_index_in_dim)/dynamic_slice | solution.py:112
  11.8 0.6 copy.63
  12.4 0.0 copy-start.3
  12.4 0.6 %copy.64 = bf16[4,4,8,256]{3,2,0,1:T(8,128)(2,1)} copy(bf16[4,4,8,256]{3,2,1,0:T(8,128)(2,1)S(1)} %bitcast.67) | data formatting | bytes 131072 | tf_op jit(solution)/shard_map/all_to_all | solution.py:92
  13.1 0.2 copy-done.3
  13.3 0.6 %copy.62 = bf16[4,4,8,256]{3,2,0,1:T(8,128)(2,1)} copy(bf16[4,4,8,256]{3,2,1,0:T(8,128)(2,1)S(1)} %bitcast.68) | data formatting | bytes 131072 | tf_op jit(solution)/shard_map/all_to_all | solution.py:94
  13.9 1.0 %all-to-all-done.4 = bf16[4,8,384]{2,1,0:T(8,128)(2,1)S(1)} async-done(((bf16[4,8,384]{2,1,0:T(8,128)(2,1)}), bf16[4,8,384]{2,1,0:T(8,128)(2,1)S(1)}, u32[]{:S(2)}, u32[]{:S(2)}) %all-to-all-start.4) | async-done | bytes 24608 | tf_op jit(solution)/shard_map/all_to_all | solution.py:114
  15.0 4.1 %all-to-all-start.1 = ((bf16[32,4,256]{2,0,1:T(8,128)(2,1)}), bf16[32,4,256]{2,0,1:T(8,128)(2,1)S(1)}, u32[]{:S(2)}, u32[]{:S(2)}) async-start(bf16[32,4,256]{2,0,1:T(8,128)(2,1)} %bitcast.55), calls=%async_computation.1 | async-start | bytes 131072 | tf_op jit(solution)/shard_map/all_to_all | solution.py:93
  19.0 0.1 fusion.20
  19.1 5.7 %all-to-all-done.1 = bf16[32,4,256]{2,0,1:T(8,128)(2,1)S(1)} async-done(((bf16[32,4,256]{2,0,1:T(8,128)(2,1)}), bf16[32,4,256]{2,0,1:T(8,128)(2,1)S(1)}, u32[]{:S(2)}, u32[]{:S(2)}) %all-to-all-start.1) | async-done | bytes 65568 | tf_op jit(solution)/shard_map/all_to_all | solution.py:93
  24.8 3.3 %all-to-all-start = ((bf16[32,4,256]{2,0,1:T(8,128)(2,1)}), bf16[32,4,256]{2,0,1:T(8,128)(2,1)S(1)}, u32[]{:S(2)}, u32[]{:S(2)}) async-start(bf16[32,4,256]{2,0,1:T(8,128)(2,1)} %bitcast.56), calls=%async_computation | async-start | bytes 131072 | tf_op jit(solution)/shard_map/all_to_all | solution.py:92
  28.1 5.8 %all_gather.6 = bf16[512,256]{1,0:T(8,128)(2,1)S(1)} all-gather(bf16[128,256]{1,0:T(8,128)(2,1)S(1)} %bitcast.63), channel_id=1, replica_groups=mesh['groups'=2,'blk'=4,'ulysses'=4] {'blk'}, dimensions={0}, use_global_device_ids=true | all-gather | bytes 327680 | tf_op jit(solution)/shard_map/all_gather | solution.py:100
  33.9 0.1 copy.41
  34.0 0.0 all-to-all-done
  34.0 5.1 %all-to-all-start.2 = ((bf16[32,4,256]{2,0,1:T(8,128)(2,1)}), bf16[32,4,256]{2,0,1:T(8,128)(2,1)S(1)}, u32[]{:S(2)}, u32[]{:S(2)}) async-start(bf16[32,4,256]{2,0,1:T(8,128)(2,1)} %bitcast.54), calls=%async_computation.2 | async-start | bytes 131072 | tf_op jit(solution)/shard_map/all_to_all | solution.py:94
  39.1 0.3 fusion.24
  39.4 0.2 fusion.7
  39.6 5.2 %all-to-all-done.2 = bf16[32,4,256]{2,0,1:T(8,128)(2,1)S(1)} async-done(((bf16[32,4,256]{2,0,1:T(8,128)(2,1)}), bf16[32,4,256]{2,0,1:T(8,128)(2,1)S(1)}, u32[]{:S(2)}, u32[]{:S(2)}) %all-to-all-start.2) | async-done | bytes 65568 | tf_op jit(solution)/shard_map/all_to_all | solution.py:94
  44.8 5.8 %all_gather.7 = bf16[512,256]{1,0:T(8,128)(2,1)S(1)} all-gather(bf16[128,256]{1,0:T(8,128)(2,1)S(1)} %bitcast.62), channel_id=1, replica_groups=mesh['groups'=2,'blk'=4,'ulysses'=4] {'blk'}, dimensions={0}, use_global_device_ids=true | all-gather | bytes 327680 | tf_op jit(solution)/shard_map/all_gather | solution.py:101
  50.6 0.1 copy.45
  50.7 0.3 fusion.2
  51.0 0.1 copy.47
  51.1 0.7 %all_to_all.64 = bf16[4,32,256]{2,1,0:T(8,128)(2,1)} reshape(bf16[128,2,128]{2,1,0:T(2,128)(2,1)S(1)} %copy.47) | data formatting | bytes 131072 | tf_op jit(solution)/shard_map/all_to_all | solution.py:105
  51.8 3.3 %all-to-all-start.3 = ((bf16[4,32,256]{2,1,0:T(8,128)(2,1)}), bf16[4,32,256]{2,1,0:T(8,128)(2,1)S(1)}, u32[]{:S(2)}, u32[]{:S(2)}) async-start(bf16[4,32,256]{2,1,0:T(8,128)(2,1)} %all_to_all.64), calls=%async_computation.3 | async-start | bytes 131072 | tf_op jit(solution)/shard_map/all_to_all | solution.py:105
  55.1 0.1 rsqrt.30
  55.2 5.6 %all-to-all-done.3 = bf16[4,32,256]{2,1,0:T(8,128)(2,1)S(1)} async-done(((bf16[4,32,256]{2,1,0:T(8,128)(2,1)}), bf16[4,32,256]{2,1,0:T(8,128)(2,1)S(1)}, u32[]{:S(2)}, u32[]{:S(2)}) %all-to-all-start.3) | async-done | bytes 65568 | tf_op jit(solution)/shard_map/all_to_all | solution.py:105
  60.8 0.0 copy-done
  60.8 0.9 %fusion.6 = bf16[32,1024]{1,0:T(8,128)(2,1)} fusion(f32[32,1024]{1,0:T(8,128)S(1)} %bitcast.61, bf16[384,1024]{1,0:T(8,128)(2,1)S(1)} %copy-done, f32[1024]{0:T(1024)S(1)} %bitcast.70, bf16[4,8,384]{2,1,0:T(8,128)(2,1)S(1)} %all-to-all-done.4, f32[32]{0:T(128)S(1)} %rsqrt.30), kind=kOutput, calls=%fused_computation.10 | convolution fusion | flops 25366528 | bytes 1011840 | tf_op jit(solution)/shard_map/dot_general | solution.py:74
  (11 shorter events, 0.1 us)
Async XLA Ops:
  0.0 60.8 %copy-start = (bf16[384,1024]{1,0:T(8,128)(2,1)S(1)}, bf16[384,1024]{1,0:T(8,128)(2,1)}, u32[]{:S(2)}) copy-start(bf16[384,1024]{1,0:T(8,128)(2,1)} %param.16) | copy-start | bytes 2359300
  0.0 0.7 %copy-start.6 = (s32[1,4]{1,0:T(1,128)S(1)}, s32[1,4]{1,0:T(1,128)}, u32[]{:S(2)}) copy-start(s32[1,4]{1,0:T(1,128)} %param.18) | copy-start | bytes 52
  0.8 8.5 %copy-start.1 = (bf16[32,1024]{1,0:T(8,128)(2,1)S(1)}, bf16[32,1024]{1,0:T(8,128)(2,1)}, u32[]{:S(2)}) copy-start(bf16[32,1024]{1,0:T(8,128)(2,1)} %param.11) | copy-start | bytes 196612
  2.9 6.6 %copy-start.2 = (bf16[32,1024]{1,0:T(8,128)(2,1)S(1)}, bf16[32,1024]{1,0:T(8,128)(2,1)}, u32[]{:S(2)}) copy-start(bf16[32,1024]{1,0:T(8,128)(2,1)} %param.10) | copy-start | bytes 196612
  2.9 12.1 %all-to-all-start.4 = ((bf16[4,8,384]{2,1,0:T(8,128)(2,1)}), bf16[4,8,384]{2,1,0:T(8,128)(2,1)S(1)}, u32[]{:S(2)}, u32[]{:S(2)}) async-start(bf16[4,8,384]{2,1,0:T(8,128)(2,1)} %broadcast_select_fusion), calls=%async_computation.4 | async-start | bytes 49152 | tf_op jit(solution)/shard_map/all_to_all | solution.py:114
  9.5 0.8 %copy-start.4 = (f32[1024]{0:T(1024)S(1)}, f32[1024]{0:T(1024)}, u32[]{:S(2)}) copy-start(f32[1024]{0:T(1024)} %param.14) | copy-start | bytes 12292
  10.3 0.7 %copy-start.5 = (f32[1024]{0:T(1024)S(1)}, f32[1024]{0:T(1024)}, u32[]{:S(2)}) copy-start(f32[1024]{0:T(1024)} %param.13) | copy-start | bytes 12292
  12.4 0.9 %copy-start.3 = (bf16[32,1024]{1,0:T(8,128)(2,1)S(1)}, bf16[32,1024]{1,0:T(8,128)(2,1)}, u32[]{:S(2)}) copy-start(bf16[32,1024]{1,0:T(8,128)(2,1)} %param.12) | copy-start | bytes 196612
  15.0 9.8 %all-to-all-start.1 = ((bf16[32,4,256]{2,0,1:T(8,128)(2,1)}), bf16[32,4,256]{2,0,1:T(8,128)(2,1)S(1)}, u32[]{:S(2)}, u32[]{:S(2)}) async-start(bf16[32,4,256]{2,0,1:T(8,128)(2,1)} %bitcast.55), calls=%async_computation.1 | async-start | bytes 131072 | tf_op jit(solution)/shard_map/all_to_all | solution.py:93
  24.8 9.2 %all-to-all-start = ((bf16[32,4,256]{2,0,1:T(8,128)(2,1)}), bf16[32,4,256]{2,0,1:T(8,128)(2,1)S(1)}, u32[]{:S(2)}, u32[]{:S(2)}) async-start(bf16[32,4,256]{2,0,1:T(8,128)(2,1)} %bitcast.56), calls=%async_computation | async-start | bytes 131072 | tf_op jit(solution)/shard_map/all_to_all | solution.py:92
  34.0 10.8 %all-to-all-start.2 = ((bf16[32,4,256]{2,0,1:T(8,128)(2,1)}), bf16[32,4,256]{2,0,1:T(8,128)(2,1)S(1)}, u32[]{:S(2)}, u32[]{:S(2)}) async-start(bf16[32,4,256]{2,0,1:T(8,128)(2,1)} %bitcast.54), calls=%async_computation.2 | async-start | bytes 131072 | tf_op jit(solution)/shard_map/all_to_all | solution.py:94
  51.8 9.0 %all-to-all-start.3 = ((bf16[4,32,256]{2,1,0:T(8,128)(2,1)}), bf16[4,32,256]{2,1,0:T(8,128)(2,1)S(1)}, u32[]{:S(2)}, u32[]{:S(2)}) async-start(bf16[4,32,256]{2,1,0:T(8,128)(2,1)} %all_to_all.64), calls=%async_computation.3 | async-start | bytes 131072 | tf_op jit(solution)/shard_map/all_to_all | solution.py:105
where the time goes:
time: 62.6 us; the launch traced here: 61.8 us
  starting transfers between devices  22.1 us (35%)
  waiting for transfers between devices  17.5 us (28%)
  blocking collectives  11.6 us (19%)
  local copies, waits for them, and re-layouts  6.69 us (11%)
  other arithmetic  1.57 us (3%)
  matrix products  1.51 us (2%)
  between operations  0.82 us (1%)
    all_to_all x1, starting transfers between devices, shards(): lax.all_to_all(outgoing, 'ulysses', split_axis=0, concat_axis=0, tiled=True)  6.45 us
    all_gather x1, blocking collectives, shards(): lax.all_gather(key_heads, 'blk', axis=0, tiled=True)  5.79 us
    all_gather x1, blocking collectives, shards(): lax.all_gather(value_heads, 'blk', axis=0, tiled=True)  5.77 us
    all_to_all x1, waiting for transfers between devices, shards(): lax.all_to_all(key_normed, 'ulysses', split_axis=1, concat_axis=0, tiled=...  5.65 us
    all_to_all x1, waiting for transfers between devices, shards(): lax.all_to_all(finish(state), 'ulysses', split_axis=0, concat_axis=1, til...  5.61 us
    all_to_all x1, waiting for transfers between devices, shards(): lax.all_to_all(value_proj, 'ulysses', split_axis=1, concat_axis=0, tiled=...  5.17 us
    all_to_all x1, starting transfers between devices, shards(): lax.all_to_all(value_proj, 'ulysses', split_axis=1, concat_axis=0, tiled=...  5.05 us
    all_to_all x1, starting transfers between devices, shards(): lax.all_to_all(key_normed, 'ulysses', split_axis=1, concat_axis=0, tiled=...  4.08 us
  transfers between devices with their start and end apart: 5, of which 4 were waited for; matrix products, arithmetic and copies ran while one was open for 6% of the time, Pallas kernels for 0%

commit v1 on v0

v1 whole, which is shorter than its diff:
```python
import functools

import jax
import jax.numpy as jnp
from jax import lax
from jax.experimental import pallas as pl
from jax.experimental.pallas import tpu as pltpu
from jax.sharding import PartitionSpec as P

HEAD_DIM = 128
EPS = 1e-06
VIDEO = ("ulysses", "blk")


def normed(rows, gain):
    values = rows.astype(jnp.float32)
    scale = lax.rsqrt(jnp.mean(values * values, axis=-1, keepdims=True) + EPS)
    return values * scale * gain


def pack_kernel(splits, q_ref, k_ref, v_ref, qg_ref, kg_ref, send_ref):
    rows, feats = q_ref.shape
    heads = feats // HEAD_DIM
    part = rows // splits
    queries = normed(q_ref[...], qg_ref[...]).astype(jnp.bfloat16)
    keys = normed(k_ref[...], kg_ref[...]).astype(jnp.bfloat16)
    values = v_ref[...]
    for head in range(heads):
        cols = slice(head * HEAD_DIM, (head + 1) * HEAD_DIM)
        for piece in range(splits):
            to = head * splits + piece
            send_ref[to, :part] = queries[piece * part : (piece + 1) * part, cols]
            send_ref[to, part : part + rows] = keys[:, cols]
            send_ref[to, part + rows :] = values[:, cols]


def slab_kernel(me_ref, owner_ref, control_ref, *out_refs):
    owners = len(out_refs)
    slab_rows = out_refs[0].shape[0]
    values = control_ref[...].astype(jnp.float32)
    slabs = [values[j * slab_rows : (j + 1) * slab_rows] for j in range(owners)]
    for shift, out_ref in enumerate(out_refs):
        owner = lax.rem(me_ref[0] + shift, owners)
        picked = slabs[0]
        for j in range(1, owners):
            picked = jnp.where(owner_ref[0, j] == owner, slabs[j], picked)
        out_ref[...] = picked.astype(jnp.bfloat16)


def attend_kernel(part, rows, got_ref, out_ref):
    count = got_ref.shape[0]
    keys = got_ref[:, part : part + rows].reshape(count * rows, HEAD_DIM)
    values = got_ref[:, part + rows :].reshape(count * rows, HEAD_DIM)
    block = max(1, min(count, 2**18 // (count * rows * part)))

    def attend(sources):
        queries = got_ref[sources, :part].reshape(block * part, HEAD_DIM)
        scores = lax.dot_general(
            queries, keys, (((1,), (1,)), ((), ())), preferred_element_type=jnp.float32
        ) * (HEAD_DIM ** (-0.5))
        peak = jnp.max(scores, axis=-1, keepdims=True)
        expo = jnp.exp(scores - peak)
        totals = jnp.sum(expo, axis=-1, keepdims=True)
        mixed = jnp.dot(expo.astype(jnp.bfloat16), values, preferred_element_type=jnp.float32)
        mixed = (mixed / totals).astype(jnp.bfloat16)
        out_ref[sources] = mixed.reshape(block, part, HEAD_DIM)

    if block == count:
        attend(slice(None))
    else:
        pl.loop(0, count // block)(lambda i: attend(pl.ds(i * block, block)))


def hint_kernel(me_ref, layer_ref, weight_ref, gain_ref, *refs):
    arrived, out_ref = refs[:-1], refs[-1]
    owners = len(arrived)
    slab_rows = arrived[0].shape[0]
    patches = jnp.concatenate([ref[...].astype(jnp.float32) for ref in arrived], axis=0)
    rows = normed(patches, 1.0).astype(jnp.bfloat16)
    hint = jnp.dot(rows, weight_ref[...], preferred_element_type=jnp.float32)
    hint = hint.astype(jnp.bfloat16).astype(jnp.float32) * gain_ref[pl.ds(layer_ref[0], 1), :]
    for shift in range(owners):
        source = lax.rem(me_ref[0] + owners - shift, owners)
        out_ref[source] = hint[shift * slab_rows : (shift + 1) * slab_rows]


def finish_kernel(splits, back_ref, hint_ref, out_ref):
    rows = out_ref.shape[0]
    part = rows // splits
    for to in range(back_ref.shape[0]):
        head, piece = divmod(to, splits)
        at = slice(piece * part, (piece + 1) * part)
        cols = slice(head * HEAD_DIM, (head + 1) * HEAD_DIM)
        out_ref[at, cols] = (back_ref[to].astype(jnp.float32) + hint_ref[at, cols]).astype(
            jnp.bfloat16
        )


VMEM = pl.BlockSpec(memory_space=pltpu.VMEM)
SMEM = pl.BlockSpec(memory_space=pltpu.SMEM)


def call(kernel, out_shape, specs, *operands, flops=0, nbytes=0):
    return pl.pallas_call(
        kernel,
        out_shape=out_shape,
        in_specs=specs,
        out_specs=jax.tree.map(lambda _: VMEM, out_shape),
        compiler_params=pltpu.CompilerParams(vmem_limit_bytes=32 * 2**20),
        cost_estimate=pl.CostEstimate(flops=flops, bytes_accessed=nbytes, transcendentals=0),
    )(*operands)


def shape(dims, dtype=jnp.bfloat16):
    return jax.ShapeDtypeStruct(dims, dtype)


def ring(owners, shift):
    return [(i, (i + shift) % owners) for i in range(owners)]


def shards(
    query_proj,
    key_proj,
    value_proj,
    query_gain,
    key_gain,
    control,
    hint_weight,
    hint_gain,
    owner_map,
    layer_index,
):
    owners = lax.axis_size("ulysses")
    count = owners * lax.axis_size("blk")
    rows, feats = query_proj.shape
    heads = feats // HEAD_DIM
    splits = count // heads
    part = rows // splits
    width = control.shape[1]
    me = lax.axis_index("ulysses").astype(jnp.int32).reshape(1)
    send = call(
        functools.partial(pack_kernel, splits),
        shape((count, part + 2 * rows, HEAD_DIM)),
        [VMEM] * 5,
        query_proj,
        key_proj,
        value_proj,
        query_gain.reshape(1, feats),
        key_gain.reshape(1, feats),
    )
    slabs = call(
        slab_kernel,
        [shape((rows // owners, width))] * owners,
        [SMEM, SMEM, VMEM],
        me,
        owner_map,
        control,
    )
    got = lax.all_to_all(send, VIDEO, split_axis=0, concat_axis=0, tiled=True)
    arrived = [slabs[0]] + [
        lax.ppermute(slabs[shift], "ulysses", ring(owners, shift)) for shift in range(1, owners)
    ]
    hint = call(
        hint_kernel,
        shape((owners, rows // owners, feats), jnp.float32),
        [SMEM, SMEM] + [VMEM] * (owners + 2),
        me,
        layer_index,
        hint_weight,
        hint_gain,
        *arrived,
        flops=2 * rows * width * feats,
        nbytes=2 * width * feats,
    )
    mixed = call(
        functools.partial(attend_kernel, part, rows),
        shape((count, part, HEAD_DIM)),
        [VMEM],
        got,
        flops=4 * count * part * count * rows * HEAD_DIM,
        nbytes=2 * got.size,
    )
    back = lax.all_to_all(mixed, VIDEO, split_axis=0, concat_axis=0, tiled=True)
    return call(
        functools.partial(finish_kernel, splits),
        shape((rows, feats)),
        [VMEM, VMEM],
        back,
        hint.reshape(rows, feats),
    )


def solution(mesh):
    split = P(("groups", "blk", "ulysses"), None)
    return jax.shard_map(
        shards,
        mesh=mesh,
        in_specs=(
            split,
            split,
            split,
            P(),
            P(),
            split,
            P(),
            P(),
            split,
            P(("groups", "blk", "ulysses")),
        ),
        out_specs=split,
        check_vma=False,
    )
```

time: 62.6 us -> 37.2 us (0.59)
  waiting for transfers between devices: 17.5 us -> 1.54 us
  starting transfers between devices: 22.1 us -> 9.36 us
  blocking collectives: 11.6 us -> 18.4 us
  local copies, waits for them, and re-layouts: 6.69 us -> 3.91 us
  Pallas kernels: 0 us -> 2.76 us
  other arithmetic: 1.57 us -> 0 us
  matrix products: 1.51 us -> 0 us
    all_to_all x5 -> x1, starting transfers between devices: 22.1 us -> 3.63 us  [shards(): back = lax.all_to_all(mixed, VIDEO, split_axis=0, concat_axis=0, tiled=True)]
    all_to_all x0 -> x1, blocking collectives: none -> 18.4 us  [shards(): got = lax.all_to_all(send, VIDEO, split_axis=0, concat_axis=0, tiled=True)]
    all_to_all x5 -> x1, waiting for transfers between devices: 17.5 us -> 0.01 us  [shards(): back = lax.all_to_all(mixed, VIDEO, split_axis=0, concat_axis=0, tiled=True)]
    all_gather x2 -> x0, blocking collectives: 11.6 us -> none  [the longest x1 5.79 us: shards(): lax.all_gather(key_heads, 'blk', axis=0, tiled=True)]
    ppermute x0 -> x3, starting transfers between devices: none -> 5.73 us  [shards(): lax.ppermute(slabs[shift], 'ulysses', ring(owners, shift))]
    pallas_call x0 -> x5, Pallas kernels: none -> 2.76 us  [call(): pl.pallas_call(kernel, out_shape=out_shape, in_specs=specs, out_specs=jax...]
    all_to_all x4 -> x0, local copies, waits for them, and re-layouts: 2.55 us -> none  [the longest x1 0.68 us: shards(): lax.all_to_all(finish(state), 'ulysses', split_axis=0, concat_axis=1, til...]
    unnamed x14 -> x18, local copies, waits for them, and re-layouts: 1.59 us -> 3.91 us
  transfers between devices with their start and end apart: 5 -> 4, of which waited for: 4 -> 1; matrix products, arithmetic and copies ran while one was open for 6% -> 0% of each run, Pallas kernels for 0% -> 2%
where the time goes in v1:
time: 37.2 us; the launch traced here: 36.7 us
  blocking collectives  18.4 us (49%)
  starting transfers between devices  9.36 us (25%)
  local copies, waits for them, and re-layouts  3.91 us (11%)
  Pallas kernels  2.76 us (7%)
  waiting for transfers between devices  1.54 us (4%)
  between operations  0.74 us (2%)
    all_to_all x1, blocking collectives, shards(): got = lax.all_to_all(send, VIDEO, split_axis=0, concat_axis=0, tiled=True)  18.4 us
    ppermute x3, starting transfers between devices, shards(): lax.ppermute(slabs[shift], 'ulysses', ring(owners, shift))  5.73 us
    unnamed x18, local copies, waits for them, and re-layouts  3.91 us
    all_to_all x1, starting transfers between devices, shards(): back = lax.all_to_all(mixed, VIDEO, split_axis=0, concat_axis=0, tiled=True)  3.63 us
    pallas_call x5, Pallas kernels, call(): pl.pallas_call(kernel, out_shape=out_shape, in_specs=specs, out_specs=jax...  2.76 us
    ppermute x3, waiting for transfers between devices, shards(): lax.ppermute(slabs[shift], 'ulysses', ring(owners, shift))  1.53 us
  transfers between devices with their start and end apart: 4, of which 1 were waited for; matrix products, arithmetic and copies ran while one was open for 0% of the time, Pallas kernels for 2%

profile of v1, /device:TPU:0, one launch (start us, length us, event | category | flops | bytes accessed | tf_op | source)
XLA Modules:
  0.0 36.7 jit_solution(9043294340570390020)
XLA Ops:
  0.0 0.0 copy-start.1
  0.0 0.8 %copy-done.1 = bf16[32,1024]{1,0:T(8,128)(2,1)S(1)} copy-done((bf16[32,1024]{1,0:T(8,128)(2,1)S(1)}, bf16[32,1024]{1,0:T(8,128)(2,1)}, u32[]{:S(2)}) %copy-start.1) | copy-done | bytes 65560
  0.8 0.0 copy-start.2
  0.8 0.8 %copy-done.2 = bf16[32,1024]{1,0:T(8,128)(2,1)S(1)} copy-done((bf16[32,1024]{1,0:T(8,128)(2,1)S(1)}, bf16[32,1024]{1,0:T(8,128)(2,1)}, u32[]{:S(2)}) %copy-start.2) | copy-done | bytes 65560
  1.7 0.0 copy-start.3
  1.7 0.8 %copy-done.3 = bf16[32,1024]{1,0:T(8,128)(2,1)S(1)} copy-done((bf16[32,1024]{1,0:T(8,128)(2,1)S(1)}, bf16[32,1024]{1,0:T(8,128)(2,1)}, u32[]{:S(2)}) %copy-start.3) | copy-done | bytes 65560
  2.5 0.0 copy-start.6
  2.5 0.7 %copy-done.6 = f32[1024]{0:T(1024)S(1)} copy-done((f32[1024]{0:T(1024)S(1)}, f32[1024]{0:T(1024)}, u32[]{:S(2)}) %copy-start.6) | copy-done | bytes 4120
  3.2 0.0 copy-start.7
  3.2 0.7 %copy-done.7 = f32[1024]{0:T(1024)S(1)} copy-done((f32[1024]{0:T(1024)S(1)}, f32[1024]{0:T(1024)}, u32[]{:S(2)}) %copy-start.7) | copy-done | bytes 4120
  3.9 0.0 copy-start
  3.9 0.1 shard_map.100
  4.0 18.4 %all_to_all.10.got_ref = bf16[16,80,128]{2,1,0:T(8,128)(2,1)S(1)} all-to-all(bf16[16,80,128]{2,1,0:T(8,128)(2,1)S(1)} %shard_map.100), channel_id=1, replica_groups=mesh['groups'=2,'blk'=4,'ulysses'=4] {'ulysses','blk'}, dimensions={0} | all-to-all | bytes 655360 | tf_op jit(solution)/shard_map/all_to_all | solution.py:160
  22.4 1.1 %shard_map.101 = bf16[16,16,128]{2,1,0:T(8,128)(2,1)} custom-call(bf16[16,80,128]{2,1,0:T(8,128)(2,1)S(1)} %all_to_all.10.got_ref), custom_call_target="tpu_custom_call" | custom-call | flops 67108864 | bytes 327680 | tf_op jit(solution)/shard_map/pallas_call | solution.py:104
  23.5 0.0 copy-start.5
  23.5 0.0 copy-start.8
  23.5 3.6 %all-to-all-start.1 = ((bf16[16,16,128]{2,1,0:T(8,128)(2,1)}), bf16[16,16,128]{2,1,0:T(8,128)(2,1)S(1)}, u32[]{:S(2)}, u32[]{:S(2)}) async-start(bf16[16,16,128]{2,1,0:T(8,128)(2,1)} %shard_map.101), calls=%async_computation.1 | async-start | bytes 131072 | tf_op jit(solution)/shard_map/all_to_all | solution.py:184
  27.2 0.0 copy-start.4
  27.2 0.0 copy-done.5
  27.2 0.0 copy-done.8
  27.2 0.6 %shard_map.102 = (bf16[8,384]{1,0:T(8,128)(2,1)S(1)}, bf16[8,384]{1,0:T(8,128)(2,1)S(1)}, bf16[8,384]{1,0:T(8,128)(2,1)S(1)}, bf16[8,384]{1,0:T(8,128)(2,1)S(1)}) custom-call(s32[1]{0:T(128)} %bitcast.2.me_ref, s32[1,4]{1,0:T(1,128)S(1)} %copy-done.8, bf16[32,384]{1,0:T(8,128)(2,1)S(1)} %copy-done.5), custom_call_target="tpu_custom_call" | custom-call | tf_op jit(solution)/shard_map/pallas_call | solution.py:104
  27.8 1.9 %collective-permute-start = (bf16[8,384]{1,0:T(8,128)(2,1)S(1)}, bf16[8,384]{1,0:T(8,128)(2,1)S(1)}, u32[]{:S(2)}, u32[]{:S(2)}) collective-permute-start(bf16[8,384]{1,0:T(8,128)(2,1)S(1)} %get-tuple-element.10), channel_id=1, source_target_pairs={{0,1},{1,2},{2,3},{3,0},{4,5},{5,6},{6,7},{7,4},{8,9},{9,10},{10,1... | collective-permute-start | bytes 18440 | tf_op jit(solution)/shard_map/ppermute | solution.py:162
  29.7 2.4 %collective-permute-start.1 = (bf16[8,384]{1,0:T(8,128)(2,1)S(1)}, bf16[8,384]{1,0:T(8,128)(2,1)S(1)}, u32[]{:S(2)}, u32[]{:S(2)}) collective-permute-start(bf16[8,384]{1,0:T(8,128)(2,1)S(1)} %get-tuple-element.11), channel_id=1, source_target_pairs={{0,2},{1,3},{2,0},{3,1},{4,6},{5,7},{6,4},{7,5},{8,10},{9,11},{10,... | collective-permute-start | bytes 18440 | tf_op jit(solution)/shard_map/ppermute | solution.py:162
  32.1 1.4 %collective-permute-start.2 = (bf16[8,384]{1,0:T(8,128)(2,1)S(1)}, bf16[8,384]{1,0:T(8,128)(2,1)S(1)}, u32[]{:S(2)}, u32[]{:S(2)}) collective-permute-start(bf16[8,384]{1,0:T(8,128)(2,1)S(1)} %get-tuple-element.12), channel_id=1, source_target_pairs={{0,3},{1,0},{2,1},{3,2},{4,7},{5,4},{6,5},{7,6},{8,11},{9,8},{10,9... | collective-permute-start | bytes 18440 | tf_op jit(solution)/shard_map/ppermute | solution.py:162
  34.2 0.0 collective-permute-done.refs_1_
  34.2 0.0 collective-permute-done.1.refs_2_
  34.2 1.5 %collective-permute-done.2.refs_3_ = bf16[8,384]{1,0:T(8,128)(2,1)S(1)} collective-permute-done((bf16[8,384]{1,0:T(8,128)(2,1)S(1)}, bf16[8,384]{1,0:T(8,128)(2,1)S(1)}, u32[]{:S(2)}, u32[]{:S(2)}) %collective-permute-start.2) | collective-permute-done | bytes 6176 | tf_op jit(solution)/shard_map/ppermute | solution.py:162
  35.7 0.0 copy-done
  35.7 0.0 copy-done.4
  35.7 0.3 shard_map.103
  36.0 0.0 all-to-all-done.1.back_ref
  36.0 0.6 %shard_map.104 = bf16[32,1024]{1,0:T(8,128)(2,1)} custom-call(bf16[16,16,128]{2,1,0:T(8,128)(2,1)S(1)} %all-to-all-done.1.back_ref, f32[32,1024]{1,0:T(8,128)S(1)} %bitcast.4), custom_call_target="tpu_custom_call" | custom-call | tf_op jit(solution)/shard_map/pallas_call | solution.py:104
Async XLA Ops:
  0.0 0.8 %copy-start.1 = (bf16[32,1024]{1,0:T(8,128)(2,1)S(1)}, bf16[32,1024]{1,0:T(8,128)(2,1)}, u32[]{:S(2)}) copy-start(bf16[32,1024]{1,0:T(8,128)(2,1)} %q_ref.1) | copy-start | bytes 196612
  0.8 0.8 %copy-start.2 = (bf16[32,1024]{1,0:T(8,128)(2,1)S(1)}, bf16[32,1024]{1,0:T(8,128)(2,1)}, u32[]{:S(2)}) copy-start(bf16[32,1024]{1,0:T(8,128)(2,1)} %k_ref.1) | copy-start | bytes 196612
  1.7 0.8 %copy-start.3 = (bf16[32,1024]{1,0:T(8,128)(2,1)S(1)}, bf16[32,1024]{1,0:T(8,128)(2,1)}, u32[]{:S(2)}) copy-start(bf16[32,1024]{1,0:T(8,128)(2,1)} %v_ref.1) | copy-start | bytes 196612
  2.5 0.7 %copy-start.6 = (f32[1024]{0:T(1024)S(1)}, f32[1024]{0:T(1024)}, u32[]{:S(2)}) copy-start(f32[1024]{0:T(1024)} %param.13) | copy-start | bytes 12292
  3.2 0.7 %copy-start.7 = (f32[1024]{0:T(1024)S(1)}, f32[1024]{0:T(1024)}, u32[]{:S(2)}) copy-start(f32[1024]{0:T(1024)} %param.14) | copy-start | bytes 12292
  3.9 31.8 %copy-start = (bf16[384,1024]{1,0:T(8,128)(2,1)S(1)}, bf16[384,1024]{1,0:T(8,128)(2,1)}, u32[]{:S(2)}) copy-start(bf16[384,1024]{1,0:T(8,128)(2,1)} %weight_ref.1) | copy-start | bytes 2359300
  23.5 3.7 %copy-start.5 = (bf16[32,384]{1,0:T(8,128)(2,1)S(1)}, bf16[32,384]{1,0:T(8,128)(2,1)}, u32[]{:S(2)}) copy-start(bf16[32,384]{1,0:T(8,128)(2,1)} %control_ref.1) | copy-start | bytes 73732
  23.5 3.7 %copy-start.8 = (s32[1,4]{1,0:T(1,128)S(1)}, s32[1,4]{1,0:T(1,128)}, u32[]{:S(2)}) copy-start(s32[1,4]{1,0:T(1,128)} %owner_ref.1) | copy-start | bytes 52
  23.5 12.5 %all-to-all-start.1 = ((bf16[16,16,128]{2,1,0:T(8,128)(2,1)}), bf16[16,16,128]{2,1,0:T(8,128)(2,1)S(1)}, u32[]{:S(2)}, u32[]{:S(2)}) async-start(bf16[16,16,128]{2,1,0:T(8,128)(2,1)} %shard_map.101), calls=%async_computation.1 | async-start | bytes 131072 | tf_op jit(solution)/shard_map/all_to_all | solution.py:184
  27.2 8.5 %copy-start.4 = (f32[8,1024]{1,0:T(8,128)S(1)}, f32[8,1024]{1,0:T(8,128)}, u32[]{:S(2)}) copy-start(f32[8,1024]{1,0:T(8,128)} %gain_ref.1) | copy-start | bytes 98308
  27.8 6.4 %collective-permute-start = (bf16[8,384]{1,0:T(8,128)(2,1)S(1)}, bf16[8,384]{1,0:T(8,128)(2,1)S(1)}, u32[]{:S(2)}, u32[]{:S(2)}) collective-permute-start(bf16[8,384]{1,0:T(8,128)(2,1)S(1)} %get-tuple-element.10), channel_id=1, source_target_pairs={{0,1},{1,2},{2,3},{3,0},{4,5},{5,6},{6,7},{7,4},{8,9},{9,10},{10,1... | collective-permute-start | bytes 18440 | tf_op jit(solution)/shard_map/ppermute | solution.py:162
  29.7 4.5 %collective-permute-start.1 = (bf16[8,384]{1,0:T(8,128)(2,1)S(1)}, bf16[8,384]{1,0:T(8,128)(2,1)S(1)}, u32[]{:S(2)}, u32[]{:S(2)}) collective-permute-start(bf16[8,384]{1,0:T(8,128)(2,1)S(1)} %get-tuple-element.11), channel_id=1, source_target_pairs={{0,2},{1,3},{2,0},{3,1},{4,6},{5,7},{6,4},{7,5},{8,10},{9,11},{10,... | collective-permute-start | bytes 18440 | tf_op jit(solution)/shard_map/ppermute | solution.py:162
  32.1 3.6 %collective-permute-start.2 = (bf16[8,384]{1,0:T(8,128)(2,1)S(1)}, bf16[8,384]{1,0:T(8,128)(2,1)S(1)}, u32[]{:S(2)}, u32[]{:S(2)}) collective-permute-start(bf16[8,384]{1,0:T(8,128)(2,1)S(1)} %get-tuple-element.12), channel_id=1, source_target_pairs={{0,3},{1,0},{2,1},{3,2},{4,7},{5,4},{6,5},{7,6},{8,11},{9,8},{10,9... | collective-permute-start | bytes 18440 | tf_op jit(solution)/shard_map/ppermute | solution.py:162

commit v2 on v1

v2 whole, which is shorter than its diff:
```python
import functools

import jax
import jax.numpy as jnp
from jax import lax
from jax.experimental import pallas as pl
from jax.experimental.pallas import tpu as pltpu
from jax.sharding import PartitionSpec as P

HEAD_DIM = 128
EPS = 1e-06
VIDEO = ("ulysses", "blk")


def normed(rows, gain):
    values = rows.astype(jnp.float32)
    scale = lax.rsqrt(jnp.mean(values * values, axis=-1, keepdims=True) + EPS)
    return values * scale * gain


def pack_kernel(splits, *refs):
    sources, send_ref, held, copy_sems = refs[:5], refs[5], refs[6:11], refs[11]
    copies = [
        pltpu.make_async_copy(source, buffer, copy_sems.at[i])
        for i, (source, buffer) in enumerate(zip(sources, held))
    ]
    for copy in copies:
        copy.start()
    q_ref, k_ref, v_ref, qg_ref, kg_ref = held
    rows, feats = q_ref.shape
    part = rows // splits
    for copy in copies:
        copy.wait()
    packed = (
        normed(q_ref[...], qg_ref[...]).astype(jnp.bfloat16),
        normed(k_ref[...], kg_ref[...]).astype(jnp.bfloat16),
        v_ref[...],
    )
    for head in range(feats // HEAD_DIM):
        cols = slice(head * HEAD_DIM, (head + 1) * HEAD_DIM)
        for piece in range(splits):
            for i, array in enumerate(packed):
                send_ref[head * splits + piece, i * part : (i + 1) * part] = array[
                    piece * part : (piece + 1) * part, cols
                ]


def attend_kernel(*refs):
    got_refs, out_ref = refs[:-1], refs[-1]
    count, part, _ = out_ref.shape
    keys = [ref[:, part : 2 * part].reshape(count * part, HEAD_DIM) for ref in got_refs]
    values = [ref[:, 2 * part :].reshape(count * part, HEAD_DIM) for ref in got_refs]
    keys, values = jnp.concatenate(keys, axis=0), jnp.concatenate(values, axis=0)
    block = max(1, min(count, 2**18 // (part * keys.shape[0])))

    def attend(sources):
        queries = got_refs[0][sources, :part].reshape(block * part, HEAD_DIM)
        scores = lax.dot_general(
            queries, keys, (((1,), (1,)), ((), ())), preferred_element_type=jnp.float32
        ) * (HEAD_DIM ** (-0.5))
        peak = jnp.max(scores, axis=-1, keepdims=True)
        expo = jnp.exp(scores - peak)
        totals = jnp.sum(expo, axis=-1, keepdims=True)
        mixed = jnp.dot(expo.astype(jnp.bfloat16), values, preferred_element_type=jnp.float32)
        mixed = (mixed / totals).astype(jnp.bfloat16)
        out_ref[sources] = mixed.reshape(block, part, HEAD_DIM)

    if block == count:
        attend(slice(None))
    else:
        pl.loop(0, count // block)(lambda i: attend(pl.ds(i * block, block)))


def finish_kernel(splits, me_ref, layer_ref, owner_ref, got_ref, weight_ref, gain_ref, back_ref, out_ref):
    owners = got_ref.shape[0]
    slabs = []
    for source in range(owners):
        slab = jnp.int32(0)
        for j in range(1, owners):
            slab = jnp.where(owner_ref[source, j] == me_ref[0], j, slab)
        slabs.append(got_ref[source, slab].astype(jnp.float32))
    patches = normed(jnp.concatenate(slabs, axis=0), 1.0).astype(jnp.bfloat16)
    hint = jnp.dot(patches, weight_ref[...], preferred_element_type=jnp.float32)
    hint = hint.astype(jnp.bfloat16).astype(jnp.float32) * gain_ref[pl.ds(layer_ref[0], 1), :]
    part = out_ref.shape[0] // splits
    for to in range(back_ref.shape[0]):
        head, piece = divmod(to, splits)
        at = slice(piece * part, (piece + 1) * part)
        cols = slice(head * HEAD_DIM, (head + 1) * HEAD_DIM)
        out_ref[at, cols] = (back_ref[to].astype(jnp.float32) + hint[at, cols]).astype(
            jnp.bfloat16
        )


VMEM = pl.BlockSpec(memory_space=pltpu.VMEM)
SMEM = pl.BlockSpec(memory_space=pltpu.SMEM)
HBM = pl.BlockSpec(memory_space=pltpu.HBM)


def call(kernel, out_shape, specs, *operands, scratch=(), flops=0, nbytes=0):
    return pl.pallas_call(
        kernel,
        out_shape=out_shape,
        in_specs=specs,
        out_specs=jax.tree.map(lambda _: VMEM, out_shape),
        scratch_shapes=scratch,
        compiler_params=pltpu.CompilerParams(vmem_limit_bytes=32 * 2**20),
        cost_estimate=pl.CostEstimate(flops=flops, bytes_accessed=nbytes, transcendentals=0),
    )(*operands)


def shape(dims, dtype=jnp.bfloat16):
    return jax.ShapeDtypeStruct(dims, dtype)


def team_ring(size, splits, shift):
    return [(i, i - i % splits + (i + shift) % splits) for i in range(size)]


def shards(
    query_proj,
    key_proj,
    value_proj,
    query_gain,
    key_gain,
    control,
    hint_weight,
    hint_gain,
    owner_map,
    layer_index,
):
    owners, blocks = lax.axis_size("ulysses"), lax.axis_size("blk")
    count = owners * blocks
    rows, feats = query_proj.shape
    splits = count // (feats // HEAD_DIM)
    part = rows // splits
    width = control.shape[1]
    me = lax.axis_index("ulysses").astype(jnp.int32).reshape(1)
    arrived = lax.all_gather(control, "ulysses", axis=0)
    owner_rows = lax.all_gather(owner_map[0], "ulysses", axis=0)
    sources = (
        query_proj,
        key_proj,
        value_proj,
        query_gain.reshape(1, feats),
        key_gain.reshape(1, feats),
    )
    sources = [pltpu.with_memory_space_constraint(source, pltpu.HBM) for source in sources]
    send = call(
        functools.partial(pack_kernel, splits),
        shape((count, 3 * part, HEAD_DIM)),
        [HBM] * len(sources),
        *sources,
        scratch=[pltpu.VMEM(source.shape, source.dtype) for source in sources]
        + [pltpu.SemaphoreType.DMA((len(sources),))],
    )
    got = lax.all_to_all(send, VIDEO, split_axis=0, concat_axis=0, tiled=True)
    team = [got] + [
        lax.ppermute(got, "blk", team_ring(blocks, splits, shift)) for shift in range(1, splits)
    ]
    mixed = call(
        attend_kernel,
        shape((count, part, HEAD_DIM)),
        [VMEM] * splits,
        *team,
        flops=4 * count * part * count * rows * HEAD_DIM,
        nbytes=6 * count * rows * HEAD_DIM,
    )
    back = lax.all_to_all(mixed, VIDEO, split_axis=0, concat_axis=0, tiled=True)
    return call(
        functools.partial(finish_kernel, splits),
        shape((rows, feats)),
        [SMEM] * 3 + [VMEM] * 4,
        me,
        layer_index,
        owner_rows,
        arrived.reshape(owners, owners, rows // owners, width),
        hint_weight,
        hint_gain,
        back,
        flops=2 * rows * width * feats,
        nbytes=2 * width * feats,
    )


def solution(mesh):
    split = P(("groups", "blk", "ulysses"), None)
    return jax.shard_map(
        shards,
        mesh=mesh,
        in_specs=(
            split,
            split,
            split,
            P(),
            P(),
            split,
            P(),
            P(),
            split,
            P(("groups", "blk", "ulysses")),
        ),
        out_specs=split,
        check_vma=False,
    )
```

time: 37.2 us -> 51.2 us (1.38)
  blocking collectives: 18.4 us -> 40.6 us
  starting transfers between devices: 9.36 us -> 3.64 us
  local copies, waits for them, and re-layouts: 3.91 us -> 0.66 us
  Pallas kernels: 2.76 us -> 3.78 us
    all_gather x0 -> x2, blocking collectives: none -> 24.4 us  [the longest x1 13.3 us: shards(): arrived = lax.all_gather(control, 'ulysses', axis=0)]
    ppermute x3 -> x1, starting transfers between devices: 5.73 us -> 0.01 us  [shards(): lax.ppermute(got, 'blk', team_ring(blocks, splits, shift))]
    unnamed x18 -> x8, local copies, waits for them, and re-layouts: 3.91 us -> 0.66 us
    all_to_all x1, blocking collectives: 18.4 us -> 16.2 us  [shards(): got = lax.all_to_all(send, VIDEO, split_axis=0, concat_axis=0, tiled=True)]
    pallas_call x5 -> x3, Pallas kernels: 2.76 us -> 3.78 us  [call(): pl.pallas_call(kernel, out_shape=out_shape, in_specs=specs, out_specs=jax...]
    ppermute x3 -> x1, waiting for transfers between devices: 1.53 us -> 1.44 us  [shards(): lax.ppermute(got, 'blk', team_ring(blocks, splits, shift))]
  transfers between devices with their start and end apart: 4 -> 2, of which waited for: 1 -> 1; matrix products, arithmetic and copies ran while one was open for 0% -> 0% of each run, Pallas kernels for 2% -> 0%
where the time goes in v2:
time: 51.2 us; the launch traced here: 50.8 us
  blocking collectives  40.6 us (79%)
  Pallas kernels  3.78 us (7%)
  starting transfers between devices  3.64 us (7%)
  waiting for transfers between devices  1.44 us (3%)
  between operations  0.7 us (1%)
  local copies, waits for them, and re-layouts  0.66 us (1%)
    all_to_all x1, blocking collectives, shards(): got = lax.all_to_all(send, VIDEO, split_axis=0, concat_axis=0, tiled=True)  16.2 us
    all_gather x1, blocking collectives, shards(): arrived = lax.all_gather(control, 'ulysses', axis=0)  13.3 us
    all_gather x1, blocking collectives, shards(): owner_rows = lax.all_gather(owner_map[0], 'ulysses', axis=0)  11.2 us
    pallas_call x3, Pallas kernels, call(): pl.pallas_call(kernel, out_shape=out_shape, in_specs=specs, out_specs=jax...  3.78 us
    all_to_all x1, starting transfers between devices, shards(): back = lax.all_to_all(mixed, VIDEO, split_axis=0, concat_axis=0, tiled=True)  3.63 us
    ppermute x1, waiting for transfers between devices, shards(): lax.ppermute(got, 'blk', team_ring(blocks, splits, shift))  1.44 us
  transfers between devices with their start and end apart: 2, of which 1 were waited for; matrix products, arithmetic and copies ran while one was open for 0% of the time, Pallas kernels for 0%

profile of v2, /device:TPU:0, one launch (start us, length us, event | category | flops | bytes accessed | tf_op | source)
XLA Modules:
  0.0 50.8 jit_solution(15826121981738246388)
XLA Ops:
  0.0 0.0 copy-start
  0.0 1.2 %shard_map.100 = bf16[16,48,128]{2,1,0:T(8,128)(2,1)S(1)} custom-call(bf16[32,1024]{1,0:T(8,128)(2,1)} %refs_0_.1, bf16[32,1024]{1,0:T(8,128)(2,1)} %refs_1_.1, bf16[32,1024]{1,0:T(8,128)(2,1)} %refs_2_.1, f32[1,1024]{1,0:T(1,128)} %bitcast.8, f32[1,1024]{1,0:T(1,128)} %bitcast.9), custom_call_target="tpu_custom_call" | custom-call | tf_op jit(solution)/shard_map/pallas_call | solution.py:101
  1.2 16.2 %all_to_all.10.refs_0_ = bf16[16,48,128]{2,1,0:T(8,128)(2,1)S(1)} all-to-all(bf16[16,48,128]{2,1,0:T(8,128)(2,1)S(1)} %shard_map.100), channel_id=1, replica_groups=mesh['groups'=2,'blk'=4,'ulysses'=4] {'ulysses','blk'}, dimensions={0} | all-to-all | bytes 393216 | tf_op jit(solution)/shard_map/all_to_all | solution.py:157
  17.3 0.0 collective-permute-start
  17.3 1.4 %collective-permute-done.refs_1_ = bf16[16,48,128]{2,1,0:T(8,128)(2,1)S(1)} collective-permute-done((bf16[16,48,128]{2,1,0:T(8,128)(2,1)S(1)}, bf16[16,48,128]{2,1,0:T(8,128)(2,1)S(1)}, u32[]{:S(2)}, u32[]{:S(2)}) %collective-permute-start) | collective-permute-done | bytes 196640 | tf_op jit(solution)/shard_map/ppermute | solution.py:159
  18.8 1.1 %shard_map.101 = bf16[16,16,128]{2,1,0:T(8,128)(2,1)} custom-call(bf16[16,48,128]{2,1,0:T(8,128)(2,1)S(1)} %all_to_all.10.refs_0_, bf16[16,48,128]{2,1,0:T(8,128)(2,1)S(1)} %collective-permute-done.refs_1_), custom_call_target="tpu_custom_call" | custom-call | flops 67108864 | bytes 393216 | tf_op jit(solution)/shard_map/pallas_call | solution.py:101
  19.9 0.0 copy-start.2
  19.9 3.6 %all-to-all-start.1 = ((bf16[16,16,128]{2,1,0:T(8,128)(2,1)}), bf16[16,16,128]{2,1,0:T(8,128)(2,1)S(1)}, u32[]{:S(2)}, u32[]{:S(2)}) async-start(bf16[16,16,128]{2,1,0:T(8,128)(2,1)} %shard_map.101), calls=%async_computation.1 | async-start | bytes 131072 | tf_op jit(solution)/shard_map/all_to_all | solution.py:169
  23.5 0.0 copy-start.3
  23.5 0.6 %copy-done.3 = s32[1,4]{1,0:T(1,128)S(1)} copy-done((s32[1,4]{1,0:T(1,128)S(1)}, s32[1,4]{1,0:T(1,128)}, u32[]{:S(2)}) %copy-start.3) | copy-done | bytes 40
  24.2 11.2 %all-gather.1 = s32[4,1,4]{2,1,0:T(1,128)S(1)} all-gather(s32[1,1,4]{2,1,0:T(1,128)S(1)} %bitcast.10), channel_id=1, replica_groups=mesh['groups'=2,'blk'=4,'ulysses'=4] {'ulysses'}, dimensions={0}, use_global_device_ids=true | all-gather | bytes 80 | tf_op jit(solution)/shard_map/all_gather | solution.py:140
  36.0 0.0 copy-done.2
  36.0 0.0 copy-start.1
  36.0 13.3 %all-gather = bf16[128,384]{1,0:T(8,128)(2,1)S(1)} all-gather(bf16[32,384]{1,0:T(8,128)(2,1)S(1)} %copy-done.2), channel_id=2, replica_groups=mesh['groups'=2,'blk'=4,'ulysses'=4] {'ulysses'}, dimensions={0}, use_global_device_ids=true | all-gather | bytes 122880 | tf_op jit(solution)/shard_map/all_gather | solution.py:139
  49.3 0.0 all-to-all-done.1.back_ref
  49.3 0.0 copy-done
  49.3 0.0 copy-done.1
  49.3 1.5 %shard_map.102 = bf16[32,1024]{1,0:T(8,128)(2,1)} custom-call(s32[1]{0:T(128)} %bitcast.me_ref, s32[1]{0:T(128)S(6)} %copy.11.layer_ref, s32[4,4]{1,0:T(4,128)S(1)} %bitcast.7, bf16[4,4,8,384]{3,2,1,0:T(8,128)(2,1)S(1)} %bitcast.6, bf16[384,1024]{1,0:T(8,128)(2,1)S(1)} %copy-done, f32[8,1024]{1,0:T(8,128)S(1)} %copy-done.1, ...), custom_call_target="tpu_custom_call" | custom-call | flops 25165824 | bytes 786432 | tf_op jit(solution)/shard_map/pallas_call | solution.py:101
Async XLA Ops:
  0.0 49.3 %copy-start = (bf16[384,1024]{1,0:T(8,128)(2,1)S(1)}, bf16[384,1024]{1,0:T(8,128)(2,1)}, u32[]{:S(2)}) copy-start(bf16[384,1024]{1,0:T(8,128)(2,1)} %weight_ref.1) | copy-start | bytes 2359300
  17.3 1.4 %collective-permute-start = (bf16[16,48,128]{2,1,0:T(8,128)(2,1)S(1)}, bf16[16,48,128]{2,1,0:T(8,128)(2,1)S(1)}, u32[]{:S(2)}, u32[]{:S(2)}) collective-permute-start(bf16[16,48,128]{2,1,0:T(8,128)(2,1)S(1)} %all_to_all.10.refs_0_), channel_id=1, source_target_pairs={{0,4},{4,0},{8,12},{12,8},{1,5},{5,1},{9,13},{13,9},{2,6},{6,2},{1... | collective-permute-start | bytes 589832 | tf_op jit(solution)/shard_map/ppermute | solution.py:159
  19.9 16.1 %copy-start.2 = (bf16[32,384]{1,0:T(8,128)(2,1)S(1)}, bf16[32,384]{1,0:T(8,128)(2,1)}, u32[]{:S(2)}) copy-start(bf16[32,384]{1,0:T(8,128)(2,1)} %param.15) | copy-start | bytes 73732
  19.9 29.4 %all-to-all-start.1 = ((bf16[16,16,128]{2,1,0:T(8,128)(2,1)}), bf16[16,16,128]{2,1,0:T(8,128)(2,1)S(1)}, u32[]{:S(2)}, u32[]{:S(2)}) async-start(bf16[16,16,128]{2,1,0:T(8,128)(2,1)} %shard_map.101), calls=%async_computation.1 | async-start | bytes 131072 | tf_op jit(solution)/shard_map/all_to_all | solution.py:169
  23.5 0.7 %copy-start.3 = (s32[1,4]{1,0:T(1,128)S(1)}, s32[1,4]{1,0:T(1,128)}, u32[]{:S(2)}) copy-start(s32[1,4]{1,0:T(1,128)} %param.18) | copy-start | bytes 52
  36.0 13.3 %copy-start.1 = (f32[8,1024]{1,0:T(8,128)S(1)}, f32[8,1024]{1,0:T(8,128)}, u32[]{:S(2)}) copy-start(f32[8,1024]{1,0:T(8,128)} %gain_ref.1) | copy-start | bytes 98308

commit v3 on v2

--- a/solution.py
+++ b/solution.py
@@ -18,17 +18,18 @@
     return values * scale * gain
 
 
-def pack_kernel(splits, *refs):
-    sources, send_ref, held, copy_sems = refs[:5], refs[5], refs[6:11], refs[11]
+def pack_kernel(splits, owners, owner_ref, *refs):
+    total = (len(refs) - 2) // 2
+    sources, send_ref, held, copy_sems = refs[:total], refs[total], refs[total + 1 : -1], refs[-1]
     copies = [
         pltpu.make_async_copy(source, buffer, copy_sems.at[i])
         for i, (source, buffer) in enumerate(zip(sources, held))
     ]
     for copy in copies:
         copy.start()
-    q_ref, k_ref, v_ref, qg_ref, kg_ref = held
+    q_ref, k_ref, v_ref, control_ref, qg_ref, kg_ref = held
     rows, feats = q_ref.shape
-    part = rows // splits
+    part, slab_rows = rows // splits, rows // owners
     for copy in copies:
         copy.wait()
     packed = (
@@ -43,13 +44,44 @@
                 send_ref[head * splits + piece, i * part : (i + 1) * part] = array[
                     piece * part : (piece + 1) * part, cols
                 ]
-
-
-def attend_kernel(*refs):
-    got_refs, out_ref = refs[:-1], refs[-1]
-    count, part, _ = out_ref.shape
+    patches = control_ref[...].astype(jnp.float32)
+    slabs = [patches[j * slab_rows : (j + 1) * slab_rows] for j in range(owners)]
+    blocks = send_ref.shape[0] // owners
+    for owner in range(owners):
+        slab = slabs[0]
+        for j in range(1, owners):
+            slab = jnp.where(owner_ref[0, j] == owner, slabs[j], slab)
+        slab = slab.astype(jnp.bfloat16)
+        for tile in range(slab.shape[1] // HEAD_DIM):
+            at = 3 * part + tile * slab_rows
+            for block in range(blocks):
+                send_ref[owner * blocks + block, at : at + slab_rows] = slab[
+                    :, tile * HEAD_DIM : (tile + 1) * HEAD_DIM
+                ]
+
+
+def gain_kernel(layer_ref, gain_ref, out_ref):
+    out_ref[...] = gain_ref[pl.ds(layer_ref[0], 1), :]
+
+
+def attend_kernel(part, owners, block_ref, *refs):
+    got_refs, (out_ref, patch_ref) = refs[:-2], refs[-2:]
+    count = out_ref.shape[0]
+    blocks = count // owners
+    rows, width = patch_ref.shape
+    slab_rows = rows // owners
+    slabs = [
+        got_refs[0][source * blocks + block_ref[0], 3 * part :].astype(jnp.float32)
+        for source in range(owners)
+    ]
+    patches = [
+        jnp.concatenate([slab[i * slab_rows : (i + 1) * slab_rows] for slab in slabs], axis=0)
+        for i in range(width // HEAD_DIM)
+    ]
+    patch_ref[...] = normed(jnp.concatenate(patches, axis=1), 1.0).astype(jnp.bfloat16)
+
     keys = [ref[:, part : 2 * part].reshape(count * part, HEAD_DIM) for ref in got_refs]
-    values = [ref[:, 2 * part :].reshape(count * part, HEAD_DIM) for ref in got_refs]
+    values = [ref[:, 2 * part : 3 * part].reshape(count * part, HEAD_DIM) for ref in got_refs]
     keys, values = jnp.concatenate(keys, axis=0), jnp.concatenate(values, axis=0)
     block = max(1, min(count, 2**18 // (part * keys.shape[0])))
 
@@ -71,23 +103,18 @@
         pl.loop(0, count // block)(lambda i: attend(pl.ds(i * block, block)))
 
 
-def finish_kernel(splits, me_ref, layer_ref, owner_ref, got_ref, weight_ref, gain_ref, back_ref, out_ref):
-    owners = got_ref.shape[0]
-    slabs = []
-    for source in range(owners):
-        slab = jnp.int32(0)
-        for j in range(1, owners):
-            slab = jnp.where(owner_ref[source, j] == me_ref[0], j, slab)
-        slabs.append(got_ref[source, slab].astype(jnp.float32))
-    patches = normed(jnp.concatenate(slabs, axis=0), 1.0).astype(jnp.bfloat16)
-    hint = jnp.dot(patches, weight_ref[...], preferred_element_type=jnp.float32)
-    hint = hint.astype(jnp.bfloat16).astype(jnp.float32) * gain_ref[pl.ds(layer_ref[0], 1), :]
+def hint_kernel(patch_ref, weight_ref, gain_ref, out_ref):
+    hint = jnp.dot(patch_ref[...], weight_ref[...], preferred_element_type=jnp.float32)
+    out_ref[...] = hint.astype(jnp.bfloat16).astype(jnp.float32) * gain_ref[...]
+
+
+def finish_kernel(splits, back_ref, hint_ref, out_ref):
     part = out_ref.shape[0] // splits
     for to in range(back_ref.shape[0]):
         head, piece = divmod(to, splits)
         at = slice(piece * part, (piece + 1) * part)
         cols = slice(head * HEAD_DIM, (head + 1) * HEAD_DIM)
-        out_ref[at, cols] = (back_ref[to].astype(jnp.float32) + hint[at, cols]).astype(
+        out_ref[at, cols] = (back_ref[to].astype(jnp.float32) + hint_ref[at, cols]).astype(
             jnp.bfloat16
         )
 
@@ -135,51 +162,63 @@
     splits = count // (feats // HEAD_DIM)
     part = rows // splits
     width = control.shape[1]
-    me = lax.axis_index("ulysses").astype(jnp.int32).reshape(1)
-    arrived = lax.all_gather(control, "ulysses", axis=0)
-    owner_rows = lax.all_gather(owner_map[0], "ulysses", axis=0)
     sources = (
         query_proj,
         key_proj,
         value_proj,
+        control,
         query_gain.reshape(1, feats),
         key_gain.reshape(1, feats),
     )
     sources = [pltpu.with_memory_space_constraint(source, pltpu.HBM) for source in sources]
     send = call(
-        functools.partial(pack_kernel, splits),
-        shape((count, 3 * part, HEAD_DIM)),
-        [HBM] * len(sources),
+        functools.partial(pack_kernel, splits, owners),
+        shape((count, 3 * part + rows // owners * (width // HEAD_DIM), HEAD_DIM)),
+        [SMEM] + [HBM] * len(sources),
+        owner_map,
         *sources,
         scratch=[pltpu.VMEM(source.shape, source.dtype) for source in sources]
         + [pltpu.SemaphoreType.DMA((len(sources),))],
     )
     got = lax.all_to_all(send, VIDEO, split_axis=0, concat_axis=0, tiled=True)
+    gain_row = call(
+        gain_kernel,
+        shape((1, feats), jnp.float32),
+        [SMEM, VMEM],
+        layer_index,
+        hint_gain,
+        nbytes=hint_gain.size * 4,
+    )
+    got, gain_row = lax.optimization_barrier((got, gain_row))
     team = [got] + [
         lax.ppermute(got, "blk", team_ring(blocks, splits, shift)) for shift in range(1, splits)
     ]
-    mixed = call(
-        attend_kernel,
-        shape((count, part, HEAD_DIM)),
-        [VMEM] * splits,
+    mixed, patches = call(
+        functools.partial(attend_kernel, part, owners),
+        [shape((count, part, HEAD_DIM)), shape((rows, width))],
+        [SMEM] + [VMEM] * splits,
+        lax.axis_index("blk").astype(jnp.int32).reshape(1),
         *team,
         flops=4 * count * part * count * rows * HEAD_DIM,
         nbytes=6 * count * rows * HEAD_DIM,
     )
     back = lax.all_to_all(mixed, VIDEO, split_axis=0, concat_axis=0, tiled=True)
+    hint = call(
+        hint_kernel,
+        shape((rows, feats), jnp.float32),
+        [VMEM] * 3,
+        patches,
+        hint_weight,
+        gain_row,
+        flops=2 * rows * width * feats,
+        nbytes=2 * width * feats,
+    )
     return call(
         functools.partial(finish_kernel, splits),
         shape((rows, feats)),
-        [SMEM] * 3 + [VMEM] * 4,
-        me,
-        layer_index,
-        owner_rows,
-        arrived.reshape(owners, owners, rows // owners, width),
-        hint_weight,
-        hint_gain,
+        [VMEM, VMEM],
         back,
-        flops=2 * rows * width * feats,
-        nbytes=2 * width * feats,
+        hint,
     )
 
 

time: 51.2 us -> 35.2 us (0.69)
  blocking collectives: 40.6 us -> 0 us
  waiting for transfers between devices: 1.44 us -> 18.1 us
  starting transfers between devices: 3.64 us -> 11 us
  Pallas kernels: 3.78 us -> 4.36 us
    all_gather x2 -> x0, blocking collectives: 24.4 us -> none  [the longest x1 13.3 us: shards(): arrived = lax.all_gather(control, 'ulysses', axis=0)]
    all_to_all x1 -> x0, blocking collectives: 16.2 us -> none  [shards(): got = lax.all_to_all(send, VIDEO, split_axis=0, concat_axis=0, tiled=True)]
    all_to_all x0 -> x1, waiting for transfers between devices: none -> 9.9 us  [shards(): got = lax.all_to_all(send, VIDEO, split_axis=0, concat_axis=0, tiled=True)]
    all_to_all x0 -> x1, starting transfers between devices: none -> 7.5 us  [shards(): got = lax.all_to_all(send, VIDEO, split_axis=0, concat_axis=0, tiled=True)]
    all_to_all x1, waiting for transfers between devices: 0.01 us -> 6.59 us  [shards(): back = lax.all_to_all(mixed, VIDEO, split_axis=0, concat_axis=0, tiled=True)]
    pallas_call x3 -> x5, Pallas kernels: 3.78 us -> 4.36 us  [call(): pl.pallas_call(kernel, out_shape=out_shape, in_specs=specs, out_specs=jax...]
  transfers between devices with their start and end apart: 2 -> 3, of which waited for: 1 -> 3; matrix products, arithmetic and copies ran while one was open for 0% -> 0% of each run, Pallas kernels for 0% -> 1%
where the time goes in v3:
time: 35.2 us; the launch traced here: 34.8 us
  waiting for transfers between devices  18.1 us (51%)
  starting transfers between devices  11 us (31%)
  Pallas kernels  4.36 us (12%)
  between operations  0.71 us (2%)
  local copies, waits for them, and re-layouts  0.66 us (2%)
    all_to_all x1, waiting for transfers between devices, shards(): got = lax.all_to_all(send, VIDEO, split_axis=0, concat_axis=0, tiled=True)  9.9 us
    all_to_all x1, starting transfers between devices, shards(): got = lax.all_to_all(send, VIDEO, split_axis=0, concat_axis=0, tiled=True)  7.5 us
    all_to_all x1, waiting for transfers between devices, shards(): back = lax.all_to_all(mixed, VIDEO, split_axis=0, concat_axis=0, tiled=True)  6.59 us
    pallas_call x5, Pallas kernels, call(): pl.pallas_call(kernel, out_shape=out_shape, in_specs=specs, out_specs=jax...  4.36 us
    all_to_all x1, starting transfers between devices, shards(): back = lax.all_to_all(mixed, VIDEO, split_axis=0, concat_axis=0, tiled=True)  3.5 us
    ppermute x1, waiting for transfers between devices, shards(): lax.ppermute(got, 'blk', team_ring(blocks, splits, shift))  1.58 us
  transfers between devices with their start and end apart: 3, of which 3 were waited for; matrix products, arithmetic and copies ran while one was open for 0% of the time, Pallas kernels for 1%

profile of v3, /device:TPU:0, one launch (start us, length us, event | category | flops | bytes accessed | tf_op | source)
XLA Modules:
  0.0 34.8 jit_solution(7243819454997473100)
XLA Ops:
  0.0 0.0 copy-start.2
  0.0 0.7 %copy-done.2 = s32[1,4]{1,0:T(1,128)S(1)} copy-done((s32[1,4]{1,0:T(1,128)S(1)}, s32[1,4]{1,0:T(1,128)}, u32[]{:S(2)}) %copy-start.2) | copy-done | bytes 40
  0.7 0.0 copy-start.1
  0.7 2.3 %shard_map.100 = bf16[16,72,128]{2,1,0:T(8,128)(2,1)} custom-call(s32[1,4]{1,0:T(1,128)S(1)} %copy-done.2, bf16[32,1024]{1,0:T(8,128)(2,1)} %refs_0_.1, bf16[32,1024]{1,0:T(8,128)(2,1)} %refs_1_.1, bf16[32,1024]{1,0:T(8,128)(2,1)} %refs_2_.1, bf16[32,384]{1,0:T(8,128)(2,1)} %refs_3_.1, f32[1,1024]{1,0:T(1,128)} %bitcast.3, f32[1,1024]{1,0:T(1,128)} %bitcast.4), custom_call_target="tpu_custom_call" | custom-call | tf_op jit(solution)/shard_map/pallas_call | solution.py:128
  3.0 0.0 copy-start
  3.0 7.5 %all-to-all-start = ((bf16[16,72,128]{2,1,0:T(8,128)(2,1)}), bf16[16,72,128]{2,1,0:T(8,128)(2,1)S(1)}, u32[]{:S(2)}, u32[]{:S(2)}) async-start(bf16[16,72,128]{2,1,0:T(8,128)(2,1)} %shard_map.100), calls=%async_computation | async-start | bytes 589824 | tf_op jit(solution)/shard_map/all_to_all | solution.py:183
  11.2 0.0 copy-done.1
  11.2 9.9 %all-to-all-done.refs_0_ = bf16[16,72,128]{2,1,0:T(8,128)(2,1)S(1)} async-done(((bf16[16,72,128]{2,1,0:T(8,128)(2,1)}), bf16[16,72,128]{2,1,0:T(8,128)(2,1)S(1)}, u32[]{:S(2)}, u32[]{:S(2)}) %all-to-all-start) | async-done | bytes 294944 | tf_op jit(solution)/shard_map/all_to_all | solution.py:183
  21.1 0.0 collective-permute-start
  21.1 1.6 %collective-permute-done.refs_1_ = bf16[16,72,128]{2,1,0:T(8,128)(2,1)S(1)} collective-permute-done((bf16[16,72,128]{2,1,0:T(8,128)(2,1)S(1)}, bf16[16,72,128]{2,1,0:T(8,128)(2,1)S(1)}, u32[]{:S(2)}, u32[]{:S(2)}) %collective-permute-start) | collective-permute-done | bytes 294944 | tf_op jit(solution)/shard_map/ppermute | solution.py:194
  22.7 1.1 %shard_map.102 = (bf16[16,16,128]{2,1,0:T(8,128)(2,1)}, bf16[32,384]{1,0:T(8,128)(2,1)S(1)}) custom-call(s32[1]{0:T(128)} %bitcast.block_ref, bf16[16,72,128]{2,1,0:T(8,128)(2,1)S(1)} %all-to-all-done.refs_0_, bf16[16,72,128]{2,1,0:T(8,128)(2,1)S(1)} %collective-permute-done.refs_1_), custom_call_target="tpu_custom_call" | custom-call | flops 67108864 | bytes 393216 | tf_op jit(solution)/shard_map/pallas_call | solution.py:128
  23.8 3.5 %all-to-all-start.1 = ((bf16[16,16,128]{2,1,0:T(8,128)(2,1)}), bf16[16,16,128]{2,1,0:T(8,128)(2,1)S(1)}, u32[]{:S(2)}, u32[]{:S(2)}) async-start(bf16[16,16,128]{2,1,0:T(8,128)(2,1)} %get-tuple-element.10), calls=%async_computation.1 | async-start | bytes 131072 | tf_op jit(solution)/shard_map/all_to_all | solution.py:205
  27.3 0.0 copy-done
  27.3 0.3 shard_map.103.hint_ref
  27.6 6.6 %all-to-all-done.1.back_ref = bf16[16,16,128]{2,1,0:T(8,128)(2,1)S(1)} async-done(((bf16[16,16,128]{2,1,0:T(8,128)(2,1)}), bf16[16,16,128]{2,1,0:T(8,128)(2,1)S(1)}, u32[]{:S(2)}, u32[]{:S(2)}) %all-to-all-start.1) | async-done | bytes 65568 | tf_op jit(solution)/shard_map/all_to_all | solution.py:205
  34.2 0.6 %shard_map.104 = bf16[32,1024]{1,0:T(8,128)(2,1)} custom-call(bf16[16,16,128]{2,1,0:T(8,128)(2,1)S(1)} %all-to-all-done.1.back_ref, f32[32,1024]{1,0:T(8,128)S(1)} %shard_map.103.hint_ref), custom_call_target="tpu_custom_call" | custom-call | tf_op jit(solution)/shard_map/pallas_call | solution.py:128
  (1 shorter events, 0.0 us)
Async XLA Ops:
  0.0 0.7 %copy-start.2 = (s32[1,4]{1,0:T(1,128)S(1)}, s32[1,4]{1,0:T(1,128)}, u32[]{:S(2)}) copy-start(s32[1,4]{1,0:T(1,128)} %owner_ref.1) | copy-start | bytes 52
  0.7 10.5 %copy-start.1 = (f32[8,1024]{1,0:T(8,128)S(1)}, f32[8,1024]{1,0:T(8,128)}, u32[]{:S(2)}) copy-start(f32[8,1024]{1,0:T(8,128)} %gain_ref.1) | copy-start | bytes 98308
  3.0 24.3 %copy-start = (bf16[384,1024]{1,0:T(8,128)(2,1)S(1)}, bf16[384,1024]{1,0:T(8,128)(2,1)}, u32[]{:S(2)}) copy-start(bf16[384,1024]{1,0:T(8,128)(2,1)} %weight_ref.1) | copy-start | bytes 2359300
  3.0 18.1 %all-to-all-start = ((bf16[16,72,128]{2,1,0:T(8,128)(2,1)}), bf16[16,72,128]{2,1,0:T(8,128)(2,1)S(1)}, u32[]{:S(2)}, u32[]{:S(2)}) async-start(bf16[16,72,128]{2,1,0:T(8,128)(2,1)} %shard_map.100), calls=%async_computation | async-start | bytes 589824 | tf_op jit(solution)/shard_map/all_to_all | solution.py:183
  21.1 1.6 %collective-permute-start = (bf16[16,72,128]{2,1,0:T(8,128)(2,1)S(1)}, bf16[16,72,128]{2,1,0:T(8,128)(2,1)S(1)}, u32[]{:S(2)}, u32[]{:S(2)}) collective-permute-start(bf16[16,72,128]{2,1,0:T(8,128)(2,1)S(1)} %all-to-all-done.refs_0_), channel_id=1, source_target_pairs={{0,4},{4,0},{8,12},{12,8},{1,5},{5,1},{9,13},{13,9},{2,6},{6,2},{1... | collective-permute-start | bytes 884744 | tf_op jit(solution)/shard_map/ppermute | solution.py:194
  23.8 10.4 %all-to-all-start.1 = ((bf16[16,16,128]{2,1,0:T(8,128)(2,1)}), bf16[16,16,128]{2,1,0:T(8,128)(2,1)S(1)}, u32[]{:S(2)}, u32[]{:S(2)}) async-start(bf16[16,16,128]{2,1,0:T(8,128)(2,1)} %get-tuple-element.10), calls=%async_computation.1 | async-start | bytes 131072 | tf_op jit(solution)/shard_map/all_to_all | solution.py:205

commit v4 on v2

v4 whole, which is shorter than its diff:
```python
import functools

import jax
import jax.numpy as jnp
from jax import lax
from jax.experimental import pallas as pl
from jax.experimental.pallas import tpu as pltpu
from jax.sharding import PartitionSpec as P

HEAD_DIM = 128
EPS = 1e-06


def normed(rows, gain):
    values = rows.astype(jnp.float32)
    scale = lax.rsqrt(jnp.mean(values * values, axis=-1, keepdims=True) + EPS)
    return values * scale * gain


def partner(me, size, step):
    if size & (size - 1) == 0:
        return me ^ step
    return (step + size - me) % size


def swap(array, axis, step):
    size = lax.axis_size(axis)
    return lax.ppermute(array, axis, [(i, partner(i, size, step)) for i in range(size)])


def pack_kernel(owners, *refs):
    total = (len(refs) - owners - 2) // 2
    sources, out_refs = refs[:total], refs[total : total + owners]
    held, (norm_ref, copy_sems) = refs[total + owners : -2], refs[-2:]
    copies = [
        pltpu.make_async_copy(source, buffer, copy_sems.at[i])
        for i, (source, buffer) in enumerate(zip(sources, held))
    ]
    for copy in copies:
        copy.start()
    owner_ref, q_ref, k_ref, v_ref, control_ref, qg_ref, kg_ref = held
    rows, feats = q_ref.shape
    share = feats // owners
    slab_rows, width = rows // owners, control_ref.shape[1]
    me = lax.axis_index("ulysses")
    for copy in copies:
        copy.wait()
    norm_ref[0] = normed(k_ref[...], kg_ref[...]).astype(jnp.bfloat16)
    norm_ref[1] = v_ref[...]
    norm_ref[2] = normed(q_ref[...], qg_ref[...]).astype(jnp.bfloat16)
    patches = control_ref[...].astype(jnp.float32)
    slabs = [patches[j * slab_rows : (j + 1) * slab_rows] for j in range(owners)]
    for step, out_ref in enumerate(out_refs):
        to = partner(me, owners, step)
        at = 0
        for i in range(3):
            for head in range(share // HEAD_DIM):
                cols = pl.ds(pl.multiple_of(to * share + head * HEAD_DIM, HEAD_DIM), HEAD_DIM)
                out_ref[at : at + rows] = norm_ref[i, :, cols]
                at = at + rows
        slab = slabs[0]
        for j in range(1, owners):
            slab = jnp.where(owner_ref[0, j] == to, slabs[j], slab)
        slab = slab.astype(jnp.bfloat16)
        for tile in range(width // HEAD_DIM):
            out_ref[at : at + slab_rows] = slab[:, tile * HEAD_DIM : (tile + 1) * HEAD_DIM]
            at = at + slab_rows


def sort_kernel(rows, *refs):
    got_refs, (pair_ref, patch_ref) = refs[:-2], refs[-2:]
    owners = len(got_refs)
    slab_rows, width = rows // owners, patch_ref.shape[1]
    size = pair_ref.shape[1]
    start = 3 * size // 2
    for step, ref in enumerate(got_refs):
        pair_ref[step] = ref[:size]
    slabs = [ref[start:].astype(jnp.float32) for ref in got_refs]
    patches = [
        jnp.concatenate([slab[i * slab_rows : (i + 1) * slab_rows] for slab in slabs], axis=0)
        for i in range(width // HEAD_DIM)
    ]
    patch_ref[...] = normed(jnp.concatenate(patches, axis=1), 1.0).astype(jnp.bfloat16)


def attend_kernel(rows, owners, *refs):
    got_refs, pair_refs, out_refs = refs[:owners], refs[owners:-owners], refs[-owners:]
    heads = out_refs[0].shape[0] // rows
    count = len(pair_refs) * owners * rows
    group = max(1, min(owners, 2**17 // (rows * count)))
    for head in range(heads):
        at, past, ask = (slice((i * heads + head) * rows, (i * heads + head + 1) * rows) for i in range(3))
        keys = jnp.concatenate([ref[:, at].reshape(-1, HEAD_DIM) for ref in pair_refs], axis=0)
        values = jnp.concatenate([ref[:, past].reshape(-1, HEAD_DIM) for ref in pair_refs], axis=0)
        for first in range(0, owners, group):
            part = range(first, min(first + group, owners))
            queries = jnp.concatenate([got_refs[i][ask] for i in part], axis=0)
            scores = lax.dot_general(
                queries, keys, (((1,), (1,)), ((), ())), preferred_element_type=jnp.float32
            ) * (HEAD_DIM ** (-0.5))
            peak = jnp.max(scores, axis=-1, keepdims=True)
            expo = jnp.exp(scores - peak)
            totals = jnp.sum(expo, axis=-1, keepdims=True)
            mixed = jnp.dot(expo.astype(jnp.bfloat16), values, preferred_element_type=jnp.float32)
            mixed = (mixed / totals).astype(jnp.bfloat16)
            for j, i in enumerate(part):
                out_refs[i][at] = mixed[j * rows : (j + 1) * rows]


def hint_kernel(layer_ref, patch_ref, weight_ref, gain_ref, out_ref):
    owners, slab_rows, _ = out_ref.shape
    hint = jnp.dot(patch_ref[...], weight_ref[...], preferred_element_type=jnp.float32)
    hint = hint.astype(jnp.bfloat16).astype(jnp.float32) * gain_ref[pl.ds(layer_ref[0], 1), :]
    me = lax.axis_index("ulysses")
    for step in range(owners):
        out_ref[partner(me, owners, step)] = hint[step * slab_rows : (step + 1) * slab_rows]


def finish_kernel(owners, hint_ref, *refs):
    back_refs, out_ref = refs[:-1], refs[-1]
    rows, feats = out_ref.shape
    share = feats // owners
    me = lax.axis_index("ulysses")
    for step, ref in enumerate(back_refs):
        for head in range(share // HEAD_DIM):
            start = partner(me, owners, step) * share + head * HEAD_DIM
            cols = pl.ds(pl.multiple_of(start, HEAD_DIM), HEAD_DIM)
            attended = ref[head * rows : (head + 1) * rows].astype(jnp.float32)
            out_ref[:, cols] = (attended + hint_ref[:, cols]).astype(jnp.bfloat16)


VMEM = pl.BlockSpec(memory_space=pltpu.VMEM)
SMEM = pl.BlockSpec(memory_space=pltpu.SMEM)
HBM = pl.BlockSpec(memory_space=pltpu.HBM)


def call(kernel, out_shape, specs, *operands, scratch=(), flops=0, nbytes=0):
    return pl.pallas_call(
        kernel,
        out_shape=out_shape,
        in_specs=specs,
        out_specs=jax.tree.map(lambda _: VMEM, out_shape),
        scratch_shapes=scratch,
        compiler_params=pltpu.CompilerParams(vmem_limit_bytes=32 * 2**20),
        cost_estimate=pl.CostEstimate(flops=flops, bytes_accessed=nbytes, transcendentals=0),
    )(*operands)


def shape(dims, dtype=jnp.bfloat16):
    return jax.ShapeDtypeStruct(dims, dtype)


def gather_pairs(pairs, axis):
    size = lax.axis_size(axis)
    if size & (size - 1):
        return [swap(pairs, axis, step) for step in range(size)]
    held = [pairs]
    step = size // 2
    while step:
        held = held + [swap(array, axis, step) for array in held]
        step = step // 2
    return held


def shards(
    query_proj,
    key_proj,
    value_proj,
    query_gain,
    key_gain,
    control,
    hint_weight,
    hint_gain,
    owner_map,
    layer_index,
):
    owners = lax.axis_size("ulysses")
    rows, feats = query_proj.shape
    width = control.shape[1]
    lines = rows * (feats // owners // HEAD_DIM)
    slab_lines = rows // owners * (width // HEAD_DIM)
    sources = (
        owner_map,
        query_proj,
        key_proj,
        value_proj,
        control,
        query_gain.reshape(1, feats),
        key_gain.reshape(1, feats),
    )
    sources = [pltpu.with_memory_space_constraint(source, pltpu.HBM) for source in sources]
    sent = call(
        functools.partial(pack_kernel, owners),
        [shape((3 * lines + slab_lines, HEAD_DIM))] * owners,
        [HBM] * len(sources),
        *sources,
        scratch=[pltpu.SMEM(owner_map.shape, owner_map.dtype)]
        + [pltpu.VMEM(source.shape, source.dtype) for source in sources[1:]]
        + [
            pltpu.VMEM((3, rows, feats), jnp.bfloat16),
            pltpu.SemaphoreType.DMA((len(sources),)),
        ],
    )
    far = [swap(sent[step], "ulysses", step) for step in range(owners - 1, 0, -1)]
    got = [sent[0]] + far[::-1]
    pairs, patches = call(
        functools.partial(sort_kernel, rows),
        [shape((owners, 2 * lines, HEAD_DIM)), shape((rows, width))],
        [VMEM] * owners,
        *got,
    )
    held = gather_pairs(pairs, "blk")
    hint = call(
        hint_kernel,
        shape((owners, rows // owners, feats), jnp.float32),
        [SMEM] + [VMEM] * 3,
        layer_index,
        patches,
        hint_weight,
        hint_gain,
        flops=2 * rows * width * feats,
        nbytes=2 * width * feats,
    )
    mixed = call(
        functools.partial(attend_kernel, rows, owners),
        [shape((lines, HEAD_DIM))] * owners,
        [VMEM] * (owners + len(held)),
        *got,
        *held,
        flops=4 * lines * owners * len(held) * owners * rows * HEAD_DIM,
        nbytes=4 * len(held) * pairs.size,
    )
    far = [swap(mixed[step], "ulysses", step) for step in range(owners - 1, 0, -1)]
    return call(
        functools.partial(finish_kernel, owners),
        shape((rows, feats)),
        [VMEM] * (owners + 1),
        hint.reshape(rows, feats),
        mixed[0],
        *far[::-1],
    )


def solution(mesh):
    split = P(("groups", "blk", "ulysses"), None)
    return jax.shard_map(
        shards,
        mesh=mesh,
        in_specs=(
            split,
            split,
            split,
            P(),
            P(),
            split,
            P(),
            P(),
            split,
            P(("groups", "blk", "ulysses")),
        ),
        out_specs=split,
        check_vma=False,
    )
```

time: 51.2 us -> 28.2 us (0.55)
  blocking collectives: 40.6 us -> 0 us
  waiting for transfers between devices: 1.44 us -> 12.7 us
  starting transfers between devices: 3.64 us -> 11.7 us
  Pallas kernels: 3.78 us -> 2.92 us
  local copies, waits for them, and re-layouts: 0.66 us -> 0.01 us
    all_gather x2 -> x0, blocking collectives: 24.4 us -> none  [the longest x1 13.3 us: shards(): arrived = lax.all_gather(control, 'ulysses', axis=0)]
    all_to_all x1 -> x0, blocking collectives: 16.2 us -> none  [shards(): got = lax.all_to_all(send, VIDEO, split_axis=0, concat_axis=0, tiled=True)]
    ppermute x1 -> x9, starting transfers between devices: 0.01 us -> 11.7 us  [swap(): lax.ppermute(array, axis, [(i, partner(i, size, step)) for i in range(siz...]
    ppermute x1 -> x9, waiting for transfers between devices: 1.44 us -> 12.7 us  [swap(): lax.ppermute(array, axis, [(i, partner(i, size, step)) for i in range(siz...]
    all_to_all x1 -> x0, starting transfers between devices: 3.63 us -> none  [shards(): back = lax.all_to_all(mixed, VIDEO, split_axis=0, concat_axis=0, tiled=True)]
    pallas_call x3 -> x5, Pallas kernels: 3.78 us -> 2.92 us  [call(): pl.pallas_call(kernel, out_shape=out_shape, in_specs=specs, out_specs=jax...]
    unnamed x8 -> x4, local copies, waits for them, and re-layouts: 0.66 us -> 0.01 us
  transfers between devices with their start and end apart: 2 -> 9, of which waited for: 1 -> 5; matrix products, arithmetic and copies ran while one was open for 0% -> 0% of each run, Pallas kernels for 0% -> 1%
where the time goes in v4:
time: 28.2 us; the launch traced here: 28 us
  waiting for transfers between devices  12.7 us (45%)
  starting transfers between devices  11.7 us (41%)
  Pallas kernels  2.92 us (10%)
  between operations  0.73 us (3%)
    ppermute x9, waiting for transfers between devices, swap(): lax.ppermute(array, axis, [(i, partner(i, size, step)) for i in range(siz...  12.7 us
    ppermute x9, starting transfers between devices, swap(): lax.ppermute(array, axis, [(i, partner(i, size, step)) for i in range(siz...  11.7 us
    pallas_call x5, Pallas kernels, call(): pl.pallas_call(kernel, out_shape=out_shape, in_specs=specs, out_specs=jax...  2.92 us
  transfers between devices with their start and end apart: 9, of which 5 were waited for; matrix products, arithmetic and copies ran while one was open for 0% of the time, Pallas kernels for 1%

profile of v4, /device:TPU:0, one launch (start us, length us, event | category | flops | bytes accessed | tf_op | source)
XLA Modules:
  0.0 28.0 jit_solution(11174610534798355641)
XLA Ops:
  0.0 0.0 copy-start
  0.0 1.2 %shard_map.100 = (bf16[216,128]{1,0:T(8,128)(2,1)S(1)}, bf16[216,128]{1,0:T(8,128)(2,1)S(1)}, bf16[216,128]{1,0:T(8,128)(2,1)S(1)}, bf16[216,128]{1,0:T(8,128)(2,1)S(1)}) custom-call(s32[1,4]{1,0:T(1,128)} %refs_0_.1, bf16[32,1024]{1,0:T(8,128)(2,1)} %refs_1_.1, bf16[32,1024]{1,0:T(8,128)(2,1)} %refs_2_.1, bf16[32,1024]{1,0:T(8,128)(2,1)} %refs_3_.1, ...), custom_call_target="tpu_custom_call" | custom-call | tf_op jit(solution)/shard_map/pallas_call | solution.py:138
  1.2 3.1 %collective-permute-start = (bf16[216,128]{1,0:T(8,128)(2,1)S(1)}, bf16[216,128]{1,0:T(8,128)(2,1)S(1)}, u32[]{:S(2)}, u32[]{:S(2)}) collective-permute-start(bf16[216,128]{1,0:T(8,128)(2,1)S(1)} %get-tuple-element.16), channel_id=1, source_target_pairs={{0,1},{1,0},{2,3},{3,2},{4,5},{5,4},{6,7},{7,6},{8,9},{9,8},{10,11... | collective-permute-start | bytes 165896 | tf_op jit(solution)/shard_map/ppermute | solution.py:28
  4.3 2.6 %collective-permute-start.1 = (bf16[216,128]{1,0:T(8,128)(2,1)S(1)}, bf16[216,128]{1,0:T(8,128)(2,1)S(1)}, u32[]{:S(2)}, u32[]{:S(2)}) collective-permute-start(bf16[216,128]{1,0:T(8,128)(2,1)S(1)} %get-tuple-element.17), channel_id=1, source_target_pairs={{0,2},{1,3},{2,0},{3,1},{4,6},{5,7},{6,4},{7,5},{8,10},{9,11},{10,... | collective-permute-start | bytes 165896 | tf_op jit(solution)/shard_map/ppermute | solution.py:28
  6.9 0.0 collective-permute-start.2
  6.9 0.0 collective-permute-done.refs_1_
  6.9 3.5 %collective-permute-done.1.refs_2_ = bf16[216,128]{1,0:T(8,128)(2,1)S(1)} collective-permute-done((bf16[216,128]{1,0:T(8,128)(2,1)S(1)}, bf16[216,128]{1,0:T(8,128)(2,1)S(1)}, u32[]{:S(2)}, u32[]{:S(2)}) %collective-permute-start.1) | collective-permute-done | bytes 55328 | tf_op jit(solution)/shard_map/ppermute | solution.py:28
  10.5 2.4 %collective-permute-done.2.refs_3_ = bf16[216,128]{1,0:T(8,128)(2,1)S(1)} collective-permute-done((bf16[216,128]{1,0:T(8,128)(2,1)S(1)}, bf16[216,128]{1,0:T(8,128)(2,1)S(1)}, u32[]{:S(2)}, u32[]{:S(2)}) %collective-permute-start.2) | collective-permute-done | bytes 55328 | tf_op jit(solution)/shard_map/ppermute | solution.py:28
  12.9 0.1 shard_map.101
  13.0 0.0 copy-start.1
  13.0 1.6 %collective-permute-start.3 = (bf16[4,128,128]{2,1,0:T(8,128)(2,1)S(1)}, bf16[4,128,128]{2,1,0:T(8,128)(2,1)S(1)}, u32[]{:S(2)}, u32[]{:S(2)}) collective-permute-start(bf16[4,128,128]{2,1,0:T(8,128)(2,1)S(1)} %get-tuple-element.20.refs_4_), channel_id=1, source_target_pairs={{0,8},{4,12},{8,0},{12,4},{1,9},{5,13},{9,1},{13,5},{2,10},{6,14},... | collective-permute-start | bytes 393224 | tf_op jit(solution)/shard_map/ppermute | solution.py:28
  14.5 0.0 collective-permute-start.4
  14.5 3.5 %collective-permute-done.3.refs_5_ = bf16[4,128,128]{2,1,0:T(8,128)(2,1)S(1)} collective-permute-done((bf16[4,128,128]{2,1,0:T(8,128)(2,1)S(1)}, bf16[4,128,128]{2,1,0:T(8,128)(2,1)S(1)}, u32[]{:S(2)}, u32[]{:S(2)}) %collective-permute-start.3) | collective-permute-done | bytes 131104 | tf_op jit(solution)/shard_map/ppermute | solution.py:28
  18.0 0.0 collective-permute-start.5
  18.0 0.0 collective-permute-done.4.refs_6_
  18.0 1.3 %collective-permute-done.5.refs_7_ = bf16[4,128,128]{2,1,0:T(8,128)(2,1)S(1)} collective-permute-done((bf16[4,128,128]{2,1,0:T(8,128)(2,1)S(1)}, bf16[4,128,128]{2,1,0:T(8,128)(2,1)S(1)}, u32[]{:S(2)}, u32[]{:S(2)}) %collective-permute-start.5) | collective-permute-done | bytes 131104 | tf_op jit(solution)/shard_map/ppermute | solution.py:28
  19.4 0.7 %shard_map.103 = (bf16[64,128]{1,0:T(8,128)(2,1)S(1)}, bf16[64,128]{1,0:T(8,128)(2,1)S(1)}, bf16[64,128]{1,0:T(8,128)(2,1)S(1)}, bf16[64,128]{1,0:T(8,128)(2,1)S(1)}) custom-call(bf16[216,128]{1,0:T(8,128)(2,1)S(1)} %get-tuple-element.15.refs_0_, bf16[216,128]{1,0:T(8,128)(2,1)S(1)} %collective-permute-done.refs_1_, ...), custom_call_target="tpu_custom_call" | custom-call | flops 67108864 | bytes 1048576 | tf_op jit(solution)/shard_map/pallas_call | solution.py:138
  20.1 0.1 collective-permute-start.6
  20.1 1.7 %collective-permute-start.7 = (bf16[64,128]{1,0:T(8,128)(2,1)S(1)}, bf16[64,128]{1,0:T(8,128)(2,1)S(1)}, u32[]{:S(2)}, u32[]{:S(2)}) collective-permute-start(bf16[64,128]{1,0:T(8,128)(2,1)S(1)} %get-tuple-element.23), channel_id=1, source_target_pairs={{0,2},{1,3},{2,0},{3,1},{4,6},{5,7},{6,4},{7,5},{8,10},{9,11},{10,... | collective-permute-start | bytes 49160 | tf_op jit(solution)/shard_map/ppermute | solution.py:28
  21.8 2.7 %collective-permute-start.8 = (bf16[64,128]{1,0:T(8,128)(2,1)S(1)}, bf16[64,128]{1,0:T(8,128)(2,1)S(1)}, u32[]{:S(2)}, u32[]{:S(2)}) collective-permute-start(bf16[64,128]{1,0:T(8,128)(2,1)S(1)} %get-tuple-element.24), channel_id=1, source_target_pairs={{0,3},{1,2},{2,1},{3,0},{4,7},{5,6},{6,5},{7,4},{8,11},{9,10},{10,... | collective-permute-start | bytes 49160 | tf_op jit(solution)/shard_map/ppermute | solution.py:28
  25.2 0.0 copy-done
  25.2 0.0 copy-done.1
  25.2 0.3 shard_map.102
  25.4 0.0 collective-permute-done.6.refs_1_
  25.5 0.0 collective-permute-done.7.refs_2_
  25.5 1.9 %collective-permute-done.8.refs_3_ = bf16[64,128]{1,0:T(8,128)(2,1)S(1)} collective-permute-done((bf16[64,128]{1,0:T(8,128)(2,1)S(1)}, bf16[64,128]{1,0:T(8,128)(2,1)S(1)}, u32[]{:S(2)}, u32[]{:S(2)}) %collective-permute-start.8) | collective-permute-done | bytes 16416 | tf_op jit(solution)/shard_map/ppermute | solution.py:28
  27.4 0.7 %shard_map.104 = bf16[32,1024]{1,0:T(8,128)(2,1)} custom-call(f32[32,1024]{1,0:T(8,128)S(1)} %bitcast.3, bf16[64,128]{1,0:T(8,128)(2,1)S(1)} %get-tuple-element.21.refs_0_, bf16[64,128]{1,0:T(8,128)(2,1)S(1)} %collective-permute-done.6.refs_1_, bf16[64,128]{1,0:T(8,128)(2,1)S(1)} %collective-permute-done.7.refs_2_, ...), custom_call_target="tpu_custom_call" | custom-call | tf_op jit(solution)/shard_map/pallas_call | solution.py:138
Async XLA Ops:
  0.0 25.2 %copy-start = (bf16[384,1024]{1,0:T(8,128)(2,1)S(1)}, bf16[384,1024]{1,0:T(8,128)(2,1)}, u32[]{:S(2)}) copy-start(bf16[384,1024]{1,0:T(8,128)(2,1)} %weight_ref.1) | copy-start | bytes 2359300
  1.2 5.7 %collective-permute-start = (bf16[216,128]{1,0:T(8,128)(2,1)S(1)}, bf16[216,128]{1,0:T(8,128)(2,1)S(1)}, u32[]{:S(2)}, u32[]{:S(2)}) collective-permute-start(bf16[216,128]{1,0:T(8,128)(2,1)S(1)} %get-tuple-element.16), channel_id=1, source_target_pairs={{0,1},{1,0},{2,3},{3,2},{4,5},{5,4},{6,7},{7,6},{8,9},{9,8},{10,11... | collective-permute-start | bytes 165896 | tf_op jit(solution)/shard_map/ppermute | solution.py:28
  4.3 6.1 %collective-permute-start.1 = (bf16[216,128]{1,0:T(8,128)(2,1)S(1)}, bf16[216,128]{1,0:T(8,128)(2,1)S(1)}, u32[]{:S(2)}, u32[]{:S(2)}) collective-permute-start(bf16[216,128]{1,0:T(8,128)(2,1)S(1)} %get-tuple-element.17), channel_id=1, source_target_pairs={{0,2},{1,3},{2,0},{3,1},{4,6},{5,7},{6,4},{7,5},{8,10},{9,11},{10,... | collective-permute-start | bytes 165896 | tf_op jit(solution)/shard_map/ppermute | solution.py:28
  6.9 6.0 %collective-permute-start.2 = (bf16[216,128]{1,0:T(8,128)(2,1)S(1)}, bf16[216,128]{1,0:T(8,128)(2,1)S(1)}, u32[]{:S(2)}, u32[]{:S(2)}) collective-permute-start(bf16[216,128]{1,0:T(8,128)(2,1)S(1)} %get-tuple-element.18), channel_id=1, source_target_pairs={{0,3},{1,2},{2,1},{3,0},{4,7},{5,6},{6,5},{7,4},{8,11},{9,10},{10,... | collective-permute-start | bytes 165896 | tf_op jit(solution)/shard_map/ppermute | solution.py:28
  13.0 12.2 %copy-start.1 = (f32[8,1024]{1,0:T(8,128)S(1)}, f32[8,1024]{1,0:T(8,128)}, u32[]{:S(2)}) copy-start(f32[8,1024]{1,0:T(8,128)} %gain_ref.1) | copy-start | bytes 98308
  13.0 5.0 %collective-permute-start.3 = (bf16[4,128,128]{2,1,0:T(8,128)(2,1)S(1)}, bf16[4,128,128]{2,1,0:T(8,128)(2,1)S(1)}, u32[]{:S(2)}, u32[]{:S(2)}) collective-permute-start(bf16[4,128,128]{2,1,0:T(8,128)(2,1)S(1)} %get-tuple-element.20.refs_4_), channel_id=1, source_target_pairs={{0,8},{4,12},{8,0},{12,4},{1,9},{5,13},{9,1},{13,5},{2,10},{6,14},... | collective-permute-start | bytes 393224 | tf_op jit(solution)/shard_map/ppermute | solution.py:28
  14.5 3.5 %collective-permute-start.4 = (bf16[4,128,128]{2,1,0:T(8,128)(2,1)S(1)}, bf16[4,128,128]{2,1,0:T(8,128)(2,1)S(1)}, u32[]{:S(2)}, u32[]{:S(2)}) collective-permute-start(bf16[4,128,128]{2,1,0:T(8,128)(2,1)S(1)} %get-tuple-element.20.refs_4_), channel_id=1, source_target_pairs={{0,4},{4,0},{8,12},{12,8},{1,5},{5,1},{9,13},{13,9},{2,6},{6,2},{1... | collective-permute-start | bytes 393224 | tf_op jit(solution)/shard_map/ppermute | solution.py:28
  18.0 1.3 %collective-permute-start.5 = (bf16[4,128,128]{2,1,0:T(8,128)(2,1)S(1)}, bf16[4,128,128]{2,1,0:T(8,128)(2,1)S(1)}, u32[]{:S(2)}, u32[]{:S(2)}) collective-permute-start(bf16[4,128,128]{2,1,0:T(8,128)(2,1)S(1)} %collective-permute-done.3.refs_5_), channel_id=1, source_target_pairs={{0,4},{4,0},{8,12},{12,8},{1,5},{5,1},{9,13},{13,9},{2,6},{6,2},{1... | collective-permute-start | bytes 393224 | tf_op jit(solution)/shard_map/ppermute | solution.py:28
  20.1 5.4 %collective-permute-start.6 = (bf16[64,128]{1,0:T(8,128)(2,1)S(1)}, bf16[64,128]{1,0:T(8,128)(2,1)S(1)}, u32[]{:S(2)}, u32[]{:S(2)}) collective-permute-start(bf16[64,128]{1,0:T(8,128)(2,1)S(1)} %get-tuple-element.22), channel_id=1, source_target_pairs={{0,1},{1,0},{2,3},{3,2},{4,5},{5,4},{6,7},{7,6},{8,9},{9,8},{10,11... | collective-permute-start | bytes 49160 | tf_op jit(solution)/shard_map/ppermute | solution.py:28
  20.1 5.3 %collective-permute-start.7 = (bf16[64,128]{1,0:T(8,128)(2,1)S(1)}, bf16[64,128]{1,0:T(8,128)(2,1)S(1)}, u32[]{:S(2)}, u32[]{:S(2)}) collective-permute-start(bf16[64,128]{1,0:T(8,128)(2,1)S(1)} %get-tuple-element.23), channel_id=1, source_target_pairs={{0,2},{1,3},{2,0},{3,1},{4,6},{5,7},{6,4},{7,5},{8,10},{9,11},{10,... | collective-permute-start | bytes 49160 | tf_op jit(solution)/shard_map/ppermute | solution.py:28
  21.8 5.5 %collective-permute-start.8 = (bf16[64,128]{1,0:T(8,128)(2,1)S(1)}, bf16[64,128]{1,0:T(8,128)(2,1)S(1)}, u32[]{:S(2)}, u32[]{:S(2)}) collective-permute-start(bf16[64,128]{1,0:T(8,128)(2,1)S(1)} %get-tuple-element.24), channel_id=1, source_target_pairs={{0,3},{1,2},{2,1},{3,0},{4,7},{5,6},{6,5},{7,4},{8,11},{9,10},{10,... | collective-permute-start | bytes 49160 | tf_op jit(solution)/shard_map/ppermute | solution.py:28

commit v5 on v4

--- a/solution.py
+++ b/solution.py
@@ -29,9 +29,9 @@
 
 
 def pack_kernel(owners, *refs):
-    total = (len(refs) - owners - 2) // 2
-    sources, out_refs = refs[:total], refs[total : total + owners]
-    held, (norm_ref, copy_sems) = refs[total + owners : -2], refs[-2:]
+    total = (len(refs) - 2 * owners - 2) // 2
+    sources, outs = refs[:total], refs[total : total + 2 * owners]
+    held, (norm_ref, copy_sems) = refs[total + 2 * owners : -2], refs[-2:]
     copies = [
         pltpu.make_async_copy(source, buffer, copy_sems.at[i])
         for i, (source, buffer) in enumerate(zip(sources, held))
@@ -50,51 +50,40 @@
     norm_ref[2] = normed(q_ref[...], qg_ref[...]).astype(jnp.bfloat16)
     patches = control_ref[...].astype(jnp.float32)
     slabs = [patches[j * slab_rows : (j + 1) * slab_rows] for j in range(owners)]
-    for step, out_ref in enumerate(out_refs):
+    for step in range(owners):
         to = partner(me, owners, step)
-        at = 0
-        for i in range(3):
+        pair_ref, ask_ref = outs[step], outs[owners + step]
+        for i, (out_ref, first) in enumerate(((pair_ref, 0), (pair_ref, 1), (ask_ref, 0))):
             for head in range(share // HEAD_DIM):
                 cols = pl.ds(pl.multiple_of(to * share + head * HEAD_DIM, HEAD_DIM), HEAD_DIM)
+                at = (first * (share // HEAD_DIM) + head) * rows
                 out_ref[at : at + rows] = norm_ref[i, :, cols]
-                at = at + rows
         slab = slabs[0]
         for j in range(1, owners):
             slab = jnp.where(owner_ref[0, j] == to, slabs[j], slab)
         slab = slab.astype(jnp.bfloat16)
         for tile in range(width // HEAD_DIM):
-            out_ref[at : at + slab_rows] = slab[:, tile * HEAD_DIM : (tile + 1) * HEAD_DIM]
-            at = at + slab_rows
-
-
-def sort_kernel(rows, *refs):
-    got_refs, (pair_ref, patch_ref) = refs[:-2], refs[-2:]
-    owners = len(got_refs)
-    slab_rows, width = rows // owners, patch_ref.shape[1]
-    size = pair_ref.shape[1]
-    start = 3 * size // 2
-    for step, ref in enumerate(got_refs):
-        pair_ref[step] = ref[:size]
-    slabs = [ref[start:].astype(jnp.float32) for ref in got_refs]
-    patches = [
-        jnp.concatenate([slab[i * slab_rows : (i + 1) * slab_rows] for slab in slabs], axis=0)
-        for i in range(width // HEAD_DIM)
-    ]
-    patch_ref[...] = normed(jnp.concatenate(patches, axis=1), 1.0).astype(jnp.bfloat16)
+            at = share // HEAD_DIM * rows + tile * slab_rows
+            ask_ref[at : at + slab_rows] = slab[:, tile * HEAD_DIM : (tile + 1) * HEAD_DIM]
+
+
+def join_kernel(*refs):
+    for i, ref in enumerate(refs[:-1]):
+        refs[-1][i] = ref[...]
 
 
 def attend_kernel(rows, owners, *refs):
     got_refs, pair_refs, out_refs = refs[:owners], refs[owners:-owners], refs[-owners:]
     heads = out_refs[0].shape[0] // rows
-    count = len(pair_refs) * owners * rows
+    count = sum(ref.shape[0] for ref in pair_refs) * rows
     group = max(1, min(owners, 2**17 // (rows * count)))
     for head in range(heads):
-        at, past, ask = (slice((i * heads + head) * rows, (i * heads + head + 1) * rows) for i in range(3))
+        at, past = (slice((i * heads + head) * rows, (i * heads + head + 1) * rows) for i in range(2))
         keys = jnp.concatenate([ref[:, at].reshape(-1, HEAD_DIM) for ref in pair_refs], axis=0)
         values = jnp.concatenate([ref[:, past].reshape(-1, HEAD_DIM) for ref in pair_refs], axis=0)
         for first in range(0, owners, group):
             part = range(first, min(first + group, owners))
-            queries = jnp.concatenate([got_refs[i][ask] for i in part], axis=0)
+            queries = jnp.concatenate([got_refs[i][at] for i in part], axis=0)
             scores = lax.dot_general(
                 queries, keys, (((1,), (1,)), ((), ())), preferred_element_type=jnp.float32
             ) * (HEAD_DIM ** (-0.5))
@@ -107,9 +96,17 @@
                 out_refs[i][at] = mixed[j * rows : (j + 1) * rows]
 
 
-def hint_kernel(layer_ref, patch_ref, weight_ref, gain_ref, out_ref):
+def hint_kernel(layer_ref, weight_ref, gain_ref, *refs):
+    got_refs, out_ref = refs[:-1], refs[-1]
     owners, slab_rows, _ = out_ref.shape
-    hint = jnp.dot(patch_ref[...], weight_ref[...], preferred_element_type=jnp.float32)
+    tiles = weight_ref.shape[0] // HEAD_DIM
+    slabs = [ref[ref.shape[0] - tiles * slab_rows :].astype(jnp.float32) for ref in got_refs]
+    patches = [
+        jnp.concatenate([slab[i * slab_rows : (i + 1) * slab_rows] for slab in slabs], axis=0)
+        for i in range(tiles)
+    ]
+    patches = normed(jnp.concatenate(patches, axis=1), 1.0).astype(jnp.bfloat16)
+    hint = jnp.dot(patches, weight_ref[...], preferred_element_type=jnp.float32)
     hint = hint.astype(jnp.bfloat16).astype(jnp.float32) * gain_ref[pl.ds(layer_ref[0], 1), :]
     me = lax.axis_index("ulysses")
     for step in range(owners):
@@ -150,16 +147,12 @@
     return jax.ShapeDtypeStruct(dims, dtype)
 
 
-def gather_pairs(pairs, axis):
-    size = lax.axis_size(axis)
-    if size & (size - 1):
-        return [swap(pairs, axis, step) for step in range(size)]
-    held = [pairs]
-    step = size // 2
-    while step:
-        held = held + [swap(array, axis, step) for array in held]
-        step = step // 2
-    return held
+def gather(pairs, axis):
+    return [pairs] + [swap(pairs, axis, step) for step in range(lax.axis_size(axis) - 1, 0, -1)]
+
+
+def exchange(arrays, axis):
+    return [arrays[0]] + [swap(array, axis, step) for step, array in enumerate(arrays) if step]
 
 
 def shards(
@@ -191,7 +184,7 @@
     sources = [pltpu.with_memory_space_constraint(source, pltpu.HBM) for source in sources]
     sent = call(
         functools.partial(pack_kernel, owners),
-        [shape((3 * lines + slab_lines, HEAD_DIM))] * owners,
+        [shape((2 * lines, HEAD_DIM))] * owners + [shape((lines + slab_lines, HEAD_DIM))] * owners,
         [HBM] * len(sources),
         *sources,
         scratch=[pltpu.SMEM(owner_map.shape, owner_map.dtype)]
@@ -201,23 +194,21 @@
             pltpu.SemaphoreType.DMA((len(sources),)),
         ],
     )
-    far = [swap(sent[step], "ulysses", step) for step in range(owners - 1, 0, -1)]
-    got = [sent[0]] + far[::-1]
-    pairs, patches = call(
-        functools.partial(sort_kernel, rows),
-        [shape((owners, 2 * lines, HEAD_DIM)), shape((rows, width))],
-        [VMEM] * owners,
-        *got,
-    )
-    held = gather_pairs(pairs, "blk")
+    pairs = exchange(sent[:owners], "ulysses")
+    near = gather(pairs[0][None], "blk")
+    got = exchange(sent[owners:], "ulysses")
+    joined = call(
+        join_kernel, shape((owners - 1, 2 * lines, HEAD_DIM)), [VMEM] * (owners - 1), *pairs[1:]
+    )
+    held = near + gather(joined, "blk")
     hint = call(
         hint_kernel,
         shape((owners, rows // owners, feats), jnp.float32),
-        [SMEM] + [VMEM] * 3,
+        [SMEM] + [VMEM] * (2 + owners),
         layer_index,
-        patches,
         hint_weight,
         hint_gain,
+        *got,
         flops=2 * rows * width * feats,
         nbytes=2 * width * feats,
     )
@@ -227,17 +218,15 @@
         [VMEM] * (owners + len(held)),
         *got,
         *held,
-        flops=4 * lines * owners * len(held) * owners * rows * HEAD_DIM,
-        nbytes=4 * len(held) * pairs.size,
-    )
-    far = [swap(mixed[step], "ulysses", step) for step in range(owners - 1, 0, -1)]
+        flops=2 * lines * sum(array.size for array in held),
+        nbytes=2 * sum(array.size for array in held),
+    )
     return call(
         functools.partial(finish_kernel, owners),
         shape((rows, feats)),
         [VMEM] * (owners + 1),
         hint.reshape(rows, feats),
-        mixed[0],
-        *far[::-1],
+        *exchange(mixed, "ulysses"),
     )
 
 

time: 28.2 us -> 38.2 us (1.35)
  waiting for transfers between devices: 12.7 us -> 18.3 us
  starting transfers between devices: 11.7 us -> 16.1 us
    ppermute x9 -> x15, waiting for transfers between devices: 12.7 us -> 18.3 us  [swap(): lax.ppermute(array, axis, [(i, partner(i, size, step)) for i in range(siz...]
    ppermute x9 -> x15, starting transfers between devices: 11.7 us -> 16.1 us  [swap(): lax.ppermute(array, axis, [(i, partner(i, size, step)) for i in range(siz...]
  transfers between devices with their start and end apart: 9 -> 15, of which waited for: 5 -> 7; matrix products, arithmetic and copies ran while one was open for 0% -> 0% of each run, Pallas kernels for 1% -> 1%
where the time goes in v5:
time: 38.2 us; the launch traced here: 38.1 us
  waiting for transfers between devices  18.3 us (48%)
  starting transfers between devices  16.1 us (42%)
  Pallas kernels  2.89 us (8%)
  between operations  0.74 us (2%)
    ppermute x15, waiting for transfers between devices, swap(): lax.ppermute(array, axis, [(i, partner(i, size, step)) for i in range(siz...  18.3 us
    ppermute x15, starting transfers between devices, swap(): lax.ppermute(array, axis, [(i, partner(i, size, step)) for i in range(siz...  16.1 us
    pallas_call x5, Pallas kernels, call(): pl.pallas_call(kernel, out_shape=out_shape, in_specs=specs, out_specs=jax...  2.89 us
  transfers between devices with their start and end apart: 15, of which 7 were waited for; matrix products, arithmetic and copies ran while one was open for 0% of the time, Pallas kernels for 1%

profile of v5, /device:TPU:0, one launch (start us, length us, event | category | flops | bytes accessed | tf_op | source)
XLA Modules:
  0.0 38.1 jit_solution(6410736876390596462)
XLA Ops:
  0.0 0.0 copy-start
  0.0 1.2 %shard_map.100 = (bf16[128,128]{1,0:T(8,128)(2,1)S(1)}, bf16[128,128]{1,0:T(8,128)(2,1)S(1)}, bf16[128,128]{1,0:T(8,128)(2,1)S(1)}, bf16[128,128]{1,0:T(8,128)(2...) custom-call(s32[1,4]{1,0:T(1,128)} %refs_0_.1, ...), custom_call_target="tpu_custom_call" | custom-call | tf_op jit(solution)/shard_map/pallas_call | solution.py:135
  1.2 3.1 %collective-permute-start.6 = (bf16[128,128]{1,0:T(8,128)(2,1)S(1)}, bf16[128,128]{1,0:T(8,128)(2,1)S(1)}, u32[]{:S(2)}, u32[]{:S(2)}) collective-permute-start(bf16[128,128]{1,0:T(8,128)(2,1)S(1)} %get-tuple-element.22), channel_id=1, source_target_pairs={{0,1},{1,0},{2,3},{3,2},{4,5},{5,4},{6,7},{7,6},{8,9},{9,8},{10,11... | collective-permute-start | bytes 98312 | tf_op jit(solution)/shard_map/ppermute | solution.py:28
  4.3 2.6 %collective-permute-start.7 = (bf16[128,128]{1,0:T(8,128)(2,1)S(1)}, bf16[128,128]{1,0:T(8,128)(2,1)S(1)}, u32[]{:S(2)}, u32[]{:S(2)}) collective-permute-start(bf16[128,128]{1,0:T(8,128)(2,1)S(1)} %get-tuple-element.23), channel_id=1, source_target_pairs={{0,2},{1,3},{2,0},{3,1},{4,6},{5,7},{6,4},{7,5},{8,10},{9,11},{10,... | collective-permute-start | bytes 98312 | tf_op jit(solution)/shard_map/ppermute | solution.py:28
  6.9 0.0 collective-permute-start.8
  6.9 0.0 collective-permute-done.6.refs_0_
  6.9 2.8 %collective-permute-done.7.refs_1_ = bf16[128,128]{1,0:T(8,128)(2,1)S(1)} collective-permute-done((bf16[128,128]{1,0:T(8,128)(2,1)S(1)}, bf16[128,128]{1,0:T(8,128)(2,1)S(1)}, u32[]{:S(2)}, u32[]{:S(2)}) %collective-permute-start.7) | collective-permute-done | bytes 32800 | tf_op jit(solution)/shard_map/ppermute | solution.py:28
  9.7 2.9 %collective-permute-done.8.refs_2_ = bf16[128,128]{1,0:T(8,128)(2,1)S(1)} collective-permute-done((bf16[128,128]{1,0:T(8,128)(2,1)S(1)}, bf16[128,128]{1,0:T(8,128)(2,1)S(1)}, u32[]{:S(2)}, u32[]{:S(2)}) %collective-permute-start.8) | collective-permute-done | bytes 32800 | tf_op jit(solution)/shard_map/ppermute | solution.py:28
  12.6 1.6 %collective-permute-start.10 = (bf16[3,128,128]{2,1,0:T(8,128)(2,1)S(1)}, bf16[3,128,128]{2,1,0:T(8,128)(2,1)S(1)}, u32[]{:S(2)}, u32[]{:S(2)}) collective-permute-start(bf16[3,128,128]{2,1,0:T(8,128)(2,1)S(1)} %shard_map.102.refs_8_), channel_id=1, source_target_pairs={{0,8},{4,12},{8,0},{12,4},{1,9},{5,13},{9,1},{13,5},{2,10},{6,14},... | collective-permute-start | bytes 294920 | tf_op jit(solution)/shard_map/ppermute | solution.py:28
  14.2 0.0 collective-permute-start.11
  14.2 0.6 %collective-permute-start.9 = (bf16[3,128,128]{2,1,0:T(8,128)(2,1)S(1)}, bf16[3,128,128]{2,1,0:T(8,128)(2,1)S(1)}, u32[]{:S(2)}, u32[]{:S(2)}) collective-permute-start(bf16[3,128,128]{2,1,0:T(8,128)(2,1)S(1)} %shard_map.102.refs_8_), channel_id=1, source_target_pairs={{0,12},{4,8},{8,4},{12,0},{1,13},{5,9},{9,5},{13,1},{2,14},{6,10},... | collective-permute-start | bytes 294920 | tf_op jit(solution)/shard_map/ppermute | solution.py:28
  14.9 0.0 collective-permute-start
  14.9 0.9 %collective-permute-start.1 = (bf16[88,128]{1,0:T(8,128)(2,1)S(1)}, bf16[88,128]{1,0:T(8,128)(2,1)S(1)}, u32[]{:S(2)}, u32[]{:S(2)}) collective-permute-start(bf16[88,128]{1,0:T(8,128)(2,1)S(1)} %get-tuple-element.19), channel_id=1, source_target_pairs={{0,2},{1,3},{2,0},{3,1},{4,6},{5,7},{6,4},{7,5},{8,10},{9,11},{10,... | collective-permute-start | bytes 67592 | tf_op jit(solution)/shard_map/ppermute | solution.py:28
  15.8 3.1 %collective-permute-done.refs_1_ = bf16[88,128]{1,0:T(8,128)(2,1)S(1)} collective-permute-done((bf16[88,128]{1,0:T(8,128)(2,1)S(1)}, bf16[88,128]{1,0:T(8,128)(2,1)S(1)}, u32[]{:S(2)}, u32[]{:S(2)}) %collective-permute-start) | collective-permute-done | bytes 22560 | tf_op jit(solution)/shard_map/ppermute | solution.py:28
  18.8 0.1 collective-permute-start.3
  18.9 0.7 %collective-permute-done.1.refs_2_ = bf16[88,128]{1,0:T(8,128)(2,1)S(1)} collective-permute-done((bf16[88,128]{1,0:T(8,128)(2,1)S(1)}, bf16[88,128]{1,0:T(8,128)(2,1)S(1)}, u32[]{:S(2)}, u32[]{:S(2)}) %collective-permute-start.1) | collective-permute-done | bytes 22560 | tf_op jit(solution)/shard_map/ppermute | solution.py:28
  19.6 1.5 %collective-permute-start.2 = (bf16[88,128]{1,0:T(8,128)(2,1)S(1)}, bf16[88,128]{1,0:T(8,128)(2,1)S(1)}, u32[]{:S(2)}, u32[]{:S(2)}) collective-permute-start(bf16[88,128]{1,0:T(8,128)(2,1)S(1)} %get-tuple-element.20), channel_id=1, source_target_pairs={{0,3},{1,2},{2,1},{3,0},{4,7},{5,6},{6,5},{7,4},{8,11},{9,10},{10,... | collective-permute-start | bytes 67592 | tf_op jit(solution)/shard_map/ppermute | solution.py:28
  21.0 4.3 %collective-permute-done.2.refs_3_ = bf16[88,128]{1,0:T(8,128)(2,1)S(1)} collective-permute-done((bf16[88,128]{1,0:T(8,128)(2,1)S(1)}, bf16[88,128]{1,0:T(8,128)(2,1)S(1)}, u32[]{:S(2)}, u32[]{:S(2)}) %collective-permute-start.2) | collective-permute-done | bytes 22560 | tf_op jit(solution)/shard_map/ppermute | solution.py:28
  25.3 1.3 %collective-permute-start.4 = (bf16[1,128,128]{2,1,0:T(8,128)(2,1)S(1)}, bf16[1,128,128]{2,1,0:T(8,128)(2,1)S(1)}, u32[]{:S(2)}, u32[]{:S(2)}) collective-permute-start(bf16[1,128,128]{2,1,0:T(8,128)(2,1)S(1)} %bitcast.6), channel_id=1, source_target_pairs={{0,8},{4,12},{8,0},{12,4},{1,9},{5,13},{9,1},{13,5},{2,10},{6,14},... | collective-permute-start | bytes 98312 | tf_op jit(solution)/shard_map/ppermute | solution.py:28
  26.7 0.0 collective-permute-done.3.refs_5_
  26.7 0.0 collective-permute-start.5
  26.7 2.6 %collective-permute-done.4.refs_6_ = bf16[1,128,128]{2,1,0:T(8,128)(2,1)S(1)} collective-permute-done((bf16[1,128,128]{2,1,0:T(8,128)(2,1)S(1)}, bf16[1,128,128]{2,1,0:T(8,128)(2,1)S(1)}, u32[]{:S(2)}, u32[]{:S(2)}) %collective-permute-start.4) | collective-permute-done | bytes 32800 | tf_op jit(solution)/shard_map/ppermute | solution.py:28
  29.2 0.0 collective-permute-done.5.refs_7_
  29.2 0.0 collective-permute-done.10.refs_10_
  29.2 0.0 collective-permute-done.11.refs_11_
  29.2 0.0 collective-permute-done.9.refs_9_
  29.3 0.0 copy-start.1
  29.3 0.7 %shard_map.103 = (bf16[64,128]{1,0:T(8,128)(2,1)S(1)}, bf16[64,128]{1,0:T(8,128)(2,1)S(1)}, bf16[64,128]{1,0:T(8,128)(2,1)S(1)}, bf16[64,128]{1,0:T(8,128)(2,1)S(1)}) custom-call(bf16[88,128]{1,0:T(8,128)(2,1)S(1)} %get-tuple-element.17.refs_0_, bf16[88,128]{1,0:T(8,128)(2,1)S(1)} %collective-permute-done.refs_1_, ...), custom_call_target="tpu_custom_call" | custom-call | flops 33554432 | bytes 524288 | tf_op jit(solution)/shard_map/pallas_call | solution.py:135
  30.0 0.1 collective-permute-start.12
  30.1 1.8 %collective-permute-start.13 = (bf16[64,128]{1,0:T(8,128)(2,1)S(1)}, bf16[64,128]{1,0:T(8,128)(2,1)S(1)}, u32[]{:S(2)}, u32[]{:S(2)}) collective-permute-start(bf16[64,128]{1,0:T(8,128)(2,1)S(1)} %get-tuple-element.27), channel_id=1, source_target_pairs={{0,2},{1,3},{2,0},{3,1},{4,6},{5,7},{6,4},{7,5},{8,10},{9,11},{10,... | collective-permute-start | bytes 49160 | tf_op jit(solution)/shard_map/ppermute | solution.py:28
  31.9 2.5 %collective-permute-start.14 = (bf16[64,128]{1,0:T(8,128)(2,1)S(1)}, bf16[64,128]{1,0:T(8,128)(2,1)S(1)}, u32[]{:S(2)}, u32[]{:S(2)}) collective-permute-start(bf16[64,128]{1,0:T(8,128)(2,1)S(1)} %get-tuple-element.28), channel_id=1, source_target_pairs={{0,3},{1,2},{2,1},{3,0},{4,7},{5,6},{6,5},{7,4},{8,11},{9,10},{10,... | collective-permute-start | bytes 49160 | tf_op jit(solution)/shard_map/ppermute | solution.py:28
  35.1 0.0 copy-done
  35.1 0.0 copy-done.1
  35.1 0.3 shard_map.101
  35.4 0.0 collective-permute-done.12.refs_1_
  35.4 0.0 collective-permute-done.13.refs_2_
  35.4 2.0 %collective-permute-done.14.refs_3_ = bf16[64,128]{1,0:T(8,128)(2,1)S(1)} collective-permute-done((bf16[64,128]{1,0:T(8,128)(2,1)S(1)}, bf16[64,128]{1,0:T(8,128)(2,1)S(1)}, u32[]{:S(2)}, u32[]{:S(2)}) %collective-permute-start.14) | collective-permute-done | bytes 16416 | tf_op jit(solution)/shard_map/ppermute | solution.py:28
  37.4 0.7 %shard_map.104 = bf16[32,1024]{1,0:T(8,128)(2,1)} custom-call(f32[32,1024]{1,0:T(8,128)S(1)} %bitcast.4, bf16[64,128]{1,0:T(8,128)(2,1)S(1)} %get-tuple-element.25.refs_0_, bf16[64,128]{1,0:T(8,128)(2,1)S(1)} %collective-permute-done.12.refs_1_, bf16[64,128]{1,0:T(8,128)(2,1)S(1)} %collective-permute-done.13.refs_2_, ...), custom_call_target="tpu_custom_call" | custom-call | tf_op jit(solution)/shard_map/pallas_call | solution.py:135
  (1 shorter events, 0.0 us)
Async XLA Ops:
  0.0 35.1 %copy-start = (bf16[384,1024]{1,0:T(8,128)(2,1)S(1)}, bf16[384,1024]{1,0:T(8,128)(2,1)}, u32[]{:S(2)}) copy-start(bf16[384,1024]{1,0:T(8,128)(2,1)} %weight_ref.1) | copy-start | bytes 2359300
  1.2 5.7 %collective-permute-start.6 = (bf16[128,128]{1,0:T(8,128)(2,1)S(1)}, bf16[128,128]{1,0:T(8,128)(2,1)S(1)}, u32[]{:S(2)}, u32[]{:S(2)}) collective-permute-start(bf16[128,128]{1,0:T(8,128)(2,1)S(1)} %get-tuple-element.22), channel_id=1, source_target_pairs={{0,1},{1,0},{2,3},{3,2},{4,5},{5,4},{6,7},{7,6},{8,9},{9,8},{10,11... | collective-permute-start | bytes 98312 | tf_op jit(solution)/shard_map/ppermute | solution.py:28
  4.3 5.4 %collective-permute-start.7 = (bf16[128,128]{1,0:T(8,128)(2,1)S(1)}, bf16[128,128]{1,0:T(8,128)(2,1)S(1)}, u32[]{:S(2)}, u32[]{:S(2)}) collective-permute-start(bf16[128,128]{1,0:T(8,128)(2,1)S(1)} %get-tuple-element.23), channel_id=1, source_target_pairs={{0,2},{1,3},{2,0},{3,1},{4,6},{5,7},{6,4},{7,5},{8,10},{9,11},{10,... | collective-permute-start | bytes 98312 | tf_op jit(solution)/shard_map/ppermute | solution.py:28
  6.9 5.7 %collective-permute-start.8 = (bf16[128,128]{1,0:T(8,128)(2,1)S(1)}, bf16[128,128]{1,0:T(8,128)(2,1)S(1)}, u32[]{:S(2)}, u32[]{:S(2)}) collective-permute-start(bf16[128,128]{1,0:T(8,128)(2,1)S(1)} %get-tuple-element.24), channel_id=1, source_target_pairs={{0,3},{1,2},{2,1},{3,0},{4,7},{5,6},{6,5},{7,4},{8,11},{9,10},{10,... | collective-permute-start | bytes 98312 | tf_op jit(solution)/shard_map/ppermute | solution.py:28
  12.6 16.6 %collective-permute-start.10 = (bf16[3,128,128]{2,1,0:T(8,128)(2,1)S(1)}, bf16[3,128,128]{2,1,0:T(8,128)(2,1)S(1)}, u32[]{:S(2)}, u32[]{:S(2)}) collective-permute-start(bf16[3,128,128]{2,1,0:T(8,128)(2,1)S(1)} %shard_map.102.refs_8_), channel_id=1, source_target_pairs={{0,8},{4,12},{8,0},{12,4},{1,9},{5,13},{9,1},{13,5},{2,10},{6,14},... | collective-permute-start | bytes 294920 | tf_op jit(solution)/shard_map/ppermute | solution.py:28
  14.2 15.0 %collective-permute-start.11 = (bf16[3,128,128]{2,1,0:T(8,128)(2,1)S(1)}, bf16[3,128,128]{2,1,0:T(8,128)(2,1)S(1)}, u32[]{:S(2)}, u32[]{:S(2)}) collective-permute-start(bf16[3,128,128]{2,1,0:T(8,128)(2,1)S(1)} %shard_map.102.refs_8_), channel_id=1, source_target_pairs={{0,4},{4,0},{8,12},{12,8},{1,5},{5,1},{9,13},{13,9},{2,6},{6,2},{1... | collective-permute-start | bytes 294920 | tf_op jit(solution)/shard_map/ppermute | solution.py:28
  14.2 15.0 %collective-permute-start.9 = (bf16[3,128,128]{2,1,0:T(8,128)(2,1)S(1)}, bf16[3,128,128]{2,1,0:T(8,128)(2,1)S(1)}, u32[]{:S(2)}, u32[]{:S(2)}) collective-permute-start(bf16[3,128,128]{2,1,0:T(8,128)(2,1)S(1)} %shard_map.102.refs_8_), channel_id=1, source_target_pairs={{0,12},{4,8},{8,4},{12,0},{1,13},{5,9},{9,5},{13,1},{2,14},{6,10},... | collective-permute-start | bytes 294920 | tf_op jit(solution)/shard_map/ppermute | solution.py:28
  14.9 4.0 %collective-permute-start = (bf16[88,128]{1,0:T(8,128)(2,1)S(1)}, bf16[88,128]{1,0:T(8,128)(2,1)S(1)}, u32[]{:S(2)}, u32[]{:S(2)}) collective-permute-start(bf16[88,128]{1,0:T(8,128)(2,1)S(1)} %get-tuple-element.18), channel_id=1, source_target_pairs={{0,1},{1,0},{2,3},{3,2},{4,5},{5,4},{6,7},{7,6},{8,9},{9,8},{10,11... | collective-permute-start | bytes 67592 | tf_op jit(solution)/shard_map/ppermute | solution.py:28
  14.9 4.7 %collective-permute-start.1 = (bf16[88,128]{1,0:T(8,128)(2,1)S(1)}, bf16[88,128]{1,0:T(8,128)(2,1)S(1)}, u32[]{:S(2)}, u32[]{:S(2)}) collective-permute-start(bf16[88,128]{1,0:T(8,128)(2,1)S(1)} %get-tuple-element.19), channel_id=1, source_target_pairs={{0,2},{1,3},{2,0},{3,1},{4,6},{5,7},{6,4},{7,5},{8,10},{9,11},{10,... | collective-permute-start | bytes 67592 | tf_op jit(solution)/shard_map/ppermute | solution.py:28
  18.8 7.8 %collective-permute-start.3 = (bf16[1,128,128]{2,1,0:T(8,128)(2,1)S(1)}, bf16[1,128,128]{2,1,0:T(8,128)(2,1)S(1)}, u32[]{:S(2)}, u32[]{:S(2)}) collective-permute-start(bf16[1,128,128]{2,1,0:T(8,128)(2,1)S(1)} %bitcast.5), channel_id=1, source_target_pairs={{0,12},{4,8},{8,4},{12,0},{1,13},{5,9},{9,5},{13,1},{2,14},{6,10},... | collective-permute-start | bytes 98312 | tf_op jit(solution)/shard_map/ppermute | solution.py:28
  19.6 5.7 %collective-permute-start.2 = (bf16[88,128]{1,0:T(8,128)(2,1)S(1)}, bf16[88,128]{1,0:T(8,128)(2,1)S(1)}, u32[]{:S(2)}, u32[]{:S(2)}) collective-permute-start(bf16[88,128]{1,0:T(8,128)(2,1)S(1)} %get-tuple-element.20), channel_id=1, source_target_pairs={{0,3},{1,2},{2,1},{3,0},{4,7},{5,6},{6,5},{7,4},{8,11},{9,10},{10,... | collective-permute-start | bytes 67592 | tf_op jit(solution)/shard_map/ppermute | solution.py:28
  25.3 3.9 %collective-permute-start.4 = (bf16[1,128,128]{2,1,0:T(8,128)(2,1)S(1)}, bf16[1,128,128]{2,1,0:T(8,128)(2,1)S(1)}, u32[]{:S(2)}, u32[]{:S(2)}) collective-permute-start(bf16[1,128,128]{2,1,0:T(8,128)(2,1)S(1)} %bitcast.6), channel_id=1, source_target_pairs={{0,8},{4,12},{8,0},{12,4},{1,9},{5,13},{9,1},{13,5},{2,10},{6,14},... | collective-permute-start | bytes 98312 | tf_op jit(solution)/shard_map/ppermute | solution.py:28
  26.7 2.6 %collective-permute-start.5 = (bf16[1,128,128]{2,1,0:T(8,128)(2,1)S(1)}, bf16[1,128,128]{2,1,0:T(8,128)(2,1)S(1)}, u32[]{:S(2)}, u32[]{:S(2)}) collective-permute-start(bf16[1,128,128]{2,1,0:T(8,128)(2,1)S(1)} %bitcast.7), channel_id=1, source_target_pairs={{0,4},{4,0},{8,12},{12,8},{1,5},{5,1},{9,13},{13,9},{2,6},{6,2},{1... | collective-permute-start | bytes 98312 | tf_op jit(solution)/shard_map/ppermute | solution.py:28
  29.3 5.8 %copy-start.1 = (f32[8,1024]{1,0:T(8,128)S(1)}, f32[8,1024]{1,0:T(8,128)}, u32[]{:S(2)}) copy-start(f32[8,1024]{1,0:T(8,128)} %gain_ref.1) | copy-start | bytes 98308
  30.0 5.4 %collective-permute-start.12 = (bf16[64,128]{1,0:T(8,128)(2,1)S(1)}, bf16[64,128]{1,0:T(8,128)(2,1)S(1)}, u32[]{:S(2)}, u32[]{:S(2)}) collective-permute-start(bf16[64,128]{1,0:T(8,128)(2,1)S(1)} %get-tuple-element.26), channel_id=1, source_target_pairs={{0,1},{1,0},{2,3},{3,2},{4,5},{5,4},{6,7},{7,6},{8,9},{9,8},{10,11... | collective-permute-start | bytes 49160 | tf_op jit(solution)/shard_map/ppermute | solution.py:28
  30.1 5.3 %collective-permute-start.13 = (bf16[64,128]{1,0:T(8,128)(2,1)S(1)}, bf16[64,128]{1,0:T(8,128)(2,1)S(1)}, u32[]{:S(2)}, u32[]{:S(2)}) collective-permute-start(bf16[64,128]{1,0:T(8,128)(2,1)S(1)} %get-tuple-element.27), channel_id=1, source_target_pairs={{0,2},{1,3},{2,0},{3,1},{4,6},{5,7},{6,4},{7,5},{8,10},{9,11},{10,... | collective-permute-start | bytes 49160 | tf_op jit(solution)/shard_map/ppermute | solution.py:28
  31.9 5.5 %collective-permute-start.14 = (bf16[64,128]{1,0:T(8,128)(2,1)S(1)}, bf16[64,128]{1,0:T(8,128)(2,1)S(1)}, u32[]{:S(2)}, u32[]{:S(2)}) collective-permute-start(bf16[64,128]{1,0:T(8,128)(2,1)S(1)} %get-tuple-element.28), channel_id=1, source_target_pairs={{0,3},{1,2},{2,1},{3,0},{4,7},{5,6},{6,5},{7,4},{8,11},{9,10},{10,... | collective-permute-start | bytes 49160 | tf_op jit(solution)/shard_map/ppermute | solution.py:28

commit v6 on v5

--- a/solution.py
+++ b/solution.py
@@ -147,12 +147,23 @@
     return jax.ShapeDtypeStruct(dims, dtype)
 
 
-def gather(pairs, axis):
-    return [pairs] + [swap(pairs, axis, step) for step in range(lax.axis_size(axis) - 1, 0, -1)]
+def gather(pairs, beside, axis):
+    size = lax.axis_size(axis)
+    if size & (size - 1):
+        return [swap(pairs, axis, step) for step in range(size)], beside
+    held = [pairs]
+    step = size // 2
+    while step:
+        moved = [swap(array, axis, step) for array in held]
+        if len(held) == 1:
+            moved, beside = lax.optimization_barrier((moved, beside))
+        held = held + moved
+        step = step // 2
+    return held, beside
 
 
 def exchange(arrays, axis):
-    return [arrays[0]] + [swap(array, axis, step) for step, array in enumerate(arrays) if step]
+    return list(arrays[:1]) + [swap(array, axis, step) for step, array in enumerate(arrays) if step]
 
 
 def shards(
@@ -195,12 +206,9 @@
         ],
     )
     pairs = exchange(sent[:owners], "ulysses")
-    near = gather(pairs[0][None], "blk")
     got = exchange(sent[owners:], "ulysses")
-    joined = call(
-        join_kernel, shape((owners - 1, 2 * lines, HEAD_DIM)), [VMEM] * (owners - 1), *pairs[1:]
-    )
-    held = near + gather(joined, "blk")
+    joined = call(join_kernel, shape((owners, 2 * lines, HEAD_DIM)), [VMEM] * owners, *pairs)
+    held, got = gather(joined, got, "blk")
     hint = call(
         hint_kernel,
         shape((owners, rows // owners, feats), jnp.float32),

time: 38.2 us -> 31 us (0.81)
  waiting for transfers between devices: 18.3 us -> 11.4 us
    ppermute x15 -> x12, waiting for transfers between devices: 18.3 us -> 11.4 us  [swap(): lax.ppermute(array, axis, [(i, partner(i, size, step)) for i in range(siz...]
    ppermute x15 -> x12, starting transfers between devices: 16.1 us -> 15.8 us  [swap(): lax.ppermute(array, axis, [(i, partner(i, size, step)) for i in range(siz...]
  transfers between devices with their start and end apart: 15 -> 12, of which waited for: 7 -> 7; matrix products, arithmetic and copies ran while one was open for 0% -> 0% of each run, Pallas kernels for 1% -> 1%
where the time goes in v6:
time: 31 us; the launch traced here: 30.8 us
  starting transfers between devices  15.8 us (51%)
  waiting for transfers between devices  11.4 us (37%)
  Pallas kernels  2.89 us (9%)
  between operations  0.72 us (2%)
    ppermute x12, starting transfers between devices, swap(): lax.ppermute(array, axis, [(i, partner(i, size, step)) for i in range(siz...  15.8 us
    ppermute x12, waiting for transfers between devices, swap(): lax.ppermute(array, axis, [(i, partner(i, size, step)) for i in range(siz...  11.4 us
    pallas_call x5, Pallas kernels, call(): pl.pallas_call(kernel, out_shape=out_shape, in_specs=specs, out_specs=jax...  2.89 us
  transfers between devices with their start and end apart: 12, of which 7 were waited for; matrix products, arithmetic and copies ran while one was open for 0% of the time, Pallas kernels for 1%

profile of v6, /device:TPU:0, one launch (start us, length us, event | category | flops | bytes accessed | tf_op | source)
XLA Modules:
  0.0 30.8 jit_solution(18375172899261564921)
XLA Ops:
  0.0 0.0 copy-start
  0.0 1.2 %shard_map.100 = (bf16[128,128]{1,0:T(8,128)(2,1)S(1)}, bf16[128,128]{1,0:T(8,128)(2,1)S(1)}, bf16[128,128]{1,0:T(8,128)(2,1)S(1)}, bf16[128,128]{1,0:T(8,128)(2...) custom-call(s32[1,4]{1,0:T(1,128)} %refs_0_.1, ...), custom_call_target="tpu_custom_call" | custom-call | tf_op jit(solution)/shard_map/pallas_call | solution.py:135
  1.2 3.1 %collective-permute-start = (bf16[128,128]{1,0:T(8,128)(2,1)S(1)}, bf16[128,128]{1,0:T(8,128)(2,1)S(1)}, u32[]{:S(2)}, u32[]{:S(2)}) collective-permute-start(bf16[128,128]{1,0:T(8,128)(2,1)S(1)} %get-tuple-element.23), channel_id=1, source_target_pairs={{0,1},{1,0},{2,3},{3,2},{4,5},{5,4},{6,7},{7,6},{8,9},{9,8},{10,11... | collective-permute-start | bytes 98312 | tf_op jit(solution)/shard_map/ppermute | solution.py:28
  4.3 2.6 %collective-permute-start.1 = (bf16[128,128]{1,0:T(8,128)(2,1)S(1)}, bf16[128,128]{1,0:T(8,128)(2,1)S(1)}, u32[]{:S(2)}, u32[]{:S(2)}) collective-permute-start(bf16[128,128]{1,0:T(8,128)(2,1)S(1)} %get-tuple-element.24), channel_id=1, source_target_pairs={{0,2},{1,3},{2,0},{3,1},{4,6},{5,7},{6,4},{7,5},{8,10},{9,11},{10,... | collective-permute-start | bytes 98312 | tf_op jit(solution)/shard_map/ppermute | solution.py:28
  6.9 0.0 collective-permute-start.2
  6.9 0.0 collective-permute-done.refs_1_
  6.9 2.8 %collective-permute-done.1.refs_2_ = bf16[128,128]{1,0:T(8,128)(2,1)S(1)} collective-permute-done((bf16[128,128]{1,0:T(8,128)(2,1)S(1)}, bf16[128,128]{1,0:T(8,128)(2,1)S(1)}, u32[]{:S(2)}, u32[]{:S(2)}) %collective-permute-start.1) | collective-permute-done | bytes 32800 | tf_op jit(solution)/shard_map/ppermute | solution.py:28
  9.7 2.9 %collective-permute-done.2.refs_3_ = bf16[128,128]{1,0:T(8,128)(2,1)S(1)} collective-permute-done((bf16[128,128]{1,0:T(8,128)(2,1)S(1)}, bf16[128,128]{1,0:T(8,128)(2,1)S(1)}, u32[]{:S(2)}, u32[]{:S(2)}) %collective-permute-start.2) | collective-permute-done | bytes 32800 | tf_op jit(solution)/shard_map/ppermute | solution.py:28
  12.6 1.6 %collective-permute-start.3 = (bf16[4,128,128]{2,1,0:T(8,128)(2,1)S(1)}, bf16[4,128,128]{2,1,0:T(8,128)(2,1)S(1)}, u32[]{:S(2)}, u32[]{:S(2)}) collective-permute-start(bf16[4,128,128]{2,1,0:T(8,128)(2,1)S(1)} %shard_map.101.refs_4_), channel_id=1, source_target_pairs={{0,8},{4,12},{8,0},{12,4},{1,9},{5,13},{9,1},{13,5},{2,10},{6,14},... | collective-permute-start | bytes 393224 | tf_op jit(solution)/shard_map/ppermute | solution.py:28
  14.2 0.0 collective-permute-start.4
  14.2 0.9 %collective-permute-start.5 = (bf16[88,128]{1,0:T(8,128)(2,1)S(1)}, bf16[88,128]{1,0:T(8,128)(2,1)S(1)}, u32[]{:S(2)}, u32[]{:S(2)}) collective-permute-start(bf16[88,128]{1,0:T(8,128)(2,1)S(1)} %get-tuple-element.28), channel_id=1, source_target_pairs={{0,2},{1,3},{2,0},{3,1},{4,6},{5,7},{6,4},{7,5},{8,10},{9,11},{10,... | collective-permute-start | bytes 67592 | tf_op jit(solution)/shard_map/ppermute | solution.py:28
  15.1 3.5 %collective-permute-start.6 = (bf16[88,128]{1,0:T(8,128)(2,1)S(1)}, bf16[88,128]{1,0:T(8,128)(2,1)S(1)}, u32[]{:S(2)}, u32[]{:S(2)}) collective-permute-start(bf16[88,128]{1,0:T(8,128)(2,1)S(1)} %get-tuple-element.29), channel_id=1, source_target_pairs={{0,3},{1,2},{2,1},{3,0},{4,7},{5,6},{6,5},{7,4},{8,11},{9,10},{10,... | collective-permute-start | bytes 67592 | tf_op jit(solution)/shard_map/ppermute | solution.py:28
  18.6 0.0 collective-permute-start.7
  18.6 0.0 collective-permute-done.4.refs_1_
  18.6 0.3 %collective-permute-done.5.refs_2_ = bf16[88,128]{1,0:T(8,128)(2,1)S(1)} collective-permute-done((bf16[88,128]{1,0:T(8,128)(2,1)S(1)}, bf16[88,128]{1,0:T(8,128)(2,1)S(1)}, u32[]{:S(2)}, u32[]{:S(2)}) %collective-permute-start.5) | collective-permute-done | bytes 22560 | tf_op jit(solution)/shard_map/ppermute | solution.py:28
  18.9 1.8 %collective-permute-done.6.refs_3_ = bf16[88,128]{1,0:T(8,128)(2,1)S(1)} collective-permute-done((bf16[88,128]{1,0:T(8,128)(2,1)S(1)}, bf16[88,128]{1,0:T(8,128)(2,1)S(1)}, u32[]{:S(2)}, u32[]{:S(2)}) %collective-permute-start.6) | collective-permute-done | bytes 22560 | tf_op jit(solution)/shard_map/ppermute | solution.py:28
  20.7 0.0 collective-permute-done.3.refs_5_
  20.7 0.0 copy-start.1
  20.7 0.0 collective-permute-start.8
  20.7 0.0 collective-permute-done.7.refs_6_
  20.7 1.3 %collective-permute-done.8.refs_7_ = bf16[4,128,128]{2,1,0:T(8,128)(2,1)S(1)} collective-permute-done((bf16[4,128,128]{2,1,0:T(8,128)(2,1)S(1)}, bf16[4,128,128]{2,1,0:T(8,128)(2,1)S(1)}, u32[]{:S(2)}, u32[]{:S(2)}) %collective-permute-start.8) | collective-permute-done | bytes 131104 | tf_op jit(solution)/shard_map/ppermute | solution.py:28
  22.1 0.7 %shard_map.103 = (bf16[64,128]{1,0:T(8,128)(2,1)S(1)}, bf16[64,128]{1,0:T(8,128)(2,1)S(1)}, bf16[64,128]{1,0:T(8,128)(2,1)S(1)}, bf16[64,128]{1,0:T(8,128)(2,1)S(1)}) custom-call(bf16[88,128]{1,0:T(8,128)(2,1)S(1)} %get-tuple-element.30.refs_0_, bf16[88,128]{1,0:T(8,128)(2,1)S(1)} %collective-permute-done.4.refs_1_, ...), custom_call_target="tpu_custom_call" | custom-call | flops 33554432 | bytes 524288 | tf_op jit(solution)/shard_map/pallas_call | solution.py:135
  22.8 0.3 %collective-permute-start.10 = (bf16[64,128]{1,0:T(8,128)(2,1)S(1)}, bf16[64,128]{1,0:T(8,128)(2,1)S(1)}, u32[]{:S(2)}, u32[]{:S(2)}) collective-permute-start(bf16[64,128]{1,0:T(8,128)(2,1)S(1)} %get-tuple-element.37), channel_id=1, source_target_pairs={{0,2},{1,3},{2,0},{3,1},{4,6},{5,7},{6,4},{7,5},{8,10},{9,11},{10,... | collective-permute-start | bytes 49160 | tf_op jit(solution)/shard_map/ppermute | solution.py:28
  23.1 3.3 %collective-permute-start.11 = (bf16[64,128]{1,0:T(8,128)(2,1)S(1)}, bf16[64,128]{1,0:T(8,128)(2,1)S(1)}, u32[]{:S(2)}, u32[]{:S(2)}) collective-permute-start(bf16[64,128]{1,0:T(8,128)(2,1)S(1)} %get-tuple-element.38), channel_id=1, source_target_pairs={{0,3},{1,2},{2,1},{3,0},{4,7},{5,6},{6,5},{7,4},{8,11},{9,10},{10,... | collective-permute-start | bytes 49160 | tf_op jit(solution)/shard_map/ppermute | solution.py:28
  26.4 0.5 %collective-permute-start.9 = (bf16[64,128]{1,0:T(8,128)(2,1)S(1)}, bf16[64,128]{1,0:T(8,128)(2,1)S(1)}, u32[]{:S(2)}, u32[]{:S(2)}) collective-permute-start(bf16[64,128]{1,0:T(8,128)(2,1)S(1)} %get-tuple-element.36), channel_id=1, source_target_pairs={{0,1},{1,0},{2,3},{3,2},{4,5},{5,4},{6,7},{7,6},{8,9},{9,8},{10,11... | collective-permute-start | bytes 49160 | tf_op jit(solution)/shard_map/ppermute | solution.py:28
  27.5 0.0 copy-done
  27.6 0.0 copy-done.1
  27.6 0.3 %shard_map.102 = f32[4,8,1024]{2,1,0:T(8,128)S(1)} custom-call(s32[1]{0:T(128)S(6)} %copy.11.layer_ref, bf16[384,1024]{1,0:T(8,128)(2,1)S(1)} %copy-done, f32[8,1024]{1,0:T(8,128)S(1)} %copy-done.1, bf16[88,128]{1,0:T(8,128)(2,1)S(1)} %get-tuple-element.30.refs_0_, bf16[88,128]{1,0:T(8,128)(2,1)S(1)} %collective-permute-done.4.refs_1_, ...), custom_call_target="tpu_custom_call" | custom-call | flops 25165824 | bytes 786432 | tf_op jit(solution)/shard_map/pallas_call | solution.py:135
  27.9 0.0 collective-permute-done.10.refs_2_
  27.9 0.7 %collective-permute-done.11.refs_3_ = bf16[64,128]{1,0:T(8,128)(2,1)S(1)} collective-permute-done((bf16[64,128]{1,0:T(8,128)(2,1)S(1)}, bf16[64,128]{1,0:T(8,128)(2,1)S(1)}, u32[]{:S(2)}, u32[]{:S(2)}) %collective-permute-start.11) | collective-permute-done | bytes 16416 | tf_op jit(solution)/shard_map/ppermute | solution.py:28
  28.6 1.5 %collective-permute-done.9.refs_1_ = bf16[64,128]{1,0:T(8,128)(2,1)S(1)} collective-permute-done((bf16[64,128]{1,0:T(8,128)(2,1)S(1)}, bf16[64,128]{1,0:T(8,128)(2,1)S(1)}, u32[]{:S(2)}, u32[]{:S(2)}) %collective-permute-start.9) | collective-permute-done | bytes 16416 | tf_op jit(solution)/shard_map/ppermute | solution.py:28
  30.1 0.7 %shard_map.104 = bf16[32,1024]{1,0:T(8,128)(2,1)} custom-call(f32[32,1024]{1,0:T(8,128)S(1)} %bitcast.3, bf16[64,128]{1,0:T(8,128)(2,1)S(1)} %get-tuple-element.35.refs_0_, bf16[64,128]{1,0:T(8,128)(2,1)S(1)} %collective-permute-done.9.refs_1_, bf16[64,128]{1,0:T(8,128)(2,1)S(1)} %collective-permute-done.10.refs_2_, ...), custom_call_target="tpu_custom_call" | custom-call | tf_op jit(solution)/shard_map/pallas_call | solution.py:135
  (1 shorter events, 0.0 us)
Async XLA Ops:
  0.0 27.5 %copy-start = (bf16[384,1024]{1,0:T(8,128)(2,1)S(1)}, bf16[384,1024]{1,0:T(8,128)(2,1)}, u32[]{:S(2)}) copy-start(bf16[384,1024]{1,0:T(8,128)(2,1)} %weight_ref.1) | copy-start | bytes 2359300
  1.2 5.7 %collective-permute-start = (bf16[128,128]{1,0:T(8,128)(2,1)S(1)}, bf16[128,128]{1,0:T(8,128)(2,1)S(1)}, u32[]{:S(2)}, u32[]{:S(2)}) collective-permute-start(bf16[128,128]{1,0:T(8,128)(2,1)S(1)} %get-tuple-element.23), channel_id=1, source_target_pairs={{0,1},{1,0},{2,3},{3,2},{4,5},{5,4},{6,7},{7,6},{8,9},{9,8},{10,11... | collective-permute-start | bytes 98312 | tf_op jit(solution)/shard_map/ppermute | solution.py:28
  4.3 5.4 %collective-permute-start.1 = (bf16[128,128]{1,0:T(8,128)(2,1)S(1)}, bf16[128,128]{1,0:T(8,128)(2,1)S(1)}, u32[]{:S(2)}, u32[]{:S(2)}) collective-permute-start(bf16[128,128]{1,0:T(8,128)(2,1)S(1)} %get-tuple-element.24), channel_id=1, source_target_pairs={{0,2},{1,3},{2,0},{3,1},{4,6},{5,7},{6,4},{7,5},{8,10},{9,11},{10,... | collective-permute-start | bytes 98312 | tf_op jit(solution)/shard_map/ppermute | solution.py:28
  6.9 5.7 %collective-permute-start.2 = (bf16[128,128]{1,0:T(8,128)(2,1)S(1)}, bf16[128,128]{1,0:T(8,128)(2,1)S(1)}, u32[]{:S(2)}, u32[]{:S(2)}) collective-permute-start(bf16[128,128]{1,0:T(8,128)(2,1)S(1)} %get-tuple-element.25), channel_id=1, source_target_pairs={{0,3},{1,2},{2,1},{3,0},{4,7},{5,6},{6,5},{7,4},{8,11},{9,10},{10,... | collective-permute-start | bytes 98312 | tf_op jit(solution)/shard_map/ppermute | solution.py:28
  12.6 8.1 %collective-permute-start.3 = (bf16[4,128,128]{2,1,0:T(8,128)(2,1)S(1)}, bf16[4,128,128]{2,1,0:T(8,128)(2,1)S(1)}, u32[]{:S(2)}, u32[]{:S(2)}) collective-permute-start(bf16[4,128,128]{2,1,0:T(8,128)(2,1)S(1)} %shard_map.101.refs_4_), channel_id=1, source_target_pairs={{0,8},{4,12},{8,0},{12,4},{1,9},{5,13},{9,1},{13,5},{2,10},{6,14},... | collective-permute-start | bytes 393224 | tf_op jit(solution)/shard_map/ppermute | solution.py:28
  14.2 4.4 %collective-permute-start.4 = (bf16[88,128]{1,0:T(8,128)(2,1)S(1)}, bf16[88,128]{1,0:T(8,128)(2,1)S(1)}, u32[]{:S(2)}, u32[]{:S(2)}) collective-permute-start(bf16[88,128]{1,0:T(8,128)(2,1)S(1)} %get-tuple-element.27), channel_id=1, source_target_pairs={{0,1},{1,0},{2,3},{3,2},{4,5},{5,4},{6,7},{7,6},{8,9},{9,8},{10,11... | collective-permute-start | bytes 67592 | tf_op jit(solution)/shard_map/ppermute | solution.py:28
  14.2 4.7 %collective-permute-start.5 = (bf16[88,128]{1,0:T(8,128)(2,1)S(1)}, bf16[88,128]{1,0:T(8,128)(2,1)S(1)}, u32[]{:S(2)}, u32[]{:S(2)}) collective-permute-start(bf16[88,128]{1,0:T(8,128)(2,1)S(1)} %get-tuple-element.28), channel_id=1, source_target_pairs={{0,2},{1,3},{2,0},{3,1},{4,6},{5,7},{6,4},{7,5},{8,10},{9,11},{10,... | collective-permute-start | bytes 67592 | tf_op jit(solution)/shard_map/ppermute | solution.py:28
  15.1 5.6 %collective-permute-start.6 = (bf16[88,128]{1,0:T(8,128)(2,1)S(1)}, bf16[88,128]{1,0:T(8,128)(2,1)S(1)}, u32[]{:S(2)}, u32[]{:S(2)}) collective-permute-start(bf16[88,128]{1,0:T(8,128)(2,1)S(1)} %get-tuple-element.29), channel_id=1, source_target_pairs={{0,3},{1,2},{2,1},{3,0},{4,7},{5,6},{6,5},{7,4},{8,11},{9,10},{10,... | collective-permute-start | bytes 67592 | tf_op jit(solution)/shard_map/ppermute | solution.py:28
  18.6 2.1 %collective-permute-start.7 = (bf16[4,128,128]{2,1,0:T(8,128)(2,1)S(1)}, bf16[4,128,128]{2,1,0:T(8,128)(2,1)S(1)}, u32[]{:S(2)}, u32[]{:S(2)}) collective-permute-start(bf16[4,128,128]{2,1,0:T(8,128)(2,1)S(1)} %shard_map.101.refs_4_), channel_id=1, source_target_pairs={{0,4},{4,0},{8,12},{12,8},{1,5},{5,1},{9,13},{13,9},{2,6},{6,2},{1... | collective-permute-start | bytes 393224 | tf_op jit(solution)/shard_map/ppermute | solution.py:28
  20.7 6.8 %copy-start.1 = (f32[8,1024]{1,0:T(8,128)S(1)}, f32[8,1024]{1,0:T(8,128)}, u32[]{:S(2)}) copy-start(f32[8,1024]{1,0:T(8,128)} %gain_ref.1) | copy-start | bytes 98308
  20.7 1.3 %collective-permute-start.8 = (bf16[4,128,128]{2,1,0:T(8,128)(2,1)S(1)}, bf16[4,128,128]{2,1,0:T(8,128)(2,1)S(1)}, u32[]{:S(2)}, u32[]{:S(2)}) collective-permute-start(bf16[4,128,128]{2,1,0:T(8,128)(2,1)S(1)} %collective-permute-done.3.refs_5_), channel_id=1, source_target_pairs={{0,4},{4,0},{8,12},{12,8},{1,5},{5,1},{9,13},{13,9},{2,6},{6,2},{1... | collective-permute-start | bytes 393224 | tf_op jit(solution)/shard_map/ppermute | solution.py:28
  22.8 5.1 %collective-permute-start.10 = (bf16[64,128]{1,0:T(8,128)(2,1)S(1)}, bf16[64,128]{1,0:T(8,128)(2,1)S(1)}, u32[]{:S(2)}, u32[]{:S(2)}) collective-permute-start(bf16[64,128]{1,0:T(8,128)(2,1)S(1)} %get-tuple-element.37), channel_id=1, source_target_pairs={{0,2},{1,3},{2,0},{3,1},{4,6},{5,7},{6,4},{7,5},{8,10},{9,11},{10,... | collective-permute-start | bytes 49160 | tf_op jit(solution)/shard_map/ppermute | solution.py:28
  23.1 5.5 %collective-permute-start.11 = (bf16[64,128]{1,0:T(8,128)(2,1)S(1)}, bf16[64,128]{1,0:T(8,128)(2,1)S(1)}, u32[]{:S(2)}, u32[]{:S(2)}) collective-permute-start(bf16[64,128]{1,0:T(8,128)(2,1)S(1)} %get-tuple-element.38), channel_id=1, source_target_pairs={{0,3},{1,2},{2,1},{3,0},{4,7},{5,6},{6,5},{7,4},{8,11},{9,10},{10,... | collective-permute-start | bytes 49160 | tf_op jit(solution)/shard_map/ppermute | solution.py:28
  26.4 3.7 %collective-permute-start.9 = (bf16[64,128]{1,0:T(8,128)(2,1)S(1)}, bf16[64,128]{1,0:T(8,128)(2,1)S(1)}, u32[]{:S(2)}, u32[]{:S(2)}) collective-permute-start(bf16[64,128]{1,0:T(8,128)(2,1)S(1)} %get-tuple-element.36), channel_id=1, source_target_pairs={{0,1},{1,0},{2,3},{3,2},{4,5},{5,4},{6,7},{7,6},{8,9},{9,8},{10,11... | collective-permute-start | bytes 49160 | tf_op jit(solution)/shard_map/ppermute | solution.py:28

commit v7 on v4

--- a/solution.py
+++ b/solution.py
@@ -21,6 +21,10 @@
     if size & (size - 1) == 0:
         return me ^ step
     return (step + size - me) % size
+
+
+def steps_of(owners):
+    return [0, *range(owners - 1, 0, -1)]
 
 
 def swap(array, axis, step):
@@ -50,7 +54,7 @@
     norm_ref[2] = normed(q_ref[...], qg_ref[...]).astype(jnp.bfloat16)
     patches = control_ref[...].astype(jnp.float32)
     slabs = [patches[j * slab_rows : (j + 1) * slab_rows] for j in range(owners)]
-    for step, out_ref in enumerate(out_refs):
+    for step, out_ref in zip(steps_of(owners), out_refs):
         to = partner(me, owners, step)
         at = 0
         for i in range(3):
@@ -73,8 +77,8 @@
     slab_rows, width = rows // owners, patch_ref.shape[1]
     size = pair_ref.shape[1]
     start = 3 * size // 2
-    for step, ref in enumerate(got_refs):
-        pair_ref[step] = ref[:size]
+    for i, ref in enumerate(got_refs):
+        pair_ref[i] = ref[:size]
     slabs = [ref[start:].astype(jnp.float32) for ref in got_refs]
     patches = [
         jnp.concatenate([slab[i * slab_rows : (i + 1) * slab_rows] for slab in slabs], axis=0)
@@ -112,8 +116,8 @@
     hint = jnp.dot(patch_ref[...], weight_ref[...], preferred_element_type=jnp.float32)
     hint = hint.astype(jnp.bfloat16).astype(jnp.float32) * gain_ref[pl.ds(layer_ref[0], 1), :]
     me = lax.axis_index("ulysses")
-    for step in range(owners):
-        out_ref[partner(me, owners, step)] = hint[step * slab_rows : (step + 1) * slab_rows]
+    for i, step in enumerate(steps_of(owners)):
+        out_ref[partner(me, owners, step)] = hint[i * slab_rows : (i + 1) * slab_rows]
 
 
 def finish_kernel(owners, hint_ref, *refs):
@@ -121,7 +125,7 @@
     rows, feats = out_ref.shape
     share = feats // owners
     me = lax.axis_index("ulysses")
-    for step, ref in enumerate(back_refs):
+    for step, ref in zip(steps_of(owners), back_refs):
         for head in range(share // HEAD_DIM):
             start = partner(me, owners, step) * share + head * HEAD_DIM
             cols = pl.ds(pl.multiple_of(start, HEAD_DIM), HEAD_DIM)
@@ -150,16 +154,26 @@
     return jax.ShapeDtypeStruct(dims, dtype)
 
 
-def gather_pairs(pairs, axis):
+def gather(pairs, beside, axis):
     size = lax.axis_size(axis)
     if size & (size - 1):
-        return [swap(pairs, axis, step) for step in range(size)]
+        return [swap(pairs, axis, step) for step in range(size)], beside
     held = [pairs]
     step = size // 2
     while step:
-        held = held + [swap(array, axis, step) for array in held]
+        moved = [swap(array, axis, step) for array in held]
+        if len(held) == 1:
+            moved, beside = lax.optimization_barrier((moved, beside))
+        held = held + moved
         step = step // 2
-    return held
+    return held, beside
+
+
+def exchange(arrays, axis):
+    return [
+        swap(array, axis, step) if step else array
+        for step, array in zip(steps_of(lax.axis_size(axis)), arrays)
+    ]
 
 
 def shards(
@@ -201,15 +215,13 @@
             pltpu.SemaphoreType.DMA((len(sources),)),
         ],
     )
-    far = [swap(sent[step], "ulysses", step) for step in range(owners - 1, 0, -1)]
-    got = [sent[0]] + far[::-1]
+    got = exchange(sent, "ulysses")
     pairs, patches = call(
         functools.partial(sort_kernel, rows),
         [shape((owners, 2 * lines, HEAD_DIM)), shape((rows, width))],
         [VMEM] * owners,
         *got,
     )
-    held = gather_pairs(pairs, "blk")
     hint = call(
         hint_kernel,
         shape((owners, rows // owners, feats), jnp.float32),
@@ -221,6 +233,7 @@
         flops=2 * rows * width * feats,
         nbytes=2 * width * feats,
     )
+    held, hint = gather(pairs, hint, "blk")
     mixed = call(
         functools.partial(attend_kernel, rows, owners),
         [shape((lines, HEAD_DIM))] * owners,
@@ -230,14 +243,12 @@
         flops=4 * lines * owners * len(held) * owners * rows * HEAD_DIM,
         nbytes=4 * len(held) * pairs.size,
     )
-    far = [swap(mixed[step], "ulysses", step) for step in range(owners - 1, 0, -1)]
     return call(
         functools.partial(finish_kernel, owners),
         shape((rows, feats)),
         [VMEM] * (owners + 1),
         hint.reshape(rows, feats),
-        mixed[0],
-        *far[::-1],
+        *exchange(mixed, "ulysses"),
     )
 
 

time: 28.2 us -> 26.6 us (0.943)
  waiting for transfers between devices: 12.7 us -> 9.85 us
  local copies, waits for them, and re-layouts: 0.01 us -> 1.13 us
    ppermute x9, waiting for transfers between devices: 12.7 us -> 9.85 us  [swap(): lax.ppermute(array, axis, [(i, partner(i, size, step)) for i in range(siz...]
    unnamed x4, local copies, waits for them, and re-layouts: 0.01 us -> 1.13 us
  transfers between devices with their start and end apart: 9 -> 9, of which waited for: 5 -> 6; matrix products, arithmetic and copies ran while one was open for 0% -> 0% of each run, Pallas kernels for 1% -> 1%
where the time goes in v7:
time: 26.6 us; the launch traced here: 26.4 us
  starting transfers between devices  11.8 us (44%)
  waiting for transfers between devices  9.85 us (37%)
  Pallas kernels  2.84 us (11%)
  local copies, waits for them, and re-layouts  1.13 us (4%)
  between operations  0.71 us (3%)
    ppermute x9, starting transfers between devices, swap(): lax.ppermute(array, axis, [(i, partner(i, size, step)) for i in range(siz...  11.8 us
    ppermute x9, waiting for transfers between devices, swap(): lax.ppermute(array, axis, [(i, partner(i, size, step)) for i in range(siz...  9.85 us
    pallas_call x5, Pallas kernels, call(): pl.pallas_call(kernel, out_shape=out_shape, in_specs=specs, out_specs=jax...  2.84 us
    unnamed x4, local copies, waits for them, and re-layouts  1.13 us
  transfers between devices with their start and end apart: 9, of which 6 were waited for; matrix products, arithmetic and copies ran while one was open for 0% of the time, Pallas kernels for 1%

profile of v7, /device:TPU:0, one launch (start us, length us, event | category | flops | bytes accessed | tf_op | source)
XLA Modules:
  0.0 26.4 jit_solution(6668183488235478699)
XLA Ops:
  0.0 1.2 %shard_map.100 = (bf16[216,128]{1,0:T(8,128)(2,1)S(1)}, bf16[216,128]{1,0:T(8,128)(2,1)S(1)}, bf16[216,128]{1,0:T(8,128)(2,1)S(1)}, bf16[216,128]{1,0:T(8,128)(2,1)S(1)}) custom-call(s32[1,4]{1,0:T(1,128)} %refs_0_.1, bf16[32,1024]{1,0:T(8,128)(2,1)} %refs_1_.1, bf16[32,1024]{1,0:T(8,128)(2,1)} %refs_2_.1, bf16[32,1024]{1,0:T(8,128)(2,1)} %refs_3_.1, ...), custom_call_target="tpu_custom_call" | custom-call | tf_op jit(solution)/shard_map/pallas_call | solution.py:142
  1.2 5.1 %collective-permute-start = (bf16[216,128]{1,0:T(8,128)(2,1)S(1)}, bf16[216,128]{1,0:T(8,128)(2,1)S(1)}, u32[]{:S(2)}, u32[]{:S(2)}) collective-permute-start(bf16[216,128]{1,0:T(8,128)(2,1)S(1)} %get-tuple-element.18), channel_id=1, source_target_pairs={{0,3},{1,2},{2,1},{3,0},{4,7},{5,6},{6,5},{7,4},{8,11},{9,10},{10,... | collective-permute-start | bytes 165896 | tf_op jit(solution)/shard_map/ppermute | solution.py:32
  6.3 0.0 collective-permute-start.1
  6.3 0.6 %collective-permute-start.2 = (bf16[216,128]{1,0:T(8,128)(2,1)S(1)}, bf16[216,128]{1,0:T(8,128)(2,1)S(1)}, u32[]{:S(2)}, u32[]{:S(2)}) collective-permute-start(bf16[216,128]{1,0:T(8,128)(2,1)S(1)} %get-tuple-element.20), channel_id=1, source_target_pairs={{0,1},{1,0},{2,3},{3,2},{4,5},{5,4},{6,7},{7,6},{8,9},{9,8},{10,11... | collective-permute-start | bytes 165896 | tf_op jit(solution)/shard_map/ppermute | solution.py:32
  6.9 1.7 %collective-permute-done.refs_1_ = bf16[216,128]{1,0:T(8,128)(2,1)S(1)} collective-permute-done((bf16[216,128]{1,0:T(8,128)(2,1)S(1)}, bf16[216,128]{1,0:T(8,128)(2,1)S(1)}, u32[]{:S(2)}, u32[]{:S(2)}) %collective-permute-start) | collective-permute-done | bytes 55328 | tf_op jit(solution)/shard_map/ppermute | solution.py:32
  8.6 2.7 %collective-permute-done.1.refs_2_ = bf16[216,128]{1,0:T(8,128)(2,1)S(1)} collective-permute-done((bf16[216,128]{1,0:T(8,128)(2,1)S(1)}, bf16[216,128]{1,0:T(8,128)(2,1)S(1)}, u32[]{:S(2)}, u32[]{:S(2)}) %collective-permute-start.1) | collective-permute-done | bytes 55328 | tf_op jit(solution)/shard_map/ppermute | solution.py:32
  11.3 0.0 collective-permute-done.2.refs_3_
  11.3 0.0 copy-start.1
  11.3 0.1 shard_map.101
  11.4 1.6 %collective-permute-start.3 = (bf16[4,128,128]{2,1,0:T(8,128)(2,1)S(1)}, bf16[4,128,128]{2,1,0:T(8,128)(2,1)S(1)}, u32[]{:S(2)}, u32[]{:S(2)}) collective-permute-start(bf16[4,128,128]{2,1,0:T(8,128)(2,1)S(1)} %get-tuple-element.21.refs_4_), channel_id=1, source_target_pairs={{0,8},{4,12},{8,0},{12,4},{1,9},{5,13},{9,1},{13,5},{2,10},{6,14},... | collective-permute-start | bytes 393224 | tf_op jit(solution)/shard_map/ppermute | solution.py:32
  13.6 0.1 collective-permute-start.4
  13.7 0.0 copy-done.1
  13.7 0.0 copy-start
  13.7 1.1 %copy-done = bf16[384,1024]{1,0:T(8,128)(2,1)S(1)} copy-done((bf16[384,1024]{1,0:T(8,128)(2,1)S(1)}, bf16[384,1024]{1,0:T(8,128)(2,1)}, u32[]{:S(2)}) %copy-start) | copy-done | bytes 786456
  14.9 0.3 shard_map.102
  15.1 1.3 %collective-permute-done.3.refs_5_ = bf16[4,128,128]{2,1,0:T(8,128)(2,1)S(1)} collective-permute-done((bf16[4,128,128]{2,1,0:T(8,128)(2,1)S(1)}, bf16[4,128,128]{2,1,0:T(8,128)(2,1)S(1)}, u32[]{:S(2)}, u32[]{:S(2)}) %collective-permute-start.3) | collective-permute-done | bytes 131104 | tf_op jit(solution)/shard_map/ppermute | solution.py:32
  16.5 0.0 collective-permute-start.5
  16.5 0.0 collective-permute-done.4.refs_6_
  16.5 1.3 %collective-permute-done.5.refs_7_ = bf16[4,128,128]{2,1,0:T(8,128)(2,1)S(1)} collective-permute-done((bf16[4,128,128]{2,1,0:T(8,128)(2,1)S(1)}, bf16[4,128,128]{2,1,0:T(8,128)(2,1)S(1)}, u32[]{:S(2)}, u32[]{:S(2)}) %collective-permute-start.5) | collective-permute-done | bytes 131104 | tf_op jit(solution)/shard_map/ppermute | solution.py:32
  17.8 0.7 %shard_map.103 = (bf16[64,128]{1,0:T(8,128)(2,1)S(1)}, bf16[64,128]{1,0:T(8,128)(2,1)S(1)}, bf16[64,128]{1,0:T(8,128)(2,1)S(1)}, bf16[64,128]{1,0:T(8,128)(2,1)S(1)}) custom-call(bf16[216,128]{1,0:T(8,128)(2,1)S(1)} %get-tuple-element.17.refs_0_, bf16[216,128]{1,0:T(8,128)(2,1)S(1)} %collective-permute-done.refs_1_, ...), custom_call_target="tpu_custom_call" | custom-call | flops 67108864 | bytes 1048576 | tf_op jit(solution)/shard_map/pallas_call | solution.py:142
  18.5 2.6 %collective-permute-start.6 = (bf16[64,128]{1,0:T(8,128)(2,1)S(1)}, bf16[64,128]{1,0:T(8,128)(2,1)S(1)}, u32[]{:S(2)}, u32[]{:S(2)}) collective-permute-start(bf16[64,128]{1,0:T(8,128)(2,1)S(1)} %get-tuple-element.26), channel_id=1, source_target_pairs={{0,3},{1,2},{2,1},{3,0},{4,7},{5,6},{6,5},{7,4},{8,11},{9,10},{10,... | collective-permute-start | bytes 49160 | tf_op jit(solution)/shard_map/ppermute | solution.py:32
  21.1 0.0 collective-permute-start.7
  21.1 1.9 %collective-permute-start.8 = (bf16[64,128]{1,0:T(8,128)(2,1)S(1)}, bf16[64,128]{1,0:T(8,128)(2,1)S(1)}, u32[]{:S(2)}, u32[]{:S(2)}) collective-permute-start(bf16[64,128]{1,0:T(8,128)(2,1)S(1)} %get-tuple-element.28), channel_id=1, source_target_pairs={{0,1},{1,0},{2,3},{3,2},{4,5},{5,4},{6,7},{7,6},{8,9},{9,8},{10,11... | collective-permute-start | bytes 49160 | tf_op jit(solution)/shard_map/ppermute | solution.py:32
  23.0 1.3 %collective-permute-done.6.refs_1_ = bf16[64,128]{1,0:T(8,128)(2,1)S(1)} collective-permute-done((bf16[64,128]{1,0:T(8,128)(2,1)S(1)}, bf16[64,128]{1,0:T(8,128)(2,1)S(1)}, u32[]{:S(2)}, u32[]{:S(2)}) %collective-permute-start.6) | collective-permute-done | bytes 16416 | tf_op jit(solution)/shard_map/ppermute | solution.py:32
  24.3 1.4 %collective-permute-done.7.refs_2_ = bf16[64,128]{1,0:T(8,128)(2,1)S(1)} collective-permute-done((bf16[64,128]{1,0:T(8,128)(2,1)S(1)}, bf16[64,128]{1,0:T(8,128)(2,1)S(1)}, u32[]{:S(2)}, u32[]{:S(2)}) %collective-permute-start.7) | collective-permute-done | bytes 16416 | tf_op jit(solution)/shard_map/ppermute | solution.py:32
  25.7 0.0 collective-permute-done.8.refs_3_
  25.7 0.7 %shard_map.104 = bf16[32,1024]{1,0:T(8,128)(2,1)} custom-call(f32[32,1024]{1,0:T(8,128)S(1)} %bitcast.3, bf16[64,128]{1,0:T(8,128)(2,1)S(1)} %get-tuple-element.25.refs_0_, bf16[64,128]{1,0:T(8,128)(2,1)S(1)} %collective-permute-done.6.refs_1_, bf16[64,128]{1,0:T(8,128)(2,1)S(1)} %collective-permute-done.7.refs_2_, ...), custom_call_target="tpu_custom_call" | custom-call | tf_op jit(solution)/shard_map/pallas_call | solution.py:142
Async XLA Ops:
  1.2 7.5 %collective-permute-start = (bf16[216,128]{1,0:T(8,128)(2,1)S(1)}, bf16[216,128]{1,0:T(8,128)(2,1)S(1)}, u32[]{:S(2)}, u32[]{:S(2)}) collective-permute-start(bf16[216,128]{1,0:T(8,128)(2,1)S(1)} %get-tuple-element.18), channel_id=1, source_target_pairs={{0,3},{1,2},{2,1},{3,0},{4,7},{5,6},{6,5},{7,4},{8,11},{9,10},{10,... | collective-permute-start | bytes 165896 | tf_op jit(solution)/shard_map/ppermute | solution.py:32
  6.3 5.1 %collective-permute-start.1 = (bf16[216,128]{1,0:T(8,128)(2,1)S(1)}, bf16[216,128]{1,0:T(8,128)(2,1)S(1)}, u32[]{:S(2)}, u32[]{:S(2)}) collective-permute-start(bf16[216,128]{1,0:T(8,128)(2,1)S(1)} %get-tuple-element.19), channel_id=1, source_target_pairs={{0,2},{1,3},{2,0},{3,1},{4,6},{5,7},{6,4},{7,5},{8,10},{9,11},{10,... | collective-permute-start | bytes 165896 | tf_op jit(solution)/shard_map/ppermute | solution.py:32
  6.3 5.1 %collective-permute-start.2 = (bf16[216,128]{1,0:T(8,128)(2,1)S(1)}, bf16[216,128]{1,0:T(8,128)(2,1)S(1)}, u32[]{:S(2)}, u32[]{:S(2)}) collective-permute-start(bf16[216,128]{1,0:T(8,128)(2,1)S(1)} %get-tuple-element.20), channel_id=1, source_target_pairs={{0,1},{1,0},{2,3},{3,2},{4,5},{5,4},{6,7},{7,6},{8,9},{9,8},{10,11... | collective-permute-start | bytes 165896 | tf_op jit(solution)/shard_map/ppermute | solution.py:32
  11.3 2.4 %copy-start.1 = (f32[8,1024]{1,0:T(8,128)S(1)}, f32[8,1024]{1,0:T(8,128)}, u32[]{:S(2)}) copy-start(f32[8,1024]{1,0:T(8,128)} %gain_ref.1) | copy-start | bytes 98308
  11.4 5.0 %collective-permute-start.3 = (bf16[4,128,128]{2,1,0:T(8,128)(2,1)S(1)}, bf16[4,128,128]{2,1,0:T(8,128)(2,1)S(1)}, u32[]{:S(2)}, u32[]{:S(2)}) collective-permute-start(bf16[4,128,128]{2,1,0:T(8,128)(2,1)S(1)} %get-tuple-element.21.refs_4_), channel_id=1, source_target_pairs={{0,8},{4,12},{8,0},{12,4},{1,9},{5,13},{9,1},{13,5},{2,10},{6,14},... | collective-permute-start | bytes 393224 | tf_op jit(solution)/shard_map/ppermute | solution.py:32
  13.6 2.8 %collective-permute-start.4 = (bf16[4,128,128]{2,1,0:T(8,128)(2,1)S(1)}, bf16[4,128,128]{2,1,0:T(8,128)(2,1)S(1)}, u32[]{:S(2)}, u32[]{:S(2)}) collective-permute-start(bf16[4,128,128]{2,1,0:T(8,128)(2,1)S(1)} %get-tuple-element.21.refs_4_), channel_id=1, source_target_pairs={{0,4},{4,0},{8,12},{12,8},{1,5},{5,1},{9,13},{13,9},{2,6},{6,2},{1... | collective-permute-start | bytes 393224 | tf_op jit(solution)/shard_map/ppermute | solution.py:32
  13.7 1.1 %copy-start = (bf16[384,1024]{1,0:T(8,128)(2,1)S(1)}, bf16[384,1024]{1,0:T(8,128)(2,1)}, u32[]{:S(2)}) copy-start(bf16[384,1024]{1,0:T(8,128)(2,1)} %weight_ref.1) | copy-start | bytes 2359300
  16.5 1.3 %collective-permute-start.5 = (bf16[4,128,128]{2,1,0:T(8,128)(2,1)S(1)}, bf16[4,128,128]{2,1,0:T(8,128)(2,1)S(1)}, u32[]{:S(2)}, u32[]{:S(2)}) collective-permute-start(bf16[4,128,128]{2,1,0:T(8,128)(2,1)S(1)} %collective-permute-done.3.refs_5_), channel_id=1, source_target_pairs={{0,4},{4,0},{8,12},{12,8},{1,5},{5,1},{9,13},{13,9},{2,6},{6,2},{1... | collective-permute-start | bytes 393224 | tf_op jit(solution)/shard_map/ppermute | solution.py:32
  18.5 5.8 %collective-permute-start.6 = (bf16[64,128]{1,0:T(8,128)(2,1)S(1)}, bf16[64,128]{1,0:T(8,128)(2,1)S(1)}, u32[]{:S(2)}, u32[]{:S(2)}) collective-permute-start(bf16[64,128]{1,0:T(8,128)(2,1)S(1)} %get-tuple-element.26), channel_id=1, source_target_pairs={{0,3},{1,2},{2,1},{3,0},{4,7},{5,6},{6,5},{7,4},{8,11},{9,10},{10,... | collective-permute-start | bytes 49160 | tf_op jit(solution)/shard_map/ppermute | solution.py:32
  21.1 4.6 %collective-permute-start.7 = (bf16[64,128]{1,0:T(8,128)(2,1)S(1)}, bf16[64,128]{1,0:T(8,128)(2,1)S(1)}, u32[]{:S(2)}, u32[]{:S(2)}) collective-permute-start(bf16[64,128]{1,0:T(8,128)(2,1)S(1)} %get-tuple-element.27), channel_id=1, source_target_pairs={{0,2},{1,3},{2,0},{3,1},{4,6},{5,7},{6,4},{7,5},{8,10},{9,11},{10,... | collective-permute-start | bytes 49160 | tf_op jit(solution)/shard_map/ppermute | solution.py:32
  21.1 4.6 %collective-permute-start.8 = (bf16[64,128]{1,0:T(8,128)(2,1)S(1)}, bf16[64,128]{1,0:T(8,128)(2,1)S(1)}, u32[]{:S(2)}, u32[]{:S(2)}) collective-permute-start(bf16[64,128]{1,0:T(8,128)(2,1)S(1)} %get-tuple-element.28), channel_id=1, source_target_pairs={{0,1},{1,0},{2,3},{3,2},{4,5},{5,4},{6,7},{7,6},{8,9},{9,8},{10,11... | collective-permute-start | bytes 49160 | tf_op jit(solution)/shard_map/ppermute | solution.py:32

commit v8 on v7

--- a/solution.py
+++ b/solution.py
@@ -24,7 +24,7 @@
 
 
 def steps_of(owners):
-    return [0, *range(owners - 1, 0, -1)]
+    return sorted(range(owners), key=lambda step: (step > 0, -step.bit_length(), step))
 
 
 def swap(array, axis, step):

time: 26.6 us -> 27 us (1.015)
  waiting for transfers between devices: 9.85 us -> 11.2 us
  starting transfers between devices: 11.8 us -> 10.9 us
    ppermute x9, waiting for transfers between devices: 9.85 us -> 11.2 us  [swap(): lax.ppermute(array, axis, [(i, partner(i, size, step)) for i in range(siz...]
    ppermute x9, starting transfers between devices: 11.8 us -> 10.9 us  [swap(): lax.ppermute(array, axis, [(i, partner(i, size, step)) for i in range(siz...]
where the time goes in v8:
time: 27 us; the launch traced here: 26.8 us
  waiting for transfers between devices  11.2 us (41%)
  starting transfers between devices  10.9 us (40%)
  Pallas kernels  2.84 us (11%)
  local copies, waits for them, and re-layouts  1.13 us (4%)
  between operations  0.71 us (3%)
    ppermute x9, waiting for transfers between devices, swap(): lax.ppermute(array, axis, [(i, partner(i, size, step)) for i in range(siz...  11.2 us
    ppermute x9, starting transfers between devices, swap(): lax.ppermute(array, axis, [(i, partner(i, size, step)) for i in range(siz...  10.9 us
    pallas_call x5, Pallas kernels, call(): pl.pallas_call(kernel, out_shape=out_shape, in_specs=specs, out_specs=jax...  2.84 us
    unnamed x4, local copies, waits for them, and re-layouts  1.13 us
  transfers between devices with their start and end apart: 9, of which 6 were waited for; matrix products, arithmetic and copies ran while one was open for 0% of the time, Pallas kernels for 1%

profile of v8, /device:TPU:0, one launch (start us, length us, event | category | flops | bytes accessed | tf_op | source)
XLA Modules:
  0.0 26.8 jit_solution(5339740346487828129)
XLA Ops:
  0.0 1.2 %shard_map.100 = (bf16[216,128]{1,0:T(8,128)(2,1)S(1)}, bf16[216,128]{1,0:T(8,128)(2,1)S(1)}, bf16[216,128]{1,0:T(8,128)(2,1)S(1)}, bf16[216,128]{1,0:T(8,128)(2,1)S(1)}) custom-call(s32[1,4]{1,0:T(1,128)} %refs_0_.1, bf16[32,1024]{1,0:T(8,128)(2,1)} %refs_1_.1, bf16[32,1024]{1,0:T(8,128)(2,1)} %refs_2_.1, bf16[32,1024]{1,0:T(8,128)(2,1)} %refs_3_.1, ...), custom_call_target="tpu_custom_call" | custom-call | tf_op jit(solution)/shard_map/pallas_call | solution.py:142
  1.2 4.1 %collective-permute-start = (bf16[216,128]{1,0:T(8,128)(2,1)S(1)}, bf16[216,128]{1,0:T(8,128)(2,1)S(1)}, u32[]{:S(2)}, u32[]{:S(2)}) collective-permute-start(bf16[216,128]{1,0:T(8,128)(2,1)S(1)} %get-tuple-element.18), channel_id=1, source_target_pairs={{0,2},{1,3},{2,0},{3,1},{4,6},{5,7},{6,4},{7,5},{8,10},{9,11},{10,... | collective-permute-start | bytes 165896 | tf_op jit(solution)/shard_map/ppermute | solution.py:32
  5.3 1.3 %collective-permute-start.1 = (bf16[216,128]{1,0:T(8,128)(2,1)S(1)}, bf16[216,128]{1,0:T(8,128)(2,1)S(1)}, u32[]{:S(2)}, u32[]{:S(2)}) collective-permute-start(bf16[216,128]{1,0:T(8,128)(2,1)S(1)} %get-tuple-element.19), channel_id=1, source_target_pairs={{0,3},{1,2},{2,1},{3,0},{4,7},{5,6},{6,5},{7,4},{8,11},{9,10},{10,... | collective-permute-start | bytes 165896 | tf_op jit(solution)/shard_map/ppermute | solution.py:32
  6.6 0.2 collective-permute-start.2
  6.8 1.1 %collective-permute-done.refs_1_ = bf16[216,128]{1,0:T(8,128)(2,1)S(1)} collective-permute-done((bf16[216,128]{1,0:T(8,128)(2,1)S(1)}, bf16[216,128]{1,0:T(8,128)(2,1)S(1)}, u32[]{:S(2)}, u32[]{:S(2)}) %collective-permute-start) | collective-permute-done | bytes 55328 | tf_op jit(solution)/shard_map/ppermute | solution.py:32
  8.0 3.3 %collective-permute-done.1.refs_2_ = bf16[216,128]{1,0:T(8,128)(2,1)S(1)} collective-permute-done((bf16[216,128]{1,0:T(8,128)(2,1)S(1)}, bf16[216,128]{1,0:T(8,128)(2,1)S(1)}, u32[]{:S(2)}, u32[]{:S(2)}) %collective-permute-start.1) | collective-permute-done | bytes 55328 | tf_op jit(solution)/shard_map/ppermute | solution.py:32
  11.3 0.0 collective-permute-done.2.refs_3_
  11.4 0.0 copy-start.1
  11.4 0.1 shard_map.101
  11.5 1.6 %collective-permute-start.3 = (bf16[4,128,128]{2,1,0:T(8,128)(2,1)S(1)}, bf16[4,128,128]{2,1,0:T(8,128)(2,1)S(1)}, u32[]{:S(2)}, u32[]{:S(2)}) collective-permute-start(bf16[4,128,128]{2,1,0:T(8,128)(2,1)S(1)} %get-tuple-element.21.refs_4_), channel_id=1, source_target_pairs={{0,8},{4,12},{8,0},{12,4},{1,9},{5,13},{9,1},{13,5},{2,10},{6,14},... | collective-permute-start | bytes 393224 | tf_op jit(solution)/shard_map/ppermute | solution.py:32
  13.7 0.1 collective-permute-start.4
  13.8 0.0 copy-done.1
  13.8 0.0 copy-start
  13.8 1.1 %copy-done = bf16[384,1024]{1,0:T(8,128)(2,1)S(1)} copy-done((bf16[384,1024]{1,0:T(8,128)(2,1)S(1)}, bf16[384,1024]{1,0:T(8,128)(2,1)}, u32[]{:S(2)}) %copy-start) | copy-done | bytes 786456
  14.9 0.3 shard_map.102
  15.2 1.3 %collective-permute-done.3.refs_5_ = bf16[4,128,128]{2,1,0:T(8,128)(2,1)S(1)} collective-permute-done((bf16[4,128,128]{2,1,0:T(8,128)(2,1)S(1)}, bf16[4,128,128]{2,1,0:T(8,128)(2,1)S(1)}, u32[]{:S(2)}, u32[]{:S(2)}) %collective-permute-start.3) | collective-permute-done | bytes 131104 | tf_op jit(solution)/shard_map/ppermute | solution.py:32
  16.5 0.0 collective-permute-start.5
  16.5 0.0 collective-permute-done.4.refs_6_
  16.5 1.3 %collective-permute-done.5.refs_7_ = bf16[4,128,128]{2,1,0:T(8,128)(2,1)S(1)} collective-permute-done((bf16[4,128,128]{2,1,0:T(8,128)(2,1)S(1)}, bf16[4,128,128]{2,1,0:T(8,128)(2,1)S(1)}, u32[]{:S(2)}, u32[]{:S(2)}) %collective-permute-start.5) | collective-permute-done | bytes 131104 | tf_op jit(solution)/shard_map/ppermute | solution.py:32
  17.8 0.7 %shard_map.103 = (bf16[64,128]{1,0:T(8,128)(2,1)S(1)}, bf16[64,128]{1,0:T(8,128)(2,1)S(1)}, bf16[64,128]{1,0:T(8,128)(2,1)S(1)}, bf16[64,128]{1,0:T(8,128)(2,1)S(1)}) custom-call(bf16[216,128]{1,0:T(8,128)(2,1)S(1)} %get-tuple-element.17.refs_0_, bf16[216,128]{1,0:T(8,128)(2,1)S(1)} %collective-permute-done.refs_1_, ...), custom_call_target="tpu_custom_call" | custom-call | flops 67108864 | bytes 1048576 | tf_op jit(solution)/shard_map/pallas_call | solution.py:142
  18.5 2.0 %collective-permute-start.6 = (bf16[64,128]{1,0:T(8,128)(2,1)S(1)}, bf16[64,128]{1,0:T(8,128)(2,1)S(1)}, u32[]{:S(2)}, u32[]{:S(2)}) collective-permute-start(bf16[64,128]{1,0:T(8,128)(2,1)S(1)} %get-tuple-element.26), channel_id=1, source_target_pairs={{0,2},{1,3},{2,0},{3,1},{4,6},{5,7},{6,4},{7,5},{8,10},{9,11},{10,... | collective-permute-start | bytes 49160 | tf_op jit(solution)/shard_map/ppermute | solution.py:32
  20.6 0.8 %collective-permute-start.7 = (bf16[64,128]{1,0:T(8,128)(2,1)S(1)}, bf16[64,128]{1,0:T(8,128)(2,1)S(1)}, u32[]{:S(2)}, u32[]{:S(2)}) collective-permute-start(bf16[64,128]{1,0:T(8,128)(2,1)S(1)} %get-tuple-element.27), channel_id=1, source_target_pairs={{0,3},{1,2},{2,1},{3,0},{4,7},{5,6},{6,5},{7,4},{8,11},{9,10},{10,... | collective-permute-start | bytes 49160 | tf_op jit(solution)/shard_map/ppermute | solution.py:32
  21.4 0.7 %collective-permute-start.8 = (bf16[64,128]{1,0:T(8,128)(2,1)S(1)}, bf16[64,128]{1,0:T(8,128)(2,1)S(1)}, u32[]{:S(2)}, u32[]{:S(2)}) collective-permute-start(bf16[64,128]{1,0:T(8,128)(2,1)S(1)} %get-tuple-element.28), channel_id=1, source_target_pairs={{0,1},{1,0},{2,3},{3,2},{4,5},{5,4},{6,7},{7,6},{8,9},{9,8},{10,11... | collective-permute-start | bytes 49160 | tf_op jit(solution)/shard_map/ppermute | solution.py:32
  22.1 1.2 %collective-permute-done.6.refs_1_ = bf16[64,128]{1,0:T(8,128)(2,1)S(1)} collective-permute-done((bf16[64,128]{1,0:T(8,128)(2,1)S(1)}, bf16[64,128]{1,0:T(8,128)(2,1)S(1)}, u32[]{:S(2)}, u32[]{:S(2)}) %collective-permute-start.6) | collective-permute-done | bytes 16416 | tf_op jit(solution)/shard_map/ppermute | solution.py:32
  23.3 2.8 %collective-permute-done.7.refs_2_ = bf16[64,128]{1,0:T(8,128)(2,1)S(1)} collective-permute-done((bf16[64,128]{1,0:T(8,128)(2,1)S(1)}, bf16[64,128]{1,0:T(8,128)(2,1)S(1)}, u32[]{:S(2)}, u32[]{:S(2)}) %collective-permute-start.7) | collective-permute-done | bytes 16416 | tf_op jit(solution)/shard_map/ppermute | solution.py:32
  26.1 0.0 collective-permute-done.8.refs_3_
  26.1 0.7 %shard_map.104 = bf16[32,1024]{1,0:T(8,128)(2,1)} custom-call(f32[32,1024]{1,0:T(8,128)S(1)} %bitcast.3, bf16[64,128]{1,0:T(8,128)(2,1)S(1)} %get-tuple-element.25.refs_0_, bf16[64,128]{1,0:T(8,128)(2,1)S(1)} %collective-permute-done.6.refs_1_, bf16[64,128]{1,0:T(8,128)(2,1)S(1)} %collective-permute-done.7.refs_2_, ...), custom_call_target="tpu_custom_call" | custom-call | tf_op jit(solution)/shard_map/pallas_call | solution.py:142
Async XLA Ops:
  1.2 6.8 %collective-permute-start = (bf16[216,128]{1,0:T(8,128)(2,1)S(1)}, bf16[216,128]{1,0:T(8,128)(2,1)S(1)}, u32[]{:S(2)}, u32[]{:S(2)}) collective-permute-start(bf16[216,128]{1,0:T(8,128)(2,1)S(1)} %get-tuple-element.18), channel_id=1, source_target_pairs={{0,2},{1,3},{2,0},{3,1},{4,6},{5,7},{6,4},{7,5},{8,10},{9,11},{10,... | collective-permute-start | bytes 165896 | tf_op jit(solution)/shard_map/ppermute | solution.py:32
  5.3 6.1 %collective-permute-start.1 = (bf16[216,128]{1,0:T(8,128)(2,1)S(1)}, bf16[216,128]{1,0:T(8,128)(2,1)S(1)}, u32[]{:S(2)}, u32[]{:S(2)}) collective-permute-start(bf16[216,128]{1,0:T(8,128)(2,1)S(1)} %get-tuple-element.19), channel_id=1, source_target_pairs={{0,3},{1,2},{2,1},{3,0},{4,7},{5,6},{6,5},{7,4},{8,11},{9,10},{10,... | collective-permute-start | bytes 165896 | tf_op jit(solution)/shard_map/ppermute | solution.py:32
  6.6 4.7 %collective-permute-start.2 = (bf16[216,128]{1,0:T(8,128)(2,1)S(1)}, bf16[216,128]{1,0:T(8,128)(2,1)S(1)}, u32[]{:S(2)}, u32[]{:S(2)}) collective-permute-start(bf16[216,128]{1,0:T(8,128)(2,1)S(1)} %get-tuple-element.20), channel_id=1, source_target_pairs={{0,1},{1,0},{2,3},{3,2},{4,5},{5,4},{6,7},{7,6},{8,9},{9,8},{10,11... | collective-permute-start | bytes 165896 | tf_op jit(solution)/shard_map/ppermute | solution.py:32
  11.4 2.4 %copy-start.1 = (f32[8,1024]{1,0:T(8,128)S(1)}, f32[8,1024]{1,0:T(8,128)}, u32[]{:S(2)}) copy-start(f32[8,1024]{1,0:T(8,128)} %gain_ref.1) | copy-start | bytes 98308
  11.5 5.0 %collective-permute-start.3 = (bf16[4,128,128]{2,1,0:T(8,128)(2,1)S(1)}, bf16[4,128,128]{2,1,0:T(8,128)(2,1)S(1)}, u32[]{:S(2)}, u32[]{:S(2)}) collective-permute-start(bf16[4,128,128]{2,1,0:T(8,128)(2,1)S(1)} %get-tuple-element.21.refs_4_), channel_id=1, source_target_pairs={{0,8},{4,12},{8,0},{12,4},{1,9},{5,13},{9,1},{13,5},{2,10},{6,14},... | collective-permute-start | bytes 393224 | tf_op jit(solution)/shard_map/ppermute | solution.py:32
  13.7 2.8 %collective-permute-start.4 = (bf16[4,128,128]{2,1,0:T(8,128)(2,1)S(1)}, bf16[4,128,128]{2,1,0:T(8,128)(2,1)S(1)}, u32[]{:S(2)}, u32[]{:S(2)}) collective-permute-start(bf16[4,128,128]{2,1,0:T(8,128)(2,1)S(1)} %get-tuple-element.21.refs_4_), channel_id=1, source_target_pairs={{0,4},{4,0},{8,12},{12,8},{1,5},{5,1},{9,13},{13,9},{2,6},{6,2},{1... | collective-permute-start | bytes 393224 | tf_op jit(solution)/shard_map/ppermute | solution.py:32
  13.8 1.1 %copy-start = (bf16[384,1024]{1,0:T(8,128)(2,1)S(1)}, bf16[384,1024]{1,0:T(8,128)(2,1)}, u32[]{:S(2)}) copy-start(bf16[384,1024]{1,0:T(8,128)(2,1)} %weight_ref.1) | copy-start | bytes 2359300
  16.5 1.3 %collective-permute-start.5 = (bf16[4,128,128]{2,1,0:T(8,128)(2,1)S(1)}, bf16[4,128,128]{2,1,0:T(8,128)(2,1)S(1)}, u32[]{:S(2)}, u32[]{:S(2)}) collective-permute-start(bf16[4,128,128]{2,1,0:T(8,128)(2,1)S(1)} %collective-permute-done.3.refs_5_), channel_id=1, source_target_pairs={{0,4},{4,0},{8,12},{12,8},{1,5},{5,1},{9,13},{13,9},{2,6},{6,2},{1... | collective-permute-start | bytes 393224 | tf_op jit(solution)/shard_map/ppermute | solution.py:32
  18.5 4.7 %collective-permute-start.6 = (bf16[64,128]{1,0:T(8,128)(2,1)S(1)}, bf16[64,128]{1,0:T(8,128)(2,1)S(1)}, u32[]{:S(2)}, u32[]{:S(2)}) collective-permute-start(bf16[64,128]{1,0:T(8,128)(2,1)S(1)} %get-tuple-element.26), channel_id=1, source_target_pairs={{0,2},{1,3},{2,0},{3,1},{4,6},{5,7},{6,4},{7,5},{8,10},{9,11},{10,... | collective-permute-start | bytes 49160 | tf_op jit(solution)/shard_map/ppermute | solution.py:32
  20.6 5.5 %collective-permute-start.7 = (bf16[64,128]{1,0:T(8,128)(2,1)S(1)}, bf16[64,128]{1,0:T(8,128)(2,1)S(1)}, u32[]{:S(2)}, u32[]{:S(2)}) collective-permute-start(bf16[64,128]{1,0:T(8,128)(2,1)S(1)} %get-tuple-element.27), channel_id=1, source_target_pairs={{0,3},{1,2},{2,1},{3,0},{4,7},{5,6},{6,5},{7,4},{8,11},{9,10},{10,... | collective-permute-start | bytes 49160 | tf_op jit(solution)/shard_map/ppermute | solution.py:32
  21.4 4.7 %collective-permute-start.8 = (bf16[64,128]{1,0:T(8,128)(2,1)S(1)}, bf16[64,128]{1,0:T(8,128)(2,1)S(1)}, u32[]{:S(2)}, u32[]{:S(2)}) collective-permute-start(bf16[64,128]{1,0:T(8,128)(2,1)S(1)} %get-tuple-element.28), channel_id=1, source_target_pairs={{0,1},{1,0},{2,3},{3,2},{4,5},{5,4},{6,7},{7,6},{8,9},{9,8},{10,11... | collective-permute-start | bytes 49160 | tf_op jit(solution)/shard_map/ppermute | solution.py:32

commit v9 on v7

--- a/solution.py
+++ b/solution.py
@@ -17,10 +17,8 @@
     return values * scale * gain
 
 
-def partner(me, size, step):
-    if size & (size - 1) == 0:
-        return me ^ step
-    return (step + size - me) % size
+def partner(me, step):
+    return me ^ step
 
 
 def steps_of(owners):
@@ -29,13 +27,13 @@
 
 def swap(array, axis, step):
     size = lax.axis_size(axis)
-    return lax.ppermute(array, axis, [(i, partner(i, size, step)) for i in range(size)])
+    return lax.ppermute(array, axis, [(i, partner(i, step)) for i in range(size)])
 
 
 def pack_kernel(owners, *refs):
-    total = (len(refs) - owners - 2) // 2
-    sources, out_refs = refs[:total], refs[total : total + owners]
-    held, (norm_ref, copy_sems) = refs[total + owners : -2], refs[-2:]
+    total = (len(refs) - owners - 3) // 2
+    sources, out_refs, own_ref = refs[:total], refs[total : total + owners], refs[total + owners]
+    held, (norm_ref, copy_sems) = refs[total + owners + 1 : -2], refs[-2:]
     copies = [
         pltpu.make_async_copy(source, buffer, copy_sems.at[i])
         for i, (source, buffer) in enumerate(zip(sources, held))
@@ -55,12 +53,15 @@
     patches = control_ref[...].astype(jnp.float32)
     slabs = [patches[j * slab_rows : (j + 1) * slab_rows] for j in range(owners)]
     for step, out_ref in zip(steps_of(owners), out_refs):
-        to = partner(me, owners, step)
+        to = partner(me, step)
         at = 0
         for i in range(3):
             for head in range(share // HEAD_DIM):
                 cols = pl.ds(pl.multiple_of(to * share + head * HEAD_DIM, HEAD_DIM), HEAD_DIM)
-                out_ref[at : at + rows] = norm_ref[i, :, cols]
+                lines = norm_ref[i, :, cols]
+                out_ref[at : at + rows] = lines
+                if step == 0 and i < 2:
+                    own_ref[0, at : at + rows] = lines
                 at = at + rows
         slab = slabs[0]
         for j in range(1, owners):
@@ -72,13 +73,15 @@
 
 
 def sort_kernel(rows, *refs):
-    got_refs, (pair_ref, patch_ref) = refs[:-2], refs[-2:]
+    got_refs, (pair_ref, rest_ref, patch_ref) = refs[:-3], refs[-3:]
     owners = len(got_refs)
     slab_rows, width = rows // owners, patch_ref.shape[1]
     size = pair_ref.shape[1]
     start = 3 * size // 2
     for i, ref in enumerate(got_refs):
         pair_ref[i] = ref[:size]
+        if i:
+            rest_ref[i - 1] = ref[:size]
     slabs = [ref[start:].astype(jnp.float32) for ref in got_refs]
     patches = [
         jnp.concatenate([slab[i * slab_rows : (i + 1) * slab_rows] for slab in slabs], axis=0)
@@ -90,7 +93,7 @@
 def attend_kernel(rows, owners, *refs):
     got_refs, pair_refs, out_refs = refs[:owners], refs[owners:-owners], refs[-owners:]
     heads = out_refs[0].shape[0] // rows
-    count = len(pair_refs) * owners * rows
+    count = sum(ref.shape[0] for ref in pair_refs) * rows
     group = max(1, min(owners, 2**17 // (rows * count)))
     for head in range(heads):
         at, past, ask = (slice((i * heads + head) * rows, (i * heads + head + 1) * rows) for i in range(3))
@@ -117,7 +120,7 @@
     hint = hint.astype(jnp.bfloat16).astype(jnp.float32) * gain_ref[pl.ds(layer_ref[0], 1), :]
     me = lax.axis_index("ulysses")
     for i, step in enumerate(steps_of(owners)):
-        out_ref[partner(me, owners, step)] = hint[i * slab_rows : (i + 1) * slab_rows]
+        out_ref[partner(me, step)] = hint[i * slab_rows : (i + 1) * slab_rows]
 
 
 def finish_kernel(owners, hint_ref, *refs):
@@ -127,7 +130,7 @@
     me = lax.axis_index("ulysses")
     for step, ref in zip(steps_of(owners), back_refs):
         for head in range(share // HEAD_DIM):
-            start = partner(me, owners, step) * share + head * HEAD_DIM
+            start = partner(me, step) * share + head * HEAD_DIM
             cols = pl.ds(pl.multiple_of(start, HEAD_DIM), HEAD_DIM)
             attended = ref[head * rows : (head + 1) * rows].astype(jnp.float32)
             out_ref[:, cols] = (attended + hint_ref[:, cols]).astype(jnp.bfloat16)
@@ -154,19 +157,11 @@
     return jax.ShapeDtypeStruct(dims, dtype)
 
 
-def gather(pairs, beside, axis):
-    size = lax.axis_size(axis)
-    if size & (size - 1):
-        return [swap(pairs, axis, step) for step in range(size)], beside
-    held = [pairs]
-    step = size // 2
+def gather(held, step, axis):
     while step:
-        moved = [swap(array, axis, step) for array in held]
-        if len(held) == 1:
-            moved, beside = lax.optimization_barrier((moved, beside))
-        held = held + moved
+        held = held + [swap(array, axis, step) for array in held]
         step = step // 2
-    return held, beside
+    return held
 
 
 def exchange(arrays, axis):
@@ -205,7 +200,7 @@
     sources = [pltpu.with_memory_space_constraint(source, pltpu.HBM) for source in sources]
     sent = call(
         functools.partial(pack_kernel, owners),
-        [shape((3 * lines + slab_lines, HEAD_DIM))] * owners,
+        [shape((3 * lines + slab_lines, HEAD_DIM))] * owners + [shape((1, 2 * lines, HEAD_DIM))],
         [HBM] * len(sources),
         *sources,
         scratch=[pltpu.SMEM(owner_map.shape, owner_map.dtype)]
@@ -215,10 +210,16 @@
             pltpu.SemaphoreType.DMA((len(sources),)),
         ],
     )
-    got = exchange(sent, "ulysses")
-    pairs, patches = call(
+    half = lax.axis_size("blk") // 2
+    own_moved = swap(sent[owners], "blk", half)
+    got, own_moved = lax.optimization_barrier((exchange(sent[:owners], "ulysses"), own_moved))
+    pairs, rest, patches = call(
         functools.partial(sort_kernel, rows),
-        [shape((owners, 2 * lines, HEAD_DIM)), shape((rows, width))],
+        [
+            shape((owners, 2 * lines, HEAD_DIM)),
+            shape((owners - 1, 2 * lines, HEAD_DIM)),
+            shape((rows, width)),
+        ],
         [VMEM] * owners,
         *got,
     )
@@ -233,15 +234,18 @@
         flops=2 * rows * width * feats,
         nbytes=2 * width * feats,
     )
-    held, hint = gather(pairs, hint, "blk")
+    moved = swap(rest, "blk", half)
+    held = gather([own_moved], half // 2, "blk")
+    moved, held, hint = lax.optimization_barrier((moved, held, hint))
+    held = held + gather([pairs, moved], half // 2, "blk")
     mixed = call(
         functools.partial(attend_kernel, rows, owners),
         [shape((lines, HEAD_DIM))] * owners,
         [VMEM] * (owners + len(held)),
         *got,
         *held,
-        flops=4 * lines * owners * len(held) * owners * rows * HEAD_DIM,
-        nbytes=4 * len(held) * pairs.size,
+        flops=2 * lines * sum(array.size for array in held),
+        nbytes=2 * sum(array.size for array in held),
     )
     return call(
         functools.partial(finish_kernel, owners),

time: 26.6 us -> 27 us (1.015)
  starting transfers between devices: 11.8 us -> 13.9 us
  waiting for transfers between devices: 9.85 us -> 8.15 us
    ppermute x9 -> x11, starting transfers between devices: 11.8 us -> 13.9 us  [swap(): lax.ppermute(array, axis, [(i, partner(i, step)) for i in range(size)])]
    ppermute x9 -> x11, waiting for transfers between devices: 9.85 us -> 8.15 us  [swap(): lax.ppermute(array, axis, [(i, partner(i, step)) for i in range(size)])]
  transfers between devices with their start and end apart: 9 -> 11, of which waited for: 6 -> 6; matrix products, arithmetic and copies ran while one was open for 0% -> 0% of each run, Pallas kernels for 1% -> 1%
where the time goes in v9:
time: 27 us; the launch traced here: 26.7 us
  starting transfers between devices  13.9 us (51%)
  waiting for transfers between devices  8.15 us (30%)
  Pallas kernels  2.85 us (11%)
  local copies, waits for them, and re-layouts  1.13 us (4%)
  between operations  0.71 us (3%)
    ppermute x11, starting transfers between devices, swap(): lax.ppermute(array, axis, [(i, partner(i, step)) for i in range(size)])  13.9 us
    ppermute x11, waiting for transfers between devices, swap(): lax.ppermute(array, axis, [(i, partner(i, step)) for i in range(size)])  8.15 us
    pallas_call x5, Pallas kernels, call(): pl.pallas_call(kernel, out_shape=out_shape, in_specs=specs, out_specs=jax...  2.85 us
    unnamed x4, local copies, waits for them, and re-layouts  1.13 us
  transfers between devices with their start and end apart: 11, of which 6 were waited for; matrix products, arithmetic and copies ran while one was open for 0% of the time, Pallas kernels for 1%

profile of v9, /device:TPU:0, one launch (start us, length us, event | category | flops | bytes accessed | tf_op | source)
XLA Modules:
  0.0 26.7 jit_solution(3418453311815830939)
XLA Ops:
  0.0 1.2 %shard_map.100 = (bf16[216,128]{1,0:T(8,128)(2,1)S(1)}, bf16[216,128]{1,0:T(8,128)(2,1)S(1)}, bf16[216,128]{1,0:T(8,128)(2,1)S(1)}, bf16[216,128]{1,0:T(8,128)(2,1)S(1)}, bf16[1,128,128]{2,1,0:T(8,128)(2,1)S(1)}) custom-call(s32[1,4]{1,0:T(1,128)} %refs_0_.1, bf16[32,1024]{1,0:T(8,128)(2,1)} %refs_1_.1, bf16[32,1024]{1,0:T(8,128)(2,1)} %refs_2_.1, ...), custom_call_target="tpu_custom_call" | custom-call | tf_op jit(solution)/shard_map/pallas_call | solution.py:145
  1.2 5.1 %collective-permute-start = (bf16[216,128]{1,0:T(8,128)(2,1)S(1)}, bf16[216,128]{1,0:T(8,128)(2,1)S(1)}, u32[]{:S(2)}, u32[]{:S(2)}) collective-permute-start(bf16[216,128]{1,0:T(8,128)(2,1)S(1)} %get-tuple-element.27), channel_id=1, source_target_pairs={{0,3},{1,2},{2,1},{3,0},{4,7},{5,6},{6,5},{7,4},{8,11},{9,10},{10,... | collective-permute-start | bytes 165896 | tf_op jit(solution)/shard_map/ppermute | solution.py:30
  6.3 0.0 collective-permute-start.1
  6.3 0.6 %collective-permute-start.2 = (bf16[216,128]{1,0:T(8,128)(2,1)S(1)}, bf16[216,128]{1,0:T(8,128)(2,1)S(1)}, u32[]{:S(2)}, u32[]{:S(2)}) collective-permute-start(bf16[216,128]{1,0:T(8,128)(2,1)S(1)} %get-tuple-element.29), channel_id=1, source_target_pairs={{0,1},{1,0},{2,3},{3,2},{4,5},{5,4},{6,7},{7,6},{8,9},{9,8},{10,11... | collective-permute-start | bytes 165896 | tf_op jit(solution)/shard_map/ppermute | solution.py:30
  6.9 1.6 %collective-permute-start.3 = (bf16[1,128,128]{2,1,0:T(8,128)(2,1)S(1)}, bf16[1,128,128]{2,1,0:T(8,128)(2,1)S(1)}, u32[]{:S(2)}, u32[]{:S(2)}) collective-permute-start(bf16[1,128,128]{2,1,0:T(8,128)(2,1)S(1)} %get-tuple-element.30), channel_id=1, source_target_pairs={{0,8},{4,12},{8,0},{12,4},{1,9},{5,13},{9,1},{13,5},{2,10},{6,14},... | collective-permute-start | bytes 98312 | tf_op jit(solution)/shard_map/ppermute | solution.py:30
  8.6 2.3 %collective-permute-done.3.refs_4_ = bf16[1,128,128]{2,1,0:T(8,128)(2,1)S(1)} collective-permute-done((bf16[1,128,128]{2,1,0:T(8,128)(2,1)S(1)}, bf16[1,128,128]{2,1,0:T(8,128)(2,1)S(1)}, u32[]{:S(2)}, u32[]{:S(2)}) %collective-permute-start.3) | collective-permute-done | bytes 32800 | tf_op jit(solution)/shard_map/ppermute | solution.py:30
  10.8 0.0 collective-permute-done.refs_1_
  10.8 0.5 %collective-permute-done.1.refs_2_ = bf16[216,128]{1,0:T(8,128)(2,1)S(1)} collective-permute-done((bf16[216,128]{1,0:T(8,128)(2,1)S(1)}, bf16[216,128]{1,0:T(8,128)(2,1)S(1)}, u32[]{:S(2)}, u32[]{:S(2)}) %collective-permute-start.1) | collective-permute-done | bytes 55328 | tf_op jit(solution)/shard_map/ppermute | solution.py:30
  11.3 0.0 collective-permute-done.2.refs_3_
  11.3 0.0 copy-start.1
  11.3 0.1 shard_map.101
  11.4 1.6 %collective-permute-start.4 = (bf16[3,128,128]{2,1,0:T(8,128)(2,1)S(1)}, bf16[3,128,128]{2,1,0:T(8,128)(2,1)S(1)}, u32[]{:S(2)}, u32[]{:S(2)}) collective-permute-start(bf16[3,128,128]{2,1,0:T(8,128)(2,1)S(1)} %get-tuple-element.35), channel_id=1, source_target_pairs={{0,8},{4,12},{8,0},{12,4},{1,9},{5,13},{9,1},{13,5},{2,10},{6,14},... | collective-permute-start | bytes 294920 | tf_op jit(solution)/shard_map/ppermute | solution.py:30
  13.0 0.0 collective-permute-start.5
  13.0 0.5 %collective-permute-start.6 = (bf16[4,128,128]{2,1,0:T(8,128)(2,1)S(1)}, bf16[4,128,128]{2,1,0:T(8,128)(2,1)S(1)}, u32[]{:S(2)}, u32[]{:S(2)}) collective-permute-start(bf16[4,128,128]{2,1,0:T(8,128)(2,1)S(1)} %get-tuple-element.41.refs_6_), channel_id=1, source_target_pairs={{0,4},{4,0},{8,12},{12,8},{1,5},{5,1},{9,13},{13,9},{2,6},{6,2},{1... | collective-permute-start | bytes 393224 | tf_op jit(solution)/shard_map/ppermute | solution.py:30
  14.2 0.0 copy-done.1
  14.2 0.0 copy-start
  14.2 1.1 %copy-done = bf16[384,1024]{1,0:T(8,128)(2,1)S(1)} copy-done((bf16[384,1024]{1,0:T(8,128)(2,1)S(1)}, bf16[384,1024]{1,0:T(8,128)(2,1)}, u32[]{:S(2)}) %copy-start) | copy-done | bytes 786456
  15.3 0.3 shard_map.102
  15.6 0.0 collective-permute-done.5.refs_5_
  15.6 0.5 %collective-permute-done.4.refs_7_ = bf16[3,128,128]{2,1,0:T(8,128)(2,1)S(1)} collective-permute-done((bf16[3,128,128]{2,1,0:T(8,128)(2,1)S(1)}, bf16[3,128,128]{2,1,0:T(8,128)(2,1)S(1)}, u32[]{:S(2)}, u32[]{:S(2)}) %collective-permute-start.4) | collective-permute-done | bytes 98336 | tf_op jit(solution)/shard_map/ppermute | solution.py:30
  16.1 0.0 collective-permute-start.7
  16.1 0.0 collective-permute-done.6.refs_8_
  16.1 1.3 %collective-permute-done.7.refs_9_ = bf16[3,128,128]{2,1,0:T(8,128)(2,1)S(1)} collective-permute-done((bf16[3,128,128]{2,1,0:T(8,128)(2,1)S(1)}, bf16[3,128,128]{2,1,0:T(8,128)(2,1)S(1)}, u32[]{:S(2)}, u32[]{:S(2)}) %collective-permute-start.7) | collective-permute-done | bytes 98336 | tf_op jit(solution)/shard_map/ppermute | solution.py:30
  17.4 0.7 %shard_map.103 = (bf16[64,128]{1,0:T(8,128)(2,1)S(1)}, bf16[64,128]{1,0:T(8,128)(2,1)S(1)}, bf16[64,128]{1,0:T(8,128)(2,1)S(1)}, bf16[64,128]{1,0:T(8,128)(2,1)S(1)}) custom-call(bf16[216,128]{1,0:T(8,128)(2,1)S(1)} %get-tuple-element.31.refs_0_, bf16[216,128]{1,0:T(8,128)(2,1)S(1)} %collective-permute-done.refs_1_, ...), custom_call_target="tpu_custom_call" | custom-call | flops 33554432 | bytes 524288 | tf_op jit(solution)/shard_map/pallas_call | solution.py:145
  18.1 3.3 %collective-permute-start.8 = (bf16[64,128]{1,0:T(8,128)(2,1)S(1)}, bf16[64,128]{1,0:T(8,128)(2,1)S(1)}, u32[]{:S(2)}, u32[]{:S(2)}) collective-permute-start(bf16[64,128]{1,0:T(8,128)(2,1)S(1)} %get-tuple-element.44), channel_id=1, source_target_pairs={{0,3},{1,2},{2,1},{3,0},{4,7},{5,6},{6,5},{7,4},{8,11},{9,10},{10,... | collective-permute-start | bytes 49160 | tf_op jit(solution)/shard_map/ppermute | solution.py:30
  21.4 0.0 collective-permute-start.9
  21.5 1.1 %collective-permute-start.10 = (bf16[64,128]{1,0:T(8,128)(2,1)S(1)}, bf16[64,128]{1,0:T(8,128)(2,1)S(1)}, u32[]{:S(2)}, u32[]{:S(2)}) collective-permute-start(bf16[64,128]{1,0:T(8,128)(2,1)S(1)} %get-tuple-element.46), channel_id=1, source_target_pairs={{0,1},{1,0},{2,3},{3,2},{4,5},{5,4},{6,7},{7,6},{8,9},{9,8},{10,11... | collective-permute-start | bytes 49160 | tf_op jit(solution)/shard_map/ppermute | solution.py:30
  22.6 1.3 %collective-permute-done.8.refs_1_ = bf16[64,128]{1,0:T(8,128)(2,1)S(1)} collective-permute-done((bf16[64,128]{1,0:T(8,128)(2,1)S(1)}, bf16[64,128]{1,0:T(8,128)(2,1)S(1)}, u32[]{:S(2)}, u32[]{:S(2)}) %collective-permute-start.8) | collective-permute-done | bytes 16416 | tf_op jit(solution)/shard_map/ppermute | solution.py:30
  23.9 2.2 %collective-permute-done.9.refs_2_ = bf16[64,128]{1,0:T(8,128)(2,1)S(1)} collective-permute-done((bf16[64,128]{1,0:T(8,128)(2,1)S(1)}, bf16[64,128]{1,0:T(8,128)(2,1)S(1)}, u32[]{:S(2)}, u32[]{:S(2)}) %collective-permute-start.9) | collective-permute-done | bytes 16416 | tf_op jit(solution)/shard_map/ppermute | solution.py:30
  26.1 0.0 collective-permute-done.10.refs_3_
  26.1 0.7 %shard_map.104 = bf16[32,1024]{1,0:T(8,128)(2,1)} custom-call(f32[32,1024]{1,0:T(8,128)S(1)} %bitcast.3, bf16[64,128]{1,0:T(8,128)(2,1)S(1)} %get-tuple-element.43.refs_0_, bf16[64,128]{1,0:T(8,128)(2,1)S(1)} %collective-permute-done.8.refs_1_, bf16[64,128]{1,0:T(8,128)(2,1)S(1)} %collective-permute-done.9.refs_2_, ...), custom_call_target="tpu_custom_call" | custom-call | tf_op jit(solution)/shard_map/pallas_call | solution.py:145
Async XLA Ops:
  1.2 9.7 %collective-permute-start = (bf16[216,128]{1,0:T(8,128)(2,1)S(1)}, bf16[216,128]{1,0:T(8,128)(2,1)S(1)}, u32[]{:S(2)}, u32[]{:S(2)}) collective-permute-start(bf16[216,128]{1,0:T(8,128)(2,1)S(1)} %get-tuple-element.27), channel_id=1, source_target_pairs={{0,3},{1,2},{2,1},{3,0},{4,7},{5,6},{6,5},{7,4},{8,11},{9,10},{10,... | collective-permute-start | bytes 165896 | tf_op jit(solution)/shard_map/ppermute | solution.py:30
  6.3 5.1 %collective-permute-start.1 = (bf16[216,128]{1,0:T(8,128)(2,1)S(1)}, bf16[216,128]{1,0:T(8,128)(2,1)S(1)}, u32[]{:S(2)}, u32[]{:S(2)}) collective-permute-start(bf16[216,128]{1,0:T(8,128)(2,1)S(1)} %get-tuple-element.28), channel_id=1, source_target_pairs={{0,2},{1,3},{2,0},{3,1},{4,6},{5,7},{6,4},{7,5},{8,10},{9,11},{10,... | collective-permute-start | bytes 165896 | tf_op jit(solution)/shard_map/ppermute | solution.py:30
  6.3 5.1 %collective-permute-start.2 = (bf16[216,128]{1,0:T(8,128)(2,1)S(1)}, bf16[216,128]{1,0:T(8,128)(2,1)S(1)}, u32[]{:S(2)}, u32[]{:S(2)}) collective-permute-start(bf16[216,128]{1,0:T(8,128)(2,1)S(1)} %get-tuple-element.29), channel_id=1, source_target_pairs={{0,1},{1,0},{2,3},{3,2},{4,5},{5,4},{6,7},{7,6},{8,9},{9,8},{10,11... | collective-permute-start | bytes 165896 | tf_op jit(solution)/shard_map/ppermute | solution.py:30
  6.9 3.9 %collective-permute-start.3 = (bf16[1,128,128]{2,1,0:T(8,128)(2,1)S(1)}, bf16[1,128,128]{2,1,0:T(8,128)(2,1)S(1)}, u32[]{:S(2)}, u32[]{:S(2)}) collective-permute-start(bf16[1,128,128]{2,1,0:T(8,128)(2,1)S(1)} %get-tuple-element.30), channel_id=1, source_target_pairs={{0,8},{4,12},{8,0},{12,4},{1,9},{5,13},{9,1},{13,5},{2,10},{6,14},... | collective-permute-start | bytes 98312 | tf_op jit(solution)/shard_map/ppermute | solution.py:30
  11.3 2.8 %copy-start.1 = (f32[8,1024]{1,0:T(8,128)S(1)}, f32[8,1024]{1,0:T(8,128)}, u32[]{:S(2)}) copy-start(f32[8,1024]{1,0:T(8,128)} %gain_ref.1) | copy-start | bytes 98308
  11.4 4.7 %collective-permute-start.4 = (bf16[3,128,128]{2,1,0:T(8,128)(2,1)S(1)}, bf16[3,128,128]{2,1,0:T(8,128)(2,1)S(1)}, u32[]{:S(2)}, u32[]{:S(2)}) collective-permute-start(bf16[3,128,128]{2,1,0:T(8,128)(2,1)S(1)} %get-tuple-element.35), channel_id=1, source_target_pairs={{0,8},{4,12},{8,0},{12,4},{1,9},{5,13},{9,1},{13,5},{2,10},{6,14},... | collective-permute-start | bytes 294920 | tf_op jit(solution)/shard_map/ppermute | solution.py:30
  13.0 2.6 %collective-permute-start.5 = (bf16[1,128,128]{2,1,0:T(8,128)(2,1)S(1)}, bf16[1,128,128]{2,1,0:T(8,128)(2,1)S(1)}, u32[]{:S(2)}, u32[]{:S(2)}) collective-permute-start(bf16[1,128,128]{2,1,0:T(8,128)(2,1)S(1)} %collective-permute-done.3.refs_4_), channel_id=1, source_target_pairs={{0,4},{4,0},{8,12},{12,8},{1,5},{5,1},{9,13},{13,9},{2,6},{6,2},{1... | collective-permute-start | bytes 98312 | tf_op jit(solution)/shard_map/ppermute | solution.py:30
  13.0 3.1 %collective-permute-start.6 = (bf16[4,128,128]{2,1,0:T(8,128)(2,1)S(1)}, bf16[4,128,128]{2,1,0:T(8,128)(2,1)S(1)}, u32[]{:S(2)}, u32[]{:S(2)}) collective-permute-start(bf16[4,128,128]{2,1,0:T(8,128)(2,1)S(1)} %get-tuple-element.41.refs_6_), channel_id=1, source_target_pairs={{0,4},{4,0},{8,12},{12,8},{1,5},{5,1},{9,13},{13,9},{2,6},{6,2},{1... | collective-permute-start | bytes 393224 | tf_op jit(solution)/shard_map/ppermute | solution.py:30
  14.2 1.1 %copy-start = (bf16[384,1024]{1,0:T(8,128)(2,1)S(1)}, bf16[384,1024]{1,0:T(8,128)(2,1)}, u32[]{:S(2)}) copy-start(bf16[384,1024]{1,0:T(8,128)(2,1)} %weight_ref.1) | copy-start | bytes 2359300
  16.1 1.3 %collective-permute-start.7 = (bf16[3,128,128]{2,1,0:T(8,128)(2,1)S(1)}, bf16[3,128,128]{2,1,0:T(8,128)(2,1)S(1)}, u32[]{:S(2)}, u32[]{:S(2)}) collective-permute-start(bf16[3,128,128]{2,1,0:T(8,128)(2,1)S(1)} %collective-permute-done.4.refs_7_), channel_id=1, source_target_pairs={{0,4},{4,0},{8,12},{12,8},{1,5},{5,1},{9,13},{13,9},{2,6},{6,2},{1... | collective-permute-start | bytes 294920 | tf_op jit(solution)/shard_map/ppermute | solution.py:30
  18.1 5.8 %collective-permute-start.8 = (bf16[64,128]{1,0:T(8,128)(2,1)S(1)}, bf16[64,128]{1,0:T(8,128)(2,1)S(1)}, u32[]{:S(2)}, u32[]{:S(2)}) collective-permute-start(bf16[64,128]{1,0:T(8,128)(2,1)S(1)} %get-tuple-element.44), channel_id=1, source_target_pairs={{0,3},{1,2},{2,1},{3,0},{4,7},{5,6},{6,5},{7,4},{8,11},{9,10},{10,... | collective-permute-start | bytes 49160 | tf_op jit(solution)/shard_map/ppermute | solution.py:30
  21.4 4.6 %collective-permute-start.9 = (bf16[64,128]{1,0:T(8,128)(2,1)S(1)}, bf16[64,128]{1,0:T(8,128)(2,1)S(1)}, u32[]{:S(2)}, u32[]{:S(2)}) collective-permute-start(bf16[64,128]{1,0:T(8,128)(2,1)S(1)} %get-tuple-element.45), channel_id=1, source_target_pairs={{0,2},{1,3},{2,0},{3,1},{4,6},{5,7},{6,4},{7,5},{8,10},{9,11},{10,... | collective-permute-start | bytes 49160 | tf_op jit(solution)/shard_map/ppermute | solution.py:30
  21.5 4.6 %collective-permute-start.10 = (bf16[64,128]{1,0:T(8,128)(2,1)S(1)}, bf16[64,128]{1,0:T(8,128)(2,1)S(1)}, u32[]{:S(2)}, u32[]{:S(2)}) collective-permute-start(bf16[64,128]{1,0:T(8,128)(2,1)S(1)} %get-tuple-element.46), channel_id=1, source_target_pairs={{0,1},{1,0},{2,3},{3,2},{4,5},{5,4},{6,7},{7,6},{8,9},{9,8},{10,11... | collective-permute-start | bytes 49160 | tf_op jit(solution)/shard_map/ppermute | solution.py:30

commit v10 on v9

--- a/solution.py
+++ b/solution.py
@@ -21,7 +21,11 @@
     return me ^ step
 
 
-def steps_of(owners):
+def steps_in(owners):
+    return sorted(range(owners), key=lambda step: (step > 0, -step.bit_length(), step))
+
+
+def steps_back(owners):
     return [0, *range(owners - 1, 0, -1)]
 
 
@@ -52,7 +56,7 @@
     norm_ref[2] = normed(q_ref[...], qg_ref[...]).astype(jnp.bfloat16)
     patches = control_ref[...].astype(jnp.float32)
     slabs = [patches[j * slab_rows : (j + 1) * slab_rows] for j in range(owners)]
-    for step, out_ref in zip(steps_of(owners), out_refs):
+    for step, out_ref in zip(steps_in(owners), out_refs):
         to = partner(me, step)
         at = 0
         for i in range(3):
@@ -90,28 +94,65 @@
     patch_ref[...] = normed(jnp.concatenate(patches, axis=1), 1.0).astype(jnp.bfloat16)
 
 
-def attend_kernel(rows, owners, *refs):
-    got_refs, pair_refs, out_refs = refs[:owners], refs[owners:-owners], refs[-owners:]
-    heads = out_refs[0].shape[0] // rows
+def fold(rows, got_refs, pair_refs, use):
+    owners = len(got_refs)
+    heads = pair_refs[0].shape[1] // (2 * rows)
     count = sum(ref.shape[0] for ref in pair_refs) * rows
     group = max(1, min(owners, 2**17 // (rows * count)))
     for head in range(heads):
-        at, past, ask = (slice((i * heads + head) * rows, (i * heads + head + 1) * rows) for i in range(3))
+        at, past, ask = (
+            slice((i * heads + head) * rows, (i * heads + head + 1) * rows) for i in range(3)
+        )
         keys = jnp.concatenate([ref[:, at].reshape(-1, HEAD_DIM) for ref in pair_refs], axis=0)
         values = jnp.concatenate([ref[:, past].reshape(-1, HEAD_DIM) for ref in pair_refs], axis=0)
         for first in range(0, owners, group):
-            part = range(first, min(first + group, owners))
-            queries = jnp.concatenate([got_refs[i][ask] for i in part], axis=0)
+            queries = [ref[ask] for ref in got_refs[first : first + group]]
             scores = lax.dot_general(
-                queries, keys, (((1,), (1,)), ((), ())), preferred_element_type=jnp.float32
+                jnp.concatenate(queries, axis=0),
+                keys,
+                (((1,), (1,)), ((), ())),
+                preferred_element_type=jnp.float32,
             ) * (HEAD_DIM ** (-0.5))
-            peak = jnp.max(scores, axis=-1, keepdims=True)
-            expo = jnp.exp(scores - peak)
-            totals = jnp.sum(expo, axis=-1, keepdims=True)
-            mixed = jnp.dot(expo.astype(jnp.bfloat16), values, preferred_element_type=jnp.float32)
-            mixed = (mixed / totals).astype(jnp.bfloat16)
-            for j, i in enumerate(part):
-                out_refs[i][at] = mixed[j * rows : (j + 1) * rows]
+            use(head, first, len(queries), scores, values)
+
+
+def weigh(scores, peak, values):
+    expo = jnp.exp(scores - peak)
+    mixed = jnp.dot(expo.astype(jnp.bfloat16), values, preferred_element_type=jnp.float32)
+    return jnp.sum(expo, axis=-1, keepdims=True), mixed
+
+
+def early_kernel(rows, owners, *refs):
+    peak_ref, total_ref, accum_ref = refs[-3:]
+
+    def use(head, first, many, scores, values):
+        at = slice(first * rows, (first + many) * rows)
+        peak = jnp.max(scores, axis=-1, keepdims=True)
+        peak_ref[head, at] = peak
+        total_ref[head, at], accum_ref[head, at] = weigh(scores, peak, values)
+
+    fold(rows, refs[:owners], refs[owners:-3], use)
+
+
+def late_kernel(rows, owners, *refs):
+    (peak_ref, total_ref, accum_ref), refs = refs[:3], refs[3:]
+    out_refs = refs[-owners:]
+    places = [steps_in(owners).index(step) for step in steps_back(owners)]
+
+    def use(head, first, many, scores, values):
+        at = slice(first * rows, (first + many) * rows)
+        before = peak_ref[head, at]
+        peak = jnp.maximum(before, jnp.max(scores, axis=-1, keepdims=True))
+        totals, mixed = weigh(scores, peak, values)
+        correction = jnp.exp(before - peak)
+        totals = total_ref[head, at] * correction + totals
+        mixed = (accum_ref[head, at] * correction + mixed) / totals
+        mixed = mixed.astype(jnp.bfloat16)
+        for i in range(many):
+            out_ref = out_refs[places.index(first + i)]
+            out_ref[head * rows : (head + 1) * rows] = mixed[i * rows : (i + 1) * rows]
+
+    fold(rows, refs[:owners], refs[owners:-owners], use)
 
 
 def hint_kernel(layer_ref, patch_ref, weight_ref, gain_ref, out_ref):
@@ -119,7 +160,7 @@
     hint = jnp.dot(patch_ref[...], weight_ref[...], preferred_element_type=jnp.float32)
     hint = hint.astype(jnp.bfloat16).astype(jnp.float32) * gain_ref[pl.ds(layer_ref[0], 1), :]
     me = lax.axis_index("ulysses")
-    for i, step in enumerate(steps_of(owners)):
+    for i, step in enumerate(steps_in(owners)):
         out_ref[partner(me, step)] = hint[i * slab_rows : (i + 1) * slab_rows]
 
 
@@ -128,7 +169,7 @@
     rows, feats = out_ref.shape
     share = feats // owners
     me = lax.axis_index("ulysses")
-    for step, ref in zip(steps_of(owners), back_refs):
+    for step, ref in zip(steps_back(owners), back_refs):
         for head in range(share // HEAD_DIM):
             start = partner(me, step) * share + head * HEAD_DIM
             cols = pl.ds(pl.multiple_of(start, HEAD_DIM), HEAD_DIM)
@@ -164,11 +205,8 @@
     return held
 
 
-def exchange(arrays, axis):
-    return [
-        swap(array, axis, step) if step else array
-        for step, array in zip(steps_of(lax.axis_size(axis)), arrays)
-    ]
+def exchange(arrays, steps, axis):
+    return [swap(array, axis, step) if step else array for step, array in zip(steps, arrays)]
 
 
 def shards(
@@ -212,7 +250,7 @@
     )
     half = lax.axis_size("blk") // 2
     own_moved = swap(sent[owners], "blk", half)
-    got, own_moved = lax.optimization_barrier((exchange(sent[:owners], "ulysses"), own_moved))
+    got, own_moved = lax.optimization_barrier((exchange(sent[:owners], steps_in(owners), "ulysses"), own_moved))
     pairs, rest, patches = call(
         functools.partial(sort_kernel, rows),
         [
@@ -237,22 +275,39 @@
     moved = swap(rest, "blk", half)
     held = gather([own_moved], half // 2, "blk")
     moved, held, hint = lax.optimization_barrier((moved, held, hint))
-    held = held + gather([pairs, moved], half // 2, "blk")
+    moved = gather([moved], half // 2, "blk")
+    early = held + gather([pairs], half // 2, "blk") + moved[: len(moved) // 2]
+    late = moved[len(moved) // 2 :]
+    heads, asks = lines // rows, owners * rows
+    state = call(
+        functools.partial(early_kernel, rows, owners),
+        [
+            shape((heads, asks, 1), jnp.float32),
+            shape((heads, asks, 1), jnp.float32),
+            shape((heads, asks, HEAD_DIM), jnp.float32),
+        ],
+        [VMEM] * (owners + len(early)),
+        *got,
+        *early,
+        flops=2 * asks * sum(array.size for array in early),
+        nbytes=2 * sum(array.size for array in early),
+    )
     mixed = call(
-        functools.partial(attend_kernel, rows, owners),
+        functools.partial(late_kernel, rows, owners),
         [shape((lines, HEAD_DIM))] * owners,
-        [VMEM] * (owners + len(held)),
+        [VMEM] * (3 + owners + len(late)),
+        *state,
         *got,
-        *held,
-        flops=2 * lines * sum(array.size for array in held),
-        nbytes=2 * sum(array.size for array in held),
+        *late,
+        flops=2 * asks * sum(array.size for array in late),
+        nbytes=2 * sum(array.size for array in late),
     )
     return call(
         functools.partial(finish_kernel, owners),
         shape((rows, feats)),
         [VMEM] * (owners + 1),
         hint.reshape(rows, feats),
-        *exchange(mixed, "ulysses"),
+        *exchange(mixed, steps_back(owners), "ulysses"),
     )
 
 

time: 27 us -> 26.3 us (0.974)
  waiting for transfers between devices: 8.15 us -> 6.95 us
  Pallas kernels: 2.85 us -> 3.62 us
    ppermute x11, waiting for transfers between devices: 8.15 us -> 6.95 us  [swap(): lax.ppermute(array, axis, [(i, partner(i, step)) for i in range(size)])]
    pallas_call x5 -> x6, Pallas kernels: 2.85 us -> 3.62 us  [call(): pl.pallas_call(kernel, out_shape=out_shape, in_specs=specs, out_specs=jax...]
  transfers between devices with their start and end apart: 11 -> 11, of which waited for: 6 -> 6; matrix products, arithmetic and copies ran while one was open for 0% -> 0% of each run, Pallas kernels for 1% -> 4%
where the time goes in v10:
time: 26.3 us; the launch traced here: 26.1 us
  starting transfers between devices  13.7 us (52%)
  waiting for transfers between devices  6.95 us (26%)
  Pallas kernels  3.62 us (14%)
  local copies, waits for them, and re-layouts  1.13 us (4%)
  between operations  0.72 us (3%)
    ppermute x11, starting transfers between devices, swap(): lax.ppermute(array, axis, [(i, partner(i, step)) for i in range(size)])  13.7 us
    ppermute x11, waiting for transfers between devices, swap(): lax.ppermute(array, axis, [(i, partner(i, step)) for i in range(size)])  6.95 us
    pallas_call x6, Pallas kernels, call(): pl.pallas_call(kernel, out_shape=out_shape, in_specs=specs, out_specs=jax...  3.62 us
    unnamed x4, local copies, waits for them, and re-layouts  1.13 us
  transfers between devices with their start and end apart: 11, of which 6 were waited for; matrix products, arithmetic and copies ran while one was open for 0% of the time, Pallas kernels for 4%

profile of v10, /device:TPU:0, one launch (start us, length us, event | category | flops | bytes accessed | tf_op | source)
XLA Modules:
  0.0 26.1 jit_solution(7461360554513518436)
XLA Ops:
  0.0 1.2 %shard_map.100 = (bf16[216,128]{1,0:T(8,128)(2,1)S(1)}, bf16[216,128]{1,0:T(8,128)(2,1)S(1)}, bf16[216,128]{1,0:T(8,128)(2,1)S(1)}, bf16[216,128]{1,0:T(8,128)(2,1)S(1)}, bf16[1,128,128]{2,1,0:T(8,128)(2,1)S(1)}) custom-call(s32[1,4]{1,0:T(1,128)} %refs_0_.1, bf16[32,1024]{1,0:T(8,128)(2,1)} %refs_1_.1, bf16[32,1024]{1,0:T(8,128)(2,1)} %refs_2_.1, ...), custom_call_target="tpu_custom_call" | custom-call | tf_op jit(solution)/shard_map/pallas_call | solution.py:186
  1.2 4.1 %collective-permute-start = (bf16[216,128]{1,0:T(8,128)(2,1)S(1)}, bf16[216,128]{1,0:T(8,128)(2,1)S(1)}, u32[]{:S(2)}, u32[]{:S(2)}) collective-permute-start(bf16[216,128]{1,0:T(8,128)(2,1)S(1)} %get-tuple-element.30), channel_id=1, source_target_pairs={{0,2},{1,3},{2,0},{3,1},{4,6},{5,7},{6,4},{7,5},{8,10},{9,11},{10,... | collective-permute-start | bytes 165896 | tf_op jit(solution)/shard_map/ppermute | solution.py:34
  5.3 1.3 %collective-permute-start.1 = (bf16[216,128]{1,0:T(8,128)(2,1)S(1)}, bf16[216,128]{1,0:T(8,128)(2,1)S(1)}, u32[]{:S(2)}, u32[]{:S(2)}) collective-permute-start(bf16[216,128]{1,0:T(8,128)(2,1)S(1)} %get-tuple-element.31), channel_id=1, source_target_pairs={{0,3},{1,2},{2,1},{3,0},{4,7},{5,6},{6,5},{7,4},{8,11},{9,10},{10,... | collective-permute-start | bytes 165896 | tf_op jit(solution)/shard_map/ppermute | solution.py:34
  6.6 0.2 collective-permute-start.2
  6.8 1.5 %collective-permute-start.3 = (bf16[1,128,128]{2,1,0:T(8,128)(2,1)S(1)}, bf16[1,128,128]{2,1,0:T(8,128)(2,1)S(1)}, u32[]{:S(2)}, u32[]{:S(2)}) collective-permute-start(bf16[1,128,128]{2,1,0:T(8,128)(2,1)S(1)} %get-tuple-element.33), channel_id=1, source_target_pairs={{0,8},{4,12},{8,0},{12,4},{1,9},{5,13},{9,1},{13,5},{2,10},{6,14},... | collective-permute-start | bytes 98312 | tf_op jit(solution)/shard_map/ppermute | solution.py:34
  8.3 2.4 %collective-permute-done.3.refs_4_ = bf16[1,128,128]{2,1,0:T(8,128)(2,1)S(1)} collective-permute-done((bf16[1,128,128]{2,1,0:T(8,128)(2,1)S(1)}, bf16[1,128,128]{2,1,0:T(8,128)(2,1)S(1)}, u32[]{:S(2)}, u32[]{:S(2)}) %collective-permute-start.3) | collective-permute-done | bytes 32800 | tf_op jit(solution)/shard_map/ppermute | solution.py:34
  10.8 0.0 collective-permute-done.refs_1_.refs_4_
  10.8 0.6 %collective-permute-done.1.refs_2_.refs_5_ = bf16[216,128]{1,0:T(8,128)(2,1)S(1)} collective-permute-done((bf16[216,128]{1,0:T(8,128)(2,1)S(1)}, bf16[216,128]{1,0:T(8,128)(2,1)S(1)}, u32[]{:S(2)}, u32[]{:S(2)}) %collective-permute-start.1) | collective-permute-done | bytes 55328 | tf_op jit(solution)/shard_map/ppermute | solution.py:34
  11.3 0.0 collective-permute-done.2.refs_3_.refs_6_
  11.4 0.0 copy-start.1
  11.4 0.1 shard_map.101
  11.5 1.6 %collective-permute-start.4 = (bf16[3,128,128]{2,1,0:T(8,128)(2,1)S(1)}, bf16[3,128,128]{2,1,0:T(8,128)(2,1)S(1)}, u32[]{:S(2)}, u32[]{:S(2)}) collective-permute-start(bf16[3,128,128]{2,1,0:T(8,128)(2,1)S(1)} %get-tuple-element.38), channel_id=1, source_target_pairs={{0,8},{4,12},{8,0},{12,4},{1,9},{5,13},{9,1},{13,5},{2,10},{6,14},... | collective-permute-start | bytes 294920 | tf_op jit(solution)/shard_map/ppermute | solution.py:34
  13.0 0.0 collective-permute-start.6
  13.0 0.5 %collective-permute-start.5 = (bf16[1,128,128]{2,1,0:T(8,128)(2,1)S(1)}, bf16[1,128,128]{2,1,0:T(8,128)(2,1)S(1)}, u32[]{:S(2)}, u32[]{:S(2)}) collective-permute-start(bf16[1,128,128]{2,1,0:T(8,128)(2,1)S(1)} %collective-permute-done.3.refs_4_), channel_id=1, source_target_pairs={{0,4},{4,0},{8,12},{12,8},{1,5},{5,1},{9,13},{13,9},{2,6},{6,2},{1... | collective-permute-start | bytes 98312 | tf_op jit(solution)/shard_map/ppermute | solution.py:34
  14.2 0.0 copy-done.1
  14.2 0.0 copy-start
  14.2 1.1 %copy-done = bf16[384,1024]{1,0:T(8,128)(2,1)S(1)} copy-done((bf16[384,1024]{1,0:T(8,128)(2,1)S(1)}, bf16[384,1024]{1,0:T(8,128)(2,1)}, u32[]{:S(2)}) %copy-start) | copy-done | bytes 786456
  15.3 0.3 shard_map.102
  15.6 0.0 collective-permute-done.5.refs_5_
  15.6 0.5 %collective-permute-done.4.refs_8_ = bf16[3,128,128]{2,1,0:T(8,128)(2,1)S(1)} collective-permute-done((bf16[3,128,128]{2,1,0:T(8,128)(2,1)S(1)}, bf16[3,128,128]{2,1,0:T(8,128)(2,1)S(1)}, u32[]{:S(2)}, u32[]{:S(2)}) %collective-permute-start.4) | collective-permute-done | bytes 98336 | tf_op jit(solution)/shard_map/ppermute | solution.py:34
  16.2 0.0 collective-permute-start.7
  16.2 0.0 collective-permute-done.6.refs_7_
  16.2 0.7 %shard_map.103 = (f32[2,128,1]{2,1,0:T(8,128)S(1)}, f32[2,128,1]{2,1,0:T(8,128)S(1)}, f32[2,128,128]{2,1,0:T(8,128)S(1)}) custom-call(bf16[216,128]{1,0:T(8,128)(2,1)S(1)} %get-tuple-element.34.refs_0_.refs_3_, bf16[216,128]{1,0:T(8,128)(2,1)S(1)} %collective-permute-done.refs_1_.refs_4_, bf16[216,128]{1,0:T(8,128)(2,1)S(1)} %collective-permute-done.1.refs_2_.refs_5_, ...), custom_call_target="tpu_custom_call" | custom-call | flops 54525952 | bytes 425984 | tf_op jit(solution)/shard_map/pallas_call | solution.py:186
  16.9 0.6 %collective-permute-done.7.refs_7_ = bf16[3,128,128]{2,1,0:T(8,128)(2,1)S(1)} collective-permute-done((bf16[3,128,128]{2,1,0:T(8,128)(2,1)S(1)}, bf16[3,128,128]{2,1,0:T(8,128)(2,1)S(1)}, u32[]{:S(2)}, u32[]{:S(2)}) %collective-permute-start.7) | collective-permute-done | bytes 98336 | tf_op jit(solution)/shard_map/ppermute | solution.py:34
  17.5 0.8 %shard_map.104 = (bf16[64,128]{1,0:T(8,128)(2,1)S(1)}, bf16[64,128]{1,0:T(8,128)(2,1)S(1)}, bf16[64,128]{1,0:T(8,128)(2,1)S(1)}, bf16[64,128]{1,0:T(8,128)(2,1)S(1)}) custom-call(f32[2,128,1]{2,1,0:T(8,128)S(1)} %get-tuple-element.46.refs_0_, f32[2,128,1]{2,1,0:T(8,128)S(1)} %get-tuple-element.47.refs_1_, f32[2,128,128]{2,1,0:T(8,128)S(1)} %get-tuple-element.48.refs_2_, ...), custom_call_target="tpu_custom_call" | custom-call | flops 12582912 | bytes 98304 | tf_op jit(solution)/shard_map/pallas_call | solution.py:186
  18.2 2.6 %collective-permute-start.8 = (bf16[64,128]{1,0:T(8,128)(2,1)S(1)}, bf16[64,128]{1,0:T(8,128)(2,1)S(1)}, u32[]{:S(2)}, u32[]{:S(2)}) collective-permute-start(bf16[64,128]{1,0:T(8,128)(2,1)S(1)} %get-tuple-element.50), channel_id=1, source_target_pairs={{0,3},{1,2},{2,1},{3,0},{4,7},{5,6},{6,5},{7,4},{8,11},{9,10},{10,... | collective-permute-start | bytes 49160 | tf_op jit(solution)/shard_map/ppermute | solution.py:34
  20.8 0.2 collective-permute-start.9
  21.0 1.7 %collective-permute-start.10 = (bf16[64,128]{1,0:T(8,128)(2,1)S(1)}, bf16[64,128]{1,0:T(8,128)(2,1)S(1)}, u32[]{:S(2)}, u32[]{:S(2)}) collective-permute-start(bf16[64,128]{1,0:T(8,128)(2,1)S(1)} %get-tuple-element.52), channel_id=1, source_target_pairs={{0,1},{1,0},{2,3},{3,2},{4,5},{5,4},{6,7},{7,6},{8,9},{9,8},{10,11... | collective-permute-start | bytes 49160 | tf_op jit(solution)/shard_map/ppermute | solution.py:34
  22.7 1.1 %collective-permute-done.8.refs_1_ = bf16[64,128]{1,0:T(8,128)(2,1)S(1)} collective-permute-done((bf16[64,128]{1,0:T(8,128)(2,1)S(1)}, bf16[64,128]{1,0:T(8,128)(2,1)S(1)}, u32[]{:S(2)}, u32[]{:S(2)}) %collective-permute-start.8) | collective-permute-done | bytes 16416 | tf_op jit(solution)/shard_map/ppermute | solution.py:34
  23.8 1.6 %collective-permute-done.9.refs_2_ = bf16[64,128]{1,0:T(8,128)(2,1)S(1)} collective-permute-done((bf16[64,128]{1,0:T(8,128)(2,1)S(1)}, bf16[64,128]{1,0:T(8,128)(2,1)S(1)}, u32[]{:S(2)}, u32[]{:S(2)}) %collective-permute-start.9) | collective-permute-done | bytes 16416 | tf_op jit(solution)/shard_map/ppermute | solution.py:34
  25.5 0.0 collective-permute-done.10.refs_3_
  25.5 0.7 %shard_map.105 = bf16[32,1024]{1,0:T(8,128)(2,1)} custom-call(f32[32,1024]{1,0:T(8,128)S(1)} %bitcast.3, bf16[64,128]{1,0:T(8,128)(2,1)S(1)} %get-tuple-element.49.refs_0_, bf16[64,128]{1,0:T(8,128)(2,1)S(1)} %collective-permute-done.8.refs_1_, bf16[64,128]{1,0:T(8,128)(2,1)S(1)} %collective-permute-done.9.refs_2_, ...), custom_call_target="tpu_custom_call" | custom-call | tf_op jit(solution)/shard_map/pallas_call | solution.py:186
Async XLA Ops:
  1.2 9.6 %collective-permute-start = (bf16[216,128]{1,0:T(8,128)(2,1)S(1)}, bf16[216,128]{1,0:T(8,128)(2,1)S(1)}, u32[]{:S(2)}, u32[]{:S(2)}) collective-permute-start(bf16[216,128]{1,0:T(8,128)(2,1)S(1)} %get-tuple-element.30), channel_id=1, source_target_pairs={{0,2},{1,3},{2,0},{3,1},{4,6},{5,7},{6,4},{7,5},{8,10},{9,11},{10,... | collective-permute-start | bytes 165896 | tf_op jit(solution)/shard_map/ppermute | solution.py:34
  5.3 6.1 %collective-permute-start.1 = (bf16[216,128]{1,0:T(8,128)(2,1)S(1)}, bf16[216,128]{1,0:T(8,128)(2,1)S(1)}, u32[]{:S(2)}, u32[]{:S(2)}) collective-permute-start(bf16[216,128]{1,0:T(8,128)(2,1)S(1)} %get-tuple-element.31), channel_id=1, source_target_pairs={{0,3},{1,2},{2,1},{3,0},{4,7},{5,6},{6,5},{7,4},{8,11},{9,10},{10,... | collective-permute-start | bytes 165896 | tf_op jit(solution)/shard_map/ppermute | solution.py:34
  6.6 4.7 %collective-permute-start.2 = (bf16[216,128]{1,0:T(8,128)(2,1)S(1)}, bf16[216,128]{1,0:T(8,128)(2,1)S(1)}, u32[]{:S(2)}, u32[]{:S(2)}) collective-permute-start(bf16[216,128]{1,0:T(8,128)(2,1)S(1)} %get-tuple-element.32), channel_id=1, source_target_pairs={{0,1},{1,0},{2,3},{3,2},{4,5},{5,4},{6,7},{7,6},{8,9},{9,8},{10,11... | collective-permute-start | bytes 165896 | tf_op jit(solution)/shard_map/ppermute | solution.py:34
  6.8 3.9 %collective-permute-start.3 = (bf16[1,128,128]{2,1,0:T(8,128)(2,1)S(1)}, bf16[1,128,128]{2,1,0:T(8,128)(2,1)S(1)}, u32[]{:S(2)}, u32[]{:S(2)}) collective-permute-start(bf16[1,128,128]{2,1,0:T(8,128)(2,1)S(1)} %get-tuple-element.33), channel_id=1, source_target_pairs={{0,8},{4,12},{8,0},{12,4},{1,9},{5,13},{9,1},{13,5},{2,10},{6,14},... | collective-permute-start | bytes 98312 | tf_op jit(solution)/shard_map/ppermute | solution.py:34
  11.4 2.8 %copy-start.1 = (f32[8,1024]{1,0:T(8,128)S(1)}, f32[8,1024]{1,0:T(8,128)}, u32[]{:S(2)}) copy-start(f32[8,1024]{1,0:T(8,128)} %gain_ref.1) | copy-start | bytes 98308
  11.5 4.7 %collective-permute-start.4 = (bf16[3,128,128]{2,1,0:T(8,128)(2,1)S(1)}, bf16[3,128,128]{2,1,0:T(8,128)(2,1)S(1)}, u32[]{:S(2)}, u32[]{:S(2)}) collective-permute-start(bf16[3,128,128]{2,1,0:T(8,128)(2,1)S(1)} %get-tuple-element.38), channel_id=1, source_target_pairs={{0,8},{4,12},{8,0},{12,4},{1,9},{5,13},{9,1},{13,5},{2,10},{6,14},... | collective-permute-start | bytes 294920 | tf_op jit(solution)/shard_map/ppermute | solution.py:34
  13.0 3.1 %collective-permute-start.6 = (bf16[4,128,128]{2,1,0:T(8,128)(2,1)S(1)}, bf16[4,128,128]{2,1,0:T(8,128)(2,1)S(1)}, u32[]{:S(2)}, u32[]{:S(2)}) collective-permute-start(bf16[4,128,128]{2,1,0:T(8,128)(2,1)S(1)} %get-tuple-element.44.refs_6_), channel_id=1, source_target_pairs={{0,4},{4,0},{8,12},{12,8},{1,5},{5,1},{9,13},{13,9},{2,6},{6,2},{1... | collective-permute-start | bytes 393224 | tf_op jit(solution)/shard_map/ppermute | solution.py:34
  13.0 2.6 %collective-permute-start.5 = (bf16[1,128,128]{2,1,0:T(8,128)(2,1)S(1)}, bf16[1,128,128]{2,1,0:T(8,128)(2,1)S(1)}, u32[]{:S(2)}, u32[]{:S(2)}) collective-permute-start(bf16[1,128,128]{2,1,0:T(8,128)(2,1)S(1)} %collective-permute-done.3.refs_4_), channel_id=1, source_target_pairs={{0,4},{4,0},{8,12},{12,8},{1,5},{5,1},{9,13},{13,9},{2,6},{6,2},{1... | collective-permute-start | bytes 98312 | tf_op jit(solution)/shard_map/ppermute | solution.py:34
  14.2 1.1 %copy-start = (bf16[384,1024]{1,0:T(8,128)(2,1)S(1)}, bf16[384,1024]{1,0:T(8,128)(2,1)}, u32[]{:S(2)}) copy-start(bf16[384,1024]{1,0:T(8,128)(2,1)} %weight_ref.1) | copy-start | bytes 2359300
  16.2 1.3 %collective-permute-start.7 = (bf16[3,128,128]{2,1,0:T(8,128)(2,1)S(1)}, bf16[3,128,128]{2,1,0:T(8,128)(2,1)S(1)}, u32[]{:S(2)}, u32[]{:S(2)}) collective-permute-start(bf16[3,128,128]{2,1,0:T(8,128)(2,1)S(1)} %collective-permute-done.4.refs_8_), channel_id=1, source_target_pairs={{0,4},{4,0},{8,12},{12,8},{1,5},{5,1},{9,13},{13,9},{2,6},{6,2},{1... | collective-permute-start | bytes 294920 | tf_op jit(solution)/shard_map/ppermute | solution.py:34
  18.2 5.6 %collective-permute-start.8 = (bf16[64,128]{1,0:T(8,128)(2,1)S(1)}, bf16[64,128]{1,0:T(8,128)(2,1)S(1)}, u32[]{:S(2)}, u32[]{:S(2)}) collective-permute-start(bf16[64,128]{1,0:T(8,128)(2,1)S(1)} %get-tuple-element.50), channel_id=1, source_target_pairs={{0,3},{1,2},{2,1},{3,0},{4,7},{5,6},{6,5},{7,4},{8,11},{9,10},{10,... | collective-permute-start | bytes 49160 | tf_op jit(solution)/shard_map/ppermute | solution.py:34
  20.8 4.6 %collective-permute-start.9 = (bf16[64,128]{1,0:T(8,128)(2,1)S(1)}, bf16[64,128]{1,0:T(8,128)(2,1)S(1)}, u32[]{:S(2)}, u32[]{:S(2)}) collective-permute-start(bf16[64,128]{1,0:T(8,128)(2,1)S(1)} %get-tuple-element.51), channel_id=1, source_target_pairs={{0,2},{1,3},{2,0},{3,1},{4,6},{5,7},{6,4},{7,5},{8,10},{9,11},{10,... | collective-permute-start | bytes 49160 | tf_op jit(solution)/shard_map/ppermute | solution.py:34
  21.0 4.5 %collective-permute-start.10 = (bf16[64,128]{1,0:T(8,128)(2,1)S(1)}, bf16[64,128]{1,0:T(8,128)(2,1)S(1)}, u32[]{:S(2)}, u32[]{:S(2)}) collective-permute-start(bf16[64,128]{1,0:T(8,128)(2,1)S(1)} %get-tuple-element.52), channel_id=1, source_target_pairs={{0,1},{1,0},{2,3},{3,2},{4,5},{5,4},{6,7},{7,6},{8,9},{9,8},{10,11... | collective-permute-start | bytes 49160 | tf_op jit(solution)/shard_map/ppermute | solution.py:34

commit v11 on v10

--- a/solution.py
+++ b/solution.py
@@ -44,16 +44,20 @@
     ]
     for copy in copies:
         copy.start()
-    owner_ref, q_ref, k_ref, v_ref, control_ref, qg_ref, kg_ref = held
+    kg_ref, k_ref, qg_ref, q_ref, v_ref, owner_ref, control_ref = held
     rows, feats = q_ref.shape
     share = feats // owners
     slab_rows, width = rows // owners, control_ref.shape[1]
     me = lax.axis_index("ulysses")
-    for copy in copies:
+    copies[0].wait()
+    copies[1].wait()
+    norm_ref[0] = normed(k_ref[...], kg_ref[...]).astype(jnp.bfloat16)
+    copies[2].wait()
+    copies[3].wait()
+    norm_ref[2] = normed(q_ref[...], qg_ref[...]).astype(jnp.bfloat16)
+    for copy in copies[4:]:
         copy.wait()
-    norm_ref[0] = normed(k_ref[...], kg_ref[...]).astype(jnp.bfloat16)
     norm_ref[1] = v_ref[...]
-    norm_ref[2] = normed(q_ref[...], qg_ref[...]).astype(jnp.bfloat16)
     patches = control_ref[...].astype(jnp.float32)
     slabs = [patches[j * slab_rows : (j + 1) * slab_rows] for j in range(owners)]
     for step, out_ref in zip(steps_in(owners), out_refs):
@@ -99,57 +103,79 @@
     heads = pair_refs[0].shape[1] // (2 * rows)
     count = sum(ref.shape[0] for ref in pair_refs) * rows
     group = max(1, min(owners, 2**17 // (rows * count)))
-    for head in range(heads):
-        at, past, ask = (
-            slice((i * heads + head) * rows, (i * heads + head + 1) * rows) for i in range(3)
+    spans = [slice(i * rows, (i + 1) * rows) for i in range(2 * heads)]
+    pieces = [
+        jnp.concatenate([ref[:, span].reshape(-1, HEAD_DIM) for ref in pair_refs], axis=0)
+        for span in spans
+    ]
+    ones = jnp.ones((count, HEAD_DIM), jnp.bfloat16)
+    values = [jnp.concatenate([piece, ones], axis=1) for piece in pieces[heads:]]
+    for first in range(0, owners, group):
+        many = min(group, owners - first)
+        scores = []
+        for head in range(heads):
+            ask = spans[0].stop * (2 * heads + head)
+            queries = [ref[ask : ask + rows] for ref in got_refs[first : first + many]]
+            scores.append(
+                lax.dot_general(
+                    jnp.concatenate(queries, axis=0),
+                    pieces[head],
+                    (((1,), (1,)), ((), ())),
+                    preferred_element_type=jnp.float32,
+                )
+            )
+        scores = jnp.concatenate(scores, axis=0) * (HEAD_DIM ** (-0.5))
+        use(slice(first * rows, (first + many) * rows), scores, values)
+
+
+def weigh(scores, peak, values):
+    probs = jnp.exp(scores - peak).astype(jnp.bfloat16)
+    each = probs.shape[0] // len(values)
+    mixed = [
+        jnp.dot(
+            probs[i * each : (i + 1) * each], value, preferred_element_type=jnp.float32
         )
-        keys = jnp.concatenate([ref[:, at].reshape(-1, HEAD_DIM) for ref in pair_refs], axis=0)
-        values = jnp.concatenate([ref[:, past].reshape(-1, HEAD_DIM) for ref in pair_refs], axis=0)
-        for first in range(0, owners, group):
-            queries = [ref[ask] for ref in got_refs[first : first + group]]
-            scores = lax.dot_general(
-                jnp.concatenate(queries, axis=0),
-                keys,
-                (((1,), (1,)), ((), ())),
-                preferred_element_type=jnp.float32,
-            ) * (HEAD_DIM ** (-0.5))
-            use(head, first, len(queries), scores, values)
-
-
-def weigh(scores, peak, values):
-    expo = jnp.exp(scores - peak)
-    mixed = jnp.dot(expo.astype(jnp.bfloat16), values, preferred_element_type=jnp.float32)
-    return jnp.sum(expo, axis=-1, keepdims=True), mixed
+        for i, value in enumerate(values)
+    ]
+    mixed = jnp.concatenate(mixed, axis=0)
+    return mixed[:, HEAD_DIM:], mixed[:, :HEAD_DIM]
 
 
 def early_kernel(rows, owners, *refs):
-    peak_ref, total_ref, accum_ref = refs[-3:]
-
-    def use(head, first, many, scores, values):
-        at = slice(first * rows, (first + many) * rows)
+    state_refs = refs[-3:]
+
+    def use(at, scores, values):
         peak = jnp.max(scores, axis=-1, keepdims=True)
-        peak_ref[head, at] = peak
-        total_ref[head, at], accum_ref[head, at] = weigh(scores, peak, values)
+        totals, mixed = weigh(scores, peak, values)
+        each = mixed.shape[0] // len(values)
+        for ref, state in zip(state_refs, (jnp.broadcast_to(peak, mixed.shape), totals, mixed)):
+            for head in range(len(values)):
+                ref[head, at] = state[head * each : (head + 1) * each]
 
     fold(rows, refs[:owners], refs[owners:-3], use)
 
 
 def late_kernel(rows, owners, *refs):
-    (peak_ref, total_ref, accum_ref), refs = refs[:3], refs[3:]
+    state_refs, refs = refs[:3], refs[3:]
     out_refs = refs[-owners:]
-    places = [steps_in(owners).index(step) for step in steps_back(owners)]
-
-    def use(head, first, many, scores, values):
-        at = slice(first * rows, (first + many) * rows)
-        before = peak_ref[head, at]
-        peak = jnp.maximum(before, jnp.max(scores, axis=-1, keepdims=True))
-        totals, mixed = weigh(scores, peak, values)
+    places = [steps_back(owners).index(step) for step in steps_in(owners)]
+
+    def use(at, scores, values):
+        heads = range(len(values))
+        before, totals, accum = (
+            jnp.concatenate([ref[head, at] for head in heads], axis=0) for ref in state_refs
+        )
+        most = jnp.max(scores, axis=-1, keepdims=True)
+        peak = jnp.maximum(before, most)
         correction = jnp.exp(before - peak)
-        totals = total_ref[head, at] * correction + totals
-        mixed = (accum_ref[head, at] * correction + mixed) / totals
+        keys = scores.shape[1]
+        new_totals, mixed = weigh(scores, peak[:, : keys if keys < HEAD_DIM else 1], values)
+        mixed = (accum * correction + mixed) / (totals * correction + new_totals)
         mixed = mixed.astype(jnp.bfloat16)
-        for i in range(many):
-            out_ref = out_refs[places.index(first + i)]
+        many = (at.stop - at.start) // rows
+        for i in range(len(values) * many):
+            head, source = divmod(i, many)
+            out_ref = out_refs[places[at.start // rows + source]]
             out_ref[head * rows : (head + 1) * rows] = mixed[i * rows : (i + 1) * rows]
 
     fold(rows, refs[:owners], refs[owners:-owners], use)
@@ -227,13 +253,13 @@
     lines = rows * (feats // owners // HEAD_DIM)
     slab_lines = rows // owners * (width // HEAD_DIM)
     sources = (
+        key_gain.reshape(1, feats),
+        key_proj,
+        query_gain.reshape(1, feats),
+        query_proj,
+        value_proj,
         owner_map,
-        query_proj,
-        key_proj,
-        value_proj,
         control,
-        query_gain.reshape(1, feats),
-        key_gain.reshape(1, feats),
     )
     sources = [pltpu.with_memory_space_constraint(source, pltpu.HBM) for source in sources]
     sent = call(
@@ -241,8 +267,10 @@
         [shape((3 * lines + slab_lines, HEAD_DIM))] * owners + [shape((1, 2 * lines, HEAD_DIM))],
         [HBM] * len(sources),
         *sources,
-        scratch=[pltpu.SMEM(owner_map.shape, owner_map.dtype)]
-        + [pltpu.VMEM(source.shape, source.dtype) for source in sources[1:]]
+        scratch=[
+            (pltpu.SMEM if source.dtype == jnp.int32 else pltpu.VMEM)(source.shape, source.dtype)
+            for source in sources
+        ]
         + [
             pltpu.VMEM((3, rows, feats), jnp.bfloat16),
             pltpu.SemaphoreType.DMA((len(sources),)),
@@ -282,10 +310,9 @@
     state = call(
         functools.partial(early_kernel, rows, owners),
         [
-            shape((heads, asks, 1), jnp.float32),
-            shape((heads, asks, 1), jnp.float32),
             shape((heads, asks, HEAD_DIM), jnp.float32),
-        ],
+        ]
+        * 3,
         [VMEM] * (owners + len(early)),
         *got,
         *early,

time: 26.3 us -> 26 us (0.989)
  Pallas kernels: 3.62 us -> 3.14 us
    pallas_call x6, Pallas kernels: 3.62 us -> 3.14 us  [call(): pl.pallas_call(kernel, out_shape=out_shape, in_specs=specs, out_specs=jax...]
  transfers between devices with their start and end apart: 11 -> 11, of which waited for: 6 -> 6; matrix products, arithmetic and copies ran while one was open for 0% -> 0% of each run, Pallas kernels for 4% -> 3%
where the time goes in v11:
time: 26 us; the launch traced here: 25.8 us
  starting transfers between devices  13.7 us (53%)
  waiting for transfers between devices  7.12 us (27%)
  Pallas kernels  3.14 us (12%)
  local copies, waits for them, and re-layouts  1.13 us (4%)
  between operations  0.72 us (3%)
    ppermute x11, starting transfers between devices, swap(): lax.ppermute(array, axis, [(i, partner(i, step)) for i in range(size)])  13.7 us
    ppermute x11, waiting for transfers between devices, swap(): lax.ppermute(array, axis, [(i, partner(i, step)) for i in range(size)])  7.12 us
    pallas_call x6, Pallas kernels, call(): pl.pallas_call(kernel, out_shape=out_shape, in_specs=specs, out_specs=jax...  3.14 us
    unnamed x4, local copies, waits for them, and re-layouts  1.13 us
  transfers between devices with their start and end apart: 11, of which 6 were waited for; matrix products, arithmetic and copies ran while one was open for 0% of the time, Pallas kernels for 3%

profile of v11, /device:TPU:0, one launch (start us, length us, event | category | flops | bytes accessed | tf_op | source)
XLA Modules:
  0.0 25.8 jit_solution(8102961422892442437)
XLA Ops:
  0.0 1.2 %shard_map.100 = (bf16[216,128]{1,0:T(8,128)(2,1)S(1)}, bf16[216,128]{1,0:T(8,128)(2,1)S(1)}, bf16[216,128]{1,0:T(8,128)(2,1)S(1)}, bf16[216,128]{1,0:T(8,128)(2,1)S(1)}, bf16[1,128,128]{2,1,0:T(8,128)(2,1)S(1)}) custom-call(f32[1,1024]{1,0:T(1,128)} %bitcast.4, bf16[32,1024]{1,0:T(8,128)(2,1)} %refs_1_.1, f32[1,1024]{1,0:T(1,128)} %bitcast.5, ...), custom_call_target="tpu_custom_call" | custom-call | tf_op jit(solution)/shard_map/pallas_call | solution.py:212
  1.2 4.1 %collective-permute-start = (bf16[216,128]{1,0:T(8,128)(2,1)S(1)}, bf16[216,128]{1,0:T(8,128)(2,1)S(1)}, u32[]{:S(2)}, u32[]{:S(2)}) collective-permute-start(bf16[216,128]{1,0:T(8,128)(2,1)S(1)} %get-tuple-element.30), channel_id=1, source_target_pairs={{0,2},{1,3},{2,0},{3,1},{4,6},{5,7},{6,4},{7,5},{8,10},{9,11},{10,... | collective-permute-start | bytes 165896 | tf_op jit(solution)/shard_map/ppermute | solution.py:34
  5.3 1.3 %collective-permute-start.1 = (bf16[216,128]{1,0:T(8,128)(2,1)S(1)}, bf16[216,128]{1,0:T(8,128)(2,1)S(1)}, u32[]{:S(2)}, u32[]{:S(2)}) collective-permute-start(bf16[216,128]{1,0:T(8,128)(2,1)S(1)} %get-tuple-element.31), channel_id=1, source_target_pairs={{0,3},{1,2},{2,1},{3,0},{4,7},{5,6},{6,5},{7,4},{8,11},{9,10},{10,... | collective-permute-start | bytes 165896 | tf_op jit(solution)/shard_map/ppermute | solution.py:34
  6.7 0.2 collective-permute-start.2
  6.9 1.5 %collective-permute-start.3 = (bf16[1,128,128]{2,1,0:T(8,128)(2,1)S(1)}, bf16[1,128,128]{2,1,0:T(8,128)(2,1)S(1)}, u32[]{:S(2)}, u32[]{:S(2)}) collective-permute-start(bf16[1,128,128]{2,1,0:T(8,128)(2,1)S(1)} %get-tuple-element.33), channel_id=1, source_target_pairs={{0,8},{4,12},{8,0},{12,4},{1,9},{5,13},{9,1},{13,5},{2,10},{6,14},... | collective-permute-start | bytes 98312 | tf_op jit(solution)/shard_map/ppermute | solution.py:34
  8.4 2.4 %collective-permute-done.3.refs_4_ = bf16[1,128,128]{2,1,0:T(8,128)(2,1)S(1)} collective-permute-done((bf16[1,128,128]{2,1,0:T(8,128)(2,1)S(1)}, bf16[1,128,128]{2,1,0:T(8,128)(2,1)S(1)}, u32[]{:S(2)}, u32[]{:S(2)}) %collective-permute-start.3) | collective-permute-done | bytes 32800 | tf_op jit(solution)/shard_map/ppermute | solution.py:34
  10.8 0.0 collective-permute-done.refs_1_.refs_4_
  10.8 0.6 %collective-permute-done.1.refs_2_.refs_5_ = bf16[216,128]{1,0:T(8,128)(2,1)S(1)} collective-permute-done((bf16[216,128]{1,0:T(8,128)(2,1)S(1)}, bf16[216,128]{1,0:T(8,128)(2,1)S(1)}, u32[]{:S(2)}, u32[]{:S(2)}) %collective-permute-start.1) | collective-permute-done | bytes 55328 | tf_op jit(solution)/shard_map/ppermute | solution.py:34
  11.4 0.0 collective-permute-done.2.refs_3_.refs_6_
  11.4 0.0 copy-start.1
  11.4 0.1 shard_map.101
  11.5 1.6 %collective-permute-start.4 = (bf16[3,128,128]{2,1,0:T(8,128)(2,1)S(1)}, bf16[3,128,128]{2,1,0:T(8,128)(2,1)S(1)}, u32[]{:S(2)}, u32[]{:S(2)}) collective-permute-start(bf16[3,128,128]{2,1,0:T(8,128)(2,1)S(1)} %get-tuple-element.38), channel_id=1, source_target_pairs={{0,8},{4,12},{8,0},{12,4},{1,9},{5,13},{9,1},{13,5},{2,10},{6,14},... | collective-permute-start | bytes 294920 | tf_op jit(solution)/shard_map/ppermute | solution.py:34
  13.1 0.0 collective-permute-start.6
  13.1 0.5 %collective-permute-start.5 = (bf16[1,128,128]{2,1,0:T(8,128)(2,1)S(1)}, bf16[1,128,128]{2,1,0:T(8,128)(2,1)S(1)}, u32[]{:S(2)}, u32[]{:S(2)}) collective-permute-start(bf16[1,128,128]{2,1,0:T(8,128)(2,1)S(1)} %collective-permute-done.3.refs_4_), channel_id=1, source_target_pairs={{0,4},{4,0},{8,12},{12,8},{1,5},{5,1},{9,13},{13,9},{2,6},{6,2},{1... | collective-permute-start | bytes 98312 | tf_op jit(solution)/shard_map/ppermute | solution.py:34
  14.2 0.0 copy-done.1
  14.3 0.0 copy-start
  14.3 1.1 %copy-done = bf16[384,1024]{1,0:T(8,128)(2,1)S(1)} copy-done((bf16[384,1024]{1,0:T(8,128)(2,1)S(1)}, bf16[384,1024]{1,0:T(8,128)(2,1)}, u32[]{:S(2)}) %copy-start) | copy-done | bytes 786456
  15.4 0.3 shard_map.102
  15.7 0.0 collective-permute-done.5.refs_5_
  15.7 0.5 %collective-permute-done.4.refs_8_ = bf16[3,128,128]{2,1,0:T(8,128)(2,1)S(1)} collective-permute-done((bf16[3,128,128]{2,1,0:T(8,128)(2,1)S(1)}, bf16[3,128,128]{2,1,0:T(8,128)(2,1)S(1)}, u32[]{:S(2)}, u32[]{:S(2)}) %collective-permute-start.4) | collective-permute-done | bytes 98336 | tf_op jit(solution)/shard_map/ppermute | solution.py:34
  16.2 0.0 collective-permute-start.7
  16.2 0.0 collective-permute-done.6.refs_7_
  16.2 0.5 %shard_map.103 = (f32[2,128,128]{2,1,0:T(8,128)S(1)}, f32[2,128,128]{2,1,0:T(8,128)S(1)}, f32[2,128,128]{2,1,0:T(8,128)S(1)}) custom-call(bf16[216,128]{1,0:T(8,128)(2,1)S(1)} %get-tuple-element.34.refs_0_.refs_3_, bf16[216,128]{1,0:T(8,128)(2,1)S(1)} %collective-permute-done.refs_1_.refs_4_, bf16[216,128]{1,0:T(8,128)(2,1)S(1)} %collective-permute-done.1.refs_2_.refs_5_, ...), custom_call_target="tpu_custom_call" | custom-call | flops 54525952 | bytes 425984 | tf_op jit(solution)/shard_map/pallas_call | solution.py:212
  16.7 0.8 %collective-permute-done.7.refs_7_ = bf16[3,128,128]{2,1,0:T(8,128)(2,1)S(1)} collective-permute-done((bf16[3,128,128]{2,1,0:T(8,128)(2,1)S(1)}, bf16[3,128,128]{2,1,0:T(8,128)(2,1)S(1)}, u32[]{:S(2)}, u32[]{:S(2)}) %collective-permute-start.7) | collective-permute-done | bytes 98336 | tf_op jit(solution)/shard_map/ppermute | solution.py:34
  17.5 0.4 %shard_map.104 = (bf16[64,128]{1,0:T(8,128)(2,1)S(1)}, bf16[64,128]{1,0:T(8,128)(2,1)S(1)}, bf16[64,128]{1,0:T(8,128)(2,1)S(1)}, bf16[64,128]{1,0:T(8,128)(2,1)S(1)}) custom-call(f32[2,128,128]{2,1,0:T(8,128)S(1)} %get-tuple-element.46.refs_0_, f32[2,128,128]{2,1,0:T(8,128)S(1)} %get-tuple-element.47.refs_1_, f32[2,128,128]{2,1,0:T(8,128)S(1)} %get-tuple-element.48.refs_2_, ...), custom_call_target="tpu_custom_call" | custom-call | flops 12582912 | bytes 98304 | tf_op jit(solution)/shard_map/pallas_call | solution.py:212
  17.9 2.6 %collective-permute-start.8 = (bf16[64,128]{1,0:T(8,128)(2,1)S(1)}, bf16[64,128]{1,0:T(8,128)(2,1)S(1)}, u32[]{:S(2)}, u32[]{:S(2)}) collective-permute-start(bf16[64,128]{1,0:T(8,128)(2,1)S(1)} %get-tuple-element.50), channel_id=1, source_target_pairs={{0,3},{1,2},{2,1},{3,0},{4,7},{5,6},{6,5},{7,4},{8,11},{9,10},{10,... | collective-permute-start | bytes 49160 | tf_op jit(solution)/shard_map/ppermute | solution.py:34
  20.5 0.2 collective-permute-start.9
  20.7 1.7 %collective-permute-start.10 = (bf16[64,128]{1,0:T(8,128)(2,1)S(1)}, bf16[64,128]{1,0:T(8,128)(2,1)S(1)}, u32[]{:S(2)}, u32[]{:S(2)}) collective-permute-start(bf16[64,128]{1,0:T(8,128)(2,1)S(1)} %get-tuple-element.52), channel_id=1, source_target_pairs={{0,1},{1,0},{2,3},{3,2},{4,5},{5,4},{6,7},{7,6},{8,9},{9,8},{10,11... | collective-permute-start | bytes 49160 | tf_op jit(solution)/shard_map/ppermute | solution.py:34
  22.4 1.1 %collective-permute-done.8.refs_1_ = bf16[64,128]{1,0:T(8,128)(2,1)S(1)} collective-permute-done((bf16[64,128]{1,0:T(8,128)(2,1)S(1)}, bf16[64,128]{1,0:T(8,128)(2,1)S(1)}, u32[]{:S(2)}, u32[]{:S(2)}) %collective-permute-start.8) | collective-permute-done | bytes 16416 | tf_op jit(solution)/shard_map/ppermute | solution.py:34
  23.5 1.6 %collective-permute-done.9.refs_2_ = bf16[64,128]{1,0:T(8,128)(2,1)S(1)} collective-permute-done((bf16[64,128]{1,0:T(8,128)(2,1)S(1)}, bf16[64,128]{1,0:T(8,128)(2,1)S(1)}, u32[]{:S(2)}, u32[]{:S(2)}) %collective-permute-start.9) | collective-permute-done | bytes 16416 | tf_op jit(solution)/shard_map/ppermute | solution.py:34
  25.1 0.0 collective-permute-done.10.refs_3_
  25.1 0.7 %shard_map.105 = bf16[32,1024]{1,0:T(8,128)(2,1)} custom-call(f32[32,1024]{1,0:T(8,128)S(1)} %bitcast.3, bf16[64,128]{1,0:T(8,128)(2,1)S(1)} %get-tuple-element.49.refs_0_, bf16[64,128]{1,0:T(8,128)(2,1)S(1)} %collective-permute-done.8.refs_1_, bf16[64,128]{1,0:T(8,128)(2,1)S(1)} %collective-permute-done.9.refs_2_, ...), custom_call_target="tpu_custom_call" | custom-call | tf_op jit(solution)/shard_map/pallas_call | solution.py:212
Async XLA Ops:
  1.2 9.6 %collective-permute-start = (bf16[216,128]{1,0:T(8,128)(2,1)S(1)}, bf16[216,128]{1,0:T(8,128)(2,1)S(1)}, u32[]{:S(2)}, u32[]{:S(2)}) collective-permute-start(bf16[216,128]{1,0:T(8,128)(2,1)S(1)} %get-tuple-element.30), channel_id=1, source_target_pairs={{0,2},{1,3},{2,0},{3,1},{4,6},{5,7},{6,4},{7,5},{8,10},{9,11},{10,... | collective-permute-start | bytes 165896 | tf_op jit(solution)/shard_map/ppermute | solution.py:34
  5.3 6.1 %collective-permute-start.1 = (bf16[216,128]{1,0:T(8,128)(2,1)S(1)}, bf16[216,128]{1,0:T(8,128)(2,1)S(1)}, u32[]{:S(2)}, u32[]{:S(2)}) collective-permute-start(bf16[216,128]{1,0:T(8,128)(2,1)S(1)} %get-tuple-element.31), channel_id=1, source_target_pairs={{0,3},{1,2},{2,1},{3,0},{4,7},{5,6},{6,5},{7,4},{8,11},{9,10},{10,... | collective-permute-start | bytes 165896 | tf_op jit(solution)/shard_map/ppermute | solution.py:34
  6.7 4.7 %collective-permute-start.2 = (bf16[216,128]{1,0:T(8,128)(2,1)S(1)}, bf16[216,128]{1,0:T(8,128)(2,1)S(1)}, u32[]{:S(2)}, u32[]{:S(2)}) collective-permute-start(bf16[216,128]{1,0:T(8,128)(2,1)S(1)} %get-tuple-element.32), channel_id=1, source_target_pairs={{0,1},{1,0},{2,3},{3,2},{4,5},{5,4},{6,7},{7,6},{8,9},{9,8},{10,11... | collective-permute-start | bytes 165896 | tf_op jit(solution)/shard_map/ppermute | solution.py:34
  6.9 3.9 %collective-permute-start.3 = (bf16[1,128,128]{2,1,0:T(8,128)(2,1)S(1)}, bf16[1,128,128]{2,1,0:T(8,128)(2,1)S(1)}, u32[]{:S(2)}, u32[]{:S(2)}) collective-permute-start(bf16[1,128,128]{2,1,0:T(8,128)(2,1)S(1)} %get-tuple-element.33), channel_id=1, source_target_pairs={{0,8},{4,12},{8,0},{12,4},{1,9},{5,13},{9,1},{13,5},{2,10},{6,14},... | collective-permute-start | bytes 98312 | tf_op jit(solution)/shard_map/ppermute | solution.py:34
  11.4 2.8 %copy-start.1 = (f32[8,1024]{1,0:T(8,128)S(1)}, f32[8,1024]{1,0:T(8,128)}, u32[]{:S(2)}) copy-start(f32[8,1024]{1,0:T(8,128)} %gain_ref.1) | copy-start | bytes 98308
  11.5 4.7 %collective-permute-start.4 = (bf16[3,128,128]{2,1,0:T(8,128)(2,1)S(1)}, bf16[3,128,128]{2,1,0:T(8,128)(2,1)S(1)}, u32[]{:S(2)}, u32[]{:S(2)}) collective-permute-start(bf16[3,128,128]{2,1,0:T(8,128)(2,1)S(1)} %get-tuple-element.38), channel_id=1, source_target_pairs={{0,8},{4,12},{8,0},{12,4},{1,9},{5,13},{9,1},{13,5},{2,10},{6,14},... | collective-permute-start | bytes 294920 | tf_op jit(solution)/shard_map/ppermute | solution.py:34
  13.1 3.1 %collective-permute-start.6 = (bf16[4,128,128]{2,1,0:T(8,128)(2,1)S(1)}, bf16[4,128,128]{2,1,0:T(8,128)(2,1)S(1)}, u32[]{:S(2)}, u32[]{:S(2)}) collective-permute-start(bf16[4,128,128]{2,1,0:T(8,128)(2,1)S(1)} %get-tuple-element.44.refs_6_), channel_id=1, source_target_pairs={{0,4},{4,0},{8,12},{12,8},{1,5},{5,1},{9,13},{13,9},{2,6},{6,2},{1... | collective-permute-start | bytes 393224 | tf_op jit(solution)/shard_map/ppermute | solution.py:34
  13.1 2.6 %collective-permute-start.5 = (bf16[1,128,128]{2,1,0:T(8,128)(2,1)S(1)}, bf16[1,128,128]{2,1,0:T(8,128)(2,1)S(1)}, u32[]{:S(2)}, u32[]{:S(2)}) collective-permute-start(bf16[1,128,128]{2,1,0:T(8,128)(2,1)S(1)} %collective-permute-done.3.refs_4_), channel_id=1, source_target_pairs={{0,4},{4,0},{8,12},{12,8},{1,5},{5,1},{9,13},{13,9},{2,6},{6,2},{1... | collective-permute-start | bytes 98312 | tf_op jit(solution)/shard_map/ppermute | solution.py:34
  14.3 1.1 %copy-start = (bf16[384,1024]{1,0:T(8,128)(2,1)S(1)}, bf16[384,1024]{1,0:T(8,128)(2,1)}, u32[]{:S(2)}) copy-start(bf16[384,1024]{1,0:T(8,128)(2,1)} %weight_ref.1) | copy-start | bytes 2359300
  16.2 1.3 %collective-permute-start.7 = (bf16[3,128,128]{2,1,0:T(8,128)(2,1)S(1)}, bf16[3,128,128]{2,1,0:T(8,128)(2,1)S(1)}, u32[]{:S(2)}, u32[]{:S(2)}) collective-permute-start(bf16[3,128,128]{2,1,0:T(8,128)(2,1)S(1)} %collective-permute-done.4.refs_8_), channel_id=1, source_target_pairs={{0,4},{4,0},{8,12},{12,8},{1,5},{5,1},{9,13},{13,9},{2,6},{6,2},{1... | collective-permute-start | bytes 294920 | tf_op jit(solution)/shard_map/ppermute | solution.py:34
  17.9 5.6 %collective-permute-start.8 = (bf16[64,128]{1,0:T(8,128)(2,1)S(1)}, bf16[64,128]{1,0:T(8,128)(2,1)S(1)}, u32[]{:S(2)}, u32[]{:S(2)}) collective-permute-start(bf16[64,128]{1,0:T(8,128)(2,1)S(1)} %get-tuple-element.50), channel_id=1, source_target_pairs={{0,3},{1,2},{2,1},{3,0},{4,7},{5,6},{6,5},{7,4},{8,11},{9,10},{10,... | collective-permute-start | bytes 49160 | tf_op jit(solution)/shard_map/ppermute | solution.py:34
  20.5 4.6 %collective-permute-start.9 = (bf16[64,128]{1,0:T(8,128)(2,1)S(1)}, bf16[64,128]{1,0:T(8,128)(2,1)S(1)}, u32[]{:S(2)}, u32[]{:S(2)}) collective-permute-start(bf16[64,128]{1,0:T(8,128)(2,1)S(1)} %get-tuple-element.51), channel_id=1, source_target_pairs={{0,2},{1,3},{2,0},{3,1},{4,6},{5,7},{6,4},{7,5},{8,10},{9,11},{10,... | collective-permute-start | bytes 49160 | tf_op jit(solution)/shard_map/ppermute | solution.py:34
  20.7 4.5 %collective-permute-start.10 = (bf16[64,128]{1,0:T(8,128)(2,1)S(1)}, bf16[64,128]{1,0:T(8,128)(2,1)S(1)}, u32[]{:S(2)}, u32[]{:S(2)}) collective-permute-start(bf16[64,128]{1,0:T(8,128)(2,1)S(1)} %get-tuple-element.52), channel_id=1, source_target_pairs={{0,1},{1,0},{2,3},{3,2},{4,5},{5,4},{6,7},{7,6},{8,9},{9,8},{10,11... | collective-permute-start | bytes 49160 | tf_op jit(solution)/shard_map/ppermute | solution.py:34

commit v12 on v11

--- a/solution.py
+++ b/solution.py
@@ -98,16 +98,18 @@
     patch_ref[...] = normed(jnp.concatenate(patches, axis=1), 1.0).astype(jnp.bfloat16)
 
 
-def fold(rows, got_refs, pair_refs, use):
+def fold(rows, got_refs, pair_refs, sides, use):
     owners = len(got_refs)
     heads = pair_refs[0].shape[1] // (2 * rows)
-    count = sum(ref.shape[0] for ref in pair_refs) * rows
+    whole, odd, even = pair_refs[: -2 * sides], pair_refs[-2 * sides : -sides], pair_refs[-sides:]
+    count = sum(ref.shape[0] for ref in (*whole, *odd)) * rows
     group = max(1, min(owners, 2**17 // (rows * count)))
     spans = [slice(i * rows, (i + 1) * rows) for i in range(2 * heads)]
-    pieces = [
-        jnp.concatenate([ref[:, span].reshape(-1, HEAD_DIM) for ref in pair_refs], axis=0)
-        for span in spans
-    ]
+    pieces = []
+    for span in spans:
+        parts = [ref[:, span] for ref in whole]
+        parts = parts + [one[:, span] + other[:, span] for one, other in zip(odd, even)]
+        pieces.append(jnp.concatenate([part.reshape(-1, HEAD_DIM) for part in parts], axis=0))
     ones = jnp.ones((count, HEAD_DIM), jnp.bfloat16)
     values = [jnp.concatenate([piece, ones], axis=1) for piece in pieces[heads:]]
     for first in range(0, owners, group):
@@ -141,7 +143,7 @@
     return mixed[:, HEAD_DIM:], mixed[:, :HEAD_DIM]
 
 
-def early_kernel(rows, owners, *refs):
+def early_kernel(rows, owners, sides, *refs):
     state_refs = refs[-3:]
 
     def use(at, scores, values):
@@ -152,10 +154,10 @@
             for head in range(len(values)):
                 ref[head, at] = state[head * each : (head + 1) * each]
 
-    fold(rows, refs[:owners], refs[owners:-3], use)
-
-
-def late_kernel(rows, owners, *refs):
+    fold(rows, refs[:owners], refs[owners:-3], sides, use)
+
+
+def late_kernel(rows, owners, sides, *refs):
     state_refs, refs = refs[:3], refs[3:]
     out_refs = refs[-owners:]
     places = [steps_back(owners).index(step) for step in steps_in(owners)]
@@ -178,7 +180,7 @@
             out_ref = out_refs[places[at.start // rows + source]]
             out_ref[head * rows : (head + 1) * rows] = mixed[i * rows : (i + 1) * rows]
 
-    fold(rows, refs[:owners], refs[owners:-owners], use)
+    fold(rows, refs[:owners], refs[owners:-owners], sides, use)
 
 
 def hint_kernel(layer_ref, patch_ref, weight_ref, gain_ref, out_ref):
@@ -229,6 +231,19 @@
         held = held + [swap(array, axis, step) for array in held]
         step = step // 2
     return held
+
+
+def swap_side(array, axis, step, side):
+    size = lax.axis_size(axis)
+    return lax.ppermute(array, axis, [(i, partner(i, step)) for i in range(side, size, 2)])
+
+
+def gather_side(array, axis, side):
+    held, step = [array], lax.axis_size(axis) // 2
+    while step > 1:
+        held = held + [swap_side(array, axis, step, side) for array in held]
+        step = step // 2
+    return held[1:]
 
 
 def exchange(arrays, steps, axis):
@@ -300,15 +315,16 @@
         flops=2 * rows * width * feats,
         nbytes=2 * width * feats,
     )
-    moved = swap(rest, "blk", half)
     held = gather([own_moved], half // 2, "blk")
-    moved, held, hint = lax.optimization_barrier((moved, held, hint))
-    moved = gather([moved], half // 2, "blk")
-    early = held + gather([pairs], half // 2, "blk") + moved[: len(moved) // 2]
-    late = moved[len(moved) // 2 :]
+    odd, even = (gather_side(rest, "blk", side) for side in (1, 0))
+    odd_sent = [swap_side(array, "blk", 1, 1) for array in odd]
+    even, odd_sent, held, hint = lax.optimization_barrier((even, odd_sent, held, hint))
+    even_sent = [swap_side(array, "blk", 1, 0) for array in even]
+    early = held + gather([pairs], half // 2, "blk") + odd + even
+    late = odd_sent + even_sent
     heads, asks = lines // rows, owners * rows
     state = call(
-        functools.partial(early_kernel, rows, owners),
+        functools.partial(early_kernel, rows, owners, len(odd)),
         [
             shape((heads, asks, HEAD_DIM), jnp.float32),
         ]
@@ -320,7 +336,7 @@
         nbytes=2 * sum(array.size for array in early),
     )
     mixed = call(
-        functools.partial(late_kernel, rows, owners),
+        functools.partial(late_kernel, rows, owners, len(late) // 2),
         [shape((lines, HEAD_DIM))] * owners,
         [VMEM] * (3 + owners + len(late)),
         *state,

time: 26 us -> 32.2 us (1.24)
  starting transfers between devices: 13.7 us -> 20.6 us
  waiting for transfers between devices: 7.12 us -> 6.2 us
    ppermute x0 -> x4, starting transfers between devices: none -> 7.7 us  [swap_side(): lax.ppermute(array, axis, [(i, partner(i, step)) for i in range(side, siz...]
    ppermute x11 -> x9, waiting for transfers between devices: 7.12 us -> 5.81 us  [swap(): lax.ppermute(array, axis, [(i, partner(i, step)) for i in range(size)])]
    ppermute x11 -> x9, starting transfers between devices: 13.7 us -> 12.9 us  [swap(): lax.ppermute(array, axis, [(i, partner(i, step)) for i in range(size)])]
    ppermute x0 -> x4, waiting for transfers between devices: none -> 0.39 us  [swap_side(): lax.ppermute(array, axis, [(i, partner(i, step)) for i in range(side, siz...]
  transfers between devices with their start and end apart: 11 -> 13, of which waited for: 6 -> 5; matrix products, arithmetic and copies ran while one was open for 0% -> 0% of each run, Pallas kernels for 3% -> 2%
where the time goes in v12:
time: 32.2 us; the launch traced here: 31.9 us
  starting transfers between devices  20.6 us (64%)
  waiting for transfers between devices  6.2 us (19%)
  Pallas kernels  3.15 us (10%)
  local copies, waits for them, and re-layouts  1.13 us (4%)
  between operations  0.78 us (2%)
    ppermute x9, starting transfers between devices, swap(): lax.ppermute(array, axis, [(i, partner(i, step)) for i in range(size)])  12.9 us
    ppermute x4, starting transfers between devices, swap_side(): lax.ppermute(array, axis, [(i, partner(i, step)) for i in range(side, siz...  7.7 us
    ppermute x9, waiting for transfers between devices, swap(): lax.ppermute(array, axis, [(i, partner(i, step)) for i in range(size)])  5.81 us
    pallas_call x6, Pallas kernels, call(): pl.pallas_call(kernel, out_shape=out_shape, in_specs=specs, out_specs=jax...  3.15 us
    unnamed x4, local copies, waits for them, and re-layouts  1.13 us
  transfers between devices with their start and end apart: 13, of which 5 were waited for; matrix products, arithmetic and copies ran while one was open for 0% of the time, Pallas kernels for 2%

profile of v12, /device:TPU:0, one launch (start us, length us, event | category | flops | bytes accessed | tf_op | source)
XLA Modules:
  0.0 31.9 jit_solution(6865474975333424230)
XLA Ops:
  0.0 1.2 %shard_map.100 = (bf16[216,128]{1,0:T(8,128)(2,1)S(1)}, bf16[216,128]{1,0:T(8,128)(2,1)S(1)}, bf16[216,128]{1,0:T(8,128)(2,1)S(1)}, bf16[216,128]{1,0:T(8,128)(2,1)S(1)}, bf16[1,128,128]{2,1,0:T(8,128)(2,1)S(1)}) custom-call(f32[1,1024]{1,0:T(1,128)} %bitcast.4, bf16[32,1024]{1,0:T(8,128)(2,1)} %refs_1_.1, f32[1,1024]{1,0:T(1,128)} %bitcast.5, ...), custom_call_target="tpu_custom_call" | custom-call | tf_op jit(solution)/shard_map/pallas_call | solution.py:214
  1.2 4.1 %collective-permute-start = (bf16[216,128]{1,0:T(8,128)(2,1)S(1)}, bf16[216,128]{1,0:T(8,128)(2,1)S(1)}, u32[]{:S(2)}, u32[]{:S(2)}) collective-permute-start(bf16[216,128]{1,0:T(8,128)(2,1)S(1)} %get-tuple-element.31), channel_id=1, source_target_pairs={{0,2},{1,3},{2,0},{3,1},{4,6},{5,7},{6,4},{7,5},{8,10},{9,11},{10,... | collective-permute-start | bytes 165896 | tf_op jit(solution)/shard_map/ppermute | solution.py:34
  5.3 1.3 %collective-permute-start.1 = (bf16[216,128]{1,0:T(8,128)(2,1)S(1)}, bf16[216,128]{1,0:T(8,128)(2,1)S(1)}, u32[]{:S(2)}, u32[]{:S(2)}) collective-permute-start(bf16[216,128]{1,0:T(8,128)(2,1)S(1)} %get-tuple-element.32), channel_id=1, source_target_pairs={{0,3},{1,2},{2,1},{3,0},{4,7},{5,6},{6,5},{7,4},{8,11},{9,10},{10,... | collective-permute-start | bytes 165896 | tf_op jit(solution)/shard_map/ppermute | solution.py:34
  6.7 0.2 collective-permute-start.2
  6.9 1.5 %collective-permute-start.3 = (bf16[1,128,128]{2,1,0:T(8,128)(2,1)S(1)}, bf16[1,128,128]{2,1,0:T(8,128)(2,1)S(1)}, u32[]{:S(2)}, u32[]{:S(2)}) collective-permute-start(bf16[1,128,128]{2,1,0:T(8,128)(2,1)S(1)} %get-tuple-element.34), channel_id=1, source_target_pairs={{0,8},{4,12},{8,0},{12,4},{1,9},{5,13},{9,1},{13,5},{2,10},{6,14},... | collective-permute-start | bytes 98312 | tf_op jit(solution)/shard_map/ppermute | solution.py:34
  8.4 2.4 %collective-permute-done.3.refs_4_ = bf16[1,128,128]{2,1,0:T(8,128)(2,1)S(1)} collective-permute-done((bf16[1,128,128]{2,1,0:T(8,128)(2,1)S(1)}, bf16[1,128,128]{2,1,0:T(8,128)(2,1)S(1)}, u32[]{:S(2)}, u32[]{:S(2)}) %collective-permute-start.3) | collective-permute-done | bytes 32800 | tf_op jit(solution)/shard_map/ppermute | solution.py:34
  10.8 0.0 collective-permute-done.refs_1_.refs_4_
  10.8 0.6 %collective-permute-done.1.refs_2_.refs_5_ = bf16[216,128]{1,0:T(8,128)(2,1)S(1)} collective-permute-done((bf16[216,128]{1,0:T(8,128)(2,1)S(1)}, bf16[216,128]{1,0:T(8,128)(2,1)S(1)}, u32[]{:S(2)}, u32[]{:S(2)}) %collective-permute-start.1) | collective-permute-done | bytes 55328 | tf_op jit(solution)/shard_map/ppermute | solution.py:34
  11.4 0.0 collective-permute-done.2.refs_3_.refs_6_
  11.4 0.0 copy-start.1
  11.4 0.1 shard_map.101
  11.5 0.7 %collective-permute-start.5 = (bf16[3,128,128]{2,1,0:T(8,128)(2,1)S(1)}, bf16[3,128,128]{2,1,0:T(8,128)(2,1)S(1)}, u32[]{:S(2)}, u32[]{:S(2)}) collective-permute-start(bf16[3,128,128]{2,1,0:T(8,128)(2,1)S(1)} %get-tuple-element.39), channel_id=1, source_target_pairs={{4,12},{12,4},{5,13},{13,5},{6,14},{14,6},{7,15},{15,7},{20,28},{2... | collective-permute-start | bytes 294920 | tf_op jit(solution)/shard_map/ppermute | solution.py:238
  12.2 3.4 %collective-permute-start.4 = (bf16[3,128,128]{2,1,0:T(8,128)(2,1)S(1)}, bf16[3,128,128]{2,1,0:T(8,128)(2,1)S(1)}, u32[]{:S(2)}, u32[]{:S(2)}) collective-permute-start(bf16[3,128,128]{2,1,0:T(8,128)(2,1)S(1)} %get-tuple-element.39), channel_id=1, source_target_pairs={{0,8},{8,0},{1,9},{9,1},{2,10},{10,2},{3,11},{11,3},{16,24},{24,16... | collective-permute-start | bytes 294920 | tf_op jit(solution)/shard_map/ppermute | solution.py:238
  15.6 0.0 collective-permute-done.5.refs_8_
  15.6 1.3 %collective-permute-start.6 = (bf16[3,128,128]{2,1,0:T(8,128)(2,1)S(1)}, bf16[3,128,128]{2,1,0:T(8,128)(2,1)S(1)}, u32[]{:S(2)}, u32[]{:S(2)}) collective-permute-start(bf16[3,128,128]{2,1,0:T(8,128)(2,1)S(1)} %collective-permute-done.5.refs_8_), channel_id=1, source_target_pairs={{4,0},{12,8},{5,1},{13,9},{6,2},{14,10},{7,3},{15,11},{20,16},{28,... | collective-permute-start | bytes 294920 | tf_op jit(solution)/shard_map/ppermute | solution.py:238
  16.9 1.2 %collective-permute-start.8 = (bf16[4,128,128]{2,1,0:T(8,128)(2,1)S(1)}, bf16[4,128,128]{2,1,0:T(8,128)(2,1)S(1)}, u32[]{:S(2)}, u32[]{:S(2)}) collective-permute-start(bf16[4,128,128]{2,1,0:T(8,128)(2,1)S(1)} %get-tuple-element.45.refs_6_), channel_id=1, source_target_pairs={{0,4},{4,0},{8,12},{12,8},{1,5},{5,1},{9,13},{13,9},{2,6},{6,2},{1... | collective-permute-start | bytes 393224 | tf_op jit(solution)/shard_map/ppermute | solution.py:34
  18.1 0.1 collective-permute-start.7
  18.8 0.0 copy-done.1
  18.9 0.0 copy-start
  18.9 1.1 %copy-done = bf16[384,1024]{1,0:T(8,128)(2,1)S(1)} copy-done((bf16[384,1024]{1,0:T(8,128)(2,1)S(1)}, bf16[384,1024]{1,0:T(8,128)(2,1)}, u32[]{:S(2)}) %copy-start) | copy-done | bytes 786456
  20.0 0.3 shard_map.102
  20.3 0.0 collective-permute-done.7.refs_5_
  20.3 0.0 collective-permute-done.4.refs_9_
  20.3 0.0 collective-permute-done.6.refs_7_
  20.3 2.3 %collective-permute-start.9 = (bf16[3,128,128]{2,1,0:T(8,128)(2,1)S(1)}, bf16[3,128,128]{2,1,0:T(8,128)(2,1)S(1)}, u32[]{:S(2)}, u32[]{:S(2)}) collective-permute-start(bf16[3,128,128]{2,1,0:T(8,128)(2,1)S(1)} %collective-permute-done.4.refs_9_), channel_id=1, source_target_pairs={{0,4},{8,12},{1,5},{9,13},{2,6},{10,14},{3,7},{11,15},{16,20},{24,... | collective-permute-start | bytes 294920 | tf_op jit(solution)/shard_map/ppermute | solution.py:238
  22.6 0.0 collective-permute-done.8.refs_7_
  22.6 0.5 %shard_map.103 = (f32[2,128,128]{2,1,0:T(8,128)S(1)}, f32[2,128,128]{2,1,0:T(8,128)S(1)}, f32[2,128,128]{2,1,0:T(8,128)S(1)}) custom-call(bf16[216,128]{1,0:T(8,128)(2,1)S(1)} %get-tuple-element.35.refs_0_.refs_3_, bf16[216,128]{1,0:T(8,128)(2,1)S(1)} %collective-permute-done.refs_1_.refs_4_, bf16[216,128]{1,0:T(8,128)(2,1)S(1)} %collective-permute-done.1.refs_2_.refs_5_, ...), custom_call_target="tpu_custom_call" | custom-call | flops 67108864 | bytes 524288 | tf_op jit(solution)/shard_map/pallas_call | solution.py:214
  23.2 0.4 %collective-permute-done.9.refs_8_ = bf16[3,128,128]{2,1,0:T(8,128)(2,1)S(1)} collective-permute-done((bf16[3,128,128]{2,1,0:T(8,128)(2,1)S(1)}, bf16[3,128,128]{2,1,0:T(8,128)(2,1)S(1)}, u32[]{:S(2)}, u32[]{:S(2)}) %collective-permute-start.9) | collective-permute-done | bytes 98336 | tf_op jit(solution)/shard_map/ppermute | solution.py:238
  23.6 0.4 %shard_map.104 = (bf16[64,128]{1,0:T(8,128)(2,1)S(1)}, bf16[64,128]{1,0:T(8,128)(2,1)S(1)}, bf16[64,128]{1,0:T(8,128)(2,1)S(1)}, bf16[64,128]{1,0:T(8,128)(2,1)S(1)}) custom-call(f32[2,128,128]{2,1,0:T(8,128)S(1)} %get-tuple-element.47.refs_0_, f32[2,128,128]{2,1,0:T(8,128)S(1)} %get-tuple-element.48.refs_1_, f32[2,128,128]{2,1,0:T(8,128)S(1)} %get-tuple-element.49.refs_2_, ...), custom_call_target="tpu_custom_call" | custom-call | flops 25165824 | bytes 196608 | tf_op jit(solution)/shard_map/pallas_call | solution.py:214
  24.0 2.6 %collective-permute-start.10 = (bf16[64,128]{1,0:T(8,128)(2,1)S(1)}, bf16[64,128]{1,0:T(8,128)(2,1)S(1)}, u32[]{:S(2)}, u32[]{:S(2)}) collective-permute-start(bf16[64,128]{1,0:T(8,128)(2,1)S(1)} %get-tuple-element.52), channel_id=1, source_target_pairs={{0,3},{1,2},{2,1},{3,0},{4,7},{5,6},{6,5},{7,4},{8,11},{9,10},{10,... | collective-permute-start | bytes 49160 | tf_op jit(solution)/shard_map/ppermute | solution.py:34
  26.6 0.2 collective-permute-start.11
  26.7 1.7 %collective-permute-start.12 = (bf16[64,128]{1,0:T(8,128)(2,1)S(1)}, bf16[64,128]{1,0:T(8,128)(2,1)S(1)}, u32[]{:S(2)}, u32[]{:S(2)}) collective-permute-start(bf16[64,128]{1,0:T(8,128)(2,1)S(1)} %get-tuple-element.54), channel_id=1, source_target_pairs={{0,1},{1,0},{2,3},{3,2},{4,5},{5,4},{6,7},{7,6},{8,9},{9,8},{10,11... | collective-permute-start | bytes 49160 | tf_op jit(solution)/shard_map/ppermute | solution.py:34
  28.4 1.1 %collective-permute-done.10.refs_1_ = bf16[64,128]{1,0:T(8,128)(2,1)S(1)} collective-permute-done((bf16[64,128]{1,0:T(8,128)(2,1)S(1)}, bf16[64,128]{1,0:T(8,128)(2,1)S(1)}, u32[]{:S(2)}, u32[]{:S(2)}) %collective-permute-start.10) | collective-permute-done | bytes 16416 | tf_op jit(solution)/shard_map/ppermute | solution.py:34
  29.6 1.6 %collective-permute-done.11.refs_2_ = bf16[64,128]{1,0:T(8,128)(2,1)S(1)} collective-permute-done((bf16[64,128]{1,0:T(8,128)(2,1)S(1)}, bf16[64,128]{1,0:T(8,128)(2,1)S(1)}, u32[]{:S(2)}, u32[]{:S(2)}) %collective-permute-start.11) | collective-permute-done | bytes 16416 | tf_op jit(solution)/shard_map/ppermute | solution.py:34
  31.2 0.0 collective-permute-done.12.refs_3_
  31.2 0.7 %shard_map.105 = bf16[32,1024]{1,0:T(8,128)(2,1)} custom-call(f32[32,1024]{1,0:T(8,128)S(1)} %bitcast.3, bf16[64,128]{1,0:T(8,128)(2,1)S(1)} %get-tuple-element.51.refs_0_, bf16[64,128]{1,0:T(8,128)(2,1)S(1)} %collective-permute-done.10.refs_1_, bf16[64,128]{1,0:T(8,128)(2,1)S(1)} %collective-permute-done.11.refs_2_, ...), custom_call_target="tpu_custom_call" | custom-call | tf_op jit(solution)/shard_map/pallas_call | solution.py:214
Async XLA Ops:
  1.2 9.6 %collective-permute-start = (bf16[216,128]{1,0:T(8,128)(2,1)S(1)}, bf16[216,128]{1,0:T(8,128)(2,1)S(1)}, u32[]{:S(2)}, u32[]{:S(2)}) collective-permute-start(bf16[216,128]{1,0:T(8,128)(2,1)S(1)} %get-tuple-element.31), channel_id=1, source_target_pairs={{0,2},{1,3},{2,0},{3,1},{4,6},{5,7},{6,4},{7,5},{8,10},{9,11},{10,... | collective-permute-start | bytes 165896 | tf_op jit(solution)/shard_map/ppermute | solution.py:34
  5.3 6.1 %collective-permute-start.1 = (bf16[216,128]{1,0:T(8,128)(2,1)S(1)}, bf16[216,128]{1,0:T(8,128)(2,1)S(1)}, u32[]{:S(2)}, u32[]{:S(2)}) collective-permute-start(bf16[216,128]{1,0:T(8,128)(2,1)S(1)} %get-tuple-element.32), channel_id=1, source_target_pairs={{0,3},{1,2},{2,1},{3,0},{4,7},{5,6},{6,5},{7,4},{8,11},{9,10},{10,... | collective-permute-start | bytes 165896 | tf_op jit(solution)/shard_map/ppermute | solution.py:34
  6.7 4.7 %collective-permute-start.2 = (bf16[216,128]{1,0:T(8,128)(2,1)S(1)}, bf16[216,128]{1,0:T(8,128)(2,1)S(1)}, u32[]{:S(2)}, u32[]{:S(2)}) collective-permute-start(bf16[216,128]{1,0:T(8,128)(2,1)S(1)} %get-tuple-element.33), channel_id=1, source_target_pairs={{0,1},{1,0},{2,3},{3,2},{4,5},{5,4},{6,7},{7,6},{8,9},{9,8},{10,11... | collective-permute-start | bytes 165896 | tf_op jit(solution)/shard_map/ppermute | solution.py:34
  6.9 3.9 %collective-permute-start.3 = (bf16[1,128,128]{2,1,0:T(8,128)(2,1)S(1)}, bf16[1,128,128]{2,1,0:T(8,128)(2,1)S(1)}, u32[]{:S(2)}, u32[]{:S(2)}) collective-permute-start(bf16[1,128,128]{2,1,0:T(8,128)(2,1)S(1)} %get-tuple-element.34), channel_id=1, source_target_pairs={{0,8},{4,12},{8,0},{12,4},{1,9},{5,13},{9,1},{13,5},{2,10},{6,14},... | collective-permute-start | bytes 98312 | tf_op jit(solution)/shard_map/ppermute | solution.py:34
  11.4 7.4 %copy-start.1 = (f32[8,1024]{1,0:T(8,128)S(1)}, f32[8,1024]{1,0:T(8,128)}, u32[]{:S(2)}) copy-start(f32[8,1024]{1,0:T(8,128)} %gain_ref.1) | copy-start | bytes 98308
  11.5 4.1 %collective-permute-start.5 = (bf16[3,128,128]{2,1,0:T(8,128)(2,1)S(1)}, bf16[3,128,128]{2,1,0:T(8,128)(2,1)S(1)}, u32[]{:S(2)}, u32[]{:S(2)}) collective-permute-start(bf16[3,128,128]{2,1,0:T(8,128)(2,1)S(1)} %get-tuple-element.39), channel_id=1, source_target_pairs={{4,12},{12,4},{5,13},{13,5},{6,14},{14,6},{7,15},{15,7},{20,28},{2... | collective-permute-start | bytes 294920 | tf_op jit(solution)/shard_map/ppermute | solution.py:238
  12.2 8.1 %collective-permute-start.4 = (bf16[3,128,128]{2,1,0:T(8,128)(2,1)S(1)}, bf16[3,128,128]{2,1,0:T(8,128)(2,1)S(1)}, u32[]{:S(2)}, u32[]{:S(2)}) collective-permute-start(bf16[3,128,128]{2,1,0:T(8,128)(2,1)S(1)} %get-tuple-element.39), channel_id=1, source_target_pairs={{0,8},{8,0},{1,9},{9,1},{2,10},{10,2},{3,11},{11,3},{16,24},{24,16... | collective-permute-start | bytes 294920 | tf_op jit(solution)/shard_map/ppermute | solution.py:238
  15.6 4.7 %collective-permute-start.6 = (bf16[3,128,128]{2,1,0:T(8,128)(2,1)S(1)}, bf16[3,128,128]{2,1,0:T(8,128)(2,1)S(1)}, u32[]{:S(2)}, u32[]{:S(2)}) collective-permute-start(bf16[3,128,128]{2,1,0:T(8,128)(2,1)S(1)} %collective-permute-done.5.refs_8_), channel_id=1, source_target_pairs={{4,0},{12,8},{5,1},{13,9},{6,2},{14,10},{7,3},{15,11},{20,16},{28,... | collective-permute-start | bytes 294920 | tf_op jit(solution)/shard_map/ppermute | solution.py:238
  16.9 5.7 %collective-permute-start.8 = (bf16[4,128,128]{2,1,0:T(8,128)(2,1)S(1)}, bf16[4,128,128]{2,1,0:T(8,128)(2,1)S(1)}, u32[]{:S(2)}, u32[]{:S(2)}) collective-permute-start(bf16[4,128,128]{2,1,0:T(8,128)(2,1)S(1)} %get-tuple-element.45.refs_6_), channel_id=1, source_target_pairs={{0,4},{4,0},{8,12},{12,8},{1,5},{5,1},{9,13},{13,9},{2,6},{6,2},{1... | collective-permute-start | bytes 393224 | tf_op jit(solution)/shard_map/ppermute | solution.py:34
  18.1 2.1 %collective-permute-start.7 = (bf16[1,128,128]{2,1,0:T(8,128)(2,1)S(1)}, bf16[1,128,128]{2,1,0:T(8,128)(2,1)S(1)}, u32[]{:S(2)}, u32[]{:S(2)}) collective-permute-start(bf16[1,128,128]{2,1,0:T(8,128)(2,1)S(1)} %collective-permute-done.3.refs_4_), channel_id=1, source_target_pairs={{0,4},{4,0},{8,12},{12,8},{1,5},{5,1},{9,13},{13,9},{2,6},{6,2},{1... | collective-permute-start | bytes 98312 | tf_op jit(solution)/shard_map/ppermute | solution.py:34
  18.9 1.1 %copy-start = (bf16[384,1024]{1,0:T(8,128)(2,1)S(1)}, bf16[384,1024]{1,0:T(8,128)(2,1)}, u32[]{:S(2)}) copy-start(bf16[384,1024]{1,0:T(8,128)(2,1)} %weight_ref.1) | copy-start | bytes 2359300
  20.3 3.3 %collective-permute-start.9 = (bf16[3,128,128]{2,1,0:T(8,128)(2,1)S(1)}, bf16[3,128,128]{2,1,0:T(8,128)(2,1)S(1)}, u32[]{:S(2)}, u32[]{:S(2)}) collective-permute-start(bf16[3,128,128]{2,1,0:T(8,128)(2,1)S(1)} %collective-permute-done.4.refs_9_), channel_id=1, source_target_pairs={{0,4},{8,12},{1,5},{9,13},{2,6},{10,14},{3,7},{11,15},{16,20},{24,... | collective-permute-start | bytes 294920 | tf_op jit(solution)/shard_map/ppermute | solution.py:238
  24.0 5.6 %collective-permute-start.10 = (bf16[64,128]{1,0:T(8,128)(2,1)S(1)}, bf16[64,128]{1,0:T(8,128)(2,1)S(1)}, u32[]{:S(2)}, u32[]{:S(2)}) collective-permute-start(bf16[64,128]{1,0:T(8,128)(2,1)S(1)} %get-tuple-element.52), channel_id=1, source_target_pairs={{0,3},{1,2},{2,1},{3,0},{4,7},{5,6},{6,5},{7,4},{8,11},{9,10},{10,... | collective-permute-start | bytes 49160 | tf_op jit(solution)/shard_map/ppermute | solution.py:34
  26.6 4.6 %collective-permute-start.11 = (bf16[64,128]{1,0:T(8,128)(2,1)S(1)}, bf16[64,128]{1,0:T(8,128)(2,1)S(1)}, u32[]{:S(2)}, u32[]{:S(2)}) collective-permute-start(bf16[64,128]{1,0:T(8,128)(2,1)S(1)} %get-tuple-element.53), channel_id=1, source_target_pairs={{0,2},{1,3},{2,0},{3,1},{4,6},{5,7},{6,4},{7,5},{8,10},{9,11},{10,... | collective-permute-start | bytes 49160 | tf_op jit(solution)/shard_map/ppermute | solution.py:34
  26.7 4.5 %collective-permute-start.12 = (bf16[64,128]{1,0:T(8,128)(2,1)S(1)}, bf16[64,128]{1,0:T(8,128)(2,1)S(1)}, u32[]{:S(2)}, u32[]{:S(2)}) collective-permute-start(bf16[64,128]{1,0:T(8,128)(2,1)S(1)} %get-tuple-element.54), channel_id=1, source_target_pairs={{0,1},{1,0},{2,3},{3,2},{4,5},{5,4},{6,7},{7,6},{8,9},{9,8},{10,11... | collective-permute-start | bytes 49160 | tf_op jit(solution)/shard_map/ppermute | solution.py:34

commit v13 on v11

--- a/solution.py
+++ b/solution.py
@@ -25,8 +25,8 @@
     return sorted(range(owners), key=lambda step: (step > 0, -step.bit_length(), step))
 
 
-def steps_back(owners):
-    return [0, *range(owners - 1, 0, -1)]
+def step_pairs(owners):
+    return range(2, owners, 2)
 
 
 def swap(array, axis, step):
@@ -81,16 +81,27 @@
 
 
 def sort_kernel(rows, *refs):
-    got_refs, (pair_ref, rest_ref, patch_ref) = refs[:-3], refs[-3:]
+    got_refs, (pair_ref, rest_ref, patch_ref, ask_ref, give_ref) = refs[:-5], refs[-5:]
     owners = len(got_refs)
     slab_rows, width = rows // owners, patch_ref.shape[1]
-    size = pair_ref.shape[1]
-    start = 3 * size // 2
+    size, lines = pair_ref.shape[1], ask_ref.shape[1]
+    asks = {step: ref.at[size : size + lines] for step, ref in zip(steps_in(owners), got_refs)}
+    ask_ref[0] = asks[0][...]
+    ask_ref[1] = asks[1][...]
+    odd = lax.axis_index("blk") & 1
+    for side in range(2):
+
+        @pl.when(odd == side)
+        def _():
+            for i, step in enumerate(step_pairs(owners)):
+                ask_ref[2 + i] = asks[step + side][...]
+                give_ref[i] = asks[step + 1 - side][...]
+
     for i, ref in enumerate(got_refs):
         pair_ref[i] = ref[:size]
         if i:
             rest_ref[i - 1] = ref[:size]
-    slabs = [ref[start:].astype(jnp.float32) for ref in got_refs]
+    slabs = [ref[size + lines :].astype(jnp.float32) for ref in got_refs]
     patches = [
         jnp.concatenate([slab[i * slab_rows : (i + 1) * slab_rows] for slab in slabs], axis=0)
         for i in range(width // HEAD_DIM)
@@ -98,8 +109,13 @@
     patch_ref[...] = normed(jnp.concatenate(patches, axis=1), 1.0).astype(jnp.bfloat16)
 
 
-def fold(rows, got_refs, pair_refs, use):
-    owners = len(got_refs)
+def queries_of(ask_ref, taken_ref):
+    both = [(ask_ref.at[2 + i], taken_ref.at[i]) for i in range(taken_ref.shape[0])]
+    return [ask_ref.at[0], ask_ref.at[1], *(view for pair in both for view in pair)]
+
+
+def fold(rows, ask_refs, pair_refs, use):
+    owners = len(ask_refs)
     heads = pair_refs[0].shape[1] // (2 * rows)
     count = sum(ref.shape[0] for ref in pair_refs) * rows
     group = max(1, min(owners, 2**17 // (rows * count)))
@@ -114,8 +130,7 @@
         many = min(group, owners - first)
         scores = []
         for head in range(heads):
-            ask = spans[0].stop * (2 * heads + head)
-            queries = [ref[ask : ask + rows] for ref in got_refs[first : first + many]]
+            queries = [ref[spans[head]] for ref in ask_refs[first : first + many]]
             scores.append(
                 lax.dot_general(
                     jnp.concatenate(queries, axis=0),
@@ -141,7 +156,7 @@
     return mixed[:, HEAD_DIM:], mixed[:, :HEAD_DIM]
 
 
-def early_kernel(rows, owners, *refs):
+def early_kernel(rows, *refs):
     state_refs = refs[-3:]
 
     def use(at, scores, values):
@@ -152,13 +167,14 @@
             for head in range(len(values)):
                 ref[head, at] = state[head * each : (head + 1) * each]
 
-    fold(rows, refs[:owners], refs[owners:-3], use)
-
-
-def late_kernel(rows, owners, *refs):
+    fold(rows, queries_of(*refs[:2]), refs[2:-3], use)
+
+
+def late_kernel(rows, *refs):
     state_refs, refs = refs[:3], refs[3:]
-    out_refs = refs[-owners:]
-    places = [steps_back(owners).index(step) for step in steps_in(owners)]
+    asks = queries_of(*refs[:2])
+    outs = refs[0].shape[0]
+    out_refs = refs[-outs:]
 
     def use(at, scores, values):
         heads = range(len(values))
@@ -175,10 +191,12 @@
         many = (at.stop - at.start) // rows
         for i in range(len(values) * many):
             head, source = divmod(i, many)
-            out_ref = out_refs[places[at.start // rows + source]]
-            out_ref[head * rows : (head + 1) * rows] = mixed[i * rows : (i + 1) * rows]
-
-    fold(rows, refs[:owners], refs[owners:-owners], use)
+            source = source + at.start // rows
+            place, half = (source, 0) if source < 2 else divmod(source + 2, 2)
+            start = (half * len(values) + head) * rows
+            out_refs[place][start : start + rows] = mixed[i * rows : (i + 1) * rows]
+
+    fold(rows, asks, refs[2:-outs], use)
 
 
 def hint_kernel(layer_ref, patch_ref, weight_ref, gain_ref, out_ref):
@@ -190,16 +208,21 @@
         out_ref[partner(me, step)] = hint[i * slab_rows : (i + 1) * slab_rows]
 
 
-def finish_kernel(owners, hint_ref, *refs):
-    back_refs, out_ref = refs[:-1], refs[-1]
+def finish_kernel(owners, hint_ref, own_ref, near_ref, *refs):
+    far_refs, out_ref = refs[:-1], refs[-1]
     rows, feats = out_ref.shape
     share = feats // owners
-    me = lax.axis_index("ulysses")
-    for step, ref in zip(steps_back(owners), back_refs):
+    lines = own_ref.shape[0]
+    me, odd = lax.axis_index("ulysses"), lax.axis_index("blk") & 1
+    parts = [(0, own_ref, 0), (1, near_ref, 0)]
+    for step, kept, crossed in zip(step_pairs(owners), far_refs[::2], far_refs[1::2]):
+        parts = parts + [(step + odd, kept, 0), (step + 1 - odd, crossed, lines)]
+    for step, ref, first in parts:
         for head in range(share // HEAD_DIM):
             start = partner(me, step) * share + head * HEAD_DIM
             cols = pl.ds(pl.multiple_of(start, HEAD_DIM), HEAD_DIM)
-            attended = ref[head * rows : (head + 1) * rows].astype(jnp.float32)
+            at = first + head * rows
+            attended = ref[at : at + rows].astype(jnp.float32)
             out_ref[:, cols] = (attended + hint_ref[:, cols]).astype(jnp.bfloat16)
 
 
@@ -222,6 +245,16 @@
 
 def shape(dims, dtype=jnp.bfloat16):
     return jax.ShapeDtypeStruct(dims, dtype)
+
+
+def swap_far(array, step):
+    blocks, owners = lax.axis_size("blk"), lax.axis_size("ulysses")
+    pairs = [
+        (block * owners + i, block * owners + partner(i, step + (block & 1)))
+        for block in range(blocks)
+        for i in range(owners)
+    ]
+    return lax.ppermute(array, ("blk", "ulysses"), pairs)
 
 
 def gather(held, step, axis):
@@ -279,12 +312,14 @@
     half = lax.axis_size("blk") // 2
     own_moved = swap(sent[owners], "blk", half)
     got, own_moved = lax.optimization_barrier((exchange(sent[:owners], steps_in(owners), "ulysses"), own_moved))
-    pairs, rest, patches = call(
+    pairs, rest, patches, asks, gives = call(
         functools.partial(sort_kernel, rows),
         [
             shape((owners, 2 * lines, HEAD_DIM)),
             shape((owners - 1, 2 * lines, HEAD_DIM)),
             shape((rows, width)),
+            shape((owners // 2 + 1, lines, HEAD_DIM)),
+            shape((owners // 2 - 1, lines, HEAD_DIM)),
         ],
         [VMEM] * owners,
         *got,
@@ -302,39 +337,47 @@
     )
     moved = swap(rest, "blk", half)
     held = gather([own_moved], half // 2, "blk")
-    moved, held, hint = lax.optimization_barrier((moved, held, hint))
+    taken = swap(gives, "blk", 1)
+    moved, held, taken, hint = lax.optimization_barrier((moved, held, taken, hint))
     moved = gather([moved], half // 2, "blk")
     early = held + gather([pairs], half // 2, "blk") + moved[: len(moved) // 2]
     late = moved[len(moved) // 2 :]
-    heads, asks = lines // rows, owners * rows
+    heads, many = lines // rows, owners * rows
     state = call(
-        functools.partial(early_kernel, rows, owners),
+        functools.partial(early_kernel, rows),
         [
-            shape((heads, asks, HEAD_DIM), jnp.float32),
+            shape((heads, many, HEAD_DIM), jnp.float32),
         ]
         * 3,
-        [VMEM] * (owners + len(early)),
-        *got,
+        [VMEM] * (2 + len(early)),
+        asks,
+        taken,
         *early,
-        flops=2 * asks * sum(array.size for array in early),
+        flops=2 * many * sum(array.size for array in early),
         nbytes=2 * sum(array.size for array in early),
     )
     mixed = call(
-        functools.partial(late_kernel, rows, owners),
-        [shape((lines, HEAD_DIM))] * owners,
-        [VMEM] * (3 + owners + len(late)),
+        functools.partial(late_kernel, rows),
+        [shape((lines, HEAD_DIM))] * 2 + [shape((2 * lines, HEAD_DIM))] * (owners // 2 - 1),
+        [VMEM] * (5 + len(late)),
         *state,
-        *got,
+        asks,
+        taken,
         *late,
-        flops=2 * asks * sum(array.size for array in late),
+        flops=2 * many * sum(array.size for array in late),
         nbytes=2 * sum(array.size for array in late),
     )
+    kept = [swap_far(array, step) for array, step in zip(mixed[2:], step_pairs(owners))]
+    kept, near = lax.optimization_barrier((kept, swap(mixed[1], "ulysses", 1)))
+    far = [array for one in kept for array in (one, swap(one, "blk", 1))]
     return call(
         functools.partial(finish_kernel, owners),
         shape((rows, feats)),
-        [VMEM] * (owners + 1),
+        [VMEM] * (3 + len(far)),
         hint.reshape(rows, feats),
-        *exchange(mixed, steps_back(owners), "ulysses"),
+        mixed[0],
+        near,
+        *far,
     )
 
 

time: 26 us -> 26 us (level)
  starting transfers between devices: 13.7 us -> 12.4 us
  waiting for transfers between devices: 7.12 us -> 8.39 us
    ppermute x11, starting transfers between devices: 13.7 us -> 10.1 us  [swap(): lax.ppermute(array, axis, [(i, partner(i, step)) for i in range(size)])]
    ppermute x0 -> x1, starting transfers between devices: none -> 2.31 us  [swap_far(): return lax.ppermute(array, ('blk', 'ulysses'), pairs)]
    ppermute x11, waiting for transfers between devices: 7.12 us -> 8.39 us  [swap(): lax.ppermute(array, axis, [(i, partner(i, step)) for i in range(size)])]
  transfers between devices with their start and end apart: 11 -> 12, of which waited for: 6 -> 6; matrix products, arithmetic and copies ran while one was open for 0% -> 0% of each run, Pallas kernels for 3% -> 3%
where the time goes in v13:
time: 26 us; the launch traced here: 25.8 us
  starting transfers between devices  12.4 us (48%)
  waiting for transfers between devices  8.39 us (32%)
  Pallas kernels  3.13 us (12%)
  local copies, waits for them, and re-layouts  1.13 us (4%)
  between operations  0.73 us (3%)
    ppermute x11, starting transfers between devices, swap(): lax.ppermute(array, axis, [(i, partner(i, step)) for i in range(size)])  10.1 us
    ppermute x11, waiting for transfers between devices, swap(): lax.ppermute(array, axis, [(i, partner(i, step)) for i in range(size)])  8.39 us
    pallas_call x6, Pallas kernels, call(): pl.pallas_call(kernel, out_shape=out_shape, in_specs=specs, out_specs=jax...  3.13 us
    ppermute x1, starting transfers between devices, swap_far(): return lax.ppermute(array, ('blk', 'ulysses'), pairs)  2.31 us
    unnamed x4, local copies, waits for them, and re-layouts  1.13 us
  transfers between devices with their start and end apart: 12, of which 6 were waited for; matrix products, arithmetic and copies ran while one was open for 0% of the time, Pallas kernels for 3%

profile of v13, /device:TPU:0, one launch (start us, length us, event | category | flops | bytes accessed | tf_op | source)
XLA Modules:
  0.0 25.8 jit_solution(13038195963694584732)
XLA Ops:
  0.0 1.2 %shard_map.100 = (bf16[216,128]{1,0:T(8,128)(2,1)S(1)}, bf16[216,128]{1,0:T(8,128)(2,1)S(1)}, bf16[216,128]{1,0:T(8,128)(2,1)S(1)}, bf16[216,128]{1,0:T(8,128)(2,1)S(1)}, bf16[1,128,128]{2,1,0:T(8,128)(2,1)S(1)}) custom-call(f32[1,1024]{1,0:T(1,128)} %bitcast.4, bf16[32,1024]{1,0:T(8,128)(2,1)} %refs_1_.1, f32[1,1024]{1,0:T(1,128)} %bitcast.5, ...), custom_call_target="tpu_custom_call" | custom-call | tf_op jit(solution)/shard_map/pallas_call | solution.py:235
  1.2 4.1 %collective-permute-start = (bf16[216,128]{1,0:T(8,128)(2,1)S(1)}, bf16[216,128]{1,0:T(8,128)(2,1)S(1)}, u32[]{:S(2)}, u32[]{:S(2)}) collective-permute-start(bf16[216,128]{1,0:T(8,128)(2,1)S(1)} %get-tuple-element.34), channel_id=1, source_target_pairs={{0,2},{1,3},{2,0},{3,1},{4,6},{5,7},{6,4},{7,5},{8,10},{9,11},{10,... | collective-permute-start | bytes 165896 | tf_op jit(solution)/shard_map/ppermute | solution.py:34
  5.3 1.3 %collective-permute-start.1 = (bf16[216,128]{1,0:T(8,128)(2,1)S(1)}, bf16[216,128]{1,0:T(8,128)(2,1)S(1)}, u32[]{:S(2)}, u32[]{:S(2)}) collective-permute-start(bf16[216,128]{1,0:T(8,128)(2,1)S(1)} %get-tuple-element.35), channel_id=1, source_target_pairs={{0,3},{1,2},{2,1},{3,0},{4,7},{5,6},{6,5},{7,4},{8,11},{9,10},{10,... | collective-permute-start | bytes 165896 | tf_op jit(solution)/shard_map/ppermute | solution.py:34
  6.7 0.2 collective-permute-start.2
  6.9 1.5 %collective-permute-start.3 = (bf16[1,128,128]{2,1,0:T(8,128)(2,1)S(1)}, bf16[1,128,128]{2,1,0:T(8,128)(2,1)S(1)}, u32[]{:S(2)}, u32[]{:S(2)}) collective-permute-start(bf16[1,128,128]{2,1,0:T(8,128)(2,1)S(1)} %get-tuple-element.37), channel_id=1, source_target_pairs={{0,8},{4,12},{8,0},{12,4},{1,9},{5,13},{9,1},{13,5},{2,10},{6,14},... | collective-permute-start | bytes 98312 | tf_op jit(solution)/shard_map/ppermute | solution.py:34
  8.4 2.4 %collective-permute-done.3.refs_2_ = bf16[1,128,128]{2,1,0:T(8,128)(2,1)S(1)} collective-permute-done((bf16[1,128,128]{2,1,0:T(8,128)(2,1)S(1)}, bf16[1,128,128]{2,1,0:T(8,128)(2,1)S(1)}, u32[]{:S(2)}, u32[]{:S(2)}) %collective-permute-start.3) | collective-permute-done | bytes 32800 | tf_op jit(solution)/shard_map/ppermute | solution.py:34
  10.8 0.0 collective-permute-done.refs_1_
  10.8 0.6 %collective-permute-done.1.refs_2_ = bf16[216,128]{1,0:T(8,128)(2,1)S(1)} collective-permute-done((bf16[216,128]{1,0:T(8,128)(2,1)S(1)}, bf16[216,128]{1,0:T(8,128)(2,1)S(1)}, u32[]{:S(2)}, u32[]{:S(2)}) %collective-permute-start.1) | collective-permute-done | bytes 55328 | tf_op jit(solution)/shard_map/ppermute | solution.py:34
  11.4 0.0 collective-permute-done.2.refs_3_
  11.4 0.0 copy-start.1
  11.4 0.1 shard_map.101
  11.5 1.6 %collective-permute-start.4 = (bf16[3,128,128]{2,1,0:T(8,128)(2,1)S(1)}, bf16[3,128,128]{2,1,0:T(8,128)(2,1)S(1)}, u32[]{:S(2)}, u32[]{:S(2)}) collective-permute-start(bf16[3,128,128]{2,1,0:T(8,128)(2,1)S(1)} %get-tuple-element.42), channel_id=1, source_target_pairs={{0,8},{4,12},{8,0},{12,4},{1,9},{5,13},{9,1},{13,5},{2,10},{6,14},... | collective-permute-start | bytes 294920 | tf_op jit(solution)/shard_map/ppermute | solution.py:34
  13.1 0.0 collective-permute-start.7
  13.1 0.5 %collective-permute-start.5 = (bf16[1,128,128]{2,1,0:T(8,128)(2,1)S(1)}, bf16[1,128,128]{2,1,0:T(8,128)(2,1)S(1)}, u32[]{:S(2)}, u32[]{:S(2)}) collective-permute-start(bf16[1,128,128]{2,1,0:T(8,128)(2,1)S(1)} %collective-permute-done.3.refs_2_), channel_id=1, source_target_pairs={{0,4},{4,0},{8,12},{12,8},{1,5},{5,1},{9,13},{13,9},{2,6},{6,2},{1... | collective-permute-start | bytes 98312 | tf_op jit(solution)/shard_map/ppermute | solution.py:34
  13.6 0.0 collective-permute-start.6
  14.2 0.0 copy-done.1
  14.3 0.0 copy-start
  14.3 1.1 %copy-done = bf16[384,1024]{1,0:T(8,128)(2,1)S(1)} copy-done((bf16[384,1024]{1,0:T(8,128)(2,1)S(1)}, bf16[384,1024]{1,0:T(8,128)(2,1)}, u32[]{:S(2)}) %copy-start) | copy-done | bytes 786456
  15.4 0.3 shard_map.102
  15.7 0.0 collective-permute-done.6.refs_1_.refs_4_
  15.7 0.0 collective-permute-done.5.refs_3_
  15.7 0.5 %collective-permute-done.4.refs_6_ = bf16[3,128,128]{2,1,0:T(8,128)(2,1)S(1)} collective-permute-done((bf16[3,128,128]{2,1,0:T(8,128)(2,1)S(1)}, bf16[3,128,128]{2,1,0:T(8,128)(2,1)S(1)}, u32[]{:S(2)}, u32[]{:S(2)}) %collective-permute-start.4) | collective-permute-done | bytes 98336 | tf_op jit(solution)/shard_map/ppermute | solution.py:34
  16.2 0.1 collective-permute-start.8
  16.3 0.0 collective-permute-done.7.refs_5_
  16.3 0.5 %shard_map.103 = (f32[2,128,128]{2,1,0:T(8,128)S(1)}, f32[2,128,128]{2,1,0:T(8,128)S(1)}, f32[2,128,128]{2,1,0:T(8,128)S(1)}) custom-call(bf16[3,64,128]{2,1,0:T(8,128)(2,1)S(1)} %get-tuple-element.47.refs_0_.refs_3_, bf16[1,64,128]{2,1,0:T(8,128)(2,1)S(1)} %collective-permute-done.6.refs_1_.refs_4_, ...), custom_call_target="tpu_custom_call" | custom-call | flops 54525952 | bytes 425984 | tf_op jit(solution)/shard_map/pallas_call | solution.py:235
  16.8 0.7 %collective-permute-done.8.refs_5_ = bf16[3,128,128]{2,1,0:T(8,128)(2,1)S(1)} collective-permute-done((bf16[3,128,128]{2,1,0:T(8,128)(2,1)S(1)}, bf16[3,128,128]{2,1,0:T(8,128)(2,1)S(1)}, u32[]{:S(2)}, u32[]{:S(2)}) %collective-permute-start.8) | collective-permute-done | bytes 98336 | tf_op jit(solution)/shard_map/ppermute | solution.py:34
  17.5 0.4 %shard_map.104 = (bf16[64,128]{1,0:T(8,128)(2,1)S(1)}, bf16[64,128]{1,0:T(8,128)(2,1)S(1)}, bf16[128,128]{1,0:T(8,128)(2,1)S(1)}) custom-call(f32[2,128,128]{2,1,0:T(8,128)S(1)} %get-tuple-element.53.refs_0_, f32[2,128,128]{2,1,0:T(8,128)S(1)} %get-tuple-element.54.refs_1_, f32[2,128,128]{2,1,0:T(8,128)S(1)} %get-tuple-element.55.refs_2_, ...), custom_call_target="tpu_custom_call" | custom-call | flops 12582912 | bytes 98304 | tf_op jit(solution)/shard_map/pallas_call | solution.py:235
  17.9 2.3 %collective-permute-start.9 = (bf16[128,128]{1,0:T(8,128)(2,1)S(1)}, bf16[128,128]{1,0:T(8,128)(2,1)S(1)}, u32[]{:S(2)}, u32[]{:S(2)}) collective-permute-start(bf16[128,128]{1,0:T(8,128)(2,1)S(1)} %get-tuple-element.57), channel_id=1, source_target_pairs={{0,2},{1,3},{2,0},{3,1},{4,7},{5,6},{6,5},{7,4},{8,10},{9,11},{10,... | collective-permute-start | bytes 98312 | tf_op jit(solution)/shard_map/ppermute | solution.py:257
  20.2 0.8 %collective-permute-start.10 = (bf16[64,128]{1,0:T(8,128)(2,1)S(1)}, bf16[64,128]{1,0:T(8,128)(2,1)S(1)}, u32[]{:S(2)}, u32[]{:S(2)}) collective-permute-start(bf16[64,128]{1,0:T(8,128)(2,1)S(1)} %get-tuple-element.58), channel_id=1, source_target_pairs={{0,1},{1,0},{2,3},{3,2},{4,5},{5,4},{6,7},{7,6},{8,9},{9,8},{10,11... | collective-permute-start | bytes 49160 | tf_op jit(solution)/shard_map/ppermute | solution.py:34
  21.1 2.9 %collective-permute-done.10.near_ref = bf16[64,128]{1,0:T(8,128)(2,1)S(1)} collective-permute-done((bf16[64,128]{1,0:T(8,128)(2,1)S(1)}, bf16[64,128]{1,0:T(8,128)(2,1)S(1)}, u32[]{:S(2)}, u32[]{:S(2)}) %collective-permute-start.10) | collective-permute-done | bytes 16416 | tf_op jit(solution)/shard_map/ppermute | solution.py:34
  24.0 0.0 collective-permute-done.9.refs_0_
  24.0 0.0 collective-permute-start.11
  24.0 1.2 %collective-permute-done.11.refs_1_ = bf16[128,128]{1,0:T(8,128)(2,1)S(1)} collective-permute-done((bf16[128,128]{1,0:T(8,128)(2,1)S(1)}, bf16[128,128]{1,0:T(8,128)(2,1)S(1)}, u32[]{:S(2)}, u32[]{:S(2)}) %collective-permute-start.11) | collective-permute-done | bytes 32800 | tf_op jit(solution)/shard_map/ppermute | solution.py:34
  25.2 0.7 %shard_map.105 = bf16[32,1024]{1,0:T(8,128)(2,1)} custom-call(f32[32,1024]{1,0:T(8,128)S(1)} %bitcast.3, bf16[64,128]{1,0:T(8,128)(2,1)S(1)} %get-tuple-element.56.own_ref, bf16[64,128]{1,0:T(8,128)(2,1)S(1)} %collective-permute-done.10.near_ref, bf16[128,128]{1,0:T(8,128)(2,1)S(1)} %collective-permute-done.9.refs_0_, ...), custom_call_target="tpu_custom_call" | custom-call | tf_op jit(solution)/shard_map/pallas_call | solution.py:235
Async XLA Ops:
  1.2 9.6 %collective-permute-start = (bf16[216,128]{1,0:T(8,128)(2,1)S(1)}, bf16[216,128]{1,0:T(8,128)(2,1)S(1)}, u32[]{:S(2)}, u32[]{:S(2)}) collective-permute-start(bf16[216,128]{1,0:T(8,128)(2,1)S(1)} %get-tuple-element.34), channel_id=1, source_target_pairs={{0,2},{1,3},{2,0},{3,1},{4,6},{5,7},{6,4},{7,5},{8,10},{9,11},{10,... | collective-permute-start | bytes 165896 | tf_op jit(solution)/shard_map/ppermute | solution.py:34
  5.3 6.1 %collective-permute-start.1 = (bf16[216,128]{1,0:T(8,128)(2,1)S(1)}, bf16[216,128]{1,0:T(8,128)(2,1)S(1)}, u32[]{:S(2)}, u32[]{:S(2)}) collective-permute-start(bf16[216,128]{1,0:T(8,128)(2,1)S(1)} %get-tuple-element.35), channel_id=1, source_target_pairs={{0,3},{1,2},{2,1},{3,0},{4,7},{5,6},{6,5},{7,4},{8,11},{9,10},{10,... | collective-permute-start | bytes 165896 | tf_op jit(solution)/shard_map/ppermute | solution.py:34
  6.7 4.7 %collective-permute-start.2 = (bf16[216,128]{1,0:T(8,128)(2,1)S(1)}, bf16[216,128]{1,0:T(8,128)(2,1)S(1)}, u32[]{:S(2)}, u32[]{:S(2)}) collective-permute-start(bf16[216,128]{1,0:T(8,128)(2,1)S(1)} %get-tuple-element.36), channel_id=1, source_target_pairs={{0,1},{1,0},{2,3},{3,2},{4,5},{5,4},{6,7},{7,6},{8,9},{9,8},{10,11... | collective-permute-start | bytes 165896 | tf_op jit(solution)/shard_map/ppermute | solution.py:34
  6.9 3.9 %collective-permute-start.3 = (bf16[1,128,128]{2,1,0:T(8,128)(2,1)S(1)}, bf16[1,128,128]{2,1,0:T(8,128)(2,1)S(1)}, u32[]{:S(2)}, u32[]{:S(2)}) collective-permute-start(bf16[1,128,128]{2,1,0:T(8,128)(2,1)S(1)} %get-tuple-element.37), channel_id=1, source_target_pairs={{0,8},{4,12},{8,0},{12,4},{1,9},{5,13},{9,1},{13,5},{2,10},{6,14},... | collective-permute-start | bytes 98312 | tf_op jit(solution)/shard_map/ppermute | solution.py:34
  11.4 2.8 %copy-start.1 = (f32[8,1024]{1,0:T(8,128)S(1)}, f32[8,1024]{1,0:T(8,128)}, u32[]{:S(2)}) copy-start(f32[8,1024]{1,0:T(8,128)} %gain_ref.1) | copy-start | bytes 98308
  11.5 4.7 %collective-permute-start.4 = (bf16[3,128,128]{2,1,0:T(8,128)(2,1)S(1)}, bf16[3,128,128]{2,1,0:T(8,128)(2,1)S(1)}, u32[]{:S(2)}, u32[]{:S(2)}) collective-permute-start(bf16[3,128,128]{2,1,0:T(8,128)(2,1)S(1)} %get-tuple-element.42), channel_id=1, source_target_pairs={{0,8},{4,12},{8,0},{12,4},{1,9},{5,13},{9,1},{13,5},{2,10},{6,14},... | collective-permute-start | bytes 294920 | tf_op jit(solution)/shard_map/ppermute | solution.py:34
  13.1 3.2 %collective-permute-start.7 = (bf16[4,128,128]{2,1,0:T(8,128)(2,1)S(1)}, bf16[4,128,128]{2,1,0:T(8,128)(2,1)S(1)}, u32[]{:S(2)}, u32[]{:S(2)}) collective-permute-start(bf16[4,128,128]{2,1,0:T(8,128)(2,1)S(1)} %get-tuple-element.51.refs_4_), channel_id=1, source_target_pairs={{0,4},{4,0},{8,12},{12,8},{1,5},{5,1},{9,13},{13,9},{2,6},{6,2},{1... | collective-permute-start | bytes 393224 | tf_op jit(solution)/shard_map/ppermute | solution.py:34
  13.1 2.6 %collective-permute-start.5 = (bf16[1,128,128]{2,1,0:T(8,128)(2,1)S(1)}, bf16[1,128,128]{2,1,0:T(8,128)(2,1)S(1)}, u32[]{:S(2)}, u32[]{:S(2)}) collective-permute-start(bf16[1,128,128]{2,1,0:T(8,128)(2,1)S(1)} %collective-permute-done.3.refs_2_), channel_id=1, source_target_pairs={{0,4},{4,0},{8,12},{12,8},{1,5},{5,1},{9,13},{13,9},{2,6},{6,2},{1... | collective-permute-start | bytes 98312 | tf_op jit(solution)/shard_map/ppermute | solution.py:34
  13.6 2.1 %collective-permute-start.6 = (bf16[1,64,128]{2,1,0:T(8,128)(2,1)S(1)}, bf16[1,64,128]{2,1,0:T(8,128)(2,1)S(1)}, u32[]{:S(2)}, u32[]{:S(2)}) collective-permute-start(bf16[1,64,128]{2,1,0:T(8,128)(2,1)S(1)} %get-tuple-element.44), channel_id=1, source_target_pairs={{0,4},{4,0},{8,12},{12,8},{1,5},{5,1},{9,13},{13,9},{2,6},{6,2},{1... | collective-permute-start | bytes 49160 | tf_op jit(solution)/shard_map/ppermute | solution.py:34
  14.3 1.1 %copy-start = (bf16[384,1024]{1,0:T(8,128)(2,1)S(1)}, bf16[384,1024]{1,0:T(8,128)(2,1)}, u32[]{:S(2)}) copy-start(bf16[384,1024]{1,0:T(8,128)(2,1)} %weight_ref.1) | copy-start | bytes 2359300
  16.2 1.3 %collective-permute-start.8 = (bf16[3,128,128]{2,1,0:T(8,128)(2,1)S(1)}, bf16[3,128,128]{2,1,0:T(8,128)(2,1)S(1)}, u32[]{:S(2)}, u32[]{:S(2)}) collective-permute-start(bf16[3,128,128]{2,1,0:T(8,128)(2,1)S(1)} %collective-permute-done.4.refs_6_), channel_id=1, source_target_pairs={{0,4},{4,0},{8,12},{12,8},{1,5},{5,1},{9,13},{13,9},{2,6},{6,2},{1... | collective-permute-start | bytes 294920 | tf_op jit(solution)/shard_map/ppermute | solution.py:34
  17.9 6.1 %collective-permute-start.9 = (bf16[128,128]{1,0:T(8,128)(2,1)S(1)}, bf16[128,128]{1,0:T(8,128)(2,1)S(1)}, u32[]{:S(2)}, u32[]{:S(2)}) collective-permute-start(bf16[128,128]{1,0:T(8,128)(2,1)S(1)} %get-tuple-element.57), channel_id=1, source_target_pairs={{0,2},{1,3},{2,0},{3,1},{4,7},{5,6},{6,5},{7,4},{8,10},{9,11},{10,... | collective-permute-start | bytes 98312 | tf_op jit(solution)/shard_map/ppermute | solution.py:257
  20.2 3.7 %collective-permute-start.10 = (bf16[64,128]{1,0:T(8,128)(2,1)S(1)}, bf16[64,128]{1,0:T(8,128)(2,1)S(1)}, u32[]{:S(2)}, u32[]{:S(2)}) collective-permute-start(bf16[64,128]{1,0:T(8,128)(2,1)S(1)} %get-tuple-element.58), channel_id=1, source_target_pairs={{0,1},{1,0},{2,3},{3,2},{4,5},{5,4},{6,7},{7,6},{8,9},{9,8},{10,11... | collective-permute-start | bytes 49160 | tf_op jit(solution)/shard_map/ppermute | solution.py:34
  24.0 1.2 %collective-permute-start.11 = (bf16[128,128]{1,0:T(8,128)(2,1)S(1)}, bf16[128,128]{1,0:T(8,128)(2,1)S(1)}, u32[]{:S(2)}, u32[]{:S(2)}) collective-permute-start(bf16[128,128]{1,0:T(8,128)(2,1)S(1)} %collective-permute-done.9.refs_0_), channel_id=1, source_target_pairs={{0,4},{4,0},{8,12},{12,8},{1,5},{5,1},{9,13},{13,9},{2,6},{6,2},{1... | collective-permute-start | bytes 98312 | tf_op jit(solution)/shard_map/ppermute | solution.py:34

commit v14 on v13

--- a/solution.py
+++ b/solution.py
@@ -187,14 +187,14 @@
         keys = scores.shape[1]
         new_totals, mixed = weigh(scores, peak[:, : keys if keys < HEAD_DIM else 1], values)
         mixed = (accum * correction + mixed) / (totals * correction + new_totals)
-        mixed = mixed.astype(jnp.bfloat16)
         many = (at.stop - at.start) // rows
         for i in range(len(values) * many):
             head, source = divmod(i, many)
             source = source + at.start // rows
             place, half = (source, 0) if source < 2 else divmod(source + 2, 2)
             start = (half * len(values) + head) * rows
-            out_refs[place][start : start + rows] = mixed[i * rows : (i + 1) * rows]
+            out_ref = out_refs[place]
+            out_ref[start : start + rows] = mixed[i * rows : (i + 1) * rows].astype(out_ref.dtype)
 
     fold(rows, asks, refs[2:-outs], use)
 
@@ -222,7 +222,7 @@
             start = partner(me, step) * share + head * HEAD_DIM
             cols = pl.ds(pl.multiple_of(start, HEAD_DIM), HEAD_DIM)
             at = first + head * rows
-            attended = ref[at : at + rows].astype(jnp.float32)
+            attended = ref[at : at + rows].astype(jnp.bfloat16).astype(jnp.float32)
             out_ref[:, cols] = (attended + hint_ref[:, cols]).astype(jnp.bfloat16)
 
 
@@ -358,7 +358,8 @@
     )
     mixed = call(
         functools.partial(late_kernel, rows),
-        [shape((lines, HEAD_DIM))] * 2 + [shape((2 * lines, HEAD_DIM))] * (owners // 2 - 1),
+        [shape((lines, HEAD_DIM)), shape((lines, HEAD_DIM), jnp.float32)]
+        + [shape((2 * lines, HEAD_DIM))] * (owners // 2 - 1),
         [VMEM] * (5 + len(late)),
         *state,
         asks,
@@ -368,7 +369,7 @@
         nbytes=2 * sum(array.size for array in late),
     )
     kept = [swap_far(array, step) for array, step in zip(mixed[2:], step_pairs(owners))]
-    kept, near = lax.optimization_barrier((kept, swap(mixed[1], "ulysses", 1)))
+    near = swap(mixed[1], "ulysses", 1)
     far = [array for one in kept for array in (one, swap(one, "blk", 1))]
     return call(
         functools.partial(finish_kernel, owners),

time: 26 us -> 25.3 us (0.973)
  waiting for transfers between devices: 8.39 us -> 7.65 us
    ppermute x11, waiting for transfers between devices: 8.39 us -> 5.49 us  [swap(): lax.ppermute(array, axis, [(i, partner(i, step)) for i in range(size)])]
    ppermute x1, waiting for transfers between devices: 0.01 us -> 2.16 us  [swap_far(): return lax.ppermute(array, ('blk', 'ulysses'), pairs)]
  transfers between devices with their start and end apart: 12 -> 12, of which waited for: 6 -> 7; matrix products, arithmetic and copies ran while one was open for 0% -> 0% of each run, Pallas kernels for 3% -> 3%
where the time goes in v14:
time: 25.3 us; the launch traced here: 25.1 us
  starting transfers between devices  12.4 us (49%)
  waiting for transfers between devices  7.65 us (30%)
  Pallas kernels  3.14 us (12%)
  local copies, waits for them, and re-layouts  1.13 us (4%)
  between operations  0.73 us (3%)
    ppermute x11, starting transfers between devices, swap(): lax.ppermute(array, axis, [(i, partner(i, step)) for i in range(size)])  10.1 us
    ppermute x11, waiting for transfers between devices, swap(): lax.ppermute(array, axis, [(i, partner(i, step)) for i in range(size)])  5.49 us
    pallas_call x6, Pallas kernels, call(): pl.pallas_call(kernel, out_shape=out_shape, in_specs=specs, out_specs=jax...  3.14 us
    ppermute x1, starting transfers between devices, swap_far(): return lax.ppermute(array, ('blk', 'ulysses'), pairs)  2.31 us
    ppermute x1, waiting for transfers between devices, swap_far(): return lax.ppermute(array, ('blk', 'ulysses'), pairs)  2.16 us
    unnamed x4, local copies, waits for them, and re-layouts  1.13 us
  transfers between devices with their start and end apart: 12, of which 7 were waited for; matrix products, arithmetic and copies ran while one was open for 0% of the time, Pallas kernels for 3%

profile of v14, /device:TPU:0, one launch (start us, length us, event | category | flops | bytes accessed | tf_op | source)
XLA Modules:
  0.0 25.1 jit_solution(9874966906191402008)
XLA Ops:
  0.0 1.2 %shard_map.100 = (bf16[216,128]{1,0:T(8,128)(2,1)S(1)}, bf16[216,128]{1,0:T(8,128)(2,1)S(1)}, bf16[216,128]{1,0:T(8,128)(2,1)S(1)}, bf16[216,128]{1,0:T(8,128)(2,1)S(1)}, bf16[1,128,128]{2,1,0:T(8,128)(2,1)S(1)}) custom-call(f32[1,1024]{1,0:T(1,128)} %bitcast.4, bf16[32,1024]{1,0:T(8,128)(2,1)} %refs_1_.1, f32[1,1024]{1,0:T(1,128)} %bitcast.5, ...), custom_call_target="tpu_custom_call" | custom-call | tf_op jit(solution)/shard_map/pallas_call | solution.py:235
  1.2 4.1 %collective-permute-start = (bf16[216,128]{1,0:T(8,128)(2,1)S(1)}, bf16[216,128]{1,0:T(8,128)(2,1)S(1)}, u32[]{:S(2)}, u32[]{:S(2)}) collective-permute-start(bf16[216,128]{1,0:T(8,128)(2,1)S(1)} %get-tuple-element.32), channel_id=1, source_target_pairs={{0,2},{1,3},{2,0},{3,1},{4,6},{5,7},{6,4},{7,5},{8,10},{9,11},{10,... | collective-permute-start | bytes 165896 | tf_op jit(solution)/shard_map/ppermute | solution.py:34
  5.3 1.3 %collective-permute-start.1 = (bf16[216,128]{1,0:T(8,128)(2,1)S(1)}, bf16[216,128]{1,0:T(8,128)(2,1)S(1)}, u32[]{:S(2)}, u32[]{:S(2)}) collective-permute-start(bf16[216,128]{1,0:T(8,128)(2,1)S(1)} %get-tuple-element.33), channel_id=1, source_target_pairs={{0,3},{1,2},{2,1},{3,0},{4,7},{5,6},{6,5},{7,4},{8,11},{9,10},{10,... | collective-permute-start | bytes 165896 | tf_op jit(solution)/shard_map/ppermute | solution.py:34
  6.7 0.2 collective-permute-start.2
  6.9 1.5 %collective-permute-start.3 = (bf16[1,128,128]{2,1,0:T(8,128)(2,1)S(1)}, bf16[1,128,128]{2,1,0:T(8,128)(2,1)S(1)}, u32[]{:S(2)}, u32[]{:S(2)}) collective-permute-start(bf16[1,128,128]{2,1,0:T(8,128)(2,1)S(1)} %get-tuple-element.35), channel_id=1, source_target_pairs={{0,8},{4,12},{8,0},{12,4},{1,9},{5,13},{9,1},{13,5},{2,10},{6,14},... | collective-permute-start | bytes 98312 | tf_op jit(solution)/shard_map/ppermute | solution.py:34
  8.4 2.4 %collective-permute-done.3.refs_2_ = bf16[1,128,128]{2,1,0:T(8,128)(2,1)S(1)} collective-permute-done((bf16[1,128,128]{2,1,0:T(8,128)(2,1)S(1)}, bf16[1,128,128]{2,1,0:T(8,128)(2,1)S(1)}, u32[]{:S(2)}, u32[]{:S(2)}) %collective-permute-start.3) | collective-permute-done | bytes 32800 | tf_op jit(solution)/shard_map/ppermute | solution.py:34
  10.8 0.0 collective-permute-done.refs_1_
  10.8 0.6 %collective-permute-done.1.refs_2_ = bf16[216,128]{1,0:T(8,128)(2,1)S(1)} collective-permute-done((bf16[216,128]{1,0:T(8,128)(2,1)S(1)}, bf16[216,128]{1,0:T(8,128)(2,1)S(1)}, u32[]{:S(2)}, u32[]{:S(2)}) %collective-permute-start.1) | collective-permute-done | bytes 55328 | tf_op jit(solution)/shard_map/ppermute | solution.py:34
  11.4 0.0 collective-permute-done.2.refs_3_
  11.4 0.0 copy-start.1
  11.4 0.1 shard_map.101
  11.5 1.6 %collective-permute-start.4 = (bf16[3,128,128]{2,1,0:T(8,128)(2,1)S(1)}, bf16[3,128,128]{2,1,0:T(8,128)(2,1)S(1)}, u32[]{:S(2)}, u32[]{:S(2)}) collective-permute-start(bf16[3,128,128]{2,1,0:T(8,128)(2,1)S(1)} %get-tuple-element.40), channel_id=1, source_target_pairs={{0,8},{4,12},{8,0},{12,4},{1,9},{5,13},{9,1},{13,5},{2,10},{6,14},... | collective-permute-start | bytes 294920 | tf_op jit(solution)/shard_map/ppermute | solution.py:34
  13.1 0.0 collective-permute-start.7
  13.1 0.5 %collective-permute-start.5 = (bf16[1,128,128]{2,1,0:T(8,128)(2,1)S(1)}, bf16[1,128,128]{2,1,0:T(8,128)(2,1)S(1)}, u32[]{:S(2)}, u32[]{:S(2)}) collective-permute-start(bf16[1,128,128]{2,1,0:T(8,128)(2,1)S(1)} %collective-permute-done.3.refs_2_), channel_id=1, source_target_pairs={{0,4},{4,0},{8,12},{12,8},{1,5},{5,1},{9,13},{13,9},{2,6},{6,2},{1... | collective-permute-start | bytes 98312 | tf_op jit(solution)/shard_map/ppermute | solution.py:34
  13.6 0.0 collective-permute-start.6
  14.2 0.0 copy-done.1
  14.3 0.0 copy-start
  14.3 1.1 %copy-done = bf16[384,1024]{1,0:T(8,128)(2,1)S(1)} copy-done((bf16[384,1024]{1,0:T(8,128)(2,1)S(1)}, bf16[384,1024]{1,0:T(8,128)(2,1)}, u32[]{:S(2)}) %copy-start) | copy-done | bytes 786456
  15.4 0.3 %shard_map.102 = f32[4,8,1024]{2,1,0:T(8,128)S(1)} custom-call(s32[1]{0:T(128)S(6)} %copy.11.layer_ref, bf16[32,384]{1,0:T(8,128)(2,1)S(1)} %get-tuple-element.43.patch_ref, bf16[384,1024]{1,0:T(8,128)(2,1)S(1)} %copy-done, f32[8,1024]{1,0:T(8,128)S(1)} %copy-done.1), custom_call_target="tpu_custom_call" | custom-call | flops 25165824 | bytes 786432 | tf_op jit(solution)/shard_map/pallas_call | solution.py:235
  15.7 0.0 collective-permute-done.6.refs_1_.refs_4_
  15.7 0.0 collective-permute-done.5.refs_3_
  15.7 0.5 %collective-permute-done.4.refs_6_ = bf16[3,128,128]{2,1,0:T(8,128)(2,1)S(1)} collective-permute-done((bf16[3,128,128]{2,1,0:T(8,128)(2,1)S(1)}, bf16[3,128,128]{2,1,0:T(8,128)(2,1)S(1)}, u32[]{:S(2)}, u32[]{:S(2)}) %collective-permute-start.4) | collective-permute-done | bytes 98336 | tf_op jit(solution)/shard_map/ppermute | solution.py:34
  16.2 0.1 collective-permute-start.8
  16.3 0.0 collective-permute-done.7.refs_5_
  16.3 0.5 %shard_map.103 = (f32[2,128,128]{2,1,0:T(8,128)S(1)}, f32[2,128,128]{2,1,0:T(8,128)S(1)}, f32[2,128,128]{2,1,0:T(8,128)S(1)}) custom-call(bf16[3,64,128]{2,1,0:T(8,128)(2,1)S(1)} %get-tuple-element.45.refs_0_.refs_3_, bf16[1,64,128]{2,1,0:T(8,128)(2,1)S(1)} %collective-permute-done.6.refs_1_.refs_4_, ...), custom_call_target="tpu_custom_call" | custom-call | flops 54525952 | bytes 425984 | tf_op jit(solution)/shard_map/pallas_call | solution.py:235
  16.8 0.7 %collective-permute-done.8.refs_5_ = bf16[3,128,128]{2,1,0:T(8,128)(2,1)S(1)} collective-permute-done((bf16[3,128,128]{2,1,0:T(8,128)(2,1)S(1)}, bf16[3,128,128]{2,1,0:T(8,128)(2,1)S(1)}, u32[]{:S(2)}, u32[]{:S(2)}) %collective-permute-start.8) | collective-permute-done | bytes 98336 | tf_op jit(solution)/shard_map/ppermute | solution.py:34
  17.5 0.4 %shard_map.104 = (bf16[64,128]{1,0:T(8,128)(2,1)S(1)}, f32[64,128]{1,0:T(8,128)S(1)}, bf16[128,128]{1,0:T(8,128)(2,1)S(1)}) custom-call(f32[2,128,128]{2,1,0:T(8,128)S(1)} %get-tuple-element.51.refs_0_, f32[2,128,128]{2,1,0:T(8,128)S(1)} %get-tuple-element.52.refs_1_, f32[2,128,128]{2,1,0:T(8,128)S(1)} %get-tuple-element.53.refs_2_, ...), custom_call_target="tpu_custom_call" | custom-call | flops 12582912 | bytes 98304 | tf_op jit(solution)/shard_map/pallas_call | solution.py:235
  17.9 2.3 %collective-permute-start.10 = (bf16[128,128]{1,0:T(8,128)(2,1)S(1)}, bf16[128,128]{1,0:T(8,128)(2,1)S(1)}, u32[]{:S(2)}, u32[]{:S(2)}) collective-permute-start(bf16[128,128]{1,0:T(8,128)(2,1)S(1)} %get-tuple-element.56), channel_id=1, source_target_pairs={{0,2},{1,3},{2,0},{3,1},{4,7},{5,6},{6,5},{7,4},{8,10},{9,11},{10,... | collective-permute-start | bytes 98312 | tf_op jit(solution)/shard_map/ppermute | solution.py:257
  20.2 0.8 %collective-permute-start.9 = (f32[64,128]{1,0:T(8,128)S(1)}, f32[64,128]{1,0:T(8,128)S(1)}, u32[]{:S(2)}, u32[]{:S(2)}) collective-permute-start(f32[64,128]{1,0:T(8,128)S(1)} %get-tuple-element.55), channel_id=1, source_target_pairs={{0,1},{1,0},{2,3},{3,2},{4,5},{5,4},{6,7},{7,6},{8,9},{9,8},{10,11... | collective-permute-start | bytes 98312 | tf_op jit(solution)/shard_map/ppermute | solution.py:34
  21.1 2.2 %collective-permute-done.10.refs_0_ = bf16[128,128]{1,0:T(8,128)(2,1)S(1)} collective-permute-done((bf16[128,128]{1,0:T(8,128)(2,1)S(1)}, bf16[128,128]{1,0:T(8,128)(2,1)S(1)}, u32[]{:S(2)}, u32[]{:S(2)}) %collective-permute-start.10) | collective-permute-done | bytes 32800 | tf_op jit(solution)/shard_map/ppermute | solution.py:257
  23.2 0.0 collective-permute-start.11
  23.2 0.9 %collective-permute-done.9.near_ref = f32[64,128]{1,0:T(8,128)S(1)} collective-permute-done((f32[64,128]{1,0:T(8,128)S(1)}, f32[64,128]{1,0:T(8,128)S(1)}, u32[]{:S(2)}, u32[]{:S(2)}) %collective-permute-start.9) | collective-permute-done | bytes 32800 | tf_op jit(solution)/shard_map/ppermute | solution.py:34
  24.1 0.3 %collective-permute-done.11.refs_1_ = bf16[128,128]{1,0:T(8,128)(2,1)S(1)} collective-permute-done((bf16[128,128]{1,0:T(8,128)(2,1)S(1)}, bf16[128,128]{1,0:T(8,128)(2,1)S(1)}, u32[]{:S(2)}, u32[]{:S(2)}) %collective-permute-start.11) | collective-permute-done | bytes 32800 | tf_op jit(solution)/shard_map/ppermute | solution.py:34
  24.4 0.7 %shard_map.105 = bf16[32,1024]{1,0:T(8,128)(2,1)} custom-call(f32[32,1024]{1,0:T(8,128)S(1)} %bitcast.3, bf16[64,128]{1,0:T(8,128)(2,1)S(1)} %get-tuple-element.54.own_ref, f32[64,128]{1,0:T(8,128)S(1)} %collective-permute-done.9.near_ref, bf16[128,128]{1,0:T(8,128)(2,1)S(1)} %collective-permute-done.10.refs_0_, ...), custom_call_target="tpu_custom_call" | custom-call | tf_op jit(solution)/shard_map/pallas_call | solution.py:235
Async XLA Ops:
  1.2 9.6 %collective-permute-start = (bf16[216,128]{1,0:T(8,128)(2,1)S(1)}, bf16[216,128]{1,0:T(8,128)(2,1)S(1)}, u32[]{:S(2)}, u32[]{:S(2)}) collective-permute-start(bf16[216,128]{1,0:T(8,128)(2,1)S(1)} %get-tuple-element.32), channel_id=1, source_target_pairs={{0,2},{1,3},{2,0},{3,1},{4,6},{5,7},{6,4},{7,5},{8,10},{9,11},{10,... | collective-permute-start | bytes 165896 | tf_op jit(solution)/shard_map/ppermute | solution.py:34
  5.3 6.1 %collective-permute-start.1 = (bf16[216,128]{1,0:T(8,128)(2,1)S(1)}, bf16[216,128]{1,0:T(8,128)(2,1)S(1)}, u32[]{:S(2)}, u32[]{:S(2)}) collective-permute-start(bf16[216,128]{1,0:T(8,128)(2,1)S(1)} %get-tuple-element.33), channel_id=1, source_target_pairs={{0,3},{1,2},{2,1},{3,0},{4,7},{5,6},{6,5},{7,4},{8,11},{9,10},{10,... | collective-permute-start | bytes 165896 | tf_op jit(solution)/shard_map/ppermute | solution.py:34
  6.7 4.7 %collective-permute-start.2 = (bf16[216,128]{1,0:T(8,128)(2,1)S(1)}, bf16[216,128]{1,0:T(8,128)(2,1)S(1)}, u32[]{:S(2)}, u32[]{:S(2)}) collective-permute-start(bf16[216,128]{1,0:T(8,128)(2,1)S(1)} %get-tuple-element.34), channel_id=1, source_target_pairs={{0,1},{1,0},{2,3},{3,2},{4,5},{5,4},{6,7},{7,6},{8,9},{9,8},{10,11... | collective-permute-start | bytes 165896 | tf_op jit(solution)/shard_map/ppermute | solution.py:34
  6.9 3.9 %collective-permute-start.3 = (bf16[1,128,128]{2,1,0:T(8,128)(2,1)S(1)}, bf16[1,128,128]{2,1,0:T(8,128)(2,1)S(1)}, u32[]{:S(2)}, u32[]{:S(2)}) collective-permute-start(bf16[1,128,128]{2,1,0:T(8,128)(2,1)S(1)} %get-tuple-element.35), channel_id=1, source_target_pairs={{0,8},{4,12},{8,0},{12,4},{1,9},{5,13},{9,1},{13,5},{2,10},{6,14},... | collective-permute-start | bytes 98312 | tf_op jit(solution)/shard_map/ppermute | solution.py:34
  11.4 2.8 %copy-start.1 = (f32[8,1024]{1,0:T(8,128)S(1)}, f32[8,1024]{1,0:T(8,128)}, u32[]{:S(2)}) copy-start(f32[8,1024]{1,0:T(8,128)} %gain_ref.1) | copy-start | bytes 98308
  11.5 4.7 %collective-permute-start.4 = (bf16[3,128,128]{2,1,0:T(8,128)(2,1)S(1)}, bf16[3,128,128]{2,1,0:T(8,128)(2,1)S(1)}, u32[]{:S(2)}, u32[]{:S(2)}) collective-permute-start(bf16[3,128,128]{2,1,0:T(8,128)(2,1)S(1)} %get-tuple-element.40), channel_id=1, source_target_pairs={{0,8},{4,12},{8,0},{12,4},{1,9},{5,13},{9,1},{13,5},{2,10},{6,14},... | collective-permute-start | bytes 294920 | tf_op jit(solution)/shard_map/ppermute | solution.py:34
  13.1 3.2 %collective-permute-start.7 = (bf16[4,128,128]{2,1,0:T(8,128)(2,1)S(1)}, bf16[4,128,128]{2,1,0:T(8,128)(2,1)S(1)}, u32[]{:S(2)}, u32[]{:S(2)}) collective-permute-start(bf16[4,128,128]{2,1,0:T(8,128)(2,1)S(1)} %get-tuple-element.49.refs_4_), channel_id=1, source_target_pairs={{0,4},{4,0},{8,12},{12,8},{1,5},{5,1},{9,13},{13,9},{2,6},{6,2},{1... | collective-permute-start | bytes 393224 | tf_op jit(solution)/shard_map/ppermute | solution.py:34
  13.1 2.6 %collective-permute-start.5 = (bf16[1,128,128]{2,1,0:T(8,128)(2,1)S(1)}, bf16[1,128,128]{2,1,0:T(8,128)(2,1)S(1)}, u32[]{:S(2)}, u32[]{:S(2)}) collective-permute-start(bf16[1,128,128]{2,1,0:T(8,128)(2,1)S(1)} %collective-permute-done.3.refs_2_), channel_id=1, source_target_pairs={{0,4},{4,0},{8,12},{12,8},{1,5},{5,1},{9,13},{13,9},{2,6},{6,2},{1... | collective-permute-start | bytes 98312 | tf_op jit(solution)/shard_map/ppermute | solution.py:34
  13.6 2.1 %collective-permute-start.6 = (bf16[1,64,128]{2,1,0:T(8,128)(2,1)S(1)}, bf16[1,64,128]{2,1,0:T(8,128)(2,1)S(1)}, u32[]{:S(2)}, u32[]{:S(2)}) collective-permute-start(bf16[1,64,128]{2,1,0:T(8,128)(2,1)S(1)} %get-tuple-element.42), channel_id=1, source_target_pairs={{0,4},{4,0},{8,12},{12,8},{1,5},{5,1},{9,13},{13,9},{2,6},{6,2},{1... | collective-permute-start | bytes 49160 | tf_op jit(solution)/shard_map/ppermute | solution.py:34
  14.3 1.1 %copy-start = (bf16[384,1024]{1,0:T(8,128)(2,1)S(1)}, bf16[384,1024]{1,0:T(8,128)(2,1)}, u32[]{:S(2)}) copy-start(bf16[384,1024]{1,0:T(8,128)(2,1)} %weight_ref.1) | copy-start | bytes 2359300
  16.2 1.3 %collective-permute-start.8 = (bf16[3,128,128]{2,1,0:T(8,128)(2,1)S(1)}, bf16[3,128,128]{2,1,0:T(8,128)(2,1)S(1)}, u32[]{:S(2)}, u32[]{:S(2)}) collective-permute-start(bf16[3,128,128]{2,1,0:T(8,128)(2,1)S(1)} %collective-permute-done.4.refs_6_), channel_id=1, source_target_pairs={{0,4},{4,0},{8,12},{12,8},{1,5},{5,1},{9,13},{13,9},{2,6},{6,2},{1... | collective-permute-start | bytes 294920 | tf_op jit(solution)/shard_map/ppermute | solution.py:34
  17.9 5.3 %collective-permute-start.10 = (bf16[128,128]{1,0:T(8,128)(2,1)S(1)}, bf16[128,128]{1,0:T(8,128)(2,1)S(1)}, u32[]{:S(2)}, u32[]{:S(2)}) collective-permute-start(bf16[128,128]{1,0:T(8,128)(2,1)S(1)} %get-tuple-element.56), channel_id=1, source_target_pairs={{0,2},{1,3},{2,0},{3,1},{4,7},{5,6},{6,5},{7,4},{8,10},{9,11},{10,... | collective-permute-start | bytes 98312 | tf_op jit(solution)/shard_map/ppermute | solution.py:257
  20.2 3.9 %collective-permute-start.9 = (f32[64,128]{1,0:T(8,128)S(1)}, f32[64,128]{1,0:T(8,128)S(1)}, u32[]{:S(2)}, u32[]{:S(2)}) collective-permute-start(f32[64,128]{1,0:T(8,128)S(1)} %get-tuple-element.55), channel_id=1, source_target_pairs={{0,1},{1,0},{2,3},{3,2},{4,5},{5,4},{6,7},{7,6},{8,9},{9,8},{10,11... | collective-permute-start | bytes 98312 | tf_op jit(solution)/shard_map/ppermute | solution.py:34
  23.2 1.2 %collective-permute-start.11 = (bf16[128,128]{1,0:T(8,128)(2,1)S(1)}, bf16[128,128]{1,0:T(8,128)(2,1)S(1)}, u32[]{:S(2)}, u32[]{:S(2)}) collective-permute-start(bf16[128,128]{1,0:T(8,128)(2,1)S(1)} %collective-permute-done.10.refs_0_), channel_id=1, source_target_pairs={{0,4},{4,0},{8,12},{12,8},{1,5},{5,1},{9,13},{13,9},{2,6},{6,2},{1... | collective-permute-start | bytes 98312 | tf_op jit(solution)/shard_map/ppermute | solution.py:34

commit v15 on v14

--- a/solution.py
+++ b/solution.py
@@ -21,8 +21,16 @@
     return me ^ step
 
 
-def steps_in(owners):
+def steps_in(owners, side):
+    if side:
+        return list(range(owners))
     return sorted(range(owners), key=lambda step: (step > 0, -step.bit_length(), step))
+
+
+def partners_in(owners):
+    me, odd = lax.axis_index("ulysses"), lax.axis_index("blk") & 1
+    both = zip(steps_in(owners, 0), steps_in(owners, 1))
+    return [partner(me, step + odd * (other - step)) for step, other in both]
 
 
 def step_pairs(owners):
@@ -48,7 +56,6 @@
     rows, feats = q_ref.shape
     share = feats // owners
     slab_rows, width = rows // owners, control_ref.shape[1]
-    me = lax.axis_index("ulysses")
     copies[0].wait()
     copies[1].wait()
     norm_ref[0] = normed(k_ref[...], kg_ref[...]).astype(jnp.bfloat16)
@@ -60,15 +67,14 @@
     norm_ref[1] = v_ref[...]
     patches = control_ref[...].astype(jnp.float32)
     slabs = [patches[j * slab_rows : (j + 1) * slab_rows] for j in range(owners)]
-    for step, out_ref in zip(steps_in(owners), out_refs):
-        to = partner(me, step)
+    for slot, (to, out_ref) in enumerate(zip(partners_in(owners), out_refs)):
         at = 0
         for i in range(3):
             for head in range(share // HEAD_DIM):
                 cols = pl.ds(pl.multiple_of(to * share + head * HEAD_DIM, HEAD_DIM), HEAD_DIM)
                 lines = norm_ref[i, :, cols]
                 out_ref[at : at + rows] = lines
-                if step == 0 and i < 2:
+                if slot == 0 and i < 2:
                     own_ref[0, at : at + rows] = lines
                 at = at + rows
         slab = slabs[0]
@@ -85,14 +91,15 @@
     owners = len(got_refs)
     slab_rows, width = rows // owners, patch_ref.shape[1]
     size, lines = pair_ref.shape[1], ask_ref.shape[1]
-    asks = {step: ref.at[size : size + lines] for step, ref in zip(steps_in(owners), got_refs)}
-    ask_ref[0] = asks[0][...]
-    ask_ref[1] = asks[1][...]
+    views = [ref.at[size : size + lines] for ref in got_refs]
+    ask_ref[0] = views[0][...]
     odd = lax.axis_index("blk") & 1
     for side in range(2):
 
         @pl.when(odd == side)
         def _():
+            asks = dict(zip(steps_in(owners, side), views))
+            ask_ref[1] = asks[1][...]
             for i, step in enumerate(step_pairs(owners)):
                 ask_ref[2 + i] = asks[step + side][...]
                 give_ref[i] = asks[step + 1 - side][...]
@@ -203,9 +210,8 @@
     owners, slab_rows, _ = out_ref.shape
     hint = jnp.dot(patch_ref[...], weight_ref[...], preferred_element_type=jnp.float32)
     hint = hint.astype(jnp.bfloat16).astype(jnp.float32) * gain_ref[pl.ds(layer_ref[0], 1), :]
-    me = lax.axis_index("ulysses")
-    for i, step in enumerate(steps_in(owners)):
-        out_ref[partner(me, step)] = hint[i * slab_rows : (i + 1) * slab_rows]
+    for i, source in enumerate(partners_in(owners)):
+        out_ref[source] = hint[i * slab_rows : (i + 1) * slab_rows]
 
 
 def finish_kernel(owners, hint_ref, own_ref, near_ref, *refs):
@@ -247,16 +253,6 @@
     return jax.ShapeDtypeStruct(dims, dtype)
 
 
-def swap_far(array, step):
-    blocks, owners = lax.axis_size("blk"), lax.axis_size("ulysses")
-    pairs = [
-        (block * owners + i, block * owners + partner(i, step + (block & 1)))
-        for block in range(blocks)
-        for i in range(owners)
-    ]
-    return lax.ppermute(array, ("blk", "ulysses"), pairs)
-
-
 def gather(held, step, axis):
     while step:
         held = held + [swap(array, axis, step) for array in held]
@@ -264,8 +260,19 @@
     return held
 
 
-def exchange(arrays, steps, axis):
-    return [swap(array, axis, step) if step else array for step, array in zip(steps, arrays)]
+def swap_sides(array, steps):
+    blocks, owners = lax.axis_size("blk"), lax.axis_size("ulysses")
+    pairs = [
+        (block * owners + i, block * owners + partner(i, steps[block & 1]))
+        for block in range(blocks)
+        for i in range(owners)
+    ]
+    return lax.ppermute(array, ("blk", "ulysses"), pairs)
+
+
+def exchange(arrays):
+    both = zip(steps_in(len(arrays), 0), steps_in(len(arrays), 1))
+    return [swap_sides(array, steps) if any(steps) else array for array, steps in zip(arrays, both)]
 
 
 def shards(
@@ -311,7 +318,7 @@
     )
     half = lax.axis_size("blk") // 2
     own_moved = swap(sent[owners], "blk", half)
-    got, own_moved = lax.optimization_barrier((exchange(sent[:owners], steps_in(owners), "ulysses"), own_moved))
+    got, own_moved = lax.optimization_barrier((exchange(sent[:owners]), own_moved))
     pairs, rest, patches, asks, gives = call(
         functools.partial(sort_kernel, rows),
         [
@@ -368,7 +375,9 @@
         flops=2 * many * sum(array.size for array in late),
         nbytes=2 * sum(array.size for array in late),
     )
-    kept = [swap_far(array, step) for array, step in zip(mixed[2:], step_pairs(owners))]
+    kept = [
+        swap_sides(array, (step, step + 1)) for array, step in zip(mixed[2:], step_pairs(owners))
+    ]
     near = swap(mixed[1], "ulysses", 1)
     far = [array for one in kept for array in (one, swap(one, "blk", 1))]
     return call(

time: 25.3 us -> 26.3 us (1.040)
  waiting for transfers between devices: 7.65 us -> 8.82 us
    ppermute x11 -> x8, starting transfers between devices: 10.1 us -> 4.84 us  [swap(): lax.ppermute(array, axis, [(i, partner(i, step)) for i in range(size)])]
    ppermute x1 -> x4, starting transfers between devices: 2.31 us -> 7.41 us  [swap_sides(): return lax.ppermute(array, ('blk', 'ulysses'), pairs)]
    ppermute x1 -> x4, waiting for transfers between devices: 2.16 us -> 3.93 us  [swap_sides(): return lax.ppermute(array, ('blk', 'ulysses'), pairs)]
    ppermute x11 -> x8, waiting for transfers between devices: 5.49 us -> 4.89 us  [swap(): lax.ppermute(array, axis, [(i, partner(i, step)) for i in range(size)])]
  transfers between devices with their start and end apart: 12 -> 12, of which waited for: 7 -> 8; matrix products, arithmetic and copies ran while one was open for 0% -> 0% of each run, Pallas kernels for 3% -> 3%
where the time goes in v15:
time: 26.3 us; the launch traced here: 26.1 us
  starting transfers between devices  12.2 us (46%)
  waiting for transfers between devices  8.82 us (34%)
  Pallas kernels  3.14 us (12%)
  local copies, waits for them, and re-layouts  1.13 us (4%)
  between operations  0.73 us (3%)
    ppermute x4, starting transfers between devices, swap_sides(): return lax.ppermute(array, ('blk', 'ulysses'), pairs)  7.41 us
    ppermute x8, waiting for transfers between devices, swap(): lax.ppermute(array, axis, [(i, partner(i, step)) for i in range(size)])  4.89 us
    ppermute x8, starting transfers between devices, swap(): lax.ppermute(array, axis, [(i, partner(i, step)) for i in range(size)])  4.84 us
    ppermute x4, waiting for transfers between devices, swap_sides(): return lax.ppermute(array, ('blk', 'ulysses'), pairs)  3.93 us
    pallas_call x6, Pallas kernels, call(): pl.pallas_call(kernel, out_shape=out_shape, in_specs=specs, out_specs=jax...  3.14 us
    unnamed x4, local copies, waits for them, and re-layouts  1.13 us
  transfers between devices with their start and end apart: 12, of which 8 were waited for; matrix products, arithmetic and copies ran while one was open for 0% of the time, Pallas kernels for 3%

profile of v15, /device:TPU:0, one launch (start us, length us, event | category | flops | bytes accessed | tf_op | source)
XLA Modules:
  0.0 26.1 jit_solution(7629265479604631238)
XLA Ops:
  0.0 1.2 %shard_map.100 = (bf16[216,128]{1,0:T(8,128)(2,1)S(1)}, bf16[216,128]{1,0:T(8,128)(2,1)S(1)}, bf16[216,128]{1,0:T(8,128)(2,1)S(1)}, bf16[216,128]{1,0:T(8,128)(2,1)S(1)}, bf16[1,128,128]{2,1,0:T(8,128)(2,1)S(1)}) custom-call(f32[1,1024]{1,0:T(1,128)} %bitcast.4, bf16[32,1024]{1,0:T(8,128)(2,1)} %refs_1_.1, f32[1,1024]{1,0:T(1,128)} %bitcast.5, ...), custom_call_target="tpu_custom_call" | custom-call | tf_op jit(solution)/shard_map/pallas_call | solution.py:241
  1.2 4.1 %collective-permute-start = (bf16[216,128]{1,0:T(8,128)(2,1)S(1)}, bf16[216,128]{1,0:T(8,128)(2,1)S(1)}, u32[]{:S(2)}, u32[]{:S(2)}) collective-permute-start(bf16[216,128]{1,0:T(8,128)(2,1)S(1)} %get-tuple-element.32), channel_id=1, source_target_pairs={{0,2},{1,3},{2,0},{3,1},{4,5},{5,4},{6,7},{7,6},{8,10},{9,11},{10,... | collective-permute-start | bytes 165896 | tf_op jit(solution)/shard_map/ppermute | solution.py:270
  5.3 1.3 %collective-permute-start.1 = (bf16[216,128]{1,0:T(8,128)(2,1)S(1)}, bf16[216,128]{1,0:T(8,128)(2,1)S(1)}, u32[]{:S(2)}, u32[]{:S(2)}) collective-permute-start(bf16[216,128]{1,0:T(8,128)(2,1)S(1)} %get-tuple-element.33), channel_id=1, source_target_pairs={{0,3},{1,2},{2,1},{3,0},{4,6},{5,7},{6,4},{7,5},{8,11},{9,10},{10,... | collective-permute-start | bytes 165896 | tf_op jit(solution)/shard_map/ppermute | solution.py:270
  6.7 0.2 collective-permute-start.2
  6.9 1.5 %collective-permute-start.3 = (bf16[1,128,128]{2,1,0:T(8,128)(2,1)S(1)}, bf16[1,128,128]{2,1,0:T(8,128)(2,1)S(1)}, u32[]{:S(2)}, u32[]{:S(2)}) collective-permute-start(bf16[1,128,128]{2,1,0:T(8,128)(2,1)S(1)} %get-tuple-element.35), channel_id=1, source_target_pairs={{0,8},{4,12},{8,0},{12,4},{1,9},{5,13},{9,1},{13,5},{2,10},{6,14},... | collective-permute-start | bytes 98312 | tf_op jit(solution)/shard_map/ppermute | solution.py:42
  8.4 2.4 %collective-permute-done.3.refs_2_ = bf16[1,128,128]{2,1,0:T(8,128)(2,1)S(1)} collective-permute-done((bf16[1,128,128]{2,1,0:T(8,128)(2,1)S(1)}, bf16[1,128,128]{2,1,0:T(8,128)(2,1)S(1)}, u32[]{:S(2)}, u32[]{:S(2)}) %collective-permute-start.3) | collective-permute-done | bytes 32800 | tf_op jit(solution)/shard_map/ppermute | solution.py:42
  10.8 0.0 collective-permute-done.refs_1_
  10.8 1.0 %collective-permute-done.1.refs_2_ = bf16[216,128]{1,0:T(8,128)(2,1)S(1)} collective-permute-done((bf16[216,128]{1,0:T(8,128)(2,1)S(1)}, bf16[216,128]{1,0:T(8,128)(2,1)S(1)}, u32[]{:S(2)}, u32[]{:S(2)}) %collective-permute-start.1) | collective-permute-done | bytes 55328 | tf_op jit(solution)/shard_map/ppermute | solution.py:270
  11.9 0.2 collective-permute-done.2.refs_3_
  12.0 0.0 copy-start.1
  12.0 0.1 shard_map.101
  12.1 1.6 %collective-permute-start.4 = (bf16[3,128,128]{2,1,0:T(8,128)(2,1)S(1)}, bf16[3,128,128]{2,1,0:T(8,128)(2,1)S(1)}, u32[]{:S(2)}, u32[]{:S(2)}) collective-permute-start(bf16[3,128,128]{2,1,0:T(8,128)(2,1)S(1)} %get-tuple-element.40), channel_id=1, source_target_pairs={{0,8},{4,12},{8,0},{12,4},{1,9},{5,13},{9,1},{13,5},{2,10},{6,14},... | collective-permute-start | bytes 294920 | tf_op jit(solution)/shard_map/ppermute | solution.py:42
  13.7 0.0 collective-permute-start.7
  13.7 0.5 %collective-permute-start.5 = (bf16[1,128,128]{2,1,0:T(8,128)(2,1)S(1)}, bf16[1,128,128]{2,1,0:T(8,128)(2,1)S(1)}, u32[]{:S(2)}, u32[]{:S(2)}) collective-permute-start(bf16[1,128,128]{2,1,0:T(8,128)(2,1)S(1)} %collective-permute-done.3.refs_2_), channel_id=1, source_target_pairs={{0,4},{4,0},{8,12},{12,8},{1,5},{5,1},{9,13},{13,9},{2,6},{6,2},{1... | collective-permute-start | bytes 98312 | tf_op jit(solution)/shard_map/ppermute | solution.py:42
  14.2 0.0 collective-permute-start.6
  14.8 0.0 copy-done.1
  14.9 0.0 copy-start
  14.9 1.1 %copy-done = bf16[384,1024]{1,0:T(8,128)(2,1)S(1)} copy-done((bf16[384,1024]{1,0:T(8,128)(2,1)S(1)}, bf16[384,1024]{1,0:T(8,128)(2,1)}, u32[]{:S(2)}) %copy-start) | copy-done | bytes 786456
  16.0 0.3 shard_map.102
  16.2 0.0 collective-permute-done.6.refs_1_.refs_4_
  16.3 0.0 collective-permute-done.5.refs_3_
  16.3 0.5 %collective-permute-done.4.refs_6_ = bf16[3,128,128]{2,1,0:T(8,128)(2,1)S(1)} collective-permute-done((bf16[3,128,128]{2,1,0:T(8,128)(2,1)S(1)}, bf16[3,128,128]{2,1,0:T(8,128)(2,1)S(1)}, u32[]{:S(2)}, u32[]{:S(2)}) %collective-permute-start.4) | collective-permute-done | bytes 98336 | tf_op jit(solution)/shard_map/ppermute | solution.py:42
  16.8 0.1 collective-permute-start.8
  16.9 0.0 collective-permute-done.7.refs_5_
  16.9 0.5 %shard_map.103 = (f32[2,128,128]{2,1,0:T(8,128)S(1)}, f32[2,128,128]{2,1,0:T(8,128)S(1)}, f32[2,128,128]{2,1,0:T(8,128)S(1)}) custom-call(bf16[3,64,128]{2,1,0:T(8,128)(2,1)S(1)} %get-tuple-element.45.refs_0_.refs_3_, bf16[1,64,128]{2,1,0:T(8,128)(2,1)S(1)} %collective-permute-done.6.refs_1_.refs_4_, ...), custom_call_target="tpu_custom_call" | custom-call | flops 54525952 | bytes 425984 | tf_op jit(solution)/shard_map/pallas_call | solution.py:241
  17.4 0.7 %collective-permute-done.8.refs_5_ = bf16[3,128,128]{2,1,0:T(8,128)(2,1)S(1)} collective-permute-done((bf16[3,128,128]{2,1,0:T(8,128)(2,1)S(1)}, bf16[3,128,128]{2,1,0:T(8,128)(2,1)S(1)}, u32[]{:S(2)}, u32[]{:S(2)}) %collective-permute-start.8) | collective-permute-done | bytes 98336 | tf_op jit(solution)/shard_map/ppermute | solution.py:42
  18.1 0.4 %shard_map.104 = (bf16[64,128]{1,0:T(8,128)(2,1)S(1)}, f32[64,128]{1,0:T(8,128)S(1)}, bf16[128,128]{1,0:T(8,128)(2,1)S(1)}) custom-call(f32[2,128,128]{2,1,0:T(8,128)S(1)} %get-tuple-element.51.refs_0_, f32[2,128,128]{2,1,0:T(8,128)S(1)} %get-tuple-element.52.refs_1_, f32[2,128,128]{2,1,0:T(8,128)S(1)} %get-tuple-element.53.refs_2_, ...), custom_call_target="tpu_custom_call" | custom-call | flops 12582912 | bytes 98304 | tf_op jit(solution)/shard_map/pallas_call | solution.py:241
  18.5 1.7 %collective-permute-start.10 = (bf16[128,128]{1,0:T(8,128)(2,1)S(1)}, bf16[128,128]{1,0:T(8,128)(2,1)S(1)}, u32[]{:S(2)}, u32[]{:S(2)}) collective-permute-start(bf16[128,128]{1,0:T(8,128)(2,1)S(1)} %get-tuple-element.56), channel_id=1, source_target_pairs={{0,2},{1,3},{2,0},{3,1},{4,7},{5,6},{6,5},{7,4},{8,10},{9,11},{10,... | collective-permute-start | bytes 98312 | tf_op jit(solution)/shard_map/ppermute | solution.py:270
  20.2 1.2 %collective-permute-start.9 = (f32[64,128]{1,0:T(8,128)S(1)}, f32[64,128]{1,0:T(8,128)S(1)}, u32[]{:S(2)}, u32[]{:S(2)}) collective-permute-start(f32[64,128]{1,0:T(8,128)S(1)} %get-tuple-element.55), channel_id=1, source_target_pairs={{0,1},{1,0},{2,3},{3,2},{4,5},{5,4},{6,7},{7,6},{8,9},{9,8},{10,11... | collective-permute-start | bytes 98312 | tf_op jit(solution)/shard_map/ppermute | solution.py:42
  21.5 2.7 %collective-permute-done.10.refs_0_ = bf16[128,128]{1,0:T(8,128)(2,1)S(1)} collective-permute-done((bf16[128,128]{1,0:T(8,128)(2,1)S(1)}, bf16[128,128]{1,0:T(8,128)(2,1)S(1)}, u32[]{:S(2)}, u32[]{:S(2)}) %collective-permute-start.10) | collective-permute-done | bytes 32800 | tf_op jit(solution)/shard_map/ppermute | solution.py:270
  24.2 0.0 collective-permute-start.11
  24.2 0.3 %collective-permute-done.9.near_ref = f32[64,128]{1,0:T(8,128)S(1)} collective-permute-done((f32[64,128]{1,0:T(8,128)S(1)}, f32[64,128]{1,0:T(8,128)S(1)}, u32[]{:S(2)}, u32[]{:S(2)}) %collective-permute-start.9) | collective-permute-done | bytes 32800 | tf_op jit(solution)/shard_map/ppermute | solution.py:42
  24.5 0.9 %collective-permute-done.11.refs_1_ = bf16[128,128]{1,0:T(8,128)(2,1)S(1)} collective-permute-done((bf16[128,128]{1,0:T(8,128)(2,1)S(1)}, bf16[128,128]{1,0:T(8,128)(2,1)S(1)}, u32[]{:S(2)}, u32[]{:S(2)}) %collective-permute-start.11) | collective-permute-done | bytes 32800 | tf_op jit(solution)/shard_map/ppermute | solution.py:42
  25.4 0.7 %shard_map.105 = bf16[32,1024]{1,0:T(8,128)(2,1)} custom-call(f32[32,1024]{1,0:T(8,128)S(1)} %bitcast.3, bf16[64,128]{1,0:T(8,128)(2,1)S(1)} %get-tuple-element.54.own_ref, f32[64,128]{1,0:T(8,128)S(1)} %collective-permute-done.9.near_ref, bf16[128,128]{1,0:T(8,128)(2,1)S(1)} %collective-permute-done.10.refs_0_, ...), custom_call_target="tpu_custom_call" | custom-call | tf_op jit(solution)/shard_map/pallas_call | solution.py:241
Async XLA Ops:
  1.2 9.6 %collective-permute-start = (bf16[216,128]{1,0:T(8,128)(2,1)S(1)}, bf16[216,128]{1,0:T(8,128)(2,1)S(1)}, u32[]{:S(2)}, u32[]{:S(2)}) collective-permute-start(bf16[216,128]{1,0:T(8,128)(2,1)S(1)} %get-tuple-element.32), channel_id=1, source_target_pairs={{0,2},{1,3},{2,0},{3,1},{4,5},{5,4},{6,7},{7,6},{8,10},{9,11},{10,... | collective-permute-start | bytes 165896 | tf_op jit(solution)/shard_map/ppermute | solution.py:270
  5.3 6.5 %collective-permute-start.1 = (bf16[216,128]{1,0:T(8,128)(2,1)S(1)}, bf16[216,128]{1,0:T(8,128)(2,1)S(1)}, u32[]{:S(2)}, u32[]{:S(2)}) collective-permute-start(bf16[216,128]{1,0:T(8,128)(2,1)S(1)} %get-tuple-element.33), channel_id=1, source_target_pairs={{0,3},{1,2},{2,1},{3,0},{4,6},{5,7},{6,4},{7,5},{8,11},{9,10},{10,... | collective-permute-start | bytes 165896 | tf_op jit(solution)/shard_map/ppermute | solution.py:270
  6.7 5.3 %collective-permute-start.2 = (bf16[216,128]{1,0:T(8,128)(2,1)S(1)}, bf16[216,128]{1,0:T(8,128)(2,1)S(1)}, u32[]{:S(2)}, u32[]{:S(2)}) collective-permute-start(bf16[216,128]{1,0:T(8,128)(2,1)S(1)} %get-tuple-element.34), channel_id=1, source_target_pairs={{0,1},{1,0},{2,3},{3,2},{4,7},{5,6},{6,5},{7,4},{8,9},{9,8},{10,11... | collective-permute-start | bytes 165896 | tf_op jit(solution)/shard_map/ppermute | solution.py:270
  6.9 3.9 %collective-permute-start.3 = (bf16[1,128,128]{2,1,0:T(8,128)(2,1)S(1)}, bf16[1,128,128]{2,1,0:T(8,128)(2,1)S(1)}, u32[]{:S(2)}, u32[]{:S(2)}) collective-permute-start(bf16[1,128,128]{2,1,0:T(8,128)(2,1)S(1)} %get-tuple-element.35), channel_id=1, source_target_pairs={{0,8},{4,12},{8,0},{12,4},{1,9},{5,13},{9,1},{13,5},{2,10},{6,14},... | collective-permute-start | bytes 98312 | tf_op jit(solution)/shard_map/ppermute | solution.py:42
  12.0 2.8 %copy-start.1 = (f32[8,1024]{1,0:T(8,128)S(1)}, f32[8,1024]{1,0:T(8,128)}, u32[]{:S(2)}) copy-start(f32[8,1024]{1,0:T(8,128)} %gain_ref.1) | copy-start | bytes 98308
  12.1 4.7 %collective-permute-start.4 = (bf16[3,128,128]{2,1,0:T(8,128)(2,1)S(1)}, bf16[3,128,128]{2,1,0:T(8,128)(2,1)S(1)}, u32[]{:S(2)}, u32[]{:S(2)}) collective-permute-start(bf16[3,128,128]{2,1,0:T(8,128)(2,1)S(1)} %get-tuple-element.40), channel_id=1, source_target_pairs={{0,8},{4,12},{8,0},{12,4},{1,9},{5,13},{9,1},{13,5},{2,10},{6,14},... | collective-permute-start | bytes 294920 | tf_op jit(solution)/shard_map/ppermute | solution.py:42
  13.7 3.2 %collective-permute-start.7 = (bf16[4,128,128]{2,1,0:T(8,128)(2,1)S(1)}, bf16[4,128,128]{2,1,0:T(8,128)(2,1)S(1)}, u32[]{:S(2)}, u32[]{:S(2)}) collective-permute-start(bf16[4,128,128]{2,1,0:T(8,128)(2,1)S(1)} %get-tuple-element.49.refs_4_), channel_id=1, source_target_pairs={{0,4},{4,0},{8,12},{12,8},{1,5},{5,1},{9,13},{13,9},{2,6},{6,2},{1... | collective-permute-start | bytes 393224 | tf_op jit(solution)/shard_map/ppermute | solution.py:42
  13.7 2.6 %collective-permute-start.5 = (bf16[1,128,128]{2,1,0:T(8,128)(2,1)S(1)}, bf16[1,128,128]{2,1,0:T(8,128)(2,1)S(1)}, u32[]{:S(2)}, u32[]{:S(2)}) collective-permute-start(bf16[1,128,128]{2,1,0:T(8,128)(2,1)S(1)} %collective-permute-done.3.refs_2_), channel_id=1, source_target_pairs={{0,4},{4,0},{8,12},{12,8},{1,5},{5,1},{9,13},{13,9},{2,6},{6,2},{1... | collective-permute-start | bytes 98312 | tf_op jit(solution)/shard_map/ppermute | solution.py:42
  14.2 2.1 %collective-permute-start.6 = (bf16[1,64,128]{2,1,0:T(8,128)(2,1)S(1)}, bf16[1,64,128]{2,1,0:T(8,128)(2,1)S(1)}, u32[]{:S(2)}, u32[]{:S(2)}) collective-permute-start(bf16[1,64,128]{2,1,0:T(8,128)(2,1)S(1)} %get-tuple-element.42), channel_id=1, source_target_pairs={{0,4},{4,0},{8,12},{12,8},{1,5},{5,1},{9,13},{13,9},{2,6},{6,2},{1... | collective-permute-start | bytes 49160 | tf_op jit(solution)/shard_map/ppermute | solution.py:42
  14.9 1.1 %copy-start = (bf16[384,1024]{1,0:T(8,128)(2,1)S(1)}, bf16[384,1024]{1,0:T(8,128)(2,1)}, u32[]{:S(2)}) copy-start(bf16[384,1024]{1,0:T(8,128)(2,1)} %weight_ref.1) | copy-start | bytes 2359300
  16.8 1.3 %collective-permute-start.8 = (bf16[3,128,128]{2,1,0:T(8,128)(2,1)S(1)}, bf16[3,128,128]{2,1,0:T(8,128)(2,1)S(1)}, u32[]{:S(2)}, u32[]{:S(2)}) collective-permute-start(bf16[3,128,128]{2,1,0:T(8,128)(2,1)S(1)} %collective-permute-done.4.refs_6_), channel_id=1, source_target_pairs={{0,4},{4,0},{8,12},{12,8},{1,5},{5,1},{9,13},{13,9},{2,6},{6,2},{1... | collective-permute-start | bytes 294920 | tf_op jit(solution)/shard_map/ppermute | solution.py:42
  18.5 5.7 %collective-permute-start.10 = (bf16[128,128]{1,0:T(8,128)(2,1)S(1)}, bf16[128,128]{1,0:T(8,128)(2,1)S(1)}, u32[]{:S(2)}, u32[]{:S(2)}) collective-permute-start(bf16[128,128]{1,0:T(8,128)(2,1)S(1)} %get-tuple-element.56), channel_id=1, source_target_pairs={{0,2},{1,3},{2,0},{3,1},{4,7},{5,6},{6,5},{7,4},{8,10},{9,11},{10,... | collective-permute-start | bytes 98312 | tf_op jit(solution)/shard_map/ppermute | solution.py:270
  20.2 4.3 %collective-permute-start.9 = (f32[64,128]{1,0:T(8,128)S(1)}, f32[64,128]{1,0:T(8,128)S(1)}, u32[]{:S(2)}, u32[]{:S(2)}) collective-permute-start(f32[64,128]{1,0:T(8,128)S(1)} %get-tuple-element.55), channel_id=1, source_target_pairs={{0,1},{1,0},{2,3},{3,2},{4,5},{5,4},{6,7},{7,6},{8,9},{9,8},{10,11... | collective-permute-start | bytes 98312 | tf_op jit(solution)/shard_map/ppermute | solution.py:42
  24.2 1.2 %collective-permute-start.11 = (bf16[128,128]{1,0:T(8,128)(2,1)S(1)}, bf16[128,128]{1,0:T(8,128)(2,1)S(1)}, u32[]{:S(2)}, u32[]{:S(2)}) collective-permute-start(bf16[128,128]{1,0:T(8,128)(2,1)S(1)} %collective-permute-done.10.refs_0_), channel_id=1, source_target_pairs={{0,4},{4,0},{8,12},{12,8},{1,5},{5,1},{9,13},{13,9},{2,6},{6,2},{1... | collective-permute-start | bytes 98312 | tf_op jit(solution)/shard_map/ppermute | solution.py:42

commit v16 on v14

--- a/solution.py
+++ b/solution.py
@@ -44,22 +44,32 @@
     ]
     for copy in copies:
         copy.start()
-    kg_ref, k_ref, qg_ref, q_ref, v_ref, owner_ref, control_ref = held
+    owner_ref, control_ref, kg_ref, k_ref, qg_ref, q_ref, v_ref = held
     rows, feats = q_ref.shape
     share = feats // owners
     slab_rows, width = rows // owners, control_ref.shape[1]
     me = lax.axis_index("ulysses")
     copies[0].wait()
     copies[1].wait()
-    norm_ref[0] = normed(k_ref[...], kg_ref[...]).astype(jnp.bfloat16)
+    patches = control_ref[...].astype(jnp.float32)
+    slabs = [patches[j * slab_rows : (j + 1) * slab_rows] for j in range(owners)]
+    for step, out_ref in zip(steps_in(owners), out_refs):
+        to = partner(me, step)
+        slab = slabs[0]
+        for j in range(1, owners):
+            slab = jnp.where(owner_ref[0, j] == to, slabs[j], slab)
+        slab = slab.astype(jnp.bfloat16)
+        for tile in range(width // HEAD_DIM):
+            at = 3 * share // HEAD_DIM * rows + tile * slab_rows
+            out_ref[at : at + slab_rows] = slab[:, tile * HEAD_DIM : (tile + 1) * HEAD_DIM]
     copies[2].wait()
     copies[3].wait()
+    norm_ref[0] = normed(k_ref[...], kg_ref[...]).astype(jnp.bfloat16)
+    copies[4].wait()
+    copies[5].wait()
     norm_ref[2] = normed(q_ref[...], qg_ref[...]).astype(jnp.bfloat16)
-    for copy in copies[4:]:
-        copy.wait()
+    copies[6].wait()
     norm_ref[1] = v_ref[...]
-    patches = control_ref[...].astype(jnp.float32)
-    slabs = [patches[j * slab_rows : (j + 1) * slab_rows] for j in range(owners)]
     for step, out_ref in zip(steps_in(owners), out_refs):
         to = partner(me, step)
         at = 0
@@ -71,19 +81,11 @@
                 if step == 0 and i < 2:
                     own_ref[0, at : at + rows] = lines
                 at = at + rows
-        slab = slabs[0]
-        for j in range(1, owners):
-            slab = jnp.where(owner_ref[0, j] == to, slabs[j], slab)
-        slab = slab.astype(jnp.bfloat16)
-        for tile in range(width // HEAD_DIM):
-            out_ref[at : at + slab_rows] = slab[:, tile * HEAD_DIM : (tile + 1) * HEAD_DIM]
-            at = at + slab_rows
-
-
-def sort_kernel(rows, *refs):
-    got_refs, (pair_ref, rest_ref, patch_ref, ask_ref, give_ref) = refs[:-5], refs[-5:]
+
+
+def sort_kernel(*refs):
+    got_refs, (pair_ref, rest_ref, ask_ref, give_ref) = refs[:-4], refs[-4:]
     owners = len(got_refs)
-    slab_rows, width = rows // owners, patch_ref.shape[1]
     size, lines = pair_ref.shape[1], ask_ref.shape[1]
     asks = {step: ref.at[size : size + lines] for step, ref in zip(steps_in(owners), got_refs)}
     ask_ref[0] = asks[0][...]
@@ -101,12 +103,6 @@
         pair_ref[i] = ref[:size]
         if i:
             rest_ref[i - 1] = ref[:size]
-    slabs = [ref[size + lines :].astype(jnp.float32) for ref in got_refs]
-    patches = [
-        jnp.concatenate([slab[i * slab_rows : (i + 1) * slab_rows] for slab in slabs], axis=0)
-        for i in range(width // HEAD_DIM)
-    ]
-    patch_ref[...] = normed(jnp.concatenate(patches, axis=1), 1.0).astype(jnp.bfloat16)
 
 
 def queries_of(ask_ref, taken_ref):
@@ -199,9 +195,18 @@
     fold(rows, asks, refs[2:-outs], use)
 
 
-def hint_kernel(layer_ref, patch_ref, weight_ref, gain_ref, out_ref):
+def hint_kernel(layer_ref, weight_ref, gain_ref, *refs):
+    got_refs, out_ref = refs[:-1], refs[-1]
     owners, slab_rows, _ = out_ref.shape
-    hint = jnp.dot(patch_ref[...], weight_ref[...], preferred_element_type=jnp.float32)
+    tiles = weight_ref.shape[0] // HEAD_DIM
+    start = got_refs[0].shape[0] - tiles * slab_rows
+    slabs = [ref[start:].astype(jnp.float32) for ref in got_refs]
+    patches = [
+        jnp.concatenate([slab[i * slab_rows : (i + 1) * slab_rows] for slab in slabs], axis=0)
+        for i in range(tiles)
+    ]
+    patches = normed(jnp.concatenate(patches, axis=1), 1.0).astype(jnp.bfloat16)
+    hint = jnp.dot(patches, weight_ref[...], preferred_element_type=jnp.float32)
     hint = hint.astype(jnp.bfloat16).astype(jnp.float32) * gain_ref[pl.ds(layer_ref[0], 1), :]
     me = lax.axis_index("ulysses")
     for i, step in enumerate(steps_in(owners)):
@@ -286,13 +291,13 @@
     lines = rows * (feats // owners // HEAD_DIM)
     slab_lines = rows // owners * (width // HEAD_DIM)
     sources = (
+        owner_map,
+        control,
         key_gain.reshape(1, feats),
         key_proj,
         query_gain.reshape(1, feats),
         query_proj,
         value_proj,
-        owner_map,
-        control,
     )
     sources = [pltpu.with_memory_space_constraint(source, pltpu.HBM) for source in sources]
     sent = call(
@@ -312,12 +317,11 @@
     half = lax.axis_size("blk") // 2
     own_moved = swap(sent[owners], "blk", half)
     got, own_moved = lax.optimization_barrier((exchange(sent[:owners], steps_in(owners), "ulysses"), own_moved))
-    pairs, rest, patches, asks, gives = call(
-        functools.partial(sort_kernel, rows),
+    pairs, rest, asks, gives = call(
+        sort_kernel,
         [
             shape((owners, 2 * lines, HEAD_DIM)),
             shape((owners - 1, 2 * lines, HEAD_DIM)),
-            shape((rows, width)),
             shape((owners // 2 + 1, lines, HEAD_DIM)),
             shape((owners // 2 - 1, lines, HEAD_DIM)),
         ],
@@ -327,11 +331,11 @@
     hint = call(
         hint_kernel,
         shape((owners, rows // owners, feats), jnp.float32),
-        [SMEM] + [VMEM] * 3,
+        [SMEM] + [VMEM] * (2 + owners),
         layer_index,
-        patches,
         hint_weight,
         hint_gain,
+        *got,
         flops=2 * rows * width * feats,
         nbytes=2 * width * feats,
     )

time: 25.3 us -> 25.3 us (level)
  no operation moved by 1% of the time
where the time goes in v16:
time: 25.3 us; the launch traced here: 25.1 us
  starting transfers between devices  12.5 us (49%)
  waiting for transfers between devices  7.55 us (30%)
  Pallas kernels  3.14 us (12%)
  local copies, waits for them, and re-layouts  1.13 us (4%)
  between operations  0.73 us (3%)
    ppermute x11, starting transfers between devices, swap(): lax.ppermute(array, axis, [(i, partner(i, step)) for i in range(size)])  10.2 us
    ppermute x11, waiting for transfers between devices, swap(): lax.ppermute(array, axis, [(i, partner(i, step)) for i in range(size)])  5.37 us
    pallas_call x6, Pallas kernels, call(): pl.pallas_call(kernel, out_shape=out_shape, in_specs=specs, out_specs=jax...  3.14 us
    ppermute x1, starting transfers between devices, swap_far(): return lax.ppermute(array, ('blk', 'ulysses'), pairs)  2.3 us
    ppermute x1, waiting for transfers between devices, swap_far(): return lax.ppermute(array, ('blk', 'ulysses'), pairs)  2.17 us
    unnamed x4, local copies, waits for them, and re-layouts  1.13 us
  transfers between devices with their start and end apart: 12, of which 7 were waited for; matrix products, arithmetic and copies ran while one was open for 0% of the time, Pallas kernels for 3%

profile of v16, /device:TPU:0, one launch (start us, length us, event | category | flops | bytes accessed | tf_op | source)
XLA Modules:
  0.0 25.1 jit_solution(694010544064168544)
XLA Ops:
  0.0 1.2 %shard_map.100 = (bf16[216,128]{1,0:T(8,128)(2,1)S(1)}, bf16[216,128]{1,0:T(8,128)(2,1)S(1)}, bf16[216,128]{1,0:T(8,128)(2,1)S(1)}, bf16[216,128]{1,0:T(8,128)(2,1)S(1)}, bf16[1,128,128]{2,1,0:T(8,128)(2,1)S(1)}) custom-call(s32[1,4]{1,0:T(1,128)} %refs_0_.1, bf16[32,384]{1,0:T(8,128)(2,1)} %refs_1_.1, f32[1,1024]{1,0:T(1,128)} %bitcast.4, ...), custom_call_target="tpu_custom_call" | custom-call | tf_op jit(solution)/shard_map/pallas_call | solution.py:240
  1.2 4.1 %collective-permute-start = (bf16[216,128]{1,0:T(8,128)(2,1)S(1)}, bf16[216,128]{1,0:T(8,128)(2,1)S(1)}, u32[]{:S(2)}, u32[]{:S(2)}) collective-permute-start(bf16[216,128]{1,0:T(8,128)(2,1)S(1)} %get-tuple-element.31), channel_id=1, source_target_pairs={{0,2},{1,3},{2,0},{3,1},{4,6},{5,7},{6,4},{7,5},{8,10},{9,11},{10,... | collective-permute-start | bytes 165896 | tf_op jit(solution)/shard_map/ppermute | solution.py:34
  5.3 1.3 %collective-permute-start.1 = (bf16[216,128]{1,0:T(8,128)(2,1)S(1)}, bf16[216,128]{1,0:T(8,128)(2,1)S(1)}, u32[]{:S(2)}, u32[]{:S(2)}) collective-permute-start(bf16[216,128]{1,0:T(8,128)(2,1)S(1)} %get-tuple-element.32), channel_id=1, source_target_pairs={{0,3},{1,2},{2,1},{3,0},{4,7},{5,6},{6,5},{7,4},{8,11},{9,10},{10,... | collective-permute-start | bytes 165896 | tf_op jit(solution)/shard_map/ppermute | solution.py:34
  6.7 0.2 collective-permute-start.2
  6.9 1.5 %collective-permute-start.3 = (bf16[1,128,128]{2,1,0:T(8,128)(2,1)S(1)}, bf16[1,128,128]{2,1,0:T(8,128)(2,1)S(1)}, u32[]{:S(2)}, u32[]{:S(2)}) collective-permute-start(bf16[1,128,128]{2,1,0:T(8,128)(2,1)S(1)} %get-tuple-element.34), channel_id=1, source_target_pairs={{0,8},{4,12},{8,0},{12,4},{1,9},{5,13},{9,1},{13,5},{2,10},{6,14},... | collective-permute-start | bytes 98312 | tf_op jit(solution)/shard_map/ppermute | solution.py:34
  8.4 2.4 %collective-permute-done.3.refs_2_ = bf16[1,128,128]{2,1,0:T(8,128)(2,1)S(1)} collective-permute-done((bf16[1,128,128]{2,1,0:T(8,128)(2,1)S(1)}, bf16[1,128,128]{2,1,0:T(8,128)(2,1)S(1)}, u32[]{:S(2)}, u32[]{:S(2)}) %collective-permute-start.3) | collective-permute-done | bytes 32800 | tf_op jit(solution)/shard_map/ppermute | solution.py:34
  10.8 0.0 collective-permute-done.refs_1_
  10.8 0.6 %collective-permute-done.1.refs_2_ = bf16[216,128]{1,0:T(8,128)(2,1)S(1)} collective-permute-done((bf16[216,128]{1,0:T(8,128)(2,1)S(1)}, bf16[216,128]{1,0:T(8,128)(2,1)S(1)}, u32[]{:S(2)}, u32[]{:S(2)}) %collective-permute-start.1) | collective-permute-done | bytes 55328 | tf_op jit(solution)/shard_map/ppermute | solution.py:34
  11.4 0.0 collective-permute-done.2.refs_3_
  11.4 0.0 copy-start.1
  11.5 1.6 %collective-permute-start.4 = (bf16[3,128,128]{2,1,0:T(8,128)(2,1)S(1)}, bf16[3,128,128]{2,1,0:T(8,128)(2,1)S(1)}, u32[]{:S(2)}, u32[]{:S(2)}) collective-permute-start(bf16[3,128,128]{2,1,0:T(8,128)(2,1)S(1)} %get-tuple-element.39), channel_id=1, source_target_pairs={{0,8},{4,12},{8,0},{12,4},{1,9},{5,13},{9,1},{13,5},{2,10},{6,14},... | collective-permute-start | bytes 294920 | tf_op jit(solution)/shard_map/ppermute | solution.py:34
  13.0 0.0 collective-permute-start.7
  13.0 0.5 %collective-permute-start.5 = (bf16[1,128,128]{2,1,0:T(8,128)(2,1)S(1)}, bf16[1,128,128]{2,1,0:T(8,128)(2,1)S(1)}, u32[]{:S(2)}, u32[]{:S(2)}) collective-permute-start(bf16[1,128,128]{2,1,0:T(8,128)(2,1)S(1)} %collective-permute-done.3.refs_2_), channel_id=1, source_target_pairs={{0,4},{4,0},{8,12},{12,8},{1,5},{5,1},{9,13},{13,9},{2,6},{6,2},{1... | collective-permute-start | bytes 98312 | tf_op jit(solution)/shard_map/ppermute | solution.py:34
  13.5 0.0 collective-permute-start.6
  14.2 0.0 copy-done.1
  14.2 0.0 copy-start
  14.2 1.1 %copy-done = bf16[384,1024]{1,0:T(8,128)(2,1)S(1)} copy-done((bf16[384,1024]{1,0:T(8,128)(2,1)S(1)}, bf16[384,1024]{1,0:T(8,128)(2,1)}, u32[]{:S(2)}) %copy-start) | copy-done | bytes 786456
  15.3 0.3 %shard_map.102 = f32[4,8,1024]{2,1,0:T(8,128)S(1)} custom-call(s32[1]{0:T(128)S(6)} %copy.11.layer_ref, bf16[384,1024]{1,0:T(8,128)(2,1)S(1)} %copy-done, f32[8,1024]{1,0:T(8,128)S(1)} %copy-done.1, bf16[216,128]{1,0:T(8,128)(2,1)S(1)} %get-tuple-element.35.refs_0_, bf16[216,128]{1,0:T(8,128)(2,1)S(1)} %collective-permute-done.refs_1_, ...), custom_call_target="tpu_custom_call" | custom-call | flops 25165824 | bytes 786432 | tf_op jit(solution)/shard_map/pallas_call | solution.py:240
  15.7 0.0 collective-permute-done.6.refs_1_.refs_4_
  15.7 0.0 collective-permute-done.5.refs_3_
  15.7 0.5 %collective-permute-done.4.refs_6_ = bf16[3,128,128]{2,1,0:T(8,128)(2,1)S(1)} collective-permute-done((bf16[3,128,128]{2,1,0:T(8,128)(2,1)S(1)}, bf16[3,128,128]{2,1,0:T(8,128)(2,1)S(1)}, u32[]{:S(2)}, u32[]{:S(2)}) %collective-permute-start.4) | collective-permute-done | bytes 98336 | tf_op jit(solution)/shard_map/ppermute | solution.py:34
  16.2 0.1 collective-permute-start.8
  16.3 0.0 collective-permute-done.7.refs_5_
  16.3 0.5 %shard_map.103 = (f32[2,128,128]{2,1,0:T(8,128)S(1)}, f32[2,128,128]{2,1,0:T(8,128)S(1)}, f32[2,128,128]{2,1,0:T(8,128)S(1)}) custom-call(bf16[3,64,128]{2,1,0:T(8,128)(2,1)S(1)} %get-tuple-element.43.refs_0_.refs_3_, bf16[1,64,128]{2,1,0:T(8,128)(2,1)S(1)} %collective-permute-done.6.refs_1_.refs_4_, ...), custom_call_target="tpu_custom_call" | custom-call | flops 54525952 | bytes 425984 | tf_op jit(solution)/shard_map/pallas_call | solution.py:240
  16.8 0.7 %collective-permute-done.8.refs_5_ = bf16[3,128,128]{2,1,0:T(8,128)(2,1)S(1)} collective-permute-done((bf16[3,128,128]{2,1,0:T(8,128)(2,1)S(1)}, bf16[3,128,128]{2,1,0:T(8,128)(2,1)S(1)}, u32[]{:S(2)}, u32[]{:S(2)}) %collective-permute-start.8) | collective-permute-done | bytes 98336 | tf_op jit(solution)/shard_map/ppermute | solution.py:34
  17.5 0.4 %shard_map.104 = (bf16[64,128]{1,0:T(8,128)(2,1)S(1)}, f32[64,128]{1,0:T(8,128)S(1)}, bf16[128,128]{1,0:T(8,128)(2,1)S(1)}) custom-call(f32[2,128,128]{2,1,0:T(8,128)S(1)} %get-tuple-element.49.refs_0_, f32[2,128,128]{2,1,0:T(8,128)S(1)} %get-tuple-element.50.refs_1_, f32[2,128,128]{2,1,0:T(8,128)S(1)} %get-tuple-element.51.refs_2_, ...), custom_call_target="tpu_custom_call" | custom-call | flops 12582912 | bytes 98304 | tf_op jit(solution)/shard_map/pallas_call | solution.py:240
  17.9 2.3 %collective-permute-start.10 = (bf16[128,128]{1,0:T(8,128)(2,1)S(1)}, bf16[128,128]{1,0:T(8,128)(2,1)S(1)}, u32[]{:S(2)}, u32[]{:S(2)}) collective-permute-start(bf16[128,128]{1,0:T(8,128)(2,1)S(1)} %get-tuple-element.54), channel_id=1, source_target_pairs={{0,2},{1,3},{2,0},{3,1},{4,7},{5,6},{6,5},{7,4},{8,10},{9,11},{10,... | collective-permute-start | bytes 98312 | tf_op jit(solution)/shard_map/ppermute | solution.py:262
  20.2 0.8 %collective-permute-start.9 = (f32[64,128]{1,0:T(8,128)S(1)}, f32[64,128]{1,0:T(8,128)S(1)}, u32[]{:S(2)}, u32[]{:S(2)}) collective-permute-start(f32[64,128]{1,0:T(8,128)S(1)} %get-tuple-element.53), channel_id=1, source_target_pairs={{0,1},{1,0},{2,3},{3,2},{4,5},{5,4},{6,7},{7,6},{8,9},{9,8},{10,11... | collective-permute-start | bytes 98312 | tf_op jit(solution)/shard_map/ppermute | solution.py:34
  21.0 2.2 %collective-permute-done.10.refs_0_ = bf16[128,128]{1,0:T(8,128)(2,1)S(1)} collective-permute-done((bf16[128,128]{1,0:T(8,128)(2,1)S(1)}, bf16[128,128]{1,0:T(8,128)(2,1)S(1)}, u32[]{:S(2)}, u32[]{:S(2)}) %collective-permute-start.10) | collective-permute-done | bytes 32800 | tf_op jit(solution)/shard_map/ppermute | solution.py:262
  23.2 0.0 collective-permute-start.11
  23.2 0.9 %collective-permute-done.9.near_ref = f32[64,128]{1,0:T(8,128)S(1)} collective-permute-done((f32[64,128]{1,0:T(8,128)S(1)}, f32[64,128]{1,0:T(8,128)S(1)}, u32[]{:S(2)}, u32[]{:S(2)}) %collective-permute-start.9) | collective-permute-done | bytes 32800 | tf_op jit(solution)/shard_map/ppermute | solution.py:34
  24.1 0.3 %collective-permute-done.11.refs_1_ = bf16[128,128]{1,0:T(8,128)(2,1)S(1)} collective-permute-done((bf16[128,128]{1,0:T(8,128)(2,1)S(1)}, bf16[128,128]{1,0:T(8,128)(2,1)S(1)}, u32[]{:S(2)}, u32[]{:S(2)}) %collective-permute-start.11) | collective-permute-done | bytes 32800 | tf_op jit(solution)/shard_map/ppermute | solution.py:34
  24.4 0.7 %shard_map.105 = bf16[32,1024]{1,0:T(8,128)(2,1)} custom-call(f32[32,1024]{1,0:T(8,128)S(1)} %bitcast.3, bf16[64,128]{1,0:T(8,128)(2,1)S(1)} %get-tuple-element.52.own_ref, f32[64,128]{1,0:T(8,128)S(1)} %collective-permute-done.9.near_ref, bf16[128,128]{1,0:T(8,128)(2,1)S(1)} %collective-permute-done.10.refs_0_, ...), custom_call_target="tpu_custom_call" | custom-call | tf_op jit(solution)/shard_map/pallas_call | solution.py:240
  (1 shorter events, 0.0 us)
Async XLA Ops:
  1.2 9.6 %collective-permute-start = (bf16[216,128]{1,0:T(8,128)(2,1)S(1)}, bf16[216,128]{1,0:T(8,128)(2,1)S(1)}, u32[]{:S(2)}, u32[]{:S(2)}) collective-permute-start(bf16[216,128]{1,0:T(8,128)(2,1)S(1)} %get-tuple-element.31), channel_id=1, source_target_pairs={{0,2},{1,3},{2,0},{3,1},{4,6},{5,7},{6,4},{7,5},{8,10},{9,11},{10,... | collective-permute-start | bytes 165896 | tf_op jit(solution)/shard_map/ppermute | solution.py:34
  5.3 6.1 %collective-permute-start.1 = (bf16[216,128]{1,0:T(8,128)(2,1)S(1)}, bf16[216,128]{1,0:T(8,128)(2,1)S(1)}, u32[]{:S(2)}, u32[]{:S(2)}) collective-permute-start(bf16[216,128]{1,0:T(8,128)(2,1)S(1)} %get-tuple-element.32), channel_id=1, source_target_pairs={{0,3},{1,2},{2,1},{3,0},{4,7},{5,6},{6,5},{7,4},{8,11},{9,10},{10,... | collective-permute-start | bytes 165896 | tf_op jit(solution)/shard_map/ppermute | solution.py:34
  6.7 4.7 %collective-permute-start.2 = (bf16[216,128]{1,0:T(8,128)(2,1)S(1)}, bf16[216,128]{1,0:T(8,128)(2,1)S(1)}, u32[]{:S(2)}, u32[]{:S(2)}) collective-permute-start(bf16[216,128]{1,0:T(8,128)(2,1)S(1)} %get-tuple-element.33), channel_id=1, source_target_pairs={{0,1},{1,0},{2,3},{3,2},{4,5},{5,4},{6,7},{7,6},{8,9},{9,8},{10,11... | collective-permute-start | bytes 165896 | tf_op jit(solution)/shard_map/ppermute | solution.py:34
  6.9 3.9 %collective-permute-start.3 = (bf16[1,128,128]{2,1,0:T(8,128)(2,1)S(1)}, bf16[1,128,128]{2,1,0:T(8,128)(2,1)S(1)}, u32[]{:S(2)}, u32[]{:S(2)}) collective-permute-start(bf16[1,128,128]{2,1,0:T(8,128)(2,1)S(1)} %get-tuple-element.34), channel_id=1, source_target_pairs={{0,8},{4,12},{8,0},{12,4},{1,9},{5,13},{9,1},{13,5},{2,10},{6,14},... | collective-permute-start | bytes 98312 | tf_op jit(solution)/shard_map/ppermute | solution.py:34
  11.4 2.8 %copy-start.1 = (f32[8,1024]{1,0:T(8,128)S(1)}, f32[8,1024]{1,0:T(8,128)}, u32[]{:S(2)}) copy-start(f32[8,1024]{1,0:T(8,128)} %gain_ref.1) | copy-start | bytes 98308
  11.5 4.7 %collective-permute-start.4 = (bf16[3,128,128]{2,1,0:T(8,128)(2,1)S(1)}, bf16[3,128,128]{2,1,0:T(8,128)(2,1)S(1)}, u32[]{:S(2)}, u32[]{:S(2)}) collective-permute-start(bf16[3,128,128]{2,1,0:T(8,128)(2,1)S(1)} %get-tuple-element.39), channel_id=1, source_target_pairs={{0,8},{4,12},{8,0},{12,4},{1,9},{5,13},{9,1},{13,5},{2,10},{6,14},... | collective-permute-start | bytes 294920 | tf_op jit(solution)/shard_map/ppermute | solution.py:34
  13.0 3.2 %collective-permute-start.7 = (bf16[4,128,128]{2,1,0:T(8,128)(2,1)S(1)}, bf16[4,128,128]{2,1,0:T(8,128)(2,1)S(1)}, u32[]{:S(2)}, u32[]{:S(2)}) collective-permute-start(bf16[4,128,128]{2,1,0:T(8,128)(2,1)S(1)} %get-tuple-element.47.refs_4_), channel_id=1, source_target_pairs={{0,4},{4,0},{8,12},{12,8},{1,5},{5,1},{9,13},{13,9},{2,6},{6,2},{1... | collective-permute-start | bytes 393224 | tf_op jit(solution)/shard_map/ppermute | solution.py:34
  13.0 2.6 %collective-permute-start.5 = (bf16[1,128,128]{2,1,0:T(8,128)(2,1)S(1)}, bf16[1,128,128]{2,1,0:T(8,128)(2,1)S(1)}, u32[]{:S(2)}, u32[]{:S(2)}) collective-permute-start(bf16[1,128,128]{2,1,0:T(8,128)(2,1)S(1)} %collective-permute-done.3.refs_2_), channel_id=1, source_target_pairs={{0,4},{4,0},{8,12},{12,8},{1,5},{5,1},{9,13},{13,9},{2,6},{6,2},{1... | collective-permute-start | bytes 98312 | tf_op jit(solution)/shard_map/ppermute | solution.py:34
  13.5 2.1 %collective-permute-start.6 = (bf16[1,64,128]{2,1,0:T(8,128)(2,1)S(1)}, bf16[1,64,128]{2,1,0:T(8,128)(2,1)S(1)}, u32[]{:S(2)}, u32[]{:S(2)}) collective-permute-start(bf16[1,64,128]{2,1,0:T(8,128)(2,1)S(1)} %get-tuple-element.41), channel_id=1, source_target_pairs={{0,4},{4,0},{8,12},{12,8},{1,5},{5,1},{9,13},{13,9},{2,6},{6,2},{1... | collective-permute-start | bytes 49160 | tf_op jit(solution)/shard_map/ppermute | solution.py:34
  14.2 1.1 %copy-start = (bf16[384,1024]{1,0:T(8,128)(2,1)S(1)}, bf16[384,1024]{1,0:T(8,128)(2,1)}, u32[]{:S(2)}) copy-start(bf16[384,1024]{1,0:T(8,128)(2,1)} %weight_ref.1) | copy-start | bytes 2359300
  16.2 1.3 %collective-permute-start.8 = (bf16[3,128,128]{2,1,0:T(8,128)(2,1)S(1)}, bf16[3,128,128]{2,1,0:T(8,128)(2,1)S(1)}, u32[]{:S(2)}, u32[]{:S(2)}) collective-permute-start(bf16[3,128,128]{2,1,0:T(8,128)(2,1)S(1)} %collective-permute-done.4.refs_6_), channel_id=1, source_target_pairs={{0,4},{4,0},{8,12},{12,8},{1,5},{5,1},{9,13},{13,9},{2,6},{6,2},{1... | collective-permute-start | bytes 294920 | tf_op jit(solution)/shard_map/ppermute | solution.py:34
  17.9 5.3 %collective-permute-start.10 = (bf16[128,128]{1,0:T(8,128)(2,1)S(1)}, bf16[128,128]{1,0:T(8,128)(2,1)S(1)}, u32[]{:S(2)}, u32[]{:S(2)}) collective-permute-start(bf16[128,128]{1,0:T(8,128)(2,1)S(1)} %get-tuple-element.54), channel_id=1, source_target_pairs={{0,2},{1,3},{2,0},{3,1},{4,7},{5,6},{6,5},{7,4},{8,10},{9,11},{10,... | collective-permute-start | bytes 98312 | tf_op jit(solution)/shard_map/ppermute | solution.py:262
  20.2 3.9 %collective-permute-start.9 = (f32[64,128]{1,0:T(8,128)S(1)}, f32[64,128]{1,0:T(8,128)S(1)}, u32[]{:S(2)}, u32[]{:S(2)}) collective-permute-start(f32[64,128]{1,0:T(8,128)S(1)} %get-tuple-element.53), channel_id=1, source_target_pairs={{0,1},{1,0},{2,3},{3,2},{4,5},{5,4},{6,7},{7,6},{8,9},{9,8},{10,11... | collective-permute-start | bytes 98312 | tf_op jit(solution)/shard_map/ppermute | solution.py:34
  23.2 1.2 %collective-permute-start.11 = (bf16[128,128]{1,0:T(8,128)(2,1)S(1)}, bf16[128,128]{1,0:T(8,128)(2,1)S(1)}, u32[]{:S(2)}, u32[]{:S(2)}) collective-permute-start(bf16[128,128]{1,0:T(8,128)(2,1)S(1)} %collective-permute-done.10.refs_0_), channel_id=1, source_target_pairs={{0,4},{4,0},{8,12},{12,8},{1,5},{5,1},{9,13},{13,9},{2,6},{6,2},{1... | collective-permute-start | bytes 98312 | tf_op jit(solution)/shard_map/ppermute | solution.py:34

commit v17 on v16

--- a/solution.py
+++ b/solution.py
@@ -214,7 +214,7 @@
 
 
 def finish_kernel(owners, hint_ref, own_ref, near_ref, *refs):
-    far_refs, out_ref = refs[:-1], refs[-1]
+    far_refs, (out_ref, held_ref, copy_sems) = refs[:-3], refs[-3:]
     rows, feats = out_ref.shape
     share = feats // owners
     lines = own_ref.shape[0]
@@ -222,13 +222,23 @@
     parts = [(0, own_ref, 0), (1, near_ref, 0)]
     for step, kept, crossed in zip(step_pairs(owners), far_refs[::2], far_refs[1::2]):
         parts = parts + [(step + odd, kept, 0), (step + 1 - odd, crossed, lines)]
-    for step, ref, first in parts:
-        for head in range(share // HEAD_DIM):
-            start = partner(me, step) * share + head * HEAD_DIM
-            cols = pl.ds(pl.multiple_of(start, HEAD_DIM), HEAD_DIM)
-            at = first + head * rows
-            attended = ref[at : at + rows].astype(jnp.bfloat16).astype(jnp.float32)
-            out_ref[:, cols] = (attended + hint_ref[:, cols]).astype(jnp.bfloat16)
+    pieces = copy_sems.shape[0]
+    many = rows // pieces
+    copies = []
+    for piece in range(pieces):
+        span = pl.ds(piece * many, many)
+        for step, ref, first in parts:
+            for head in range(share // HEAD_DIM):
+                start = partner(me, step) * share + head * HEAD_DIM
+                cols = pl.ds(pl.multiple_of(start, HEAD_DIM), HEAD_DIM)
+                at = first + head * rows + piece * many
+                attended = ref[at : at + many].astype(jnp.bfloat16).astype(jnp.float32)
+                held_ref[span, cols] = (attended + hint_ref[span, cols]).astype(jnp.bfloat16)
+        copy = pltpu.make_async_copy(held_ref.at[span], out_ref.at[span], copy_sems.at[piece])
+        copy.start()
+        copies.append(copy)
+    for copy in copies:
+        copy.wait()
 
 
 VMEM = pl.BlockSpec(memory_space=pltpu.VMEM)
@@ -236,12 +246,12 @@
 HBM = pl.BlockSpec(memory_space=pltpu.HBM)
 
 
-def call(kernel, out_shape, specs, *operands, scratch=(), flops=0, nbytes=0):
+def call(kernel, out_shape, specs, *operands, out=None, scratch=(), flops=0, nbytes=0):
     return pl.pallas_call(
         kernel,
         out_shape=out_shape,
         in_specs=specs,
-        out_specs=jax.tree.map(lambda _: VMEM, out_shape),
+        out_specs=jax.tree.map(lambda _: out or VMEM, out_shape),
         scratch_shapes=scratch,
         compiler_params=pltpu.CompilerParams(vmem_limit_bytes=32 * 2**20),
         cost_estimate=pl.CostEstimate(flops=flops, bytes_accessed=nbytes, transcendentals=0),
@@ -383,6 +393,11 @@
         mixed[0],
         near,
         *far,
+        out=HBM,
+        scratch=[
+            pltpu.VMEM((rows, feats), jnp.bfloat16),
+            pltpu.SemaphoreType.DMA((2 if rows % 32 == 0 else 1,)),
+        ],
     )
 
 

time: 25.3 us -> 25.3 us (level)
  no operation moved by 1% of the time
where the time goes in v17:
time: 25.3 us; the launch traced here: 25.1 us
  starting transfers between devices  12.5 us (49%)
  waiting for transfers between devices  7.55 us (30%)
  Pallas kernels  3.15 us (12%)
  local copies, waits for them, and re-layouts  1.13 us (4%)
  between operations  0.73 us (3%)
    ppermute x11, starting transfers between devices, swap(): lax.ppermute(array, axis, [(i, partner(i, step)) for i in range(size)])  10.2 us
    ppermute x11, waiting for transfers between devices, swap(): lax.ppermute(array, axis, [(i, partner(i, step)) for i in range(size)])  5.37 us
    pallas_call x6, Pallas kernels, call(): pl.pallas_call(kernel, out_shape=out_shape, in_specs=specs, out_specs=jax...  3.15 us
    ppermute x1, starting transfers between devices, swap_far(): return lax.ppermute(array, ('blk', 'ulysses'), pairs)  2.3 us
    ppermute x1, waiting for transfers between devices, swap_far(): return lax.ppermute(array, ('blk', 'ulysses'), pairs)  2.17 us
    unnamed x4, local copies, waits for them, and re-layouts  1.13 us
  transfers between devices with their start and end apart: 12, of which 7 were waited for; matrix products, arithmetic and copies ran while one was open for 0% of the time, Pallas kernels for 3%

profile of v17, /device:TPU:0, one launch (start us, length us, event | category | flops | bytes accessed | tf_op | source)
XLA Modules:
  0.0 25.1 jit_solution(11987496642002134483)
XLA Ops:
  0.0 1.2 %shard_map.100 = (bf16[216,128]{1,0:T(8,128)(2,1)S(1)}, bf16[216,128]{1,0:T(8,128)(2,1)S(1)}, bf16[216,128]{1,0:T(8,128)(2,1)S(1)}, bf16[216,128]{1,0:T(8,128)(2,1)S(1)}, bf16[1,128,128]{2,1,0:T(8,128)(2,1)S(1)}) custom-call(s32[1,4]{1,0:T(1,128)} %refs_0_.1, bf16[32,384]{1,0:T(8,128)(2,1)} %refs_1_.1, f32[1,1024]{1,0:T(1,128)} %bitcast.4, ...), custom_call_target="tpu_custom_call" | custom-call | tf_op jit(solution)/shard_map/pallas_call | solution.py:250
  1.2 4.1 %collective-permute-start = (bf16[216,128]{1,0:T(8,128)(2,1)S(1)}, bf16[216,128]{1,0:T(8,128)(2,1)S(1)}, u32[]{:S(2)}, u32[]{:S(2)}) collective-permute-start(bf16[216,128]{1,0:T(8,128)(2,1)S(1)} %get-tuple-element.31), channel_id=1, source_target_pairs={{0,2},{1,3},{2,0},{3,1},{4,6},{5,7},{6,4},{7,5},{8,10},{9,11},{10,... | collective-permute-start | bytes 165896 | tf_op jit(solution)/shard_map/ppermute | solution.py:34
  5.3 1.3 %collective-permute-start.1 = (bf16[216,128]{1,0:T(8,128)(2,1)S(1)}, bf16[216,128]{1,0:T(8,128)(2,1)S(1)}, u32[]{:S(2)}, u32[]{:S(2)}) collective-permute-start(bf16[216,128]{1,0:T(8,128)(2,1)S(1)} %get-tuple-element.32), channel_id=1, source_target_pairs={{0,3},{1,2},{2,1},{3,0},{4,7},{5,6},{6,5},{7,4},{8,11},{9,10},{10,... | collective-permute-start | bytes 165896 | tf_op jit(solution)/shard_map/ppermute | solution.py:34
  6.7 0.2 collective-permute-start.2
  6.9 1.5 %collective-permute-start.3 = (bf16[1,128,128]{2,1,0:T(8,128)(2,1)S(1)}, bf16[1,128,128]{2,1,0:T(8,128)(2,1)S(1)}, u32[]{:S(2)}, u32[]{:S(2)}) collective-permute-start(bf16[1,128,128]{2,1,0:T(8,128)(2,1)S(1)} %get-tuple-element.34), channel_id=1, source_target_pairs={{0,8},{4,12},{8,0},{12,4},{1,9},{5,13},{9,1},{13,5},{2,10},{6,14},... | collective-permute-start | bytes 98312 | tf_op jit(solution)/shard_map/ppermute | solution.py:34
  8.4 2.4 %collective-permute-done.3.refs_2_ = bf16[1,128,128]{2,1,0:T(8,128)(2,1)S(1)} collective-permute-done((bf16[1,128,128]{2,1,0:T(8,128)(2,1)S(1)}, bf16[1,128,128]{2,1,0:T(8,128)(2,1)S(1)}, u32[]{:S(2)}, u32[]{:S(2)}) %collective-permute-start.3) | collective-permute-done | bytes 32800 | tf_op jit(solution)/shard_map/ppermute | solution.py:34
  10.8 0.0 collective-permute-done.refs_1_
  10.8 0.6 %collective-permute-done.1.refs_2_ = bf16[216,128]{1,0:T(8,128)(2,1)S(1)} collective-permute-done((bf16[216,128]{1,0:T(8,128)(2,1)S(1)}, bf16[216,128]{1,0:T(8,128)(2,1)S(1)}, u32[]{:S(2)}, u32[]{:S(2)}) %collective-permute-start.1) | collective-permute-done | bytes 55328 | tf_op jit(solution)/shard_map/ppermute | solution.py:34
  11.4 0.0 collective-permute-done.2.refs_3_
  11.4 0.0 copy-start.1
  11.5 1.6 %collective-permute-start.4 = (bf16[3,128,128]{2,1,0:T(8,128)(2,1)S(1)}, bf16[3,128,128]{2,1,0:T(8,128)(2,1)S(1)}, u32[]{:S(2)}, u32[]{:S(2)}) collective-permute-start(bf16[3,128,128]{2,1,0:T(8,128)(2,1)S(1)} %get-tuple-element.39), channel_id=1, source_target_pairs={{0,8},{4,12},{8,0},{12,4},{1,9},{5,13},{9,1},{13,5},{2,10},{6,14},... | collective-permute-start | bytes 294920 | tf_op jit(solution)/shard_map/ppermute | solution.py:34
  13.0 0.0 collective-permute-start.7
  13.0 0.5 %collective-permute-start.5 = (bf16[1,128,128]{2,1,0:T(8,128)(2,1)S(1)}, bf16[1,128,128]{2,1,0:T(8,128)(2,1)S(1)}, u32[]{:S(2)}, u32[]{:S(2)}) collective-permute-start(bf16[1,128,128]{2,1,0:T(8,128)(2,1)S(1)} %collective-permute-done.3.refs_2_), channel_id=1, source_target_pairs={{0,4},{4,0},{8,12},{12,8},{1,5},{5,1},{9,13},{13,9},{2,6},{6,2},{1... | collective-permute-start | bytes 98312 | tf_op jit(solution)/shard_map/ppermute | solution.py:34
  13.5 0.0 collective-permute-start.6
  14.2 0.0 copy-done.1
  14.2 0.0 copy-start
  14.2 1.1 %copy-done = bf16[384,1024]{1,0:T(8,128)(2,1)S(1)} copy-done((bf16[384,1024]{1,0:T(8,128)(2,1)S(1)}, bf16[384,1024]{1,0:T(8,128)(2,1)}, u32[]{:S(2)}) %copy-start) | copy-done | bytes 786456
  15.3 0.3 %shard_map.102 = f32[4,8,1024]{2,1,0:T(8,128)S(1)} custom-call(s32[1]{0:T(128)S(6)} %copy.11.layer_ref, bf16[384,1024]{1,0:T(8,128)(2,1)S(1)} %copy-done, f32[8,1024]{1,0:T(8,128)S(1)} %copy-done.1, bf16[216,128]{1,0:T(8,128)(2,1)S(1)} %get-tuple-element.35.refs_0_, bf16[216,128]{1,0:T(8,128)(2,1)S(1)} %collective-permute-done.refs_1_, ...), custom_call_target="tpu_custom_call" | custom-call | flops 25165824 | bytes 786432 | tf_op jit(solution)/shard_map/pallas_call | solution.py:250
  15.7 0.0 collective-permute-done.6.refs_1_.refs_4_
  15.7 0.0 collective-permute-done.5.refs_3_
  15.7 0.5 %collective-permute-done.4.refs_6_ = bf16[3,128,128]{2,1,0:T(8,128)(2,1)S(1)} collective-permute-done((bf16[3,128,128]{2,1,0:T(8,128)(2,1)S(1)}, bf16[3,128,128]{2,1,0:T(8,128)(2,1)S(1)}, u32[]{:S(2)}, u32[]{:S(2)}) %collective-permute-start.4) | collective-permute-done | bytes 98336 | tf_op jit(solution)/shard_map/ppermute | solution.py:34
  16.2 0.1 collective-permute-start.8
  16.3 0.0 collective-permute-done.7.refs_5_
  16.3 0.5 %shard_map.103 = (f32[2,128,128]{2,1,0:T(8,128)S(1)}, f32[2,128,128]{2,1,0:T(8,128)S(1)}, f32[2,128,128]{2,1,0:T(8,128)S(1)}) custom-call(bf16[3,64,128]{2,1,0:T(8,128)(2,1)S(1)} %get-tuple-element.43.refs_0_.refs_3_, bf16[1,64,128]{2,1,0:T(8,128)(2,1)S(1)} %collective-permute-done.6.refs_1_.refs_4_, ...), custom_call_target="tpu_custom_call" | custom-call | flops 54525952 | bytes 425984 | tf_op jit(solution)/shard_map/pallas_call | solution.py:250
  16.8 0.7 %collective-permute-done.8.refs_5_ = bf16[3,128,128]{2,1,0:T(8,128)(2,1)S(1)} collective-permute-done((bf16[3,128,128]{2,1,0:T(8,128)(2,1)S(1)}, bf16[3,128,128]{2,1,0:T(8,128)(2,1)S(1)}, u32[]{:S(2)}, u32[]{:S(2)}) %collective-permute-start.8) | collective-permute-done | bytes 98336 | tf_op jit(solution)/shard_map/ppermute | solution.py:34
  17.5 0.4 %shard_map.104 = (bf16[64,128]{1,0:T(8,128)(2,1)S(1)}, f32[64,128]{1,0:T(8,128)S(1)}, bf16[128,128]{1,0:T(8,128)(2,1)S(1)}) custom-call(f32[2,128,128]{2,1,0:T(8,128)S(1)} %get-tuple-element.49.refs_0_, f32[2,128,128]{2,1,0:T(8,128)S(1)} %get-tuple-element.50.refs_1_, f32[2,128,128]{2,1,0:T(8,128)S(1)} %get-tuple-element.51.refs_2_, ...), custom_call_target="tpu_custom_call" | custom-call | flops 12582912 | bytes 98304 | tf_op jit(solution)/shard_map/pallas_call | solution.py:250
  17.9 2.3 %collective-permute-start.10 = (bf16[128,128]{1,0:T(8,128)(2,1)S(1)}, bf16[128,128]{1,0:T(8,128)(2,1)S(1)}, u32[]{:S(2)}, u32[]{:S(2)}) collective-permute-start(bf16[128,128]{1,0:T(8,128)(2,1)S(1)} %get-tuple-element.54), channel_id=1, source_target_pairs={{0,2},{1,3},{2,0},{3,1},{4,7},{5,6},{6,5},{7,4},{8,10},{9,11},{10,... | collective-permute-start | bytes 98312 | tf_op jit(solution)/shard_map/ppermute | solution.py:272
  20.2 0.8 %collective-permute-start.9 = (f32[64,128]{1,0:T(8,128)S(1)}, f32[64,128]{1,0:T(8,128)S(1)}, u32[]{:S(2)}, u32[]{:S(2)}) collective-permute-start(f32[64,128]{1,0:T(8,128)S(1)} %get-tuple-element.53), channel_id=1, source_target_pairs={{0,1},{1,0},{2,3},{3,2},{4,5},{5,4},{6,7},{7,6},{8,9},{9,8},{10,11... | collective-permute-start | bytes 98312 | tf_op jit(solution)/shard_map/ppermute | solution.py:34
  21.0 2.2 %collective-permute-done.10.refs_0_ = bf16[128,128]{1,0:T(8,128)(2,1)S(1)} collective-permute-done((bf16[128,128]{1,0:T(8,128)(2,1)S(1)}, bf16[128,128]{1,0:T(8,128)(2,1)S(1)}, u32[]{:S(2)}, u32[]{:S(2)}) %collective-permute-start.10) | collective-permute-done | bytes 32800 | tf_op jit(solution)/shard_map/ppermute | solution.py:272
  23.2 0.0 collective-permute-start.11
  23.2 0.9 %collective-permute-done.9.near_ref = f32[64,128]{1,0:T(8,128)S(1)} collective-permute-done((f32[64,128]{1,0:T(8,128)S(1)}, f32[64,128]{1,0:T(8,128)S(1)}, u32[]{:S(2)}, u32[]{:S(2)}) %collective-permute-start.9) | collective-permute-done | bytes 32800 | tf_op jit(solution)/shard_map/ppermute | solution.py:34
  24.1 0.3 %collective-permute-done.11.refs_1_ = bf16[128,128]{1,0:T(8,128)(2,1)S(1)} collective-permute-done((bf16[128,128]{1,0:T(8,128)(2,1)S(1)}, bf16[128,128]{1,0:T(8,128)(2,1)S(1)}, u32[]{:S(2)}, u32[]{:S(2)}) %collective-permute-start.11) | collective-permute-done | bytes 32800 | tf_op jit(solution)/shard_map/ppermute | solution.py:34
  24.4 0.7 %shard_map.105 = bf16[32,1024]{1,0:T(8,128)(2,1)} custom-call(f32[32,1024]{1,0:T(8,128)S(1)} %bitcast.3, bf16[64,128]{1,0:T(8,128)(2,1)S(1)} %get-tuple-element.52.own_ref, f32[64,128]{1,0:T(8,128)S(1)} %collective-permute-done.9.near_ref, bf16[128,128]{1,0:T(8,128)(2,1)S(1)} %collective-permute-done.10.refs_0_, ...), custom_call_target="tpu_custom_call" | custom-call | tf_op jit(solution)/shard_map/pallas_call | solution.py:250
  (1 shorter events, 0.0 us)
Async XLA Ops:
  1.2 9.6 %collective-permute-start = (bf16[216,128]{1,0:T(8,128)(2,1)S(1)}, bf16[216,128]{1,0:T(8,128)(2,1)S(1)}, u32[]{:S(2)}, u32[]{:S(2)}) collective-permute-start(bf16[216,128]{1,0:T(8,128)(2,1)S(1)} %get-tuple-element.31), channel_id=1, source_target_pairs={{0,2},{1,3},{2,0},{3,1},{4,6},{5,7},{6,4},{7,5},{8,10},{9,11},{10,... | collective-permute-start | bytes 165896 | tf_op jit(solution)/shard_map/ppermute | solution.py:34
  5.3 6.1 %collective-permute-start.1 = (bf16[216,128]{1,0:T(8,128)(2,1)S(1)}, bf16[216,128]{1,0:T(8,128)(2,1)S(1)}, u32[]{:S(2)}, u32[]{:S(2)}) collective-permute-start(bf16[216,128]{1,0:T(8,128)(2,1)S(1)} %get-tuple-element.32), channel_id=1, source_target_pairs={{0,3},{1,2},{2,1},{3,0},{4,7},{5,6},{6,5},{7,4},{8,11},{9,10},{10,... | collective-permute-start | bytes 165896 | tf_op jit(solution)/shard_map/ppermute | solution.py:34
  6.7 4.7 %collective-permute-start.2 = (bf16[216,128]{1,0:T(8,128)(2,1)S(1)}, bf16[216,128]{1,0:T(8,128)(2,1)S(1)}, u32[]{:S(2)}, u32[]{:S(2)}) collective-permute-start(bf16[216,128]{1,0:T(8,128)(2,1)S(1)} %get-tuple-element.33), channel_id=1, source_target_pairs={{0,1},{1,0},{2,3},{3,2},{4,5},{5,4},{6,7},{7,6},{8,9},{9,8},{10,11... | collective-permute-start | bytes 165896 | tf_op jit(solution)/shard_map/ppermute | solution.py:34
  6.9 3.9 %collective-permute-start.3 = (bf16[1,128,128]{2,1,0:T(8,128)(2,1)S(1)}, bf16[1,128,128]{2,1,0:T(8,128)(2,1)S(1)}, u32[]{:S(2)}, u32[]{:S(2)}) collective-permute-start(bf16[1,128,128]{2,1,0:T(8,128)(2,1)S(1)} %get-tuple-element.34), channel_id=1, source_target_pairs={{0,8},{4,12},{8,0},{12,4},{1,9},{5,13},{9,1},{13,5},{2,10},{6,14},... | collective-permute-start | bytes 98312 | tf_op jit(solution)/shard_map/ppermute | solution.py:34
  11.4 2.8 %copy-start.1 = (f32[8,1024]{1,0:T(8,128)S(1)}, f32[8,1024]{1,0:T(8,128)}, u32[]{:S(2)}) copy-start(f32[8,1024]{1,0:T(8,128)} %gain_ref.1) | copy-start | bytes 98308
  11.5 4.7 %collective-permute-start.4 = (bf16[3,128,128]{2,1,0:T(8,128)(2,1)S(1)}, bf16[3,128,128]{2,1,0:T(8,128)(2,1)S(1)}, u32[]{:S(2)}, u32[]{:S(2)}) collective-permute-start(bf16[3,128,128]{2,1,0:T(8,128)(2,1)S(1)} %get-tuple-element.39), channel_id=1, source_target_pairs={{0,8},{4,12},{8,0},{12,4},{1,9},{5,13},{9,1},{13,5},{2,10},{6,14},... | collective-permute-start | bytes 294920 | tf_op jit(solution)/shard_map/ppermute | solution.py:34
  13.0 3.2 %collective-permute-start.7 = (bf16[4,128,128]{2,1,0:T(8,128)(2,1)S(1)}, bf16[4,128,128]{2,1,0:T(8,128)(2,1)S(1)}, u32[]{:S(2)}, u32[]{:S(2)}) collective-permute-start(bf16[4,128,128]{2,1,0:T(8,128)(2,1)S(1)} %get-tuple-element.47.refs_4_), channel_id=1, source_target_pairs={{0,4},{4,0},{8,12},{12,8},{1,5},{5,1},{9,13},{13,9},{2,6},{6,2},{1... | collective-permute-start | bytes 393224 | tf_op jit(solution)/shard_map/ppermute | solution.py:34
  13.0 2.6 %collective-permute-start.5 = (bf16[1,128,128]{2,1,0:T(8,128)(2,1)S(1)}, bf16[1,128,128]{2,1,0:T(8,128)(2,1)S(1)}, u32[]{:S(2)}, u32[]{:S(2)}) collective-permute-start(bf16[1,128,128]{2,1,0:T(8,128)(2,1)S(1)} %collective-permute-done.3.refs_2_), channel_id=1, source_target_pairs={{0,4},{4,0},{8,12},{12,8},{1,5},{5,1},{9,13},{13,9},{2,6},{6,2},{1... | collective-permute-start | bytes 98312 | tf_op jit(solution)/shard_map/ppermute | solution.py:34
  13.5 2.1 %collective-permute-start.6 = (bf16[1,64,128]{2,1,0:T(8,128)(2,1)S(1)}, bf16[1,64,128]{2,1,0:T(8,128)(2,1)S(1)}, u32[]{:S(2)}, u32[]{:S(2)}) collective-permute-start(bf16[1,64,128]{2,1,0:T(8,128)(2,1)S(1)} %get-tuple-element.41), channel_id=1, source_target_pairs={{0,4},{4,0},{8,12},{12,8},{1,5},{5,1},{9,13},{13,9},{2,6},{6,2},{1... | collective-permute-start | bytes 49160 | tf_op jit(solution)/shard_map/ppermute | solution.py:34
  14.2 1.1 %copy-start = (bf16[384,1024]{1,0:T(8,128)(2,1)S(1)}, bf16[384,1024]{1,0:T(8,128)(2,1)}, u32[]{:S(2)}) copy-start(bf16[384,1024]{1,0:T(8,128)(2,1)} %weight_ref.1) | copy-start | bytes 2359300
  16.2 1.3 %collective-permute-start.8 = (bf16[3,128,128]{2,1,0:T(8,128)(2,1)S(1)}, bf16[3,128,128]{2,1,0:T(8,128)(2,1)S(1)}, u32[]{:S(2)}, u32[]{:S(2)}) collective-permute-start(bf16[3,128,128]{2,1,0:T(8,128)(2,1)S(1)} %collective-permute-done.4.refs_6_), channel_id=1, source_target_pairs={{0,4},{4,0},{8,12},{12,8},{1,5},{5,1},{9,13},{13,9},{2,6},{6,2},{1... | collective-permute-start | bytes 294920 | tf_op jit(solution)/shard_map/ppermute | solution.py:34
  17.9 5.3 %collective-permute-start.10 = (bf16[128,128]{1,0:T(8,128)(2,1)S(1)}, bf16[128,128]{1,0:T(8,128)(2,1)S(1)}, u32[]{:S(2)}, u32[]{:S(2)}) collective-permute-start(bf16[128,128]{1,0:T(8,128)(2,1)S(1)} %get-tuple-element.54), channel_id=1, source_target_pairs={{0,2},{1,3},{2,0},{3,1},{4,7},{5,6},{6,5},{7,4},{8,10},{9,11},{10,... | collective-permute-start | bytes 98312 | tf_op jit(solution)/shard_map/ppermute | solution.py:272
  20.2 3.9 %collective-permute-start.9 = (f32[64,128]{1,0:T(8,128)S(1)}, f32[64,128]{1,0:T(8,128)S(1)}, u32[]{:S(2)}, u32[]{:S(2)}) collective-permute-start(f32[64,128]{1,0:T(8,128)S(1)} %get-tuple-element.53), channel_id=1, source_target_pairs={{0,1},{1,0},{2,3},{3,2},{4,5},{5,4},{6,7},{7,6},{8,9},{9,8},{10,11... | collective-permute-start | bytes 98312 | tf_op jit(solution)/shard_map/ppermute | solution.py:34
  23.2 1.2 %collective-permute-start.11 = (bf16[128,128]{1,0:T(8,128)(2,1)S(1)}, bf16[128,128]{1,0:T(8,128)(2,1)S(1)}, u32[]{:S(2)}, u32[]{:S(2)}) collective-permute-start(bf16[128,128]{1,0:T(8,128)(2,1)S(1)} %collective-permute-done.10.refs_0_), channel_id=1, source_target_pairs={{0,4},{4,0},{8,12},{12,8},{1,5},{5,1},{9,13},{13,9},{2,6},{6,2},{1... | collective-permute-start | bytes 98312 | tf_op jit(solution)/shard_map/ppermute | solution.py:34

commit v18 on v16

--- a/solution.py
+++ b/solution.py
@@ -67,16 +67,15 @@
     norm_ref[0] = normed(k_ref[...], kg_ref[...]).astype(jnp.bfloat16)
     copies[4].wait()
     copies[5].wait()
-    norm_ref[2] = normed(q_ref[...], qg_ref[...]).astype(jnp.bfloat16)
+    norm_ref[1] = normed(q_ref[...], qg_ref[...]).astype(jnp.bfloat16)
     copies[6].wait()
-    norm_ref[1] = v_ref[...]
     for step, out_ref in zip(steps_in(owners), out_refs):
         to = partner(me, step)
         at = 0
         for i in range(3):
             for head in range(share // HEAD_DIM):
                 cols = pl.ds(pl.multiple_of(to * share + head * HEAD_DIM, HEAD_DIM), HEAD_DIM)
-                lines = norm_ref[i, :, cols]
+                lines = v_ref[:, cols] if i == 1 else norm_ref[i // 2, :, cols]
                 out_ref[at : at + rows] = lines
                 if step == 0 and i < 2:
                     own_ref[0, at : at + rows] = lines
@@ -310,7 +309,7 @@
             for source in sources
         ]
         + [
-            pltpu.VMEM((3, rows, feats), jnp.bfloat16),
+            pltpu.VMEM((2, rows, feats), jnp.bfloat16),
             pltpu.SemaphoreType.DMA((len(sources),)),
         ],
     )

time: 25.3 us -> 25.2 us (level)
  no operation moved by 1% of the time
where the time goes in v18:
time: 25.2 us; the launch traced here: 25 us
  starting transfers between devices  12.5 us (50%)
  waiting for transfers between devices  7.53 us (30%)
  Pallas kernels  3.13 us (12%)
  local copies, waits for them, and re-layouts  1.13 us (4%)
  between operations  0.73 us (3%)
    ppermute x11, starting transfers between devices, swap(): lax.ppermute(array, axis, [(i, partner(i, step)) for i in range(size)])  10.2 us
    ppermute x11, waiting for transfers between devices, swap(): lax.ppermute(array, axis, [(i, partner(i, step)) for i in range(size)])  5.37 us
    pallas_call x6, Pallas kernels, call(): pl.pallas_call(kernel, out_shape=out_shape, in_specs=specs, out_specs=jax...  3.13 us
    ppermute x1, starting transfers between devices, swap_far(): return lax.ppermute(array, ('blk', 'ulysses'), pairs)  2.3 us
    ppermute x1, waiting for transfers between devices, swap_far(): return lax.ppermute(array, ('blk', 'ulysses'), pairs)  2.16 us
    unnamed x4, local copies, waits for them, and re-layouts  1.13 us
  transfers between devices with their start and end apart: 12, of which 7 were waited for; matrix products, arithmetic and copies ran while one was open for 0% of the time, Pallas kernels for 3%

profile of v18, /device:TPU:0, one launch (start us, length us, event | category | flops | bytes accessed | tf_op | source)
XLA Modules:
  0.0 25.0 jit_solution(3493413932134705559)
XLA Ops:
  0.0 1.2 %shard_map.100 = (bf16[216,128]{1,0:T(8,128)(2,1)S(1)}, bf16[216,128]{1,0:T(8,128)(2,1)S(1)}, bf16[216,128]{1,0:T(8,128)(2,1)S(1)}, bf16[216,128]{1,0:T(8,128)(2,1)S(1)}, bf16[1,128,128]{2,1,0:T(8,128)(2,1)S(1)}) custom-call(s32[1,4]{1,0:T(1,128)} %refs_0_.1, bf16[32,384]{1,0:T(8,128)(2,1)} %refs_1_.1, f32[1,1024]{1,0:T(1,128)} %bitcast.4, ...), custom_call_target="tpu_custom_call" | custom-call | tf_op jit(solution)/shard_map/pallas_call | solution.py:239
  1.2 4.1 %collective-permute-start = (bf16[216,128]{1,0:T(8,128)(2,1)S(1)}, bf16[216,128]{1,0:T(8,128)(2,1)S(1)}, u32[]{:S(2)}, u32[]{:S(2)}) collective-permute-start(bf16[216,128]{1,0:T(8,128)(2,1)S(1)} %get-tuple-element.31), channel_id=1, source_target_pairs={{0,2},{1,3},{2,0},{3,1},{4,6},{5,7},{6,4},{7,5},{8,10},{9,11},{10,... | collective-permute-start | bytes 165896 | tf_op jit(solution)/shard_map/ppermute | solution.py:34
  5.3 1.3 %collective-permute-start.1 = (bf16[216,128]{1,0:T(8,128)(2,1)S(1)}, bf16[216,128]{1,0:T(8,128)(2,1)S(1)}, u32[]{:S(2)}, u32[]{:S(2)}) collective-permute-start(bf16[216,128]{1,0:T(8,128)(2,1)S(1)} %get-tuple-element.32), channel_id=1, source_target_pairs={{0,3},{1,2},{2,1},{3,0},{4,7},{5,6},{6,5},{7,4},{8,11},{9,10},{10,... | collective-permute-start | bytes 165896 | tf_op jit(solution)/shard_map/ppermute | solution.py:34
  6.7 0.2 collective-permute-start.2
  6.9 1.5 %collective-permute-start.3 = (bf16[1,128,128]{2,1,0:T(8,128)(2,1)S(1)}, bf16[1,128,128]{2,1,0:T(8,128)(2,1)S(1)}, u32[]{:S(2)}, u32[]{:S(2)}) collective-permute-start(bf16[1,128,128]{2,1,0:T(8,128)(2,1)S(1)} %get-tuple-element.34), channel_id=1, source_target_pairs={{0,8},{4,12},{8,0},{12,4},{1,9},{5,13},{9,1},{13,5},{2,10},{6,14},... | collective-permute-start | bytes 98312 | tf_op jit(solution)/shard_map/ppermute | solution.py:34
  8.4 2.4 %collective-permute-done.3.refs_2_ = bf16[1,128,128]{2,1,0:T(8,128)(2,1)S(1)} collective-permute-done((bf16[1,128,128]{2,1,0:T(8,128)(2,1)S(1)}, bf16[1,128,128]{2,1,0:T(8,128)(2,1)S(1)}, u32[]{:S(2)}, u32[]{:S(2)}) %collective-permute-start.3) | collective-permute-done | bytes 32800 | tf_op jit(solution)/shard_map/ppermute | solution.py:34
  10.8 0.0 collective-permute-done.refs_1_
  10.8 0.6 %collective-permute-done.1.refs_2_ = bf16[216,128]{1,0:T(8,128)(2,1)S(1)} collective-permute-done((bf16[216,128]{1,0:T(8,128)(2,1)S(1)}, bf16[216,128]{1,0:T(8,128)(2,1)S(1)}, u32[]{:S(2)}, u32[]{:S(2)}) %collective-permute-start.1) | collective-permute-done | bytes 55328 | tf_op jit(solution)/shard_map/ppermute | solution.py:34
  11.4 0.0 collective-permute-done.2.refs_3_
  11.4 0.0 copy-start.1
  11.5 1.6 %collective-permute-start.4 = (bf16[3,128,128]{2,1,0:T(8,128)(2,1)S(1)}, bf16[3,128,128]{2,1,0:T(8,128)(2,1)S(1)}, u32[]{:S(2)}, u32[]{:S(2)}) collective-permute-start(bf16[3,128,128]{2,1,0:T(8,128)(2,1)S(1)} %get-tuple-element.39), channel_id=1, source_target_pairs={{0,8},{4,12},{8,0},{12,4},{1,9},{5,13},{9,1},{13,5},{2,10},{6,14},... | collective-permute-start | bytes 294920 | tf_op jit(solution)/shard_map/ppermute | solution.py:34
  13.0 0.0 collective-permute-start.7
  13.0 0.5 %collective-permute-start.5 = (bf16[1,128,128]{2,1,0:T(8,128)(2,1)S(1)}, bf16[1,128,128]{2,1,0:T(8,128)(2,1)S(1)}, u32[]{:S(2)}, u32[]{:S(2)}) collective-permute-start(bf16[1,128,128]{2,1,0:T(8,128)(2,1)S(1)} %collective-permute-done.3.refs_2_), channel_id=1, source_target_pairs={{0,4},{4,0},{8,12},{12,8},{1,5},{5,1},{9,13},{13,9},{2,6},{6,2},{1... | collective-permute-start | bytes 98312 | tf_op jit(solution)/shard_map/ppermute | solution.py:34
  13.5 0.0 collective-permute-start.6
  14.2 0.0 copy-done.1
  14.2 0.0 copy-start
  14.2 1.1 %copy-done = bf16[384,1024]{1,0:T(8,128)(2,1)S(1)} copy-done((bf16[384,1024]{1,0:T(8,128)(2,1)S(1)}, bf16[384,1024]{1,0:T(8,128)(2,1)}, u32[]{:S(2)}) %copy-start) | copy-done | bytes 786456
  15.3 0.3 %shard_map.102 = f32[4,8,1024]{2,1,0:T(8,128)S(1)} custom-call(s32[1]{0:T(128)S(6)} %copy.11.layer_ref, bf16[384,1024]{1,0:T(8,128)(2,1)S(1)} %copy-done, f32[8,1024]{1,0:T(8,128)S(1)} %copy-done.1, bf16[216,128]{1,0:T(8,128)(2,1)S(1)} %get-tuple-element.35.refs_0_, bf16[216,128]{1,0:T(8,128)(2,1)S(1)} %collective-permute-done.refs_1_, ...), custom_call_target="tpu_custom_call" | custom-call | flops 25165824 | bytes 786432 | tf_op jit(solution)/shard_map/pallas_call | solution.py:239
  15.7 0.0 collective-permute-done.6.refs_1_.refs_4_
  15.7 0.0 collective-permute-done.5.refs_3_
  15.7 0.5 %collective-permute-done.4.refs_6_ = bf16[3,128,128]{2,1,0:T(8,128)(2,1)S(1)} collective-permute-done((bf16[3,128,128]{2,1,0:T(8,128)(2,1)S(1)}, bf16[3,128,128]{2,1,0:T(8,128)(2,1)S(1)}, u32[]{:S(2)}, u32[]{:S(2)}) %collective-permute-start.4) | collective-permute-done | bytes 98336 | tf_op jit(solution)/shard_map/ppermute | solution.py:34
  16.1 0.1 collective-permute-start.8
  16.3 0.0 collective-permute-done.7.refs_5_
  16.3 0.5 %shard_map.103 = (f32[2,128,128]{2,1,0:T(8,128)S(1)}, f32[2,128,128]{2,1,0:T(8,128)S(1)}, f32[2,128,128]{2,1,0:T(8,128)S(1)}) custom-call(bf16[3,64,128]{2,1,0:T(8,128)(2,1)S(1)} %get-tuple-element.43.refs_0_.refs_3_, bf16[1,64,128]{2,1,0:T(8,128)(2,1)S(1)} %collective-permute-done.6.refs_1_.refs_4_, ...), custom_call_target="tpu_custom_call" | custom-call | flops 54525952 | bytes 425984 | tf_op jit(solution)/shard_map/pallas_call | solution.py:239
  16.8 0.7 %collective-permute-done.8.refs_5_ = bf16[3,128,128]{2,1,0:T(8,128)(2,1)S(1)} collective-permute-done((bf16[3,128,128]{2,1,0:T(8,128)(2,1)S(1)}, bf16[3,128,128]{2,1,0:T(8,128)(2,1)S(1)}, u32[]{:S(2)}, u32[]{:S(2)}) %collective-permute-start.8) | collective-permute-done | bytes 98336 | tf_op jit(solution)/shard_map/ppermute | solution.py:34
  17.4 0.4 %shard_map.104 = (bf16[64,128]{1,0:T(8,128)(2,1)S(1)}, f32[64,128]{1,0:T(8,128)S(1)}, bf16[128,128]{1,0:T(8,128)(2,1)S(1)}) custom-call(f32[2,128,128]{2,1,0:T(8,128)S(1)} %get-tuple-element.49.refs_0_, f32[2,128,128]{2,1,0:T(8,128)S(1)} %get-tuple-element.50.refs_1_, f32[2,128,128]{2,1,0:T(8,128)S(1)} %get-tuple-element.51.refs_2_, ...), custom_call_target="tpu_custom_call" | custom-call | flops 12582912 | bytes 98304 | tf_op jit(solution)/shard_map/pallas_call | solution.py:239
  17.9 2.3 %collective-permute-start.10 = (bf16[128,128]{1,0:T(8,128)(2,1)S(1)}, bf16[128,128]{1,0:T(8,128)(2,1)S(1)}, u32[]{:S(2)}, u32[]{:S(2)}) collective-permute-start(bf16[128,128]{1,0:T(8,128)(2,1)S(1)} %get-tuple-element.54), channel_id=1, source_target_pairs={{0,2},{1,3},{2,0},{3,1},{4,7},{5,6},{6,5},{7,4},{8,10},{9,11},{10,... | collective-permute-start | bytes 98312 | tf_op jit(solution)/shard_map/ppermute | solution.py:261
  20.2 0.9 %collective-permute-start.9 = (f32[64,128]{1,0:T(8,128)S(1)}, f32[64,128]{1,0:T(8,128)S(1)}, u32[]{:S(2)}, u32[]{:S(2)}) collective-permute-start(f32[64,128]{1,0:T(8,128)S(1)} %get-tuple-element.53), channel_id=1, source_target_pairs={{0,1},{1,0},{2,3},{3,2},{4,5},{5,4},{6,7},{7,6},{8,9},{9,8},{10,11... | collective-permute-start | bytes 98312 | tf_op jit(solution)/shard_map/ppermute | solution.py:34
  21.0 2.2 %collective-permute-done.10.refs_0_ = bf16[128,128]{1,0:T(8,128)(2,1)S(1)} collective-permute-done((bf16[128,128]{1,0:T(8,128)(2,1)S(1)}, bf16[128,128]{1,0:T(8,128)(2,1)S(1)}, u32[]{:S(2)}, u32[]{:S(2)}) %collective-permute-start.10) | collective-permute-done | bytes 32800 | tf_op jit(solution)/shard_map/ppermute | solution.py:261
  23.2 0.0 collective-permute-start.11
  23.2 0.9 %collective-permute-done.9.near_ref = f32[64,128]{1,0:T(8,128)S(1)} collective-permute-done((f32[64,128]{1,0:T(8,128)S(1)}, f32[64,128]{1,0:T(8,128)S(1)}, u32[]{:S(2)}, u32[]{:S(2)}) %collective-permute-start.9) | collective-permute-done | bytes 32800 | tf_op jit(solution)/shard_map/ppermute | solution.py:34
  24.1 0.3 %collective-permute-done.11.refs_1_ = bf16[128,128]{1,0:T(8,128)(2,1)S(1)} collective-permute-done((bf16[128,128]{1,0:T(8,128)(2,1)S(1)}, bf16[128,128]{1,0:T(8,128)(2,1)S(1)}, u32[]{:S(2)}, u32[]{:S(2)}) %collective-permute-start.11) | collective-permute-done | bytes 32800 | tf_op jit(solution)/shard_map/ppermute | solution.py:34
  24.4 0.7 %shard_map.105 = bf16[32,1024]{1,0:T(8,128)(2,1)} custom-call(f32[32,1024]{1,0:T(8,128)S(1)} %bitcast.3, bf16[64,128]{1,0:T(8,128)(2,1)S(1)} %get-tuple-element.52.own_ref, f32[64,128]{1,0:T(8,128)S(1)} %collective-permute-done.9.near_ref, bf16[128,128]{1,0:T(8,128)(2,1)S(1)} %collective-permute-done.10.refs_0_, ...), custom_call_target="tpu_custom_call" | custom-call | tf_op jit(solution)/shard_map/pallas_call | solution.py:239
  (1 shorter events, 0.0 us)
Async XLA Ops:
  1.2 9.6 %collective-permute-start = (bf16[216,128]{1,0:T(8,128)(2,1)S(1)}, bf16[216,128]{1,0:T(8,128)(2,1)S(1)}, u32[]{:S(2)}, u32[]{:S(2)}) collective-permute-start(bf16[216,128]{1,0:T(8,128)(2,1)S(1)} %get-tuple-element.31), channel_id=1, source_target_pairs={{0,2},{1,3},{2,0},{3,1},{4,6},{5,7},{6,4},{7,5},{8,10},{9,11},{10,... | collective-permute-start | bytes 165896 | tf_op jit(solution)/shard_map/ppermute | solution.py:34
  5.3 6.1 %collective-permute-start.1 = (bf16[216,128]{1,0:T(8,128)(2,1)S(1)}, bf16[216,128]{1,0:T(8,128)(2,1)S(1)}, u32[]{:S(2)}, u32[]{:S(2)}) collective-permute-start(bf16[216,128]{1,0:T(8,128)(2,1)S(1)} %get-tuple-element.32), channel_id=1, source_target_pairs={{0,3},{1,2},{2,1},{3,0},{4,7},{5,6},{6,5},{7,4},{8,11},{9,10},{10,... | collective-permute-start | bytes 165896 | tf_op jit(solution)/shard_map/ppermute | solution.py:34
  6.7 4.7 %collective-permute-start.2 = (bf16[216,128]{1,0:T(8,128)(2,1)S(1)}, bf16[216,128]{1,0:T(8,128)(2,1)S(1)}, u32[]{:S(2)}, u32[]{:S(2)}) collective-permute-start(bf16[216,128]{1,0:T(8,128)(2,1)S(1)} %get-tuple-element.33), channel_id=1, source_target_pairs={{0,1},{1,0},{2,3},{3,2},{4,5},{5,4},{6,7},{7,6},{8,9},{9,8},{10,11... | collective-permute-start | bytes 165896 | tf_op jit(solution)/shard_map/ppermute | solution.py:34
  6.9 3.9 %collective-permute-start.3 = (bf16[1,128,128]{2,1,0:T(8,128)(2,1)S(1)}, bf16[1,128,128]{2,1,0:T(8,128)(2,1)S(1)}, u32[]{:S(2)}, u32[]{:S(2)}) collective-permute-start(bf16[1,128,128]{2,1,0:T(8,128)(2,1)S(1)} %get-tuple-element.34), channel_id=1, source_target_pairs={{0,8},{4,12},{8,0},{12,4},{1,9},{5,13},{9,1},{13,5},{2,10},{6,14},... | collective-permute-start | bytes 98312 | tf_op jit(solution)/shard_map/ppermute | solution.py:34
  11.4 2.8 %copy-start.1 = (f32[8,1024]{1,0:T(8,128)S(1)}, f32[8,1024]{1,0:T(8,128)}, u32[]{:S(2)}) copy-start(f32[8,1024]{1,0:T(8,128)} %gain_ref.1) | copy-start | bytes 98308
  11.5 4.7 %collective-permute-start.4 = (bf16[3,128,128]{2,1,0:T(8,128)(2,1)S(1)}, bf16[3,128,128]{2,1,0:T(8,128)(2,1)S(1)}, u32[]{:S(2)}, u32[]{:S(2)}) collective-permute-start(bf16[3,128,128]{2,1,0:T(8,128)(2,1)S(1)} %get-tuple-element.39), channel_id=1, source_target_pairs={{0,8},{4,12},{8,0},{12,4},{1,9},{5,13},{9,1},{13,5},{2,10},{6,14},... | collective-permute-start | bytes 294920 | tf_op jit(solution)/shard_map/ppermute | solution.py:34
  13.0 3.2 %collective-permute-start.7 = (bf16[4,128,128]{2,1,0:T(8,128)(2,1)S(1)}, bf16[4,128,128]{2,1,0:T(8,128)(2,1)S(1)}, u32[]{:S(2)}, u32[]{:S(2)}) collective-permute-start(bf16[4,128,128]{2,1,0:T(8,128)(2,1)S(1)} %get-tuple-element.47.refs_4_), channel_id=1, source_target_pairs={{0,4},{4,0},{8,12},{12,8},{1,5},{5,1},{9,13},{13,9},{2,6},{6,2},{1... | collective-permute-start | bytes 393224 | tf_op jit(solution)/shard_map/ppermute | solution.py:34
  13.0 2.6 %collective-permute-start.5 = (bf16[1,128,128]{2,1,0:T(8,128)(2,1)S(1)}, bf16[1,128,128]{2,1,0:T(8,128)(2,1)S(1)}, u32[]{:S(2)}, u32[]{:S(2)}) collective-permute-start(bf16[1,128,128]{2,1,0:T(8,128)(2,1)S(1)} %collective-permute-done.3.refs_2_), channel_id=1, source_target_pairs={{0,4},{4,0},{8,12},{12,8},{1,5},{5,1},{9,13},{13,9},{2,6},{6,2},{1... | collective-permute-start | bytes 98312 | tf_op jit(solution)/shard_map/ppermute | solution.py:34
  13.5 2.1 %collective-permute-start.6 = (bf16[1,64,128]{2,1,0:T(8,128)(2,1)S(1)}, bf16[1,64,128]{2,1,0:T(8,128)(2,1)S(1)}, u32[]{:S(2)}, u32[]{:S(2)}) collective-permute-start(bf16[1,64,128]{2,1,0:T(8,128)(2,1)S(1)} %get-tuple-element.41), channel_id=1, source_target_pairs={{0,4},{4,0},{8,12},{12,8},{1,5},{5,1},{9,13},{13,9},{2,6},{6,2},{1... | collective-permute-start | bytes 49160 | tf_op jit(solution)/shard_map/ppermute | solution.py:34
  14.2 1.1 %copy-start = (bf16[384,1024]{1,0:T(8,128)(2,1)S(1)}, bf16[384,1024]{1,0:T(8,128)(2,1)}, u32[]{:S(2)}) copy-start(bf16[384,1024]{1,0:T(8,128)(2,1)} %weight_ref.1) | copy-start | bytes 2359300
  16.1 1.3 %collective-permute-start.8 = (bf16[3,128,128]{2,1,0:T(8,128)(2,1)S(1)}, bf16[3,128,128]{2,1,0:T(8,128)(2,1)S(1)}, u32[]{:S(2)}, u32[]{:S(2)}) collective-permute-start(bf16[3,128,128]{2,1,0:T(8,128)(2,1)S(1)} %collective-permute-done.4.refs_6_), channel_id=1, source_target_pairs={{0,4},{4,0},{8,12},{12,8},{1,5},{5,1},{9,13},{13,9},{2,6},{6,2},{1... | collective-permute-start | bytes 294920 | tf_op jit(solution)/shard_map/ppermute | solution.py:34
  17.9 5.3 %collective-permute-start.10 = (bf16[128,128]{1,0:T(8,128)(2,1)S(1)}, bf16[128,128]{1,0:T(8,128)(2,1)S(1)}, u32[]{:S(2)}, u32[]{:S(2)}) collective-permute-start(bf16[128,128]{1,0:T(8,128)(2,1)S(1)} %get-tuple-element.54), channel_id=1, source_target_pairs={{0,2},{1,3},{2,0},{3,1},{4,7},{5,6},{6,5},{7,4},{8,10},{9,11},{10,... | collective-permute-start | bytes 98312 | tf_op jit(solution)/shard_map/ppermute | solution.py:261
  20.2 3.9 %collective-permute-start.9 = (f32[64,128]{1,0:T(8,128)S(1)}, f32[64,128]{1,0:T(8,128)S(1)}, u32[]{:S(2)}, u32[]{:S(2)}) collective-permute-start(f32[64,128]{1,0:T(8,128)S(1)} %get-tuple-element.53), channel_id=1, source_target_pairs={{0,1},{1,0},{2,3},{3,2},{4,5},{5,4},{6,7},{7,6},{8,9},{9,8},{10,11... | collective-permute-start | bytes 98312 | tf_op jit(solution)/shard_map/ppermute | solution.py:34
  23.2 1.2 %collective-permute-start.11 = (bf16[128,128]{1,0:T(8,128)(2,1)S(1)}, bf16[128,128]{1,0:T(8,128)(2,1)S(1)}, u32[]{:S(2)}, u32[]{:S(2)}) collective-permute-start(bf16[128,128]{1,0:T(8,128)(2,1)S(1)} %collective-permute-done.10.refs_0_), channel_id=1, source_target_pairs={{0,4},{4,0},{8,12},{12,8},{1,5},{5,1},{9,13},{13,9},{2,6},{6,2},{1... | collective-permute-start | bytes 98312 | tf_op jit(solution)/shard_map/ppermute | solution.py:34
